TPU v7x, 32 devices: a whole 2x2x4 slice. The times are simulated.
32 devices in a mesh: group: 8 (over y, x, core), dp: 4 (over z).
Axes of the slice: x: 2, y: 2, z: 4, core: 2. Of those that a mesh axis runs over, the one named last changes fastest.
Arguments:
- latents: bfloat16 [8, 128, 6144], P('group', 'dp'), may hold values from -6 to 6
- steps: int32 [8], P('group'), may hold values from 0 to 15
- segment_ids: int32 [128], replicated, may hold values from 0 to 3, never falling along the last dimension, each value on 1 to 64 neighbouring positions
- mod_table: float32 [16, 2, 6144], replicated, may hold values from -3 to 3
- w_query: bfloat16 [6144, 1024], P(None, 'dp')
- w_key: bfloat16 [6144, 1024], P(None, 'dp')
- w_value: bfloat16 [6144, 1024], P(None, 'dp'), may hold values from -0.3125 to 0.3125
Outputs:
- attended: bfloat16 [8, 128, 1024], P('group', 'dp')
Inputs may be any that keep to these rules, and one draw needn't show every extreme that they name: `segment_ids`: rows of one clip are contiguous; every clip index occurs, a clip holds 1 to 64 rows and one holds exactly that many.
All inputs are finite; a program needn't handle non-finite values.
Results may differ from a plain program's by a relative error of at most 0.011.
Values may be sent and summed in bfloat16 or wider, within the bound.
No kernel may reach another device: no remote copies, remote signals or barrier semaphores. Data moves between devices by JAX's collectives and lax.ppermute only.
A program may use at most 128 MiB of HBM per device.

v0:
```python
import math

import jax
import jax.numpy as jnp
from jax import lax
from jax.sharding import PartitionSpec as P

D = 6144
HD = 128
HEAD_DEV = 2
STEPS = 16


def per_device(latents, steps, segment_ids, mod_table, w_query, w_key, w_value):
    rows_here = latents.shape[1]
    tokc = rows_here * lax.axis_size("dp")
    width = HEAD_DEV * HD
    x = latents[0].astype(jnp.float32)
    normed = x * lax.rsqrt(jnp.mean(x * x, axis=-1, keepdims=True) + 1e-06)
    picker = (steps[:, None] == jnp.arange(STEPS, dtype=jnp.int32)[None, :]).astype(jnp.float32)
    modulation = jnp.dot(picker, mod_table.reshape(STEPS, 2 * D), precision=lax.Precision.HIGHEST)
    modulated = (normed * (1.0 + modulation[:, :D]) + modulation[:, D:]).astype(jnp.bfloat16)
    piece = lax.all_gather(modulated, "dp", axis=0, tiled=True)
    first = jnp.dot(piece, w_query, preferred_element_type=jnp.float32).astype(jnp.bfloat16)
    second = jnp.dot(piece, w_key, preferred_element_type=jnp.float32).astype(jnp.bfloat16)
    third = jnp.dot(piece, w_value, preferred_element_type=jnp.float32).astype(jnp.bfloat16)
    projected = jnp.concatenate([first, second, third], axis=1)
    query = projected[:, :width].reshape(tokc, HEAD_DEV, HD)
    keys_own = projected[:, width : 2 * width]
    values_own = projected[:, 2 * width :]
    mine = lax.axis_index("group")
    same_clip = segment_ids[:, None] == segment_ids[None, :]
    inverse = 1.0 / math.sqrt(HD)

    def update(carry, key_block, value_block):
        best, total, accum = carry
        scores = (
            jnp.einsum(
                "thd,khd->htk",
                query,
                key_block.reshape(tokc, HEAD_DEV, HD),
                preferred_element_type=jnp.float32,
            )
            * inverse
        )
        scores = jnp.where(same_clip[None], scores, -1e30)
        new_best = jnp.maximum(best, jnp.max(scores, axis=-1))
        weights = jnp.where(same_clip[None], jnp.exp(scores - new_best[:, :, None]), 0.0)
        fade = jnp.exp(best - new_best)
        total = total * fade + jnp.sum(weights, axis=-1)
        added = jnp.einsum(
            "htk,khd->thd",
            weights.astype(jnp.bfloat16),
            value_block.reshape(tokc, HEAD_DEV, HD),
            preferred_element_type=jnp.float32,
        )
        accum = accum * jnp.transpose(fade)[:, :, None] + added
        return (new_best, total, accum)

    def visit(carry, key_block, value_block, source):
        usable = jnp.logical_and(source <= mine, source >= 0)
        return lax.cond(
            usable, lambda state: update(state, key_block, value_block), lambda state: state, carry
        )

    start_state = (
        jnp.full((HEAD_DEV, tokc), -1e30, jnp.float32),
        jnp.zeros((HEAD_DEV, tokc), jnp.float32),
        jnp.zeros((tokc, HEAD_DEV, HD), jnp.float32),
    )
    piece = (
        lax.all_gather(keys_own, "group", axis=0, tiled=True),
        lax.all_gather(values_own, "group", axis=0, tiled=True),
    )
    count = piece[0].shape[0] // tokc

    def single(index, state):
        key_block = lax.dynamic_slice_in_dim(piece[0], index * tokc, tokc, 0)
        value_block = lax.dynamic_slice_in_dim(piece[1], index * tokc, tokc, 0)
        return visit(state, key_block, value_block, index)

    carry = lax.fori_loop(0, count, single, start_state)
    best, total, accum = carry
    result = (accum / jnp.transpose(total)[:, :, None]).reshape(tokc, width).astype(jnp.bfloat16)
    regrouped = lax.all_to_all(result, "dp", split_axis=0, concat_axis=1, tiled=True)
    return regrouped[None]


def solution(mesh):
    placed = (
        P("group", "dp", None),
        P("group"),
        P(),
        P(),
        P(None, "dp"),
        P(None, "dp"),
        P(None, "dp"),
    )
    return jax.shard_map(
        per_device, mesh=mesh, in_specs=placed, out_specs=P("group", "dp", None), check_vma=False
    )
```

profile of v0, /device:TPU:7, one launch (start us, length us, event | category | flops | bytes accessed | tf_op | source)
XLA Modules:
  0.0 109.5 jit_solution(13010123446682388973)
XLA Ops:
  7.3 1.3 %fusion.14 = f32[32]{0:T(128)S(1)} fusion(bf16[1,32,6144]{2,1,0:T(8,128)(2,1)} %param.11), kind=kLoop, calls=%fused_computation.25 | loop fusion | flops 589792 | bytes 393344 | tf_op jit(solution)/shard_map/reduce_sum | solution.py:19
  8.7 1.6 %copy.29 = f32[2,8,2,6144]{3,1,2,0:T(8,128)S(1)} copy(f32[2,8,2,6144]{3,2,1,0:T(2,128)} %bitcast.48) | data formatting | bytes 1572864
  10.3 0.4 fusion.18
  10.7 0.9 fusion.17
  11.7 38.3 %all-gather.2.cloned.1.call-done = bf16[128,6144]{1,0:T(8,128)(2,1)} async-done(((bf16[32,6144]{1,0:T(8,128)(2,1)}), bf16[128,6144]{1,0:T(8,128)(2,1)}) %all-gather.2.cloned.1.call-update) | async-done | bytes 1572880 | tf_op jit(solution)/shard_map/all_gather | solution.py:23
  50.0 2.1 %fusion.13 = bf16[16,2,8,128]{3,2,1,0:T(8,128)(2,1)S(1)} fusion(bf16[128,6144]{1,0:T(8,128)(2,1)} %all-gather.2.cloned.1.call-done, bf16[6144,256]{1,0:T(8,128)(2,1)S(1)} %copy-done), kind=kOutput, calls=%fused_computation.22 | convolution fusion | flops 402685952 | bytes 4784128 | tf_op jit(solution)/shard_map/dot_general | solution.py:24
  52.1 0.7 copy-done.2
  52.8 0.6 convolution_convert_fusion.2
  53.4 10.6 %all_gather.10 = bf16[1024,256]{1,0:T(8,128)(2,1)} all-gather(bf16[128,256]{1,0:T(8,128)(2,1)S(1)} %convolution_convert_fusion.2), channel_id=1, replica_groups=mesh['group'=8,'dp'=4] {'group'}, dimensions={0}, use_global_device_ids=true | all-gather | bytes 589824 | tf_op jit(solution)/shard_map/all_gather | solution.py:72
  63.9 2.0 %copy.20 = bf16[1024,256]{0,1:T(8,128)(2,1)} copy(bf16[1024,256]{1,0:T(8,128)(2,1)} %all_gather.10) | data formatting | bytes 1048576
  66.0 3.0 %convolution_convert_fusion = bf16[128,256]{1,0:T(8,128)(2,1)S(1)} fusion(bf16[128,6144]{1,0:T(8,128)(2,1)} %all-gather.2.cloned.1.call-done, bf16[6144,256]{1,0:T(8,128)(2,1)} %param.17), kind=kOutput, calls=%fused_computation.19 | convolution fusion | flops 402685952 | bytes 4784128 | tf_op jit(solution)/shard_map/dot_general | solution.py:26
  69.0 10.8 %all_gather.11 = bf16[1024,256]{1,0:T(8,128)(2,1)} all-gather(bf16[128,256]{1,0:T(8,128)(2,1)S(1)} %convolution_convert_fusion), channel_id=1, replica_groups=mesh['group'=8,'dp'=4] {'group'}, dimensions={0}, use_global_device_ids=true | all-gather | bytes 589824 | tf_op jit(solution)/shard_map/all_gather | solution.py:73
  79.7 2.0 %copy.22 = bf16[1024,256]{0,1:T(8,128)(2,1)} copy(bf16[1024,256]{1,0:T(8,128)(2,1)} %all_gather.11) | data formatting | bytes 1048576
  81.8 13.0 %while.18 = (s32[]{:T(128)}, f32[2,128]{1,0:T(2,128)S(1)}, f32[2,128]{1,0:T(2,128)S(1)}, f32[128,2,128]{2,0,1:T(8,128)S(1)}, s32[]{:T(128)}, /*index=5*/bf16[102...) while((s32[]{:T(128)}, f32[2,128]{1,0:T(2,128)S(1)}, ...), condition=%wide.region_6.7_spmd.clone, body=%wide.region_1.6_spmd.clone.sunk | while | flops 17154824 | bytes 1197377 | solution.py:82
  81.8 1.6 %conditional.3 = ((f32[2,128]{1,0:T(2,128)S(1)}, f32[2,128]{1,0:T(2,128)S(1)}, f32[128,2,128]{2,0,1:T(8,128)S(1)})) conditional(s32[]{:T(128)} %convert_element_type.60, (f32[2,128]{1,0:T(2,128)S(1)}, f32[2,128]{1,0:T(2,128)S(1)}, f32[128,2,128]{2,0,1:T(8,128)S(1)}) %tuple.60, (s32[128]{0:T(128)S(1)}, s32[]{:T(128)}, bf16[1024,256]{0,1:T(8,128)(2,1)}, ...), branch_computations={%region_2.0_spmd, %region_3.5_spmd} | conditional | flops 17154820 | bytes 1197138 | solution.py:62
  81.9 0.9 constant_dynamic-slice_fusion
  82.8 0.2 fusion.23
  83.1 0.2 fusion.2
  83.4 1.6 %conditional.3 = ((f32[2,128]{1,0:T(2,128)S(1)}, f32[2,128]{1,0:T(2,128)S(1)}, f32[128,2,128]{2,0,1:T(8,128)S(1)})) conditional(s32[]{:T(128)} %convert_element_type.60, (f32[2,128]{1,0:T(2,128)S(1)}, f32[2,128]{1,0:T(2,128)S(1)}, f32[128,2,128]{2,0,1:T(8,128)S(1)}) %tuple.60, (s32[128]{0:T(128)S(1)}, s32[]{:T(128)}, bf16[1024,256]{0,1:T(8,128)(2,1)}, ...), branch_computations={%region_2.0_spmd, %region_3.5_spmd} | conditional | flops 17154820 | bytes 1197138 | solution.py:62
  83.5 0.9 constant_dynamic-slice_fusion
  84.4 0.2 fusion.23
  84.7 0.2 fusion.2
  85.0 1.6 %conditional.3 = ((f32[2,128]{1,0:T(2,128)S(1)}, f32[2,128]{1,0:T(2,128)S(1)}, f32[128,2,128]{2,0,1:T(8,128)S(1)})) conditional(s32[]{:T(128)} %convert_element_type.60, (f32[2,128]{1,0:T(2,128)S(1)}, f32[2,128]{1,0:T(2,128)S(1)}, f32[128,2,128]{2,0,1:T(8,128)S(1)}) %tuple.60, (s32[128]{0:T(128)S(1)}, s32[]{:T(128)}, bf16[1024,256]{0,1:T(8,128)(2,1)}, ...), branch_computations={%region_2.0_spmd, %region_3.5_spmd} | conditional | flops 17154820 | bytes 1197138 | solution.py:62
  85.1 0.9 constant_dynamic-slice_fusion
  86.0 0.2 fusion.23
  86.3 0.2 fusion.2
  86.7 1.6 %conditional.3 = ((f32[2,128]{1,0:T(2,128)S(1)}, f32[2,128]{1,0:T(2,128)S(1)}, f32[128,2,128]{2,0,1:T(8,128)S(1)})) conditional(s32[]{:T(128)} %convert_element_type.60, (f32[2,128]{1,0:T(2,128)S(1)}, f32[2,128]{1,0:T(2,128)S(1)}, f32[128,2,128]{2,0,1:T(8,128)S(1)}) %tuple.60, (s32[128]{0:T(128)S(1)}, s32[]{:T(128)}, bf16[1024,256]{0,1:T(8,128)(2,1)}, ...), branch_computations={%region_2.0_spmd, %region_3.5_spmd} | conditional | flops 17154820 | bytes 1197138 | solution.py:62
  86.8 0.9 constant_dynamic-slice_fusion
  87.7 0.2 fusion.23
  88.0 0.2 fusion.2
  88.3 1.6 %conditional.3 = ((f32[2,128]{1,0:T(2,128)S(1)}, f32[2,128]{1,0:T(2,128)S(1)}, f32[128,2,128]{2,0,1:T(8,128)S(1)})) conditional(s32[]{:T(128)} %convert_element_type.60, (f32[2,128]{1,0:T(2,128)S(1)}, f32[2,128]{1,0:T(2,128)S(1)}, f32[128,2,128]{2,0,1:T(8,128)S(1)}) %tuple.60, (s32[128]{0:T(128)S(1)}, s32[]{:T(128)}, bf16[1024,256]{0,1:T(8,128)(2,1)}, ...), branch_computations={%region_2.0_spmd, %region_3.5_spmd} | conditional | flops 17154820 | bytes 1197138 | solution.py:62
  88.4 0.9 constant_dynamic-slice_fusion
  89.3 0.2 fusion.23
  89.6 0.2 fusion.2
  89.9 1.6 %conditional.3 = ((f32[2,128]{1,0:T(2,128)S(1)}, f32[2,128]{1,0:T(2,128)S(1)}, f32[128,2,128]{2,0,1:T(8,128)S(1)})) conditional(s32[]{:T(128)} %convert_element_type.60, (f32[2,128]{1,0:T(2,128)S(1)}, f32[2,128]{1,0:T(2,128)S(1)}, f32[128,2,128]{2,0,1:T(8,128)S(1)}) %tuple.60, (s32[128]{0:T(128)S(1)}, s32[]{:T(128)}, bf16[1024,256]{0,1:T(8,128)(2,1)}, ...), branch_computations={%region_2.0_spmd, %region_3.5_spmd} | conditional | flops 17154820 | bytes 1197138 | solution.py:62
  90.0 0.9 constant_dynamic-slice_fusion
  90.9 0.2 fusion.23
  91.2 0.2 fusion.2
  91.5 1.6 %conditional.3 = ((f32[2,128]{1,0:T(2,128)S(1)}, f32[2,128]{1,0:T(2,128)S(1)}, f32[128,2,128]{2,0,1:T(8,128)S(1)})) conditional(s32[]{:T(128)} %convert_element_type.60, (f32[2,128]{1,0:T(2,128)S(1)}, f32[2,128]{1,0:T(2,128)S(1)}, f32[128,2,128]{2,0,1:T(8,128)S(1)}) %tuple.60, (s32[128]{0:T(128)S(1)}, s32[]{:T(128)}, bf16[1024,256]{0,1:T(8,128)(2,1)}, ...), branch_computations={%region_2.0_spmd, %region_3.5_spmd} | conditional | flops 17154820 | bytes 1197138 | solution.py:62
  91.6 0.9 constant_dynamic-slice_fusion
  92.5 0.2 fusion.23
  92.8 0.2 fusion.2
  93.1 1.6 %conditional.3 = ((f32[2,128]{1,0:T(2,128)S(1)}, f32[2,128]{1,0:T(2,128)S(1)}, f32[128,2,128]{2,0,1:T(8,128)S(1)})) conditional(s32[]{:T(128)} %convert_element_type.60, (f32[2,128]{1,0:T(2,128)S(1)}, f32[2,128]{1,0:T(2,128)S(1)}, f32[128,2,128]{2,0,1:T(8,128)S(1)}) %tuple.60, (s32[128]{0:T(128)S(1)}, s32[]{:T(128)}, bf16[1024,256]{0,1:T(8,128)(2,1)}, ...), branch_computations={%region_2.0_spmd, %region_3.5_spmd} | conditional | flops 17154820 | bytes 1197138 | solution.py:62
  93.2 0.9 constant_dynamic-slice_fusion
  94.1 0.2 fusion.23
  94.4 0.2 fusion.2
  95.0 7.0 %all_to_all.13 = bf16[4,32,256]{2,1,0:T(8,128)(2,1)S(1)} all-to-all(bf16[4,32,256]{2,1,0:T(8,128)(2,1)S(1)} %convert_element_type.47), channel_id=1, replica_groups=mesh['group'=8,'dp'=4] {'dp'}, dimensions={0} | all-to-all | bytes 131072 | tf_op jit(solution)/shard_map/all_to_all | solution.py:85
  102.0 0.7 broadcast_in_dim.55
  (61 shorter events, 1.7 us)
Async XLA Ops:
  6.5 43.4 %copy-start = (bf16[6144,256]{1,0:T(8,128)(2,1)S(1)}, bf16[6144,256]{1,0:T(8,128)(2,1)}, u32[]{:S(2)}) copy-start(bf16[6144,256]{1,0:T(8,128)(2,1)} %param.15) | copy-start | bytes 9437188
  6.5 43.4 %all-gather.2.cloned.1.call-start = ((), (), s32[]{:S(2)}) async-start(), calls=%async_computation.1 | async-start | bytes 1966080 | tf_op jit(solution)/shard_map/all_gather | solution.py:23
  6.5 4.1 %copy-start.3 = (bf16[1,32,6144]{2,1,0:T(8,128)(2,1)S(1)}, bf16[1,32,6144]{2,1,0:T(8,128)(2,1)}, u32[]{:S(2)}) copy-start(bf16[1,32,6144]{2,1,0:T(8,128)(2,1)} %param.11) | copy-start | bytes 1179652
  50.0 2.2 %copy-start.1 = (bf16[128,6144]{1,0:T(8,128)(2,1)S(1)}, bf16[128,6144]{1,0:T(8,128)(2,1)}, u32[]{:S(2)}) copy-start(bf16[128,6144]{1,0:T(8,128)(2,1)} %all-gather.2.cloned.1.call-done) | copy-start | bytes 4718596
  50.0 2.8 %copy-start.2 = (bf16[6144,256]{1,0:T(8,128)(2,1)S(1)}, bf16[6144,256]{1,0:T(8,128)(2,1)}, u32[]{:S(2)}) copy-start(bf16[6144,256]{1,0:T(8,128)(2,1)} %param.16) | copy-start | bytes 9437188
  66.0 15.8 %copy-start.4 = (s32[128]{0:T(128)S(1)}, s32[128]{0:T(128)}, u32[]{:S(2)}) copy-start(s32[128]{0:T(128)} %param.13) | copy-start | bytes 1540
Sparse Core Ops, SparseCore 0:
  11.8 38.1 all-gather.1
where the time goes:
time: 110 us
  waiting for transfers between devices  38.3 us (35%)
  blocking collectives  28.3 us (26%)
  local copies, waits for them, and re-layouts  14.4 us (13%)
  between operations  14.3 us (13%)
  matrix products  9.87 us (9%)
  other arithmetic  3.64 us (3%)
    all_gather x1, waiting for transfers between devices, per_device(): piece = lax.all_gather(modulated, 'dp', axis=0, tiled=True)  38.3 us
    all_gather x1, blocking collectives, per_device(): lax.all_gather(values_own, 'group', axis=0, tiled=True)  10.8 us
    all_gather x1, blocking collectives, per_device(): lax.all_gather(keys_own, 'group', axis=0, tiled=True)  10.6 us
    dynamic_slice x8, local copies, waits for them, and re-layouts, single(): value_block = lax.dynamic_slice_in_dim(piece[1], index * tokc, tokc, 0)  7.13 us
    all_to_all x1, blocking collectives, per_device(): lax.all_to_all(result, 'dp', split_axis=0, concat_axis=1, tiled=True)  6.96 us
    unnamed x13, local copies, waits for them, and re-layouts  6.37 us
    dot_general x1, matrix products, per_device(): jnp.dot(piece, w_value, preferred_element_type=jnp.float32)  2.95 us
  transfers between devices with their start and end apart: 1, of which 1 were waited for; matrix products, arithmetic and copies ran while one was open for 0% of the time, Pallas kernels for 0%

commit v1 on v0

v1 whole, which is shorter than its diff:
```python
import functools
import math

import jax
import jax.numpy as jnp
from jax import lax
from jax.experimental import pallas as pl
from jax.experimental.pallas import tpu as pltpu
from jax.sharding import PartitionSpec as P

HD = 128
CHUNKS = 2
VMEM = pltpu.MemorySpace.VMEM
BIG = 100 * 1024 * 1024 // 2


def params():
    return pltpu.CompilerParams(vmem_limit_bytes=BIG)


def modulate_kernel(steps, x_ref, table_ref, *outs):
    x = x_ref[...].astype(jnp.float32)
    scale = lax.rsqrt(jnp.mean(x * x, axis=-1, keepdims=True) + 1e-06)
    rows = (x * scale * (1.0 + table_ref[0, 0:1]) + table_ref[0, 1:2]).astype(jnp.bfloat16)
    width = outs[0].shape[1]
    for index, out in enumerate(outs):
        out[...] = rows[:, index * width : (index + 1) * width]


def modulate(latents, steps, mod_table):
    rows, depth = latents.shape
    width = depth // CHUNKS
    return pl.pallas_call(
        modulate_kernel,
        grid_spec=pltpu.PrefetchScalarGridSpec(
            num_scalar_prefetch=1,
            grid=(1,),
            in_specs=[
                pl.BlockSpec((rows, depth), lambda i, steps: (0, 0)),
                pl.BlockSpec((1, 2, depth), lambda i, steps: (steps[0], 0, 0)),
            ],
            out_specs=[pl.BlockSpec((rows, width), lambda i, steps: (0, 0))] * CHUNKS,
        ),
        out_shape=[jax.ShapeDtypeStruct((rows, width), jnp.bfloat16)] * CHUNKS,
        compiler_params=params(),
        name="modulate",
    )(steps, latents, mod_table)


def project_kernel(places, first, last, *refs):
    pieces, refs = refs[: len(places)], refs[len(places) :]
    weights, refs = refs[:3], refs[3:]
    if not first:
        start, refs = refs[0], refs[1:]
    width = weights[0].shape[1]
    depth = pieces[0].shape[1]
    for index, weight in enumerate(weights):
        total = None if first else start[:, index * width : (index + 1) * width]
        for place, piece in zip(places, pieces):
            part = jnp.dot(
                piece[...],
                weight[place * depth : (place + 1) * depth, :],
                preferred_element_type=jnp.float32,
            )
            total = part if total is None else total + part
        if not last:
            refs[0][:, index * width : (index + 1) * width] = total
        elif index == 0:
            refs[0][...] = total.astype(jnp.bfloat16)
        else:
            refs[1][:, (index - 1) * width : index * width] = total.astype(jnp.bfloat16)


def project(pieces, places, weights, start, last):
    rows = pieces[0].shape[0]
    width = weights[0].shape[1]
    if last:
        shapes = [
            jax.ShapeDtypeStruct((rows, width), jnp.bfloat16),
            jax.ShapeDtypeStruct((rows, 2 * width), jnp.bfloat16),
        ]
    else:
        shapes = [jax.ShapeDtypeStruct((rows, 3 * width), jnp.float32)]
    extra = [] if start is None else [start]
    whole = pl.BlockSpec(memory_space=VMEM)
    return pl.pallas_call(
        functools.partial(project_kernel, tuple(places), start is None, last),
        in_specs=[whole] * (len(pieces) + 3 + len(extra)),
        out_specs=[whole] * len(shapes),
        out_shape=shapes,
        compiler_params=params(),
        name="project",
    )(*pieces, *weights, *extra)


def attend_kernel(shards, sources, mine, seg_col, seg_row, *refs):
    queries, refs = refs[:shards], refs[shards:]
    early, refs = refs[:sources], refs[sources:]
    late, refs = refs[:sources], refs[sources:]
    outs, (q_all, kv_all) = refs[:shards], refs[shards:]
    rows, width = queries[0].shape
    heads = width // HD
    tokc = rows * shards
    many = early[0].shape[0]
    for s in range(shards):
        q_all[s * rows : (s + 1) * rows, :] = queries[s][...]
    for m in range(sources):
        kv_all[m * tokc : m * tokc + many, :] = early[m][...]
        kv_all[m * tokc + many : (m + 1) * tokc, :] = late[m][...]
    here = mine[0]
    column = lax.broadcasted_iota(jnp.int32, (1, tokc), 1)
    clip = []
    for m in range(sources):
        usable = jnp.where((here ^ m) <= here, 0, 1000)
        clip.append(seg_row[...] + usable + column * 0)
    clip = jnp.concatenate(clip, axis=1)
    inverse = 1.0 / math.sqrt(HD)
    block = min(tokc, 128)
    for b in range(tokc // block):
        span = slice(b * block, (b + 1) * block)
        allowed = seg_col[span, :] == clip
        for h in range(heads):
            cols = slice(h * HD, (h + 1) * HD)
            vcols = slice(width + h * HD, width + (h + 1) * HD)
            scores = lax.dot_general(
                q_all[span, cols],
                kv_all[:, cols],
                (((1,), (1,)), ((), ())),
                preferred_element_type=jnp.float32,
            )
            scores = jnp.where(allowed, scores * inverse, -1e30)
            best = jnp.max(scores, axis=-1, keepdims=True)
            weights = jnp.where(allowed, jnp.exp(scores - best), 0.0)
            total = jnp.sum(weights, axis=-1, keepdims=True)
            summed = jnp.dot(
                weights.astype(jnp.bfloat16), kv_all[:, vcols], preferred_element_type=jnp.float32
            )
            result = (summed / total).astype(jnp.bfloat16)
            for s in range(block // rows):
                outs[b * (block // rows) + s][:, cols] = result[s * rows : (s + 1) * rows]


def attend(mine, segments, queries, early, late):
    shards, sources = len(queries), len(early)
    rows, width = queries[0].shape
    tokc = rows * shards
    whole = pl.BlockSpec(memory_space=VMEM)
    return pl.pallas_call(
        functools.partial(attend_kernel, shards, sources),
        in_specs=[pl.BlockSpec(memory_space=pltpu.MemorySpace.SMEM)]
        + [whole] * (2 + shards + 2 * sources),
        out_specs=[whole] * shards,
        out_shape=[jax.ShapeDtypeStruct((rows, width), jnp.bfloat16)] * shards,
        scratch_shapes=[
            pltpu.VMEM((tokc, width), jnp.bfloat16),
            pltpu.VMEM((sources * tokc, 2 * width), jnp.bfloat16),
        ],
        compiler_params=params(),
        name="attend",
    )(mine, segments[:, None], segments[None, :], *queries, *early, *late)


def place_kernel(place, *refs):
    pieces, out = refs[:-1], refs[-1]
    width = pieces[0].shape[1]
    count = len(pieces)
    for s, piece in enumerate(pieces):
        column = lax.rem(place[0] + s, count) * width
        out[0, :, pl.ds(pl.multiple_of(column, width), width)] = piece[...]


def place_columns(place, pieces):
    rows, width = pieces[0].shape
    whole = pl.BlockSpec(memory_space=VMEM)
    return pl.pallas_call(
        place_kernel,
        in_specs=[pl.BlockSpec(memory_space=pltpu.MemorySpace.SMEM)] + [whole] * len(pieces),
        out_specs=whole,
        out_shape=jax.ShapeDtypeStruct((1, rows, width * len(pieces)), jnp.bfloat16),
        compiler_params=params(),
        name="place",
    )(place, *pieces)


def share(block, groups):
    held = {0: block}
    for m in range(2, groups, 2):
        held[m] = lax.ppermute(block, "group", [(i, i ^ m) for i in range(groups)])
    for m in range(0, groups, 2):
        held[m + 1] = lax.ppermute(held[m], "group", [(i, i ^ 1) for i in range(groups)])
    return [held[m] for m in range(groups)]


def per_device(latents, steps, segment_ids, mod_table, w_query, w_key, w_value):
    shards = lax.axis_size("dp")
    groups = lax.axis_size("group")
    rows = latents.shape[1]
    place = lax.axis_index("dp").astype(jnp.int32)
    mine = lax.axis_index("group").astype(jnp.int32)
    ring = [(i, (i + 1) % shards) for i in range(shards)]

    weights = [pltpu.with_memory_space_constraint(w, VMEM) for w in (w_query, w_key, w_value)]
    pieces = modulate(latents[0], steps, mod_table)
    arrived = [list(pieces)]
    for s in range(1, shards):
        arrived.append([lax.ppermute(piece, "dp", ring) for piece in arrived[-1]])

    order = [lax.rem(place - s + shards, shards) for s in range(shards)]
    segments = jnp.concatenate(
        [lax.dynamic_slice_in_dim(segment_ids, o * rows, rows) for o in order]
    )

    queries, shared = [], []
    for s in range(shards):
        if s < shards - 1:
            query, keyval = project(arrived[s], range(CHUNKS), weights, None, True)
        else:
            start = project(arrived[s][:-1], range(CHUNKS - 1), weights, None, False)[0]
            query, keyval = project(arrived[s][-1:], [CHUNKS - 1], weights, start, True)
        queries.append(query)
        shared.append(keyval)
    early = share(jnp.concatenate(shared[:-1], axis=0), groups)
    late = share(shared[-1], groups)
    results = attend(mine[None], segments, queries, early, late)
    landed = [results[0]]
    for s in range(1, shards):
        landed.append(
            lax.ppermute(results[s], "dp", [(i, (i - s) % shards) for i in range(shards)])
        )
    return place_columns(place[None], landed)


def solution(mesh):
    placed = (
        P("group", "dp", None),
        P("group"),
        P(),
        P(),
        P(None, "dp"),
        P(None, "dp"),
        P(None, "dp"),
    )
    return jax.shard_map(
        per_device, mesh=mesh, in_specs=placed, out_specs=P("group", "dp", None), check_vma=False
    )
```

time: 110 us -> 76.2 us (0.69)
  the two profiles are of different devices: /device:TPU:7 before, /device:TPU:0 now
where the time goes in v1:
time: 76.2 us; the launch traced here: 75.2 us
  starting transfers between devices  21.8 us (29%)
  local copies, waits for them, and re-layouts  20.7 us (27%)
  Pallas kernels  17.8 us (23%)
  waiting for transfers between devices  13.9 us (18%)
  between operations  0.78 us (1%)
    unnamed x48, local copies, waits for them, and re-layouts  19.8 us
    pallas_call x5, Pallas kernels, project(): pl.pallas_call(functools.partial(project_kernel, tuple(places), start is...  15.1 us
    ppermute x6, starting transfers between devices, share(): held[m] = lax.ppermute(block, 'group', [(i, i ^ m) for i in range(groups)])  8.95 us
    ppermute x6, starting transfers between devices, per_device(): arrived.append([lax.ppermute(piece, 'dp', ring) for piece in arrived[-1]])  6.43 us
    ppermute x6, waiting for transfers between devices, per_device(): arrived.append([lax.ppermute(piece, 'dp', ring) for piece in arrived[-1]])  5.66 us
    ppermute x3, starting transfers between devices, per_device(): lax.ppermute(results[s], 'dp', [(i, (i - s) % shards) for i in range(shar...  4.93 us
    ppermute x3, waiting for transfers between devices, per_device(): lax.ppermute(results[s], 'dp', [(i, (i - s) % shards) for i in range(shar...  4 us
    ppermute x6, waiting for transfers between devices, share(): held[m] = lax.ppermute(block, 'group', [(i, i ^ m) for i in range(groups)])  3.25 us
  transfers between devices with their start and end apart: 23, of which 6 were waited for; matrix products, arithmetic and copies ran while one was open for 3% of the time, Pallas kernels for 20%

profile of v1, /device:TPU:0, one launch (start us, length us, event | category | flops | bytes accessed | tf_op | source)
XLA Modules:
  0.0 75.2 jit_solution(8533397807611626488)
XLA Ops:
  0.7 1.1 %copy-done.6 = f32[16,2,6144]{2,1,0:T(2,128)S(1)} copy-done((f32[16,2,6144]{2,1,0:T(2,128)S(1)}, f32[16,2,6144]{2,1,0:T(2,128)}, u32[]{:S(2)}) %copy-start.6) | copy-done | bytes 786456
  1.8 1.0 %copy-done.7 = bf16[1,32,6144]{2,1,0:T(8,128)(2,1)S(1)} copy-done((bf16[1,32,6144]{2,1,0:T(8,128)(2,1)S(1)}, bf16[1,32,6144]{2,1,0:T(8,128)(2,1)}, u32[]{:S(2)}) %copy-start.7) | copy-done | bytes 393240
  2.8 0.3 modulate.1
  3.1 3.1 %collective-permute-start = (bf16[32,3072]{1,0:T(8,128)(2,1)S(1)}, bf16[32,3072]{1,0:T(8,128)(2,1)S(1)}, u32[]{:S(2)}, u32[]{:S(2)}) collective-permute-start(bf16[32,3072]{1,0:T(8,128)(2,1)S(1)} %get-tuple-element.19.refs_0_), channel_id=1, source_target_pairs={{0,1},{1,2},{2,3},{3,0},{4,5},{5,6},{6,7},{7,4},{8,9},{9,10},{10,1... | collective-permute-start | bytes 589832 | tf_op jit(solution)/shard_map/ppermute | solution.py:206
  6.2 1.6 %collective-permute-start.1 = (bf16[32,3072]{1,0:T(8,128)(2,1)S(1)}, bf16[32,3072]{1,0:T(8,128)(2,1)S(1)}, u32[]{:S(2)}, u32[]{:S(2)}) collective-permute-start(bf16[32,3072]{1,0:T(8,128)(2,1)S(1)} %get-tuple-element.20.refs_1_), channel_id=1, source_target_pairs={{0,1},{1,2},{2,3},{3,0},{4,5},{5,6},{6,7},{7,4},{8,9},{9,10},{10,1... | collective-permute-start | bytes 589832 | tf_op jit(solution)/shard_map/ppermute | solution.py:206
  7.8 1.9 %copy-done = bf16[6144,256]{1,0:T(8,128)(2,1)S(1)} copy-done((bf16[6144,256]{1,0:T(8,128)(2,1)S(1)}, bf16[6144,256]{1,0:T(8,128)(2,1)}, u32[]{:S(2)}) %copy-start) | copy-done | bytes 3145752
  9.7 1.9 %copy-done.2 = bf16[6144,256]{1,0:T(8,128)(2,1)S(1)} copy-done((bf16[6144,256]{1,0:T(8,128)(2,1)S(1)}, bf16[6144,256]{1,0:T(8,128)(2,1)}, u32[]{:S(2)}) %copy-start.2) | copy-done | bytes 3145752
  11.5 1.9 %copy-done.4 = bf16[6144,256]{1,0:T(8,128)(2,1)S(1)} copy-done((bf16[6144,256]{1,0:T(8,128)(2,1)S(1)}, bf16[6144,256]{1,0:T(8,128)(2,1)}, u32[]{:S(2)}) %copy-start.4) | copy-done | bytes 3145752
  13.4 3.4 %project.5 = (bf16[32,256]{1,0:T(8,128)(2,1)}, bf16[32,512]{1,0:T(8,128)(2,1)}) custom-call(bf16[32,3072]{1,0:T(8,128)(2,1)} %copy-done.9, bf16[32,3072]{1,0:T(8,128)(2,1)} %copy-done.8, bf16[6144,256]{1,0:T(8,128)(2,1)S(1)} %copy-done, bf16[6144,256]{1,0:T(8,128)(2,1)S(1)} %copy-done.2, bf16[6144,256]{1,0:T(8,128)(2,1)S(1)} %copy-done.4), custom_call_target="tpu_custom_call" | custom-call | tf_op jit(solution)/shard_map/project/pallas_call | solution.py:86
  16.8 1.6 %collective-permute-start.2 = (bf16[32,3072]{1,0:T(8,128)(2,1)S(1)}, bf16[32,3072]{1,0:T(8,128)(2,1)S(1)}, u32[]{:S(2)}, u32[]{:S(2)}) collective-permute-start(bf16[32,3072]{1,0:T(8,128)(2,1)S(1)} %collective-permute-done.refs_0_), channel_id=1, source_target_pairs={{0,1},{1,2},{2,3},{3,0},{4,5},{5,6},{6,7},{7,4},{8,9},{9,10},{10,1... | collective-permute-start | bytes 589832 | tf_op jit(solution)/shard_map/ppermute | solution.py:206
  18.5 0.8 %constant_dynamic-update-slice_fusion.2 = bf16[96,512]{1,0:T(8,128)(2,1)S(1)} fusion(bf16[32,512]{1,0:T(8,128)(2,1)} %get-tuple-element.25), kind=kLoop, calls=%fused_computation.2 | loop fusion | bytes 65536
  19.2 3.4 %project.6 = (bf16[32,256]{1,0:T(8,128)(2,1)}, bf16[32,512]{1,0:T(8,128)(2,1)}) custom-call(bf16[32,3072]{1,0:T(8,128)(2,1)} %copy-done.20, bf16[32,3072]{1,0:T(8,128)(2,1)} %copy-done.21, bf16[6144,256]{1,0:T(8,128)(2,1)S(1)} %copy-done, bf16[6144,256]{1,0:T(8,128)(2,1)S(1)} %copy-done.2, bf16[6144,256]{1,0:T(8,128)(2,1)S(1)} %copy-done.4), custom_call_target="tpu_custom_call" | custom-call | tf_op jit(solution)/shard_map/project/pallas_call | solution.py:86
  22.6 0.8 %constant_dynamic-update-slice_fusion.1 = bf16[96,512]{1,0:T(8,128)(2,1)S(1)} fusion(bf16[96,512]{1,0:T(8,128)(2,1)S(1)} %constant_dynamic-update-slice_fusion.2, bf16[32,512]{1,0:T(8,128)(2,1)} %get-tuple-element.26), kind=kLoop, calls=%fused_computation.1 | loop fusion | bytes 65536
  23.3 5.6 %collective-permute-done.3.refs_1_ = bf16[32,3072]{1,0:T(8,128)(2,1)} collective-permute-done((bf16[32,3072]{1,0:T(8,128)(2,1)S(1)}, bf16[32,3072]{1,0:T(8,128)(2,1)}, u32[]{:S(2)}, u32[]{:S(2)}) %collective-permute-start.3) | collective-permute-done | bytes 196640 | tf_op jit(solution)/shard_map/ppermute | solution.py:206
  29.0 0.7 copy-done.19
  29.7 3.4 %project.7 = (bf16[32,256]{1,0:T(8,128)(2,1)}, bf16[32,512]{1,0:T(8,128)(2,1)}) custom-call(bf16[32,3072]{1,0:T(8,128)(2,1)} %copy-done.19, bf16[32,3072]{1,0:T(8,128)(2,1)} %collective-permute-done.3.refs_1_, bf16[6144,256]{1,0:T(8,128)(2,1)S(1)} %copy-done, bf16[6144,256]{1,0:T(8,128)(2,1)S(1)} %copy-done.2, bf16[6144,256]{1,0:T(8,128)(2,1)S(1)} %copy-done.4), custom_call_target="tpu_custom_call" | custom-call | tf_op jit(solution)/shard_map/project/pallas_call | solution.py:86
  33.0 0.1 collective-permute-start.5
  33.2 0.8 %constant_dynamic-update-slice_fusion.refs_4_ = bf16[96,512]{1,0:T(8,128)(2,1)S(1)} fusion(bf16[96,512]{1,0:T(8,128)(2,1)S(1)} %constant_dynamic-update-slice_fusion.1, bf16[32,512]{1,0:T(8,128)(2,1)} %get-tuple-element.27), kind=kLoop, calls=%fused_computation | loop fusion | bytes 65536 | tf_op jit(solution)/shard_map/concatenate | solution.py:222
  33.9 1.5 %collective-permute-start.7 = (bf16[96,512]{1,0:T(8,128)(2,1)S(1)}, bf16[96,512]{1,0:T(8,128)(2,1)S(1)}, u32[]{:S(2)}, u32[]{:S(2)}) collective-permute-start(bf16[96,512]{1,0:T(8,128)(2,1)S(1)} %constant_dynamic-update-slice_fusion.refs_4_), channel_id=1, source_target_pairs={{0,8},{4,12},{8,0},{12,4},{16,24},{20,28},{24,16},{28,20},{1,9},{5... | collective-permute-start | bytes 294920 | tf_op jit(solution)/shard_map/ppermute | solution.py:188
  35.4 1.5 %collective-permute-start.9 = (bf16[96,512]{1,0:T(8,128)(2,1)S(1)}, bf16[96,512]{1,0:T(8,128)(2,1)S(1)}, u32[]{:S(2)}, u32[]{:S(2)}) collective-permute-start(bf16[96,512]{1,0:T(8,128)(2,1)S(1)} %constant_dynamic-update-slice_fusion.refs_4_), channel_id=1, source_target_pairs={{0,16},{4,20},{8,24},{12,28},{16,0},{20,4},{24,8},{28,12},{1,17},{... | collective-permute-start | bytes 294920 | tf_op jit(solution)/shard_map/ppermute | solution.py:188
  36.9 1.6 %collective-permute-done.7.refs_6_ = bf16[96,512]{1,0:T(8,128)(2,1)S(1)} collective-permute-done((bf16[96,512]{1,0:T(8,128)(2,1)S(1)}, bf16[96,512]{1,0:T(8,128)(2,1)S(1)}, u32[]{:S(2)}, u32[]{:S(2)}) %collective-permute-start.7) | collective-permute-done | bytes 98336 | tf_op jit(solution)/shard_map/ppermute | solution.py:188
  38.5 2.4 %collective-permute-start.11 = (bf16[96,512]{1,0:T(8,128)(2,1)S(1)}, bf16[96,512]{1,0:T(8,128)(2,1)}, u32[]{:S(2)}, u32[]{:S(2)}) collective-permute-start(bf16[96,512]{1,0:T(8,128)(2,1)S(1)} %constant_dynamic-update-slice_fusion.refs_4_), channel_id=1, source_target_pairs={{0,24},{4,28},{8,16},{12,20},{16,8},{20,12},{24,0},{28,4},{1,25},{... | collective-permute-start | bytes 294920 | tf_op jit(solution)/shard_map/ppermute | solution.py:188
  41.0 0.5 collective-permute-start.10
  41.5 1.9 %copy-done.3 = bf16[6144,256]{1,0:T(8,128)(2,1)S(1)} copy-done((bf16[6144,256]{1,0:T(8,128)(2,1)S(1)}, bf16[6144,256]{1,0:T(8,128)(2,1)}, u32[]{:S(2)}) %copy-start.3) | copy-done | bytes 3145752
  43.4 1.9 %copy-done.5 = bf16[6144,256]{1,0:T(8,128)(2,1)S(1)} copy-done((bf16[6144,256]{1,0:T(8,128)(2,1)S(1)}, bf16[6144,256]{1,0:T(8,128)(2,1)}, u32[]{:S(2)}) %copy-start.5) | copy-done | bytes 3145752
  45.3 2.5 %project.8.refs_4_ = f32[32,768]{1,0:T(8,128)} custom-call(bf16[32,3072]{1,0:T(8,128)(2,1)} %collective-permute-done.5.refs_0_, bf16[6144,256]{1,0:T(8,128)(2,1)S(1)} %copy-done.1, bf16[6144,256]{1,0:T(8,128)(2,1)S(1)} %copy-done.3, bf16[6144,256]{1,0:T(8,128)(2,1)S(1)} %copy-done.5), custom_call_target="tpu_custom_call" | custom-call | tf_op jit(solution)/shard_map/project/pallas_call | solution.py:86
  47.8 2.5 %project.9 = (bf16[32,256]{1,0:T(8,128)(2,1)}, bf16[32,512]{1,0:T(8,128)(2,1)}) custom-call(bf16[32,3072]{1,0:T(8,128)(2,1)} %collective-permute-done.4.refs_0_, bf16[6144,256]{1,0:T(8,128)(2,1)S(1)} %copy-done.1, bf16[6144,256]{1,0:T(8,128)(2,1)S(1)} %copy-done.3, bf16[6144,256]{1,0:T(8,128)(2,1)S(1)} %copy-done.5, f32[32,768]{1,0:T(8,128)} %project.8.refs_4_), custom_call_target="tpu_custom_call" | custom-call | tf_op jit(solution)/shard_map/project/pallas_call | solution.py:86
  50.3 1.0 %collective-permute-start.14 = (bf16[32,512]{1,0:T(8,128)(2,1)}, bf16[32,512]{1,0:T(8,128)(2,1)S(1)}, u32[]{:S(2)}, u32[]{:S(2)}) collective-permute-start(bf16[32,512]{1,0:T(8,128)(2,1)} %get-tuple-element.28.refs_12_), channel_id=1, source_target_pairs={{0,8},{4,12},{8,0},{12,4},{16,24},{20,28},{24,16},{28,20},{1,9},{5... | collective-permute-start | bytes 98312 | tf_op jit(solution)/shard_map/ppermute | solution.py:188
  51.3 1.5 %collective-permute-start.16 = (bf16[32,512]{1,0:T(8,128)(2,1)}, bf16[32,512]{1,0:T(8,128)(2,1)S(1)}, u32[]{:S(2)}, u32[]{:S(2)}) collective-permute-start(bf16[32,512]{1,0:T(8,128)(2,1)} %get-tuple-element.28.refs_12_), channel_id=1, source_target_pairs={{0,16},{4,20},{8,24},{12,28},{16,0},{20,4},{24,8},{28,12},{1,17},{... | collective-permute-start | bytes 98312 | tf_op jit(solution)/shard_map/ppermute | solution.py:188
  52.8 1.0 %collective-permute-start.18 = (bf16[32,512]{1,0:T(8,128)(2,1)}, bf16[32,512]{1,0:T(8,128)(2,1)S(1)}, u32[]{:S(2)}, u32[]{:S(2)}) collective-permute-start(bf16[32,512]{1,0:T(8,128)(2,1)} %get-tuple-element.28.refs_12_), channel_id=1, source_target_pairs={{0,24},{4,28},{8,16},{12,20},{16,8},{20,12},{24,0},{28,4},{1,25},{... | collective-permute-start | bytes 98312 | tf_op jit(solution)/shard_map/ppermute | solution.py:188
  53.9 0.6 copy-done.10
  54.5 0.6 copy-done.12
  55.2 0.5 collective-permute-start.13
  55.7 0.5 collective-permute-start.17
  56.2 1.6 %collective-permute-done.18.refs_18_ = bf16[32,512]{1,0:T(8,128)(2,1)S(1)} collective-permute-done((bf16[32,512]{1,0:T(8,128)(2,1)}, bf16[32,512]{1,0:T(8,128)(2,1)S(1)}, u32[]{:S(2)}, u32[]{:S(2)}) %collective-permute-start.18) | collective-permute-done | bytes 32800 | tf_op jit(solution)/shard_map/ppermute | solution.py:188
  58.1 1.0 %collective-permute-done.19.refs_19_ = bf16[32,512]{1,0:T(8,128)(2,1)S(1)} collective-permute-done((bf16[32,512]{1,0:T(8,128)(2,1)S(1)}, bf16[32,512]{1,0:T(8,128)(2,1)S(1)}, u32[]{:S(2)}, u32[]{:S(2)}) %collective-permute-start.19) | collective-permute-done | bytes 32800 | tf_op jit(solution)/shard_map/ppermute | solution.py:190
  59.1 0.9 %copy-done.11 = bf16[96,512]{1,0:T(8,128)(2,1)S(1)} copy-done((bf16[96,512]{1,0:T(8,128)(2,1)S(1)}, bf16[96,512]{1,0:T(8,128)(2,1)}, u32[]{:S(2)}) %copy-start.11) | copy-done | bytes 98328
  59.9 0.9 %copy-done.13 = bf16[96,512]{1,0:T(8,128)(2,1)S(1)} copy-done((bf16[96,512]{1,0:T(8,128)(2,1)S(1)}, bf16[96,512]{1,0:T(8,128)(2,1)}, u32[]{:S(2)}) %copy-start.13) | copy-done | bytes 98328
  60.8 0.8 %copy-done.14 = bf16[32,512]{1,0:T(8,128)(2,1)S(1)} copy-done((bf16[32,512]{1,0:T(8,128)(2,1)S(1)}, bf16[32,512]{1,0:T(8,128)(2,1)}, u32[]{:S(2)}) %copy-start.14) | copy-done | bytes 32792
  61.6 0.7 copy-done.16
  62.3 0.7 copy-done.17
  63.0 0.7 copy-done.18
  63.8 1.8 %attend.1 = (bf16[32,256]{1,0:T(8,128)(2,1)S(1)}, bf16[32,256]{1,0:T(8,128)(2,1)S(1)}, bf16[32,256]{1,0:T(8,128)(2,1)S(1)}, bf16[32,256]{1,0:T(8,128)(2,1)S(1)}) custom-call(s32[1]{0:T(128)} %bitcast.1.mine, s32[128,1]{1,0:T(8,128)S(1)} %copy.8.seg_col, s32[1,128]{1,0:T(1,128)S(1)} %bitcast.7, bf16[32,256]{1,0:T(8,128)(2,1)S(1)} %copy-done.15, ...), custom_call_target="tpu_custom_call" | custom-call | tf_op jit(solution)/shard_map/attend/pallas_call | solution.py:148
  65.6 3.4 %collective-permute-start.20 = (bf16[32,256]{1,0:T(8,128)(2,1)S(1)}, bf16[32,256]{1,0:T(8,128)(2,1)S(1)}, u32[]{:S(2)}, u32[]{:S(2)}) collective-permute-start(bf16[32,256]{1,0:T(8,128)(2,1)S(1)} %get-tuple-element.30), channel_id=1, source_target_pairs={{0,3},{1,0},{2,1},{3,2},{4,7},{5,4},{6,5},{7,6},{8,11},{9,8},{10,9... | collective-permute-start | bytes 49160 | tf_op jit(solution)/shard_map/ppermute | solution.py:228
  69.0 1.5 %collective-permute-start.22 = (bf16[32,256]{1,0:T(8,128)(2,1)S(1)}, bf16[32,256]{1,0:T(8,128)(2,1)S(1)}, u32[]{:S(2)}, u32[]{:S(2)}) collective-permute-start(bf16[32,256]{1,0:T(8,128)(2,1)S(1)} %get-tuple-element.32), channel_id=1, source_target_pairs={{0,1},{1,2},{2,3},{3,0},{4,5},{5,6},{6,7},{7,4},{8,9},{9,10},{10,1... | collective-permute-start | bytes 49160 | tf_op jit(solution)/shard_map/ppermute | solution.py:228
  70.5 3.1 %collective-permute-done.21.refs_2_ = bf16[32,256]{1,0:T(8,128)(2,1)S(1)} collective-permute-done((bf16[32,256]{1,0:T(8,128)(2,1)S(1)}, bf16[32,256]{1,0:T(8,128)(2,1)S(1)}, u32[]{:S(2)}, u32[]{:S(2)}) %collective-permute-start.21) | collective-permute-done | bytes 16416 | tf_op jit(solution)/shard_map/ppermute | solution.py:228
  73.6 0.9 %collective-permute-done.22.refs_3_ = bf16[32,256]{1,0:T(8,128)(2,1)S(1)} collective-permute-done((bf16[32,256]{1,0:T(8,128)(2,1)S(1)}, bf16[32,256]{1,0:T(8,128)(2,1)S(1)}, u32[]{:S(2)}, u32[]{:S(2)}) %collective-permute-start.22) | collective-permute-done | bytes 16416 | tf_op jit(solution)/shard_map/ppermute | solution.py:228
  74.5 0.6 place.1
  (58 shorter events, 0.5 us)
Async XLA Ops:
  0.7 1.1 %copy-start.6 = (f32[16,2,6144]{2,1,0:T(2,128)S(1)}, f32[16,2,6144]{2,1,0:T(2,128)}, u32[]{:S(2)}) copy-start(f32[16,2,6144]{2,1,0:T(2,128)} %table_ref.1) | copy-start | bytes 2359300
  1.8 1.0 %copy-start.7 = (bf16[1,32,6144]{2,1,0:T(8,128)(2,1)S(1)}, bf16[1,32,6144]{2,1,0:T(8,128)(2,1)}, u32[]{:S(2)}) copy-start(bf16[1,32,6144]{2,1,0:T(8,128)(2,1)} %param.7) | copy-start | bytes 1179652
  3.1 4.7 %copy-start.8 = (bf16[32,3072]{1,0:T(8,128)(2,1)}, bf16[32,3072]{1,0:T(8,128)(2,1)S(1)}, u32[]{:S(2)}) copy-start(bf16[32,3072]{1,0:T(8,128)(2,1)S(1)} %get-tuple-element.20.refs_1_) | copy-start | bytes 589828
  3.1 4.7 %copy-start.9 = (bf16[32,3072]{1,0:T(8,128)(2,1)}, bf16[32,3072]{1,0:T(8,128)(2,1)S(1)}, u32[]{:S(2)}) copy-start(bf16[32,3072]{1,0:T(8,128)(2,1)S(1)} %get-tuple-element.19.refs_0_) | copy-start | bytes 589828
  3.1 13.7 %collective-permute-start = (bf16[32,3072]{1,0:T(8,128)(2,1)S(1)}, bf16[32,3072]{1,0:T(8,128)(2,1)S(1)}, u32[]{:S(2)}, u32[]{:S(2)}) collective-permute-start(bf16[32,3072]{1,0:T(8,128)(2,1)S(1)} %get-tuple-element.19.refs_0_), channel_id=1, source_target_pairs={{0,1},{1,2},{2,3},{3,0},{4,5},{5,6},{6,7},{7,4},{8,9},{9,10},{10,1... | collective-permute-start | bytes 589832 | tf_op jit(solution)/shard_map/ppermute | solution.py:206
  6.2 12.2 %collective-permute-start.1 = (bf16[32,3072]{1,0:T(8,128)(2,1)S(1)}, bf16[32,3072]{1,0:T(8,128)(2,1)S(1)}, u32[]{:S(2)}, u32[]{:S(2)}) collective-permute-start(bf16[32,3072]{1,0:T(8,128)(2,1)S(1)} %get-tuple-element.20.refs_1_), channel_id=1, source_target_pairs={{0,1},{1,2},{2,3},{3,0},{4,5},{5,6},{6,7},{7,4},{8,9},{9,10},{10,1... | collective-permute-start | bytes 589832 | tf_op jit(solution)/shard_map/ppermute | solution.py:206
  7.8 1.9 %copy-start = (bf16[6144,256]{1,0:T(8,128)(2,1)S(1)}, bf16[6144,256]{1,0:T(8,128)(2,1)}, u32[]{:S(2)}) copy-start(bf16[6144,256]{1,0:T(8,128)(2,1)} %refs_1_.3) | copy-start | bytes 9437188
  9.7 1.9 %copy-start.2 = (bf16[6144,256]{1,0:T(8,128)(2,1)S(1)}, bf16[6144,256]{1,0:T(8,128)(2,1)}, u32[]{:S(2)}) copy-start(bf16[6144,256]{1,0:T(8,128)(2,1)} %refs_2_.9) | copy-start | bytes 9437188
  11.5 1.9 %copy-start.4 = (bf16[6144,256]{1,0:T(8,128)(2,1)S(1)}, bf16[6144,256]{1,0:T(8,128)(2,1)}, u32[]{:S(2)}) copy-start(bf16[6144,256]{1,0:T(8,128)(2,1)} %refs_3_.9) | copy-start | bytes 9437188
  16.8 2.4 %copy-start.20 = (bf16[32,3072]{1,0:T(8,128)(2,1)}, bf16[32,3072]{1,0:T(8,128)(2,1)S(1)}, u32[]{:S(2)}) copy-start(bf16[32,3072]{1,0:T(8,128)(2,1)S(1)} %collective-permute-done.refs_0_) | copy-start | bytes 589828
  16.8 12.2 %collective-permute-start.2 = (bf16[32,3072]{1,0:T(8,128)(2,1)S(1)}, bf16[32,3072]{1,0:T(8,128)(2,1)S(1)}, u32[]{:S(2)}, u32[]{:S(2)}) collective-permute-start(bf16[32,3072]{1,0:T(8,128)(2,1)S(1)} %collective-permute-done.refs_0_), channel_id=1, source_target_pairs={{0,1},{1,2},{2,3},{3,0},{4,5},{5,6},{6,7},{7,4},{8,9},{9,10},{10,1... | collective-permute-start | bytes 589832 | tf_op jit(solution)/shard_map/ppermute | solution.py:206
  18.4 0.9 %copy-start.21 = (bf16[32,3072]{1,0:T(8,128)(2,1)}, bf16[32,3072]{1,0:T(8,128)(2,1)S(1)}, u32[]{:S(2)}) copy-start(bf16[32,3072]{1,0:T(8,128)(2,1)S(1)} %collective-permute-done.1.refs_1_) | copy-start | bytes 589828
  18.4 10.6 %collective-permute-start.3 = (bf16[32,3072]{1,0:T(8,128)(2,1)S(1)}, bf16[32,3072]{1,0:T(8,128)(2,1)}, u32[]{:S(2)}, u32[]{:S(2)}) collective-permute-start(bf16[32,3072]{1,0:T(8,128)(2,1)S(1)} %collective-permute-done.1.refs_1_), channel_id=1, source_target_pairs={{0,1},{1,2},{2,3},{3,0},{4,5},{5,6},{6,7},{7,4},{8,9},{9,10},{10,1... | collective-permute-start | bytes 589832 | tf_op jit(solution)/shard_map/ppermute | solution.py:206
  23.3 18.2 %copy-start.1 = (bf16[6144,256]{1,0:T(8,128)(2,1)S(1)}, bf16[6144,256]{1,0:T(8,128)(2,1)}, u32[]{:S(2)}) copy-start(bf16[6144,256]{1,0:T(8,128)(2,1)} %refs_1_.3) | copy-start | bytes 9437188
  29.0 18.8 %collective-permute-start.4 = (bf16[32,3072]{1,0:T(8,128)(2,1)}, bf16[32,3072]{1,0:T(8,128)(2,1)}, u32[]{:S(2)}, u32[]{:S(2)}) collective-permute-start(bf16[32,3072]{1,0:T(8,128)(2,1)} %collective-permute-done.3.refs_1_), channel_id=1, source_target_pairs={{0,1},{1,2},{2,3},{3,0},{4,5},{5,6},{6,7},{7,4},{8,9},{9,10},{10,1... | collective-permute-start | bytes 589832 | tf_op jit(solution)/shard_map/ppermute | solution.py:206
  29.0 0.7 copy-start.19
  33.0 8.0 %collective-permute-start.5 = (bf16[32,3072]{1,0:T(8,128)(2,1)}, bf16[32,3072]{1,0:T(8,128)(2,1)}, u32[]{:S(2)}, u32[]{:S(2)}) collective-permute-start(bf16[32,3072]{1,0:T(8,128)(2,1)} %copy-done.19), channel_id=1, source_target_pairs={{0,1},{1,2},{2,3},{3,0},{4,5},{5,6},{6,7},{7,4},{8,9},{9,10},{10,1... | collective-permute-start | bytes 589832 | tf_op jit(solution)/shard_map/ppermute | solution.py:206
  33.9 4.6 %collective-permute-start.7 = (bf16[96,512]{1,0:T(8,128)(2,1)S(1)}, bf16[96,512]{1,0:T(8,128)(2,1)S(1)}, u32[]{:S(2)}, u32[]{:S(2)}) collective-permute-start(bf16[96,512]{1,0:T(8,128)(2,1)S(1)} %constant_dynamic-update-slice_fusion.refs_4_), channel_id=1, source_target_pairs={{0,8},{4,12},{8,0},{12,4},{16,24},{20,28},{24,16},{28,20},{1,9},{5... | collective-permute-start | bytes 294920 | tf_op jit(solution)/shard_map/ppermute | solution.py:188
  35.4 5.6 %collective-permute-start.9 = (bf16[96,512]{1,0:T(8,128)(2,1)S(1)}, bf16[96,512]{1,0:T(8,128)(2,1)S(1)}, u32[]{:S(2)}, u32[]{:S(2)}) collective-permute-start(bf16[96,512]{1,0:T(8,128)(2,1)S(1)} %constant_dynamic-update-slice_fusion.refs_4_), channel_id=1, source_target_pairs={{0,16},{4,20},{8,24},{12,28},{16,0},{20,4},{24,8},{28,12},{1,17},{... | collective-permute-start | bytes 294920 | tf_op jit(solution)/shard_map/ppermute | solution.py:188
  36.9 14.4 %collective-permute-start.6 = (bf16[96,512]{1,0:T(8,128)(2,1)S(1)}, bf16[96,512]{1,0:T(8,128)(2,1)S(1)}, u32[]{:S(2)}, u32[]{:S(2)}) collective-permute-start(bf16[96,512]{1,0:T(8,128)(2,1)S(1)} %constant_dynamic-update-slice_fusion.refs_4_), channel_id=1, source_target_pairs={{0,4},{4,0},{8,12},{12,8},{16,20},{20,16},{24,28},{28,24},{1,5},{5... | collective-permute-start | bytes 294920 | tf_op jit(solution)/shard_map/ppermute | solution.py:190
  38.5 14.3 %collective-permute-start.11 = (bf16[96,512]{1,0:T(8,128)(2,1)S(1)}, bf16[96,512]{1,0:T(8,128)(2,1)}, u32[]{:S(2)}, u32[]{:S(2)}) collective-permute-start(bf16[96,512]{1,0:T(8,128)(2,1)S(1)} %constant_dynamic-update-slice_fusion.refs_4_), channel_id=1, source_target_pairs={{0,24},{4,28},{8,16},{12,20},{16,8},{20,12},{24,0},{28,4},{1,25},{... | collective-permute-start | bytes 294920 | tf_op jit(solution)/shard_map/ppermute | solution.py:188
  41.0 12.9 %collective-permute-start.8 = (bf16[96,512]{1,0:T(8,128)(2,1)S(1)}, bf16[96,512]{1,0:T(8,128)(2,1)S(1)}, u32[]{:S(2)}, u32[]{:S(2)}) collective-permute-start(bf16[96,512]{1,0:T(8,128)(2,1)S(1)} %collective-permute-done.7.refs_6_), channel_id=1, source_target_pairs={{0,4},{4,0},{8,12},{12,8},{16,20},{20,16},{24,28},{28,24},{1,5},{5... | collective-permute-start | bytes 294920 | tf_op jit(solution)/shard_map/ppermute | solution.py:190
  41.0 13.5 %collective-permute-start.10 = (bf16[96,512]{1,0:T(8,128)(2,1)S(1)}, bf16[96,512]{1,0:T(8,128)(2,1)S(1)}, u32[]{:S(2)}, u32[]{:S(2)}) collective-permute-start(bf16[96,512]{1,0:T(8,128)(2,1)S(1)} %collective-permute-done.9.refs_8_), channel_id=1, source_target_pairs={{0,4},{4,0},{8,12},{12,8},{16,20},{20,16},{24,28},{28,24},{1,5},{5... | collective-permute-start | bytes 294920 | tf_op jit(solution)/shard_map/ppermute | solution.py:190
  41.5 1.9 %copy-start.3 = (bf16[6144,256]{1,0:T(8,128)(2,1)S(1)}, bf16[6144,256]{1,0:T(8,128)(2,1)}, u32[]{:S(2)}) copy-start(bf16[6144,256]{1,0:T(8,128)(2,1)} %refs_2_.9) | copy-start | bytes 9437188
  43.4 1.9 %copy-start.5 = (bf16[6144,256]{1,0:T(8,128)(2,1)S(1)}, bf16[6144,256]{1,0:T(8,128)(2,1)}, u32[]{:S(2)}) copy-start(bf16[6144,256]{1,0:T(8,128)(2,1)} %refs_3_.9) | copy-start | bytes 9437188
  47.8 6.0 %copy-start.22 = (s32[128]{0:T(128)S(1)}, s32[128]{0:T(128)}, u32[]{:S(2)}) copy-start(s32[128]{0:T(128)} %param.9) | copy-start | bytes 1540
  47.8 11.3 %copy-start.15 = (bf16[32,256]{1,0:T(8,128)(2,1)S(1)}, bf16[32,256]{1,0:T(8,128)(2,1)}, u32[]{:S(2)}) copy-start(bf16[32,256]{1,0:T(8,128)(2,1)} %get-tuple-element.21.refs_0_) | copy-start | bytes 49156
  50.3 5.4 %collective-permute-start.14 = (bf16[32,512]{1,0:T(8,128)(2,1)}, bf16[32,512]{1,0:T(8,128)(2,1)S(1)}, u32[]{:S(2)}, u32[]{:S(2)}) collective-permute-start(bf16[32,512]{1,0:T(8,128)(2,1)} %get-tuple-element.28.refs_12_), channel_id=1, source_target_pairs={{0,8},{4,12},{8,0},{12,4},{16,24},{20,28},{24,16},{28,20},{1,9},{5... | collective-permute-start | bytes 98312 | tf_op jit(solution)/shard_map/ppermute | solution.py:188
  51.3 4.4 %collective-permute-start.16 = (bf16[32,512]{1,0:T(8,128)(2,1)}, bf16[32,512]{1,0:T(8,128)(2,1)S(1)}, u32[]{:S(2)}, u32[]{:S(2)}) collective-permute-start(bf16[32,512]{1,0:T(8,128)(2,1)} %get-tuple-element.28.refs_12_), channel_id=1, source_target_pairs={{0,16},{4,20},{8,24},{12,28},{16,0},{20,4},{24,8},{28,12},{1,17},{... | collective-permute-start | bytes 98312 | tf_op jit(solution)/shard_map/ppermute | solution.py:188
  52.8 5.0 %collective-permute-start.18 = (bf16[32,512]{1,0:T(8,128)(2,1)}, bf16[32,512]{1,0:T(8,128)(2,1)S(1)}, u32[]{:S(2)}, u32[]{:S(2)}) collective-permute-start(bf16[32,512]{1,0:T(8,128)(2,1)} %get-tuple-element.28.refs_12_), channel_id=1, source_target_pairs={{0,24},{4,28},{8,16},{12,20},{16,8},{20,12},{24,0},{28,4},{1,25},{... | collective-permute-start | bytes 98312 | tf_op jit(solution)/shard_map/ppermute | solution.py:188
  53.9 0.6 copy-start.10
  54.5 3.5 %collective-permute-start.12 = (bf16[96,512]{1,0:T(8,128)(2,1)}, bf16[96,512]{1,0:T(8,128)(2,1)S(1)}, u32[]{:S(2)}, u32[]{:S(2)}) collective-permute-start(bf16[96,512]{1,0:T(8,128)(2,1)} %collective-permute-done.11.refs_10_), channel_id=1, source_target_pairs={{0,4},{4,0},{8,12},{12,8},{16,20},{20,16},{24,28},{28,24},{1,5},{5... | collective-permute-start | bytes 294920 | tf_op jit(solution)/shard_map/ppermute | solution.py:190
  54.5 0.7 copy-start.12
  55.2 2.9 %collective-permute-start.13 = (bf16[32,512]{1,0:T(8,128)(2,1)}, bf16[32,512]{1,0:T(8,128)(2,1)S(1)}, u32[]{:S(2)}, u32[]{:S(2)}) collective-permute-start(bf16[32,512]{1,0:T(8,128)(2,1)} %get-tuple-element.28.refs_12_), channel_id=1, source_target_pairs={{0,4},{4,0},{8,12},{12,8},{16,20},{20,16},{24,28},{28,24},{1,5},{5... | collective-permute-start | bytes 98312 | tf_op jit(solution)/shard_map/ppermute | solution.py:190
  55.7 2.4 %collective-permute-start.15 = (bf16[32,512]{1,0:T(8,128)(2,1)S(1)}, bf16[32,512]{1,0:T(8,128)(2,1)S(1)}, u32[]{:S(2)}, u32[]{:S(2)}) collective-permute-start(bf16[32,512]{1,0:T(8,128)(2,1)S(1)} %collective-permute-done.14.refs_14_), channel_id=1, source_target_pairs={{0,4},{4,0},{8,12},{12,8},{16,20},{20,16},{24,28},{28,24},{1,5},{5... | collective-permute-start | bytes 98312 | tf_op jit(solution)/shard_map/ppermute | solution.py:190
  55.7 2.4 %collective-permute-start.17 = (bf16[32,512]{1,0:T(8,128)(2,1)S(1)}, bf16[32,512]{1,0:T(8,128)(2,1)S(1)}, u32[]{:S(2)}, u32[]{:S(2)}) collective-permute-start(bf16[32,512]{1,0:T(8,128)(2,1)S(1)} %collective-permute-done.16.refs_16_), channel_id=1, source_target_pairs={{0,4},{4,0},{8,12},{12,8},{16,20},{20,16},{24,28},{28,24},{1,5},{5... | collective-permute-start | bytes 98312 | tf_op jit(solution)/shard_map/ppermute | solution.py:190
  57.8 1.2 %collective-permute-start.19 = (bf16[32,512]{1,0:T(8,128)(2,1)S(1)}, bf16[32,512]{1,0:T(8,128)(2,1)S(1)}, u32[]{:S(2)}, u32[]{:S(2)}) collective-permute-start(bf16[32,512]{1,0:T(8,128)(2,1)S(1)} %collective-permute-done.18.refs_18_), channel_id=1, source_target_pairs={{0,4},{4,0},{8,12},{12,8},{16,20},{20,16},{24,28},{28,24},{1,5},{5... | collective-permute-start | bytes 98312 | tf_op jit(solution)/shard_map/ppermute | solution.py:190
  59.1 0.9 %copy-start.11 = (bf16[96,512]{1,0:T(8,128)(2,1)S(1)}, bf16[96,512]{1,0:T(8,128)(2,1)}, u32[]{:S(2)}) copy-start(bf16[96,512]{1,0:T(8,128)(2,1)} %copy-done.10) | copy-start | bytes 294916
  59.9 0.9 %copy-start.13 = (bf16[96,512]{1,0:T(8,128)(2,1)S(1)}, bf16[96,512]{1,0:T(8,128)(2,1)}, u32[]{:S(2)}) copy-start(bf16[96,512]{1,0:T(8,128)(2,1)} %copy-done.12) | copy-start | bytes 294916
  60.8 0.8 %copy-start.14 = (bf16[32,512]{1,0:T(8,128)(2,1)S(1)}, bf16[32,512]{1,0:T(8,128)(2,1)}, u32[]{:S(2)}) copy-start(bf16[32,512]{1,0:T(8,128)(2,1)} %get-tuple-element.28.refs_12_) | copy-start | bytes 98308
  61.6 0.7 copy-start.16
  62.3 0.7 copy-start.17
  63.0 0.7 copy-start.18
  65.6 4.9 %collective-permute-start.20 = (bf16[32,256]{1,0:T(8,128)(2,1)S(1)}, bf16[32,256]{1,0:T(8,128)(2,1)S(1)}, u32[]{:S(2)}, u32[]{:S(2)}) collective-permute-start(bf16[32,256]{1,0:T(8,128)(2,1)S(1)} %get-tuple-element.30), channel_id=1, source_target_pairs={{0,3},{1,0},{2,1},{3,2},{4,7},{5,4},{6,5},{7,6},{8,11},{9,8},{10,9... | collective-permute-start | bytes 49160 | tf_op jit(solution)/shard_map/ppermute | solution.py:228
  69.0 4.6 %collective-permute-start.21 = (bf16[32,256]{1,0:T(8,128)(2,1)S(1)}, bf16[32,256]{1,0:T(8,128)(2,1)S(1)}, u32[]{:S(2)}, u32[]{:S(2)}) collective-permute-start(bf16[32,256]{1,0:T(8,128)(2,1)S(1)} %get-tuple-element.31), channel_id=1, source_target_pairs={{0,2},{1,3},{2,0},{3,1},{4,6},{5,7},{6,4},{7,5},{8,10},{9,11},{10,... | collective-permute-start | bytes 49160 | tf_op jit(solution)/shard_map/ppermute | solution.py:228
  69.0 5.5 %collective-permute-start.22 = (bf16[32,256]{1,0:T(8,128)(2,1)S(1)}, bf16[32,256]{1,0:T(8,128)(2,1)S(1)}, u32[]{:S(2)}, u32[]{:S(2)}) collective-permute-start(bf16[32,256]{1,0:T(8,128)(2,1)S(1)} %get-tuple-element.32), channel_id=1, source_target_pairs={{0,1},{1,2},{2,3},{3,0},{4,5},{5,6},{6,7},{7,4},{8,9},{9,10},{10,1... | collective-permute-start | bytes 49160 | tf_op jit(solution)/shard_map/ppermute | solution.py:228

commit v2 on v1

v2 whole, which is shorter than its diff:
```python
import functools
import math

import jax
import jax.numpy as jnp
from jax import lax
from jax.experimental import pallas as pl
from jax.experimental.pallas import tpu as pltpu
from jax.sharding import PartitionSpec as P

HD = 128
CHUNKS = 3
VMEM = pltpu.MemorySpace.VMEM
HBM = pltpu.MemorySpace.HBM
SMEM = pltpu.MemorySpace.SMEM
IN_VMEM = pl.BlockSpec(memory_space=VMEM)
IN_HBM = pl.BlockSpec(memory_space=HBM)
IN_SMEM = pl.BlockSpec(memory_space=SMEM)


def params(mebibytes):
    return pltpu.CompilerParams(vmem_limit_bytes=mebibytes * 1024 * 1024)


def near(*arrays):
    return [pltpu.with_memory_space_constraint(a, VMEM) for a in arrays]


def far(*arrays):
    return [pltpu.with_memory_space_constraint(a, HBM) for a in arrays]


def modulate_kernel(chunks, steps_ref, x_hbm, table_hbm, *refs):
    outs, (x_ref, table, steps, sems) = refs[:chunks], refs[chunks:]
    copies = [
        pltpu.make_async_copy(x_hbm.at[0], x_ref, sems.at[0]),
        pltpu.make_async_copy(table_hbm, table, sems.at[1]),
        pltpu.make_async_copy(steps_ref, steps, sems.at[2]),
    ]
    for copy in copies:
        copy.start()
    for copy in copies:
        copy.wait()
    x = x_ref[...].astype(jnp.float32)
    scale = lax.rsqrt(jnp.mean(x * x, axis=-1, keepdims=True) + 1e-06)
    mod = table[steps[0, 0]]
    rows = (x * scale * (1.0 + mod[0:1]) + mod[1:2]).astype(jnp.bfloat16)
    width = outs[0].shape[1]
    for index, out in enumerate(outs):
        out[...] = rows[:, index * width : (index + 1) * width]


def modulate(latents, steps, mod_table):
    _, rows, depth = latents.shape
    width = depth // CHUNKS
    return pl.pallas_call(
        functools.partial(modulate_kernel, CHUNKS),
        in_specs=[pl.BlockSpec((1, 1)), IN_HBM, IN_HBM],
        out_specs=[IN_VMEM] * CHUNKS,
        out_shape=[VMEM((rows, width), jnp.bfloat16)] * CHUNKS,
        scratch_shapes=[
            pltpu.VMEM((rows, depth), jnp.bfloat16),
            pltpu.VMEM(mod_table.shape, jnp.float32),
            pltpu.SMEM((1, 1), jnp.int32),
            pltpu.SemaphoreType.DMA((3,)),
        ],
        compiler_params=params(4),
        name="modulate",
    )(steps[None], *far(latents, mod_table))


def load_kernel(shards, place, segments, *refs):
    sources, outs, (seg_col, seg_row, sems) = refs[:3], refs[3:6], refs[6:]
    copies = [pltpu.make_async_copy(sources[i], outs[i], sems.at[i]) for i in range(3)]
    for copy in copies:
        copy.start()
    tokc = segments.shape[1]
    rows = tokc // shards

    def owner(position):
        shard = place[0] - position // rows
        return jnp.where(shard < 0, shard + shards, shard) * rows + position % rows

    down = lax.broadcasted_iota(jnp.int32, (tokc, tokc), 0)
    across = lax.broadcasted_iota(jnp.int32, (tokc, tokc), 1)
    natural = segments[...]
    column = jnp.sum(jnp.where(down == across, natural, 0), axis=1, keepdims=True)
    seg_col[...] = jnp.sum(jnp.where(owner(down) == across, natural, 0), axis=1, keepdims=True)
    seg_row[...] = jnp.sum(jnp.where(owner(across) == down, column, 0), axis=0, keepdims=True)
    for copy in copies:
        copy.wait()


def load(weights, segments, place, shards):
    tokc = segments.shape[0]
    return pl.pallas_call(
        functools.partial(load_kernel, shards),
        in_specs=[IN_SMEM, pl.BlockSpec((1, tokc))] + [IN_HBM] * 3,
        out_specs=[IN_VMEM] * 5,
        out_shape=[VMEM(w.shape, w.dtype) for w in weights]
        + [VMEM((tokc, 1), jnp.int32), VMEM((1, tokc), jnp.int32)],
        scratch_shapes=[pltpu.SemaphoreType.DMA((3,))],
        compiler_params=params(2 + tokc * tokc * 32 // 2**20),
        name="load",
    )(place, segments[None], *far(*weights))


def project_kernel(places, first, last, before, *refs):
    pieces, refs = refs[: len(places)], refs[len(places) :]
    weights, refs = refs[:3], refs[3:]
    if not first:
        start, refs = refs[0], refs[1:]
    older, refs = refs[:before], refs[before:]
    width = weights[0].shape[1]
    rows, depth = pieces[0].shape
    for s in range(before):
        refs[1][s * rows : (s + 1) * rows, :] = older[s][...]
    for index, weight in enumerate(weights):
        total = None if first else start[:, index * width : (index + 1) * width]
        for place, piece in zip(places, pieces):
            part = jnp.dot(
                piece[...],
                weight[place * depth : (place + 1) * depth, :],
                preferred_element_type=jnp.float32,
            )
            total = part if total is None else total + part
        if not last:
            refs[0][:, index * width : (index + 1) * width] = total
        elif index == 0:
            refs[0][...] = total.astype(jnp.bfloat16)
        else:
            refs[1][before * rows :, (index - 1) * width : index * width] = total.astype(
                jnp.bfloat16
            )


def project(pieces, places, weights, start, last, older=()):
    rows = pieces[0].shape[0]
    width = weights[0].shape[1]
    if last:
        shapes = [
            VMEM((rows, width), jnp.bfloat16),
            VMEM((rows * (len(older) + 1), 2 * width), jnp.bfloat16),
        ]
    else:
        shapes = [VMEM((rows, 3 * width), jnp.float32)]
    extra = ([] if start is None else [start]) + list(older)
    return pl.pallas_call(
        functools.partial(project_kernel, tuple(places), start is None, last, len(older)),
        in_specs=[IN_VMEM] * (len(pieces) + 3 + len(extra)),
        out_specs=[IN_VMEM] * len(shapes),
        out_shape=shapes,
        compiler_params=params(2),
        name="project",
    )(*near(*pieces, *weights, *extra))


def attend_kernel(shards, sources, mine, seg_col, seg_row, *refs):
    queries, refs = refs[:shards], refs[shards:]
    early, refs = refs[:sources], refs[sources:]
    late, refs = refs[:sources], refs[sources:]
    outs, (q_all, kv_all) = refs[:shards], refs[shards:]
    rows, width = queries[0].shape
    heads = width // HD
    tokc = rows * shards
    many = early[0].shape[0]
    for s in range(shards):
        q_all[s * rows : (s + 1) * rows, :] = queries[s][...]
    for m in range(sources):
        kv_all[m * tokc : m * tokc + many, :] = early[m][...]
        kv_all[m * tokc + many : (m + 1) * tokc, :] = late[m][...]
    here = mine[0]
    clip = []
    for m in range(sources):
        usable = jnp.where((here ^ m) <= here, 0, 1000)
        clip.append(seg_row[...] + usable)
    clip = jnp.concatenate(clip, axis=1)
    inverse = 1.0 / math.sqrt(HD)
    block = min(tokc, 128)
    for b in range(tokc // block):
        span = slice(b * block, (b + 1) * block)
        allowed = seg_col[span, :] == clip
        for h in range(heads):
            cols = slice(h * HD, (h + 1) * HD)
            vcols = slice(width + h * HD, width + (h + 1) * HD)
            scores = lax.dot_general(
                q_all[span, cols],
                kv_all[:, cols],
                (((1,), (1,)), ((), ())),
                preferred_element_type=jnp.float32,
            )
            scores = jnp.where(allowed, scores * inverse, -1e30)
            best = jnp.max(scores, axis=-1, keepdims=True)
            weights = jnp.where(allowed, jnp.exp(scores - best), 0.0)
            total = jnp.sum(weights, axis=-1, keepdims=True)
            summed = jnp.dot(
                weights.astype(jnp.bfloat16), kv_all[:, vcols], preferred_element_type=jnp.float32
            )
            result = (summed / total).astype(jnp.bfloat16)
            for s in range(block // rows):
                outs[b * (block // rows) + s][:, cols] = result[s * rows : (s + 1) * rows]


def attend(mine, seg_col, seg_row, queries, early, late):
    shards, sources = len(queries), len(early)
    rows, width = queries[0].shape
    tokc = rows * shards
    return pl.pallas_call(
        functools.partial(attend_kernel, shards, sources),
        in_specs=[IN_SMEM] + [IN_VMEM] * (2 + shards + 2 * sources),
        out_specs=[IN_VMEM] * shards,
        out_shape=[VMEM((rows, width), jnp.bfloat16)] * shards,
        scratch_shapes=[
            pltpu.VMEM((tokc, width), jnp.bfloat16),
            pltpu.VMEM((sources * tokc, 2 * width), jnp.bfloat16),
        ],
        compiler_params=params(3 + sources * tokc * 8 // 2048),
        name="attend",
    )(mine, *near(seg_col, seg_row, *queries, *early, *late))


def place_kernel(place, *refs):
    pieces, out = refs[:-1], refs[-1]
    width = pieces[0].shape[1]
    count = len(pieces)
    for s, piece in enumerate(pieces):
        column = lax.rem(place[0] + s, count) * width
        out[0, :, pl.ds(pl.multiple_of(column, width), width)] = piece[...]


def place_columns(place, pieces):
    rows, width = pieces[0].shape
    return pl.pallas_call(
        place_kernel,
        in_specs=[IN_SMEM] + [IN_VMEM] * len(pieces),
        out_specs=IN_VMEM,
        out_shape=jax.ShapeDtypeStruct((1, rows, width * len(pieces)), jnp.bfloat16),
        compiler_params=params(2),
        name="place",
    )(place, *near(*pieces))


def share(block, groups):
    held = {0: block}
    for m in range(2, groups, 2):
        held[m] = lax.ppermute(block, "group", [(i, i ^ m) for i in range(groups)])
    for m in range(0, groups, 2):
        held[m + 1] = lax.ppermute(held[m], "group", [(i, i ^ 1) for i in range(groups)])
    return [held[m] for m in range(groups)]


def per_device(latents, steps, segment_ids, mod_table, w_query, w_key, w_value):
    shards = lax.axis_size("dp")
    groups = lax.axis_size("group")
    rows = latents.shape[1]
    place = lax.axis_index("dp").astype(jnp.int32)
    mine = lax.axis_index("group").astype(jnp.int32)
    ring = [(i, (i + 1) % shards) for i in range(shards)]

    pieces = list(modulate(latents, steps, mod_table))
    *weights, seg_col, seg_row = load(
        (w_query, w_key, w_value), segment_ids, place[None], shards
    )
    moved = [lax.ppermute(piece, "dp", ring) for piece in pieces]
    queries, shared, early = [], [], None
    for s in range(shards - 1):
        if s == shards - 2:
            early = share(shared[-1], groups)
            moved[0], pieces, early = lax.optimization_barrier((moved[0], pieces, early))
            shared = []
        older = shared if s == shards - 3 else ()
        query, keyval = project(pieces, range(CHUNKS), weights, None, True, older)
        queries.append(query)
        shared.append(keyval)
        pieces = moved
        if s < shards - 2:
            first, keyval = lax.optimization_barrier((moved[0], keyval))
            shared[-1] = keyval
            moved = [lax.ppermute(piece, "dp", ring) for piece in [first] + moved[1:]]
    start = project(pieces[:-1], range(CHUNKS - 1), weights, None, False)[0]
    query, keyval = project(pieces[-1:], [CHUNKS - 1], weights, start, True, shared)
    queries.append(query)
    late = share(keyval, groups)
    results = attend(mine[None], seg_col, seg_row, queries, early, late)
    landed = [results[0]]
    for s in range(1, shards):
        landed.append(
            lax.ppermute(results[s], "dp", [(i, (i - s) % shards) for i in range(shards)])
        )
    return place_columns(place[None], landed)


def solution(mesh):
    placed = (
        P("group", "dp", None),
        P("group"),
        P(),
        P(),
        P(None, "dp"),
        P(None, "dp"),
        P(None, "dp"),
    )
    return jax.shard_map(
        per_device, mesh=mesh, in_specs=placed, out_specs=P("group", "dp", None), check_vma=False
    )
```

time: 76.2 us -> 55.7 us (0.73); the launches traced: 75.2 us -> 55.5 us
  local copies, waits for them, and re-layouts: 20.7 us -> 0.65 us
  waiting for transfers between devices: 13.9 us -> 18.7 us
  Pallas kernels: 17.8 us -> 14 us
    unnamed x48 -> x2, local copies, waits for them, and re-layouts: 19.8 us -> 0.65 us
    pallas_call x5, Pallas kernels: 15.1 us -> 6.99 us  [project(): pl.pallas_call(functools.partial(project_kernel, tuple(places), start is...]
    pallas_call x2 -> x3, Pallas kernels: 0.93 us -> 6.03 us  [the longest x1 3.78 us: load(): pl.pallas_call(functools.partial(load_kernel, shards), in_specs=[IN_SMEM,...]
    ppermute x6 -> x9, starting transfers between devices: 6.43 us -> 9.74 us  [the longest x3 6.23 us: per_device(): moved = [lax.ppermute(piece, 'dp', ring) for piece in pieces]]
    ppermute x6, waiting for transfers between devices: 3.25 us -> 6.19 us  [share(): held[m] = lax.ppermute(block, 'group', [(i, i ^ m) for i in range(groups)])]
    ppermute x3, starting transfers between devices: 4.93 us -> 2.15 us  [per_device(): lax.ppermute(results[s], 'dp', [(i, (i - s) % shards) for i in range(shar...]
    ppermute x8, waiting for transfers between devices: 0.99 us -> 2.14 us  [share(): lax.ppermute(held[m], 'group', [(i, i ^ 1) for i in range(groups)])]
    ppermute x8, starting transfers between devices: 1.53 us -> 0.56 us  [share(): lax.ppermute(held[m], 'group', [(i, i ^ 1) for i in range(groups)])]
  transfers between devices with their start and end apart: 23 -> 26, of which waited for: 6 -> 16; matrix products, arithmetic and copies ran while one was open for 3% -> 0% of each run, Pallas kernels for 20% -> 18%
where the time goes in v2:
time: 55.7 us; the launch traced here: 55.5 us
  starting transfers between devices  21.5 us (39%)
  waiting for transfers between devices  18.7 us (34%)
  Pallas kernels  14 us (25%)
  between operations  0.74 us (1%)
  local copies, waits for them, and re-layouts  0.65 us (1%)
    ppermute x6, starting transfers between devices, share(): held[m] = lax.ppermute(block, 'group', [(i, i ^ m) for i in range(groups)])  9.02 us
    pallas_call x5, Pallas kernels, project(): pl.pallas_call(functools.partial(project_kernel, tuple(places), start is...  6.99 us
    ppermute x3, starting transfers between devices, per_device(): moved = [lax.ppermute(piece, 'dp', ring) for piece in pieces]  6.23 us
    ppermute x6, waiting for transfers between devices, per_device(): moved = [lax.ppermute(piece, 'dp', ring) for piece in [first] + moved[1:]]  6.21 us
    ppermute x6, waiting for transfers between devices, share(): held[m] = lax.ppermute(block, 'group', [(i, i ^ m) for i in range(groups)])  6.19 us
    ppermute x3, waiting for transfers between devices, per_device(): lax.ppermute(results[s], 'dp', [(i, (i - s) % shards) for i in range(shar...  4.18 us
    pallas_call x1, Pallas kernels, load(): pl.pallas_call(functools.partial(load_kernel, shards), in_specs=[IN_SMEM,...  3.78 us
    ppermute x6, starting transfers between devices, per_device(): moved = [lax.ppermute(piece, 'dp', ring) for piece in [first] + moved[1:]]  3.51 us
  transfers between devices with their start and end apart: 26, of which 16 were waited for; matrix products, arithmetic and copies ran while one was open for 0% of the time, Pallas kernels for 18%

profile of v2, /device:TPU:0, one launch (start us, length us, event | category | flops | bytes accessed | tf_op | source)
XLA Modules:
  0.0 55.5 jit_solution(16482853965539491260)
XLA Ops:
  0.7 1.6 %modulate.1 = (bf16[32,2048]{1,0:T(8,128)(2,1)S(1)}, bf16[32,2048]{1,0:T(8,128)(2,1)S(1)}, bf16[32,2048]{1,0:T(8,128)(2,1)S(1)}) custom-call(s32[1,1]{1,0:T(1,128)} %bitcast.4.steps_ref, bf16[1,32,6144]{2,1,0:T(8,128)(2,1)} %x_hbm.1, f32[16,2,6144]{2,1,0:T(2,128)} %table_hbm.1), custom_call_target="tpu_custom_call" | custom-call | tf_op jit(solution)/shard_map/modulate/pallas_call | solution.py:56
  2.3 3.1 %collective-permute-start = (bf16[32,2048]{1,0:T(8,128)(2,1)S(1)}, bf16[32,2048]{1,0:T(8,128)(2,1)S(1)}, u32[]{:S(2)}, u32[]{:S(2)}) collective-permute-start(bf16[32,2048]{1,0:T(8,128)(2,1)S(1)} %get-tuple-element.43.refs_0_), channel_id=1, source_target_pairs={{0,1},{1,2},{2,3},{3,0},{4,5},{5,6},{6,7},{7,4},{8,9},{9,10},{10,1... | collective-permute-start | bytes 393224 | tf_op jit(solution)/shard_map/ppermute | solution.py:264
  5.3 1.6 %collective-permute-start.1 = (bf16[32,2048]{1,0:T(8,128)(2,1)S(1)}, bf16[32,2048]{1,0:T(8,128)(2,1)S(1)}, u32[]{:S(2)}, u32[]{:S(2)}) collective-permute-start(bf16[32,2048]{1,0:T(8,128)(2,1)S(1)} %get-tuple-element.44.refs_1_), channel_id=1, source_target_pairs={{0,1},{1,2},{2,3},{3,0},{4,5},{5,6},{6,7},{7,4},{8,9},{9,10},{10,1... | collective-permute-start | bytes 393224 | tf_op jit(solution)/shard_map/ppermute | solution.py:264
  6.9 1.6 %collective-permute-start.2 = (bf16[32,2048]{1,0:T(8,128)(2,1)S(1)}, bf16[32,2048]{1,0:T(8,128)(2,1)S(1)}, u32[]{:S(2)}, u32[]{:S(2)}) collective-permute-start(bf16[32,2048]{1,0:T(8,128)(2,1)S(1)} %get-tuple-element.45.refs_2_), channel_id=1, source_target_pairs={{0,1},{1,2},{2,3},{3,0},{4,5},{5,6},{6,7},{7,4},{8,9},{9,10},{10,1... | collective-permute-start | bytes 393224 | tf_op jit(solution)/shard_map/ppermute | solution.py:264
  8.5 0.7 %copy-done = s32[128]{0:T(128)S(1)} copy-done((s32[128]{0:T(128)S(1)}, s32[128]{0:T(128)}, u32[]{:S(2)}) %copy-start) | copy-done | bytes 536
  9.2 3.8 %load.1 = (bf16[6144,256]{1,0:T(8,128)(2,1)S(1)}, bf16[6144,256]{1,0:T(8,128)(2,1)S(1)}, bf16[6144,256]{1,0:T(8,128)(2,1)S(1)}, s32[128,1]{1,0:T(8,128)S(1)}, s32[1,128]{1,0:T(1,128)S(1)}) custom-call(s32[1]{0:T(128)} %bitcast.place, s32[1,128]{1,0:T(1,128)S(1)} %bitcast.5, bf16[6144,256]{1,0:T(8,128)(2,1)} %refs_0_.1, bf16[6144,256]{1,0:T(8,128)(2,1)} %refs_1_.1, ...), custom_call_target="tpu_custom_call" | custom-call | tf_op jit(solution)/shard_map/load/pallas_call | solution.py:96
  12.9 1.7 %project.5 = (bf16[32,256]{1,0:T(8,128)(2,1)S(1)}, bf16[32,512]{1,0:T(8,128)(2,1)S(1)}) custom-call(bf16[32,2048]{1,0:T(8,128)(2,1)S(1)} %get-tuple-element.43.refs_0_, bf16[32,2048]{1,0:T(8,128)(2,1)S(1)} %get-tuple-element.44.refs_1_, bf16[32,2048]{1,0:T(8,128)(2,1)S(1)} %get-tuple-element.45.refs_2_, ...), custom_call_target="tpu_custom_call" | custom-call | tf_op jit(solution)/shard_map/project/pallas_call | solution.py:148
  14.7 0.0 collective-permute-done.refs_0_
  14.7 0.1 collective-permute-start.3
  14.8 0.0 collective-permute-done.1.refs_1_
  14.8 1.7 %collective-permute-start.5 = (bf16[32,2048]{1,0:T(8,128)(2,1)S(1)}, bf16[32,2048]{1,0:T(8,128)(2,1)S(1)}, u32[]{:S(2)}, u32[]{:S(2)}) collective-permute-start(bf16[32,2048]{1,0:T(8,128)(2,1)S(1)} %collective-permute-done.1.refs_1_), channel_id=1, source_target_pairs={{0,1},{1,2},{2,3},{3,0},{4,5},{5,6},{6,7},{7,4},{8,9},{9,10},{10,1... | collective-permute-start | bytes 393224 | tf_op jit(solution)/shard_map/ppermute | solution.py:279
  16.5 1.6 %collective-permute-start.6 = (bf16[32,2048]{1,0:T(8,128)(2,1)S(1)}, bf16[32,2048]{1,0:T(8,128)(2,1)S(1)}, u32[]{:S(2)}, u32[]{:S(2)}) collective-permute-start(bf16[32,2048]{1,0:T(8,128)(2,1)S(1)} %collective-permute-done.2.refs_2_), channel_id=1, source_target_pairs={{0,1},{1,2},{2,3},{3,0},{4,5},{5,6},{6,7},{7,4},{8,9},{9,10},{10,1... | collective-permute-start | bytes 393224 | tf_op jit(solution)/shard_map/ppermute | solution.py:279
  18.1 1.7 %project.6 = (bf16[32,256]{1,0:T(8,128)(2,1)S(1)}, bf16[64,512]{1,0:T(8,128)(2,1)S(1)}) custom-call(bf16[32,2048]{1,0:T(8,128)(2,1)S(1)} %collective-permute-done.refs_0_, bf16[32,2048]{1,0:T(8,128)(2,1)S(1)} %collective-permute-done.1.refs_1_, bf16[32,2048]{1,0:T(8,128)(2,1)S(1)} %collective-permute-done.2.refs_2_, ...), custom_call_target="tpu_custom_call" | custom-call | tf_op jit(solution)/shard_map/project/pallas_call | solution.py:148
  19.8 3.1 %collective-permute-done.3.refs_0_ = bf16[32,2048]{1,0:T(8,128)(2,1)S(1)} collective-permute-done((bf16[32,2048]{1,0:T(8,128)(2,1)S(1)}, bf16[32,2048]{1,0:T(8,128)(2,1)S(1)}, u32[]{:S(2)}, u32[]{:S(2)}) %collective-permute-start.3) | collective-permute-done | bytes 131104 | tf_op jit(solution)/shard_map/ppermute | solution.py:279
  23.0 0.0 collective-permute-start.4
  23.0 1.5 %collective-permute-start.8 = (bf16[64,512]{1,0:T(8,128)(2,1)S(1)}, bf16[64,512]{1,0:T(8,128)(2,1)S(1)}, u32[]{:S(2)}, u32[]{:S(2)}) collective-permute-start(bf16[64,512]{1,0:T(8,128)(2,1)S(1)} %get-tuple-element.64.refs_4_), channel_id=1, source_target_pairs={{0,8},{4,12},{8,0},{12,4},{16,24},{20,28},{24,16},{28,20},{1,9},{5... | collective-permute-start | bytes 196616 | tf_op jit(solution)/shard_map/ppermute | solution.py:246
  24.5 1.3 %collective-permute-done.5.refs_1_ = bf16[32,2048]{1,0:T(8,128)(2,1)S(1)} collective-permute-done((bf16[32,2048]{1,0:T(8,128)(2,1)S(1)}, bf16[32,2048]{1,0:T(8,128)(2,1)S(1)}, u32[]{:S(2)}, u32[]{:S(2)}) %collective-permute-start.5) | collective-permute-done | bytes 131104 | tf_op jit(solution)/shard_map/ppermute | solution.py:279
  25.8 1.5 %collective-permute-start.10 = (bf16[64,512]{1,0:T(8,128)(2,1)S(1)}, bf16[64,512]{1,0:T(8,128)(2,1)S(1)}, u32[]{:S(2)}, u32[]{:S(2)}) collective-permute-start(bf16[64,512]{1,0:T(8,128)(2,1)S(1)} %get-tuple-element.64.refs_4_), channel_id=1, source_target_pairs={{0,16},{4,20},{8,24},{12,28},{16,0},{20,4},{24,8},{28,12},{1,17},{... | collective-permute-start | bytes 196616 | tf_op jit(solution)/shard_map/ppermute | solution.py:246
  27.3 0.6 %collective-permute-done.6.refs_2_ = bf16[32,2048]{1,0:T(8,128)(2,1)S(1)} collective-permute-done((bf16[32,2048]{1,0:T(8,128)(2,1)S(1)}, bf16[32,2048]{1,0:T(8,128)(2,1)S(1)}, u32[]{:S(2)}, u32[]{:S(2)}) %collective-permute-start.6) | collective-permute-done | bytes 131104 | tf_op jit(solution)/shard_map/ppermute | solution.py:279
  27.9 2.4 %collective-permute-start.12 = (bf16[64,512]{1,0:T(8,128)(2,1)S(1)}, bf16[64,512]{1,0:T(8,128)(2,1)S(1)}, u32[]{:S(2)}, u32[]{:S(2)}) collective-permute-start(bf16[64,512]{1,0:T(8,128)(2,1)S(1)} %get-tuple-element.64.refs_4_), channel_id=1, source_target_pairs={{0,24},{4,28},{8,16},{12,20},{16,8},{20,12},{24,0},{28,4},{1,25},{... | collective-permute-start | bytes 196616 | tf_op jit(solution)/shard_map/ppermute | solution.py:246
  30.4 0.0 collective-permute-done.7.refs_5_
  30.4 0.0 collective-permute-start.15
  30.4 0.1 collective-permute-start.14
  30.5 0.3 collective-permute-done.10.refs_8_
  30.7 2.4 %collective-permute-done.12.refs_10_ = bf16[64,512]{1,0:T(8,128)(2,1)S(1)} collective-permute-done((bf16[64,512]{1,0:T(8,128)(2,1)S(1)}, bf16[64,512]{1,0:T(8,128)(2,1)S(1)}, u32[]{:S(2)}, u32[]{:S(2)}) %collective-permute-start.12) | collective-permute-done | bytes 65568 | tf_op jit(solution)/shard_map/ppermute | solution.py:246
  33.1 0.5 collective-permute-start.13
  33.6 0.7 %collective-permute-done.11.refs_9_ = bf16[64,512]{1,0:T(8,128)(2,1)S(1)} collective-permute-done((bf16[64,512]{1,0:T(8,128)(2,1)S(1)}, bf16[64,512]{1,0:T(8,128)(2,1)S(1)}, u32[]{:S(2)}, u32[]{:S(2)}) %collective-permute-start.11) | collective-permute-done | bytes 65568 | tf_op jit(solution)/shard_map/ppermute | solution.py:248
  34.4 0.2 collective-permute-done.13.refs_11_
  34.5 1.7 %project.7 = (bf16[32,256]{1,0:T(8,128)(2,1)S(1)}, bf16[32,512]{1,0:T(8,128)(2,1)S(1)}) custom-call(bf16[32,2048]{1,0:T(8,128)(2,1)S(1)} %collective-permute-done.3.refs_0_, bf16[32,2048]{1,0:T(8,128)(2,1)S(1)} %collective-permute-done.5.refs_1_, bf16[32,2048]{1,0:T(8,128)(2,1)S(1)} %collective-permute-done.6.refs_2_, ...), custom_call_target="tpu_custom_call" | custom-call | tf_op jit(solution)/shard_map/project/pallas_call | solution.py:148
  36.3 0.9 %collective-permute-done.15.refs_1_ = bf16[32,2048]{1,0:T(8,128)(2,1)S(1)} collective-permute-done((bf16[32,2048]{1,0:T(8,128)(2,1)S(1)}, bf16[32,2048]{1,0:T(8,128)(2,1)S(1)}, u32[]{:S(2)}, u32[]{:S(2)}) %collective-permute-start.15) | collective-permute-done | bytes 131104 | tf_op jit(solution)/shard_map/ppermute | solution.py:279
  37.2 1.2 %project.8.refs_4_ = f32[32,768]{1,0:T(8,128)S(1)} custom-call(bf16[32,2048]{1,0:T(8,128)(2,1)S(1)} %collective-permute-done.4.refs_0_, bf16[32,2048]{1,0:T(8,128)(2,1)S(1)} %collective-permute-done.15.refs_1_, bf16[6144,256]{1,0:T(8,128)(2,1)S(1)} %get-tuple-element.46.refs_3_.refs_2_.refs_1_, ...), custom_call_target="tpu_custom_call" | custom-call | tf_op jit(solution)/shard_map/project/pallas_call | solution.py:148
  38.4 0.2 collective-permute-done.14.refs_0_
  38.6 0.7 %project.9 = (bf16[32,256]{1,0:T(8,128)(2,1)S(1)}, bf16[64,512]{1,0:T(8,128)(2,1)S(1)}) custom-call(bf16[32,2048]{1,0:T(8,128)(2,1)S(1)} %collective-permute-done.14.refs_0_, bf16[6144,256]{1,0:T(8,128)(2,1)S(1)} %get-tuple-element.46.refs_3_.refs_2_.refs_1_, bf16[6144,256]{1,0:T(8,128)(2,1)S(1)} %get-tuple-element.47.refs_4_.refs_3_.refs_2_, ...), custom_call_target="tpu_custom_call" | custom-call | tf_op jit(solution)/shard_map/project/pallas_call | solution.py:148
  39.2 0.6 %collective-permute-start.17 = (bf16[64,512]{1,0:T(8,128)(2,1)S(1)}, bf16[64,512]{1,0:T(8,128)(2,1)S(1)}, u32[]{:S(2)}, u32[]{:S(2)}) collective-permute-start(bf16[64,512]{1,0:T(8,128)(2,1)S(1)} %get-tuple-element.72.refs_12_), channel_id=1, source_target_pairs={{0,8},{4,12},{8,0},{12,4},{16,24},{20,28},{24,16},{28,20},{1,9},{5... | collective-permute-start | bytes 196616 | tf_op jit(solution)/shard_map/ppermute | solution.py:246
  39.8 1.4 %collective-permute-start.19 = (bf16[64,512]{1,0:T(8,128)(2,1)S(1)}, bf16[64,512]{1,0:T(8,128)(2,1)S(1)}, u32[]{:S(2)}, u32[]{:S(2)}) collective-permute-start(bf16[64,512]{1,0:T(8,128)(2,1)S(1)} %get-tuple-element.72.refs_12_), channel_id=1, source_target_pairs={{0,16},{4,20},{8,24},{12,28},{16,0},{20,4},{24,8},{28,12},{1,17},{... | collective-permute-start | bytes 196616 | tf_op jit(solution)/shard_map/ppermute | solution.py:246
  41.2 1.6 %collective-permute-start.21 = (bf16[64,512]{1,0:T(8,128)(2,1)S(1)}, bf16[64,512]{1,0:T(8,128)(2,1)S(1)}, u32[]{:S(2)}, u32[]{:S(2)}) collective-permute-start(bf16[64,512]{1,0:T(8,128)(2,1)S(1)} %get-tuple-element.72.refs_12_), channel_id=1, source_target_pairs={{0,24},{4,28},{8,16},{12,20},{16,8},{20,12},{24,0},{28,4},{1,25},{... | collective-permute-start | bytes 196616 | tf_op jit(solution)/shard_map/ppermute | solution.py:246
  42.8 0.8 %collective-permute-done.17.refs_14_ = bf16[64,512]{1,0:T(8,128)(2,1)S(1)} collective-permute-done((bf16[64,512]{1,0:T(8,128)(2,1)S(1)}, bf16[64,512]{1,0:T(8,128)(2,1)S(1)}, u32[]{:S(2)}, u32[]{:S(2)}) %collective-permute-start.17) | collective-permute-done | bytes 65568 | tf_op jit(solution)/shard_map/ppermute | solution.py:246
  43.6 0.5 collective-permute-done.19.refs_16_
  44.1 0.0 collective-permute-start.20
  44.1 2.3 %collective-permute-done.21.refs_18_ = bf16[64,512]{1,0:T(8,128)(2,1)S(1)} collective-permute-done((bf16[64,512]{1,0:T(8,128)(2,1)S(1)}, bf16[64,512]{1,0:T(8,128)(2,1)S(1)}, u32[]{:S(2)}, u32[]{:S(2)}) %collective-permute-start.21) | collective-permute-done | bytes 65568 | tf_op jit(solution)/shard_map/ppermute | solution.py:246
  46.4 1.2 %collective-permute-done.22.refs_19_ = bf16[64,512]{1,0:T(8,128)(2,1)S(1)} collective-permute-done((bf16[64,512]{1,0:T(8,128)(2,1)S(1)}, bf16[64,512]{1,0:T(8,128)(2,1)S(1)}, u32[]{:S(2)}, u32[]{:S(2)}) %collective-permute-start.22) | collective-permute-done | bytes 65568 | tf_op jit(solution)/shard_map/ppermute | solution.py:248
  47.6 0.9 %attend.1 = (bf16[32,256]{1,0:T(8,128)(2,1)S(1)}, bf16[32,256]{1,0:T(8,128)(2,1)S(1)}, bf16[32,256]{1,0:T(8,128)(2,1)S(1)}, bf16[32,256]{1,0:T(8,128)(2,1)S(1)}) custom-call(s32[1]{0:T(128)} %bitcast.1.mine, s32[128,1]{1,0:T(8,128)S(1)} %get-tuple-element.41.seg_col, s32[1,128]{1,0:T(1,128)S(1)} %get-tuple-element.42.seg_row, ...), custom_call_target="tpu_custom_call" | custom-call | tf_op jit(solution)/shard_map/attend/pallas_call | solution.py:208
  48.6 0.7 %collective-permute-start.23 = (bf16[32,256]{1,0:T(8,128)(2,1)S(1)}, bf16[32,256]{1,0:T(8,128)(2,1)S(1)}, u32[]{:S(2)}, u32[]{:S(2)}) collective-permute-start(bf16[32,256]{1,0:T(8,128)(2,1)S(1)} %get-tuple-element.74), channel_id=1, source_target_pairs={{0,3},{1,0},{2,1},{3,2},{4,7},{5,4},{6,5},{7,6},{8,11},{9,8},{10,9... | collective-permute-start | bytes 49160 | tf_op jit(solution)/shard_map/ppermute | solution.py:288
  49.3 1.4 %collective-permute-start.25 = (bf16[32,256]{1,0:T(8,128)(2,1)S(1)}, bf16[32,256]{1,0:T(8,128)(2,1)S(1)}, u32[]{:S(2)}, u32[]{:S(2)}) collective-permute-start(bf16[32,256]{1,0:T(8,128)(2,1)S(1)} %get-tuple-element.76), channel_id=1, source_target_pairs={{0,1},{1,2},{2,3},{3,0},{4,5},{5,6},{6,7},{7,4},{8,9},{9,10},{10,1... | collective-permute-start | bytes 49160 | tf_op jit(solution)/shard_map/ppermute | solution.py:288
  50.7 1.6 %collective-permute-done.23.refs_1_ = bf16[32,256]{1,0:T(8,128)(2,1)S(1)} collective-permute-done((bf16[32,256]{1,0:T(8,128)(2,1)S(1)}, bf16[32,256]{1,0:T(8,128)(2,1)S(1)}, u32[]{:S(2)}, u32[]{:S(2)}) %collective-permute-start.23) | collective-permute-done | bytes 16416 | tf_op jit(solution)/shard_map/ppermute | solution.py:288
  52.4 1.6 %collective-permute-done.24.refs_2_ = bf16[32,256]{1,0:T(8,128)(2,1)S(1)} collective-permute-done((bf16[32,256]{1,0:T(8,128)(2,1)S(1)}, bf16[32,256]{1,0:T(8,128)(2,1)S(1)}, u32[]{:S(2)}, u32[]{:S(2)}) %collective-permute-start.24) | collective-permute-done | bytes 16416 | tf_op jit(solution)/shard_map/ppermute | solution.py:288
  54.0 0.9 %collective-permute-done.25.refs_3_ = bf16[32,256]{1,0:T(8,128)(2,1)S(1)} collective-permute-done((bf16[32,256]{1,0:T(8,128)(2,1)S(1)}, bf16[32,256]{1,0:T(8,128)(2,1)S(1)}, u32[]{:S(2)}, u32[]{:S(2)}) %collective-permute-start.25) | collective-permute-done | bytes 16416 | tf_op jit(solution)/shard_map/ppermute | solution.py:288
  54.9 0.6 %place.1 = bf16[1,32,1024]{2,1,0:T(8,128)(2,1)} custom-call(s32[1]{0:T(128)} %bitcast.place, bf16[32,256]{1,0:T(8,128)(2,1)S(1)} %get-tuple-element.73.refs_0_, bf16[32,256]{1,0:T(8,128)(2,1)S(1)} %collective-permute-done.23.refs_1_, bf16[32,256]{1,0:T(8,128)(2,1)S(1)} %collective-permute-done.24.refs_2_, bf16[32,256]{1,0:T(8,128)(2,1)S(1)} %collective-permute-done.25.refs_3_), custom_call_target="tpu_custom_call" | custom-call | tf_op jit(solution)/shard_map/place/pallas_call | solution.py:233
  (15 shorter events, 0.0 us)
Async XLA Ops:
  2.3 12.4 %collective-permute-start = (bf16[32,2048]{1,0:T(8,128)(2,1)S(1)}, bf16[32,2048]{1,0:T(8,128)(2,1)S(1)}, u32[]{:S(2)}, u32[]{:S(2)}) collective-permute-start(bf16[32,2048]{1,0:T(8,128)(2,1)S(1)} %get-tuple-element.43.refs_0_), channel_id=1, source_target_pairs={{0,1},{1,2},{2,3},{3,0},{4,5},{5,6},{6,7},{7,4},{8,9},{9,10},{10,1... | collective-permute-start | bytes 393224 | tf_op jit(solution)/shard_map/ppermute | solution.py:264
  5.3 9.5 %collective-permute-start.1 = (bf16[32,2048]{1,0:T(8,128)(2,1)S(1)}, bf16[32,2048]{1,0:T(8,128)(2,1)S(1)}, u32[]{:S(2)}, u32[]{:S(2)}) collective-permute-start(bf16[32,2048]{1,0:T(8,128)(2,1)S(1)} %get-tuple-element.44.refs_1_), channel_id=1, source_target_pairs={{0,1},{1,2},{2,3},{3,0},{4,5},{5,6},{6,7},{7,4},{8,9},{9,10},{10,1... | collective-permute-start | bytes 393224 | tf_op jit(solution)/shard_map/ppermute | solution.py:264
  6.9 9.6 %collective-permute-start.2 = (bf16[32,2048]{1,0:T(8,128)(2,1)S(1)}, bf16[32,2048]{1,0:T(8,128)(2,1)S(1)}, u32[]{:S(2)}, u32[]{:S(2)}) collective-permute-start(bf16[32,2048]{1,0:T(8,128)(2,1)S(1)} %get-tuple-element.45.refs_2_), channel_id=1, source_target_pairs={{0,1},{1,2},{2,3},{3,0},{4,5},{5,6},{6,7},{7,4},{8,9},{9,10},{10,1... | collective-permute-start | bytes 393224 | tf_op jit(solution)/shard_map/ppermute | solution.py:264
  8.5 0.7 %copy-start = (s32[128]{0:T(128)S(1)}, s32[128]{0:T(128)}, u32[]{:S(2)}) copy-start(s32[128]{0:T(128)} %param.9) | copy-start | bytes 1540
  14.7 8.3 %collective-permute-start.3 = (bf16[32,2048]{1,0:T(8,128)(2,1)S(1)}, bf16[32,2048]{1,0:T(8,128)(2,1)S(1)}, u32[]{:S(2)}, u32[]{:S(2)}) collective-permute-start(bf16[32,2048]{1,0:T(8,128)(2,1)S(1)} %collective-permute-done.refs_0_), channel_id=1, source_target_pairs={{0,1},{1,2},{2,3},{3,0},{4,5},{5,6},{6,7},{7,4},{8,9},{9,10},{10,1... | collective-permute-start | bytes 393224 | tf_op jit(solution)/shard_map/ppermute | solution.py:279
  14.8 11.0 %collective-permute-start.5 = (bf16[32,2048]{1,0:T(8,128)(2,1)S(1)}, bf16[32,2048]{1,0:T(8,128)(2,1)S(1)}, u32[]{:S(2)}, u32[]{:S(2)}) collective-permute-start(bf16[32,2048]{1,0:T(8,128)(2,1)S(1)} %collective-permute-done.1.refs_1_), channel_id=1, source_target_pairs={{0,1},{1,2},{2,3},{3,0},{4,5},{5,6},{6,7},{7,4},{8,9},{9,10},{10,1... | collective-permute-start | bytes 393224 | tf_op jit(solution)/shard_map/ppermute | solution.py:279
  16.5 11.4 %collective-permute-start.6 = (bf16[32,2048]{1,0:T(8,128)(2,1)S(1)}, bf16[32,2048]{1,0:T(8,128)(2,1)S(1)}, u32[]{:S(2)}, u32[]{:S(2)}) collective-permute-start(bf16[32,2048]{1,0:T(8,128)(2,1)S(1)} %collective-permute-done.2.refs_2_), channel_id=1, source_target_pairs={{0,1},{1,2},{2,3},{3,0},{4,5},{5,6},{6,7},{7,4},{8,9},{9,10},{10,1... | collective-permute-start | bytes 393224 | tf_op jit(solution)/shard_map/ppermute | solution.py:279
  23.0 10.2 %collective-permute-start.4 = (bf16[32,2048]{1,0:T(8,128)(2,1)S(1)}, bf16[32,2048]{1,0:T(8,128)(2,1)S(1)}, u32[]{:S(2)}, u32[]{:S(2)}) collective-permute-start(bf16[32,2048]{1,0:T(8,128)(2,1)S(1)} %collective-permute-done.3.refs_0_), channel_id=1, source_target_pairs={{0,1},{1,2},{2,3},{3,0},{4,5},{5,6},{6,7},{7,4},{8,9},{9,10},{10,1... | collective-permute-start | bytes 393224 | tf_op jit(solution)/shard_map/ppermute | solution.py:279
  23.0 7.4 %collective-permute-start.7 = (bf16[64,512]{1,0:T(8,128)(2,1)S(1)}, bf16[64,512]{1,0:T(8,128)(2,1)S(1)}, u32[]{:S(2)}, u32[]{:S(2)}) collective-permute-start(bf16[64,512]{1,0:T(8,128)(2,1)S(1)} %get-tuple-element.64.refs_4_), channel_id=1, source_target_pairs={{0,4},{4,0},{8,12},{12,8},{16,20},{20,16},{24,28},{28,24},{1,5},{5... | collective-permute-start | bytes 196616 | tf_op jit(solution)/shard_map/ppermute | solution.py:248
  23.0 7.4 %collective-permute-start.8 = (bf16[64,512]{1,0:T(8,128)(2,1)S(1)}, bf16[64,512]{1,0:T(8,128)(2,1)S(1)}, u32[]{:S(2)}, u32[]{:S(2)}) collective-permute-start(bf16[64,512]{1,0:T(8,128)(2,1)S(1)} %get-tuple-element.64.refs_4_), channel_id=1, source_target_pairs={{0,8},{4,12},{8,0},{12,4},{16,24},{20,28},{24,16},{28,20},{1,9},{5... | collective-permute-start | bytes 196616 | tf_op jit(solution)/shard_map/ppermute | solution.py:246
  25.8 5.0 %collective-permute-start.10 = (bf16[64,512]{1,0:T(8,128)(2,1)S(1)}, bf16[64,512]{1,0:T(8,128)(2,1)S(1)}, u32[]{:S(2)}, u32[]{:S(2)}) collective-permute-start(bf16[64,512]{1,0:T(8,128)(2,1)S(1)} %get-tuple-element.64.refs_4_), channel_id=1, source_target_pairs={{0,16},{4,20},{8,24},{12,28},{16,0},{20,4},{24,8},{28,12},{1,17},{... | collective-permute-start | bytes 196616 | tf_op jit(solution)/shard_map/ppermute | solution.py:246
  27.9 5.2 %collective-permute-start.12 = (bf16[64,512]{1,0:T(8,128)(2,1)S(1)}, bf16[64,512]{1,0:T(8,128)(2,1)S(1)}, u32[]{:S(2)}, u32[]{:S(2)}) collective-permute-start(bf16[64,512]{1,0:T(8,128)(2,1)S(1)} %get-tuple-element.64.refs_4_), channel_id=1, source_target_pairs={{0,24},{4,28},{8,16},{12,20},{16,8},{20,12},{24,0},{28,4},{1,25},{... | collective-permute-start | bytes 196616 | tf_op jit(solution)/shard_map/ppermute | solution.py:246
  30.4 6.8 %collective-permute-start.15 = (bf16[32,2048]{1,0:T(8,128)(2,1)S(1)}, bf16[32,2048]{1,0:T(8,128)(2,1)S(1)}, u32[]{:S(2)}, u32[]{:S(2)}) collective-permute-start(bf16[32,2048]{1,0:T(8,128)(2,1)S(1)} %collective-permute-done.5.refs_1_), channel_id=1, source_target_pairs={{0,1},{1,2},{2,3},{3,0},{4,5},{5,6},{6,7},{7,4},{8,9},{9,10},{10,1... | collective-permute-start | bytes 393224 | tf_op jit(solution)/shard_map/ppermute | solution.py:279
  30.4 8.2 %collective-permute-start.14 = (bf16[32,2048]{1,0:T(8,128)(2,1)S(1)}, bf16[32,2048]{1,0:T(8,128)(2,1)S(1)}, u32[]{:S(2)}, u32[]{:S(2)}) collective-permute-start(bf16[32,2048]{1,0:T(8,128)(2,1)S(1)} %collective-permute-done.6.refs_2_), channel_id=1, source_target_pairs={{0,1},{1,2},{2,3},{3,0},{4,5},{5,6},{6,7},{7,4},{8,9},{9,10},{10,1... | collective-permute-start | bytes 393224 | tf_op jit(solution)/shard_map/ppermute | solution.py:279
  30.7 2.9 %collective-permute-start.9 = (bf16[64,512]{1,0:T(8,128)(2,1)S(1)}, bf16[64,512]{1,0:T(8,128)(2,1)S(1)}, u32[]{:S(2)}, u32[]{:S(2)}) collective-permute-start(bf16[64,512]{1,0:T(8,128)(2,1)S(1)} %collective-permute-done.8.refs_6_), channel_id=1, source_target_pairs={{0,4},{4,0},{8,12},{12,8},{16,20},{20,16},{24,28},{28,24},{1,5},{5... | collective-permute-start | bytes 196616 | tf_op jit(solution)/shard_map/ppermute | solution.py:248
  33.1 1.3 %collective-permute-start.11 = (bf16[64,512]{1,0:T(8,128)(2,1)S(1)}, bf16[64,512]{1,0:T(8,128)(2,1)S(1)}, u32[]{:S(2)}, u32[]{:S(2)}) collective-permute-start(bf16[64,512]{1,0:T(8,128)(2,1)S(1)} %collective-permute-done.10.refs_8_), channel_id=1, source_target_pairs={{0,4},{4,0},{8,12},{12,8},{16,20},{20,16},{24,28},{28,24},{1,5},{5... | collective-permute-start | bytes 196616 | tf_op jit(solution)/shard_map/ppermute | solution.py:248
  33.1 1.4 %collective-permute-start.13 = (bf16[64,512]{1,0:T(8,128)(2,1)S(1)}, bf16[64,512]{1,0:T(8,128)(2,1)S(1)}, u32[]{:S(2)}, u32[]{:S(2)}) collective-permute-start(bf16[64,512]{1,0:T(8,128)(2,1)S(1)} %collective-permute-done.12.refs_10_), channel_id=1, source_target_pairs={{0,4},{4,0},{8,12},{12,8},{16,20},{20,16},{24,28},{28,24},{1,5},{5... | collective-permute-start | bytes 196616 | tf_op jit(solution)/shard_map/ppermute | solution.py:248
  39.2 4.4 %collective-permute-start.17 = (bf16[64,512]{1,0:T(8,128)(2,1)S(1)}, bf16[64,512]{1,0:T(8,128)(2,1)S(1)}, u32[]{:S(2)}, u32[]{:S(2)}) collective-permute-start(bf16[64,512]{1,0:T(8,128)(2,1)S(1)} %get-tuple-element.72.refs_12_), channel_id=1, source_target_pairs={{0,8},{4,12},{8,0},{12,4},{16,24},{20,28},{24,16},{28,20},{1,9},{5... | collective-permute-start | bytes 196616 | tf_op jit(solution)/shard_map/ppermute | solution.py:246
  39.8 4.3 %collective-permute-start.19 = (bf16[64,512]{1,0:T(8,128)(2,1)S(1)}, bf16[64,512]{1,0:T(8,128)(2,1)S(1)}, u32[]{:S(2)}, u32[]{:S(2)}) collective-permute-start(bf16[64,512]{1,0:T(8,128)(2,1)S(1)} %get-tuple-element.72.refs_12_), channel_id=1, source_target_pairs={{0,16},{4,20},{8,24},{12,28},{16,0},{20,4},{24,8},{28,12},{1,17},{... | collective-permute-start | bytes 196616 | tf_op jit(solution)/shard_map/ppermute | solution.py:246
  41.2 5.2 %collective-permute-start.21 = (bf16[64,512]{1,0:T(8,128)(2,1)S(1)}, bf16[64,512]{1,0:T(8,128)(2,1)S(1)}, u32[]{:S(2)}, u32[]{:S(2)}) collective-permute-start(bf16[64,512]{1,0:T(8,128)(2,1)S(1)} %get-tuple-element.72.refs_12_), channel_id=1, source_target_pairs={{0,24},{4,28},{8,16},{12,20},{16,8},{20,12},{24,0},{28,4},{1,25},{... | collective-permute-start | bytes 196616 | tf_op jit(solution)/shard_map/ppermute | solution.py:246
  42.8 3.6 %collective-permute-start.16 = (bf16[64,512]{1,0:T(8,128)(2,1)S(1)}, bf16[64,512]{1,0:T(8,128)(2,1)S(1)}, u32[]{:S(2)}, u32[]{:S(2)}) collective-permute-start(bf16[64,512]{1,0:T(8,128)(2,1)S(1)} %get-tuple-element.72.refs_12_), channel_id=1, source_target_pairs={{0,4},{4,0},{8,12},{12,8},{16,20},{20,16},{24,28},{28,24},{1,5},{5... | collective-permute-start | bytes 196616 | tf_op jit(solution)/shard_map/ppermute | solution.py:248
  43.6 2.8 %collective-permute-start.18 = (bf16[64,512]{1,0:T(8,128)(2,1)S(1)}, bf16[64,512]{1,0:T(8,128)(2,1)S(1)}, u32[]{:S(2)}, u32[]{:S(2)}) collective-permute-start(bf16[64,512]{1,0:T(8,128)(2,1)S(1)} %collective-permute-done.17.refs_14_), channel_id=1, source_target_pairs={{0,4},{4,0},{8,12},{12,8},{16,20},{20,16},{24,28},{28,24},{1,5},{5... | collective-permute-start | bytes 196616 | tf_op jit(solution)/shard_map/ppermute | solution.py:248
  44.1 2.3 %collective-permute-start.20 = (bf16[64,512]{1,0:T(8,128)(2,1)S(1)}, bf16[64,512]{1,0:T(8,128)(2,1)S(1)}, u32[]{:S(2)}, u32[]{:S(2)}) collective-permute-start(bf16[64,512]{1,0:T(8,128)(2,1)S(1)} %collective-permute-done.19.refs_16_), channel_id=1, source_target_pairs={{0,4},{4,0},{8,12},{12,8},{16,20},{20,16},{24,28},{28,24},{1,5},{5... | collective-permute-start | bytes 196616 | tf_op jit(solution)/shard_map/ppermute | solution.py:248
  46.4 1.3 %collective-permute-start.22 = (bf16[64,512]{1,0:T(8,128)(2,1)S(1)}, bf16[64,512]{1,0:T(8,128)(2,1)S(1)}, u32[]{:S(2)}, u32[]{:S(2)}) collective-permute-start(bf16[64,512]{1,0:T(8,128)(2,1)S(1)} %collective-permute-done.21.refs_18_), channel_id=1, source_target_pairs={{0,4},{4,0},{8,12},{12,8},{16,20},{20,16},{24,28},{28,24},{1,5},{5... | collective-permute-start | bytes 196616 | tf_op jit(solution)/shard_map/ppermute | solution.py:248
  48.6 3.8 %collective-permute-start.23 = (bf16[32,256]{1,0:T(8,128)(2,1)S(1)}, bf16[32,256]{1,0:T(8,128)(2,1)S(1)}, u32[]{:S(2)}, u32[]{:S(2)}) collective-permute-start(bf16[32,256]{1,0:T(8,128)(2,1)S(1)} %get-tuple-element.74), channel_id=1, source_target_pairs={{0,3},{1,0},{2,1},{3,2},{4,7},{5,4},{6,5},{7,6},{8,11},{9,8},{10,9... | collective-permute-start | bytes 49160 | tf_op jit(solution)/shard_map/ppermute | solution.py:288
  49.3 4.7 %collective-permute-start.24 = (bf16[32,256]{1,0:T(8,128)(2,1)S(1)}, bf16[32,256]{1,0:T(8,128)(2,1)S(1)}, u32[]{:S(2)}, u32[]{:S(2)}) collective-permute-start(bf16[32,256]{1,0:T(8,128)(2,1)S(1)} %get-tuple-element.75), channel_id=1, source_target_pairs={{0,2},{1,3},{2,0},{3,1},{4,6},{5,7},{6,4},{7,5},{8,10},{9,11},{10,... | collective-permute-start | bytes 49160 | tf_op jit(solution)/shard_map/ppermute | solution.py:288
  49.3 5.6 %collective-permute-start.25 = (bf16[32,256]{1,0:T(8,128)(2,1)S(1)}, bf16[32,256]{1,0:T(8,128)(2,1)S(1)}, u32[]{:S(2)}, u32[]{:S(2)}) collective-permute-start(bf16[32,256]{1,0:T(8,128)(2,1)S(1)} %get-tuple-element.76), channel_id=1, source_target_pairs={{0,1},{1,2},{2,3},{3,0},{4,5},{5,6},{6,7},{7,4},{8,9},{9,10},{10,1... | collective-permute-start | bytes 49160 | tf_op jit(solution)/shard_map/ppermute | solution.py:288

commit v3 on v2

--- a/solution.py
+++ b/solution.py
@@ -9,7 +9,7 @@
 from jax.sharding import PartitionSpec as P
 
 HD = 128
-CHUNKS = 3
+CHUNKS = 2
 VMEM = pltpu.MemorySpace.VMEM
 HBM = pltpu.MemorySpace.HBM
 SMEM = pltpu.MemorySpace.SMEM
@@ -43,7 +43,7 @@
         copy.wait()
     x = x_ref[...].astype(jnp.float32)
     scale = lax.rsqrt(jnp.mean(x * x, axis=-1, keepdims=True) + 1e-06)
-    mod = table[steps[0, 0]]
+    mod = table[steps[0]]
     rows = (x * scale * (1.0 + mod[0:1]) + mod[1:2]).astype(jnp.bfloat16)
     width = outs[0].shape[1]
     for index, out in enumerate(outs):
@@ -55,25 +55,38 @@
     width = depth // CHUNKS
     return pl.pallas_call(
         functools.partial(modulate_kernel, CHUNKS),
-        in_specs=[pl.BlockSpec((1, 1)), IN_HBM, IN_HBM],
+        in_specs=[IN_HBM, IN_HBM, IN_HBM],
         out_specs=[IN_VMEM] * CHUNKS,
         out_shape=[VMEM((rows, width), jnp.bfloat16)] * CHUNKS,
         scratch_shapes=[
             pltpu.VMEM((rows, depth), jnp.bfloat16),
             pltpu.VMEM(mod_table.shape, jnp.float32),
-            pltpu.SMEM((1, 1), jnp.int32),
+            pltpu.SMEM((1,), jnp.int32),
             pltpu.SemaphoreType.DMA((3,)),
         ],
         compiler_params=params(4),
         name="modulate",
-    )(steps[None], *far(latents, mod_table))
-
-
-def load_kernel(shards, place, segments, *refs):
-    sources, outs, (seg_col, seg_row, sems) = refs[:3], refs[3:6], refs[6:]
-    copies = [pltpu.make_async_copy(sources[i], outs[i], sems.at[i]) for i in range(3)]
-    for copy in copies:
-        copy.start()
+    )(steps, *far(latents, mod_table))
+
+
+def begin_kernel(shards, place, segments, *refs):
+    sources, refs = refs[:3], refs[3:]
+    pieces, refs = refs[:CHUNKS], refs[CHUNKS:]
+    query, keyval = refs[:2]
+    outs, (seg_col, seg_row, sems) = refs[2:5], refs[5:]
+    depth = pieces[0].shape[1]
+    width = query.shape[1]
+    spans = [slice(k * depth, (k + 1) * depth) for k in range(CHUNKS)]
+    copies = [
+        [
+            pltpu.make_async_copy(sources[i].at[span], outs[i].at[span], sems.at[i, k])
+            for k, span in enumerate(spans)
+        ]
+        for i in range(3)
+    ]
+    for column in copies:
+        for copy in column:
+            copy.start()
     tokc = segments.shape[1]
     rows = tokc // shards
 
@@ -87,39 +100,54 @@
     column = jnp.sum(jnp.where(down == across, natural, 0), axis=1, keepdims=True)
     seg_col[...] = jnp.sum(jnp.where(owner(down) == across, natural, 0), axis=1, keepdims=True)
     seg_row[...] = jnp.sum(jnp.where(owner(across) == down, column, 0), axis=0, keepdims=True)
-    for copy in copies:
-        copy.wait()
-
-
-def load(weights, segments, place, shards):
+    for i in range(3):
+        total = None
+        for k, span in enumerate(spans):
+            copies[i][k].wait()
+            part = jnp.dot(pieces[k][...], outs[i][span], preferred_element_type=jnp.float32)
+            total = part if total is None else total + part
+        if i == 0:
+            query[...] = total.astype(jnp.bfloat16)
+        else:
+            keyval[:, (i - 1) * width : i * width] = total.astype(jnp.bfloat16)
+
+
+def begin(weights, segments, pieces, place, shards):
     tokc = segments.shape[0]
-    return pl.pallas_call(
-        functools.partial(load_kernel, shards),
-        in_specs=[IN_SMEM, pl.BlockSpec((1, tokc))] + [IN_HBM] * 3,
-        out_specs=[IN_VMEM] * 5,
-        out_shape=[VMEM(w.shape, w.dtype) for w in weights]
+    rows = pieces[0].shape[0]
+    width = weights[0].shape[1]
+    return pl.pallas_call(
+        functools.partial(begin_kernel, shards),
+        in_specs=[IN_SMEM, pl.BlockSpec((1, tokc))] + [IN_HBM] * 3 + [IN_VMEM] * CHUNKS,
+        out_specs=[IN_VMEM] * 7,
+        out_shape=[VMEM((rows, width), jnp.bfloat16), VMEM((rows, 2 * width), jnp.bfloat16)]
+        + [VMEM(w.shape, w.dtype) for w in weights]
         + [VMEM((tokc, 1), jnp.int32), VMEM((1, tokc), jnp.int32)],
-        scratch_shapes=[pltpu.SemaphoreType.DMA((3,))],
+        scratch_shapes=[pltpu.SemaphoreType.DMA((3, CHUNKS))],
         compiler_params=params(2 + tokc * tokc * 32 // 2**20),
-        name="load",
-    )(place, segments[None], *far(*weights))
-
-
-def project_kernel(places, first, last, before, *refs):
-    pieces, refs = refs[: len(places)], refs[len(places) :]
+        name="begin",
+    )(place, segments[None], *far(*weights), *near(*pieces))
+
+
+def project_kernel(count, places, first, last, older, *refs):
+    pieces, refs = refs[: count * len(places)], refs[count * len(places) :]
     weights, refs = refs[:3], refs[3:]
     if not first:
         start, refs = refs[0], refs[1:]
-    older, refs = refs[:before], refs[before:]
+    if older:
+        before, refs = refs[0], refs[1:]
+        refs[1][:older, :] = before[...]
     width = weights[0].shape[1]
-    rows, depth = pieces[0].shape
-    for s in range(before):
-        refs[1][s * rows : (s + 1) * rows, :] = older[s][...]
+    depth = pieces[0].shape[1]
+    stacked = [
+        jnp.concatenate([pieces[s * len(places) + k][...] for s in range(count)], axis=0)
+        for k in range(len(places))
+    ]
     for index, weight in enumerate(weights):
         total = None if first else start[:, index * width : (index + 1) * width]
-        for place, piece in zip(places, pieces):
+        for k, place in enumerate(places):
             part = jnp.dot(
-                piece[...],
+                stacked[k],
                 weight[place * depth : (place + 1) * depth, :],
                 preferred_element_type=jnp.float32,
             )
@@ -129,43 +157,46 @@
         elif index == 0:
             refs[0][...] = total.astype(jnp.bfloat16)
         else:
-            refs[1][before * rows :, (index - 1) * width : index * width] = total.astype(
-                jnp.bfloat16
-            )
-
-
-def project(pieces, places, weights, start, last, older=()):
-    rows = pieces[0].shape[0]
+            refs[1][older:, (index - 1) * width : index * width] = total.astype(jnp.bfloat16)
+
+
+def project(shard_pieces, places, weights, start, last, before=None):
+    count = len(shard_pieces)
+    rows = shard_pieces[0][0].shape[0] * count
+    older = 0 if before is None else before.shape[0]
     width = weights[0].shape[1]
     if last:
         shapes = [
             VMEM((rows, width), jnp.bfloat16),
-            VMEM((rows * (len(older) + 1), 2 * width), jnp.bfloat16),
+            VMEM((older + rows, 2 * width), jnp.bfloat16),
         ]
     else:
         shapes = [VMEM((rows, 3 * width), jnp.float32)]
-    extra = ([] if start is None else [start]) + list(older)
-    return pl.pallas_call(
-        functools.partial(project_kernel, tuple(places), start is None, last, len(older)),
+    pieces = [piece for shard in shard_pieces for piece in shard]
+    extra = [array for array in (start, before) if array is not None]
+    return pl.pallas_call(
+        functools.partial(project_kernel, count, tuple(places), start is None, last, older),
         in_specs=[IN_VMEM] * (len(pieces) + 3 + len(extra)),
         out_specs=[IN_VMEM] * len(shapes),
         out_shape=shapes,
-        compiler_params=params(2),
+        compiler_params=params(3 + count),
         name="project",
     )(*near(*pieces, *weights, *extra))
 
 
-def attend_kernel(shards, sources, mine, seg_col, seg_row, *refs):
-    queries, refs = refs[:shards], refs[shards:]
+def attend_kernel(shards, parts, sources, mine, seg_col, seg_row, *refs):
+    queries, refs = refs[:parts], refs[parts:]
     early, refs = refs[:sources], refs[sources:]
     late, refs = refs[:sources], refs[sources:]
     outs, (q_all, kv_all) = refs[:shards], refs[shards:]
-    rows, width = queries[0].shape
+    tokc, width = q_all.shape
+    rows = tokc // shards
     heads = width // HD
-    tokc = rows * shards
     many = early[0].shape[0]
-    for s in range(shards):
-        q_all[s * rows : (s + 1) * rows, :] = queries[s][...]
+    filled = 0
+    for query in queries:
+        q_all[filled : filled + query.shape[0], :] = query[...]
+        filled += query.shape[0]
     for m in range(sources):
         kv_all[m * tokc : m * tokc + many, :] = early[m][...]
         kv_all[m * tokc + many : (m + 1) * tokc, :] = late[m][...]
@@ -201,13 +232,14 @@
                 outs[b * (block // rows) + s][:, cols] = result[s * rows : (s + 1) * rows]
 
 
-def attend(mine, seg_col, seg_row, queries, early, late):
-    shards, sources = len(queries), len(early)
-    rows, width = queries[0].shape
-    tokc = rows * shards
-    return pl.pallas_call(
-        functools.partial(attend_kernel, shards, sources),
-        in_specs=[IN_SMEM] + [IN_VMEM] * (2 + shards + 2 * sources),
+def attend(shards, mine, seg_col, seg_row, queries, early, late):
+    sources = len(early)
+    width = queries[0].shape[1]
+    tokc = seg_col.shape[0]
+    rows = tokc // shards
+    return pl.pallas_call(
+        functools.partial(attend_kernel, shards, len(queries), sources),
+        in_specs=[IN_SMEM] + [IN_VMEM] * (2 + len(queries) + 2 * sources),
         out_specs=[IN_VMEM] * shards,
         out_shape=[VMEM((rows, width), jnp.bfloat16)] * shards,
         scratch_shapes=[
@@ -240,13 +272,16 @@
     )(place, *near(*pieces))
 
 
-def share(block, groups):
-    held = {0: block}
-    for m in range(2, groups, 2):
-        held[m] = lax.ppermute(block, "group", [(i, i ^ m) for i in range(groups)])
-    for m in range(0, groups, 2):
-        held[m + 1] = lax.ppermute(held[m], "group", [(i, i ^ 1) for i in range(groups)])
-    return [held[m] for m in range(groups)]
+def across_chips(block, groups):
+    return [block] + [
+        lax.ppermute(block, "group", [(i, i ^ m) for i in range(groups)])
+        for m in range(2, groups, 2)
+    ]
+
+
+def across_cores(held, groups):
+    swap = [(i, i ^ 1) for i in range(groups)]
+    return [each for block in held for each in (block, lax.ppermute(block, "group", swap))]
 
 
 def per_device(latents, steps, segment_ids, mod_table, w_query, w_key, w_value):
@@ -258,30 +293,31 @@
     ring = [(i, (i + 1) % shards) for i in range(shards)]
 
     pieces = list(modulate(latents, steps, mod_table))
-    *weights, seg_col, seg_row = load(
-        (w_query, w_key, w_value), segment_ids, place[None], shards
+    query, keyval, *rest = begin(
+        (w_query, w_key, w_value), segment_ids, pieces, place[None], shards
     )
+    weights, (seg_col, seg_row) = rest[:3], rest[3:]
+    queries = [query]
+    pieces = [lax.ppermute(piece, "dp", ring) for piece in pieces]
+    pieces[0], keyval = lax.optimization_barrier((pieces[0], keyval))
+    arrived = []
+    for s in range(1, shards - 2):
+        arrived.append(pieces)
+        pieces = [lax.ppermute(piece, "dp", ring) for piece in pieces]
+    query, keyval = project(arrived, range(CHUNKS), weights, None, True, keyval)
+    queries.append(query)
+    early = across_chips(keyval, groups)
+    pieces[-1], early = lax.optimization_barrier((pieces[-1], early))
+    early = across_cores(early, groups)
     moved = [lax.ppermute(piece, "dp", ring) for piece in pieces]
-    queries, shared, early = [], [], None
-    for s in range(shards - 1):
-        if s == shards - 2:
-            early = share(shared[-1], groups)
-            moved[0], pieces, early = lax.optimization_barrier((moved[0], pieces, early))
-            shared = []
-        older = shared if s == shards - 3 else ()
-        query, keyval = project(pieces, range(CHUNKS), weights, None, True, older)
-        queries.append(query)
-        shared.append(keyval)
-        pieces = moved
-        if s < shards - 2:
-            first, keyval = lax.optimization_barrier((moved[0], keyval))
-            shared[-1] = keyval
-            moved = [lax.ppermute(piece, "dp", ring) for piece in [first] + moved[1:]]
-    start = project(pieces[:-1], range(CHUNKS - 1), weights, None, False)[0]
-    query, keyval = project(pieces[-1:], [CHUNKS - 1], weights, start, True, shared)
+    moved[0], early = lax.optimization_barrier((moved[0], early))
+    query, keyval = project([pieces], range(CHUNKS), weights, None, True)
     queries.append(query)
-    late = share(keyval, groups)
-    results = attend(mine[None], seg_col, seg_row, queries, early, late)
+    start = project([moved[:-1]], range(CHUNKS - 1), weights, None, False)[0]
+    query, keyval = project([moved[-1:]], [CHUNKS - 1], weights, start, True, keyval)
+    queries.append(query)
+    late = across_cores(across_chips(keyval, groups), groups)
+    results = attend(shards, mine[None], seg_col, seg_row, queries, early, late)
     landed = [results[0]]
     for s in range(1, shards):
         landed.append(

time: 55.7 us -> 52.8 us (0.948)
  starting transfers between devices: 21.5 us -> 20.3 us
  waiting for transfers between devices: 18.7 us -> 17.7 us
  Pallas kernels: 14 us -> 13.3 us
    ppermute x20 -> x18, waiting for transfers between devices: 14.5 us -> 12 us  [the longest x6 6.7 us: across_chips(): lax.ppermute(block, 'group', [(i, i ^ m) for i in range(groups)])]
    ppermute x3 -> x2, starting transfers between devices: 6.23 us -> 4.37 us  [per_device(): moved = [lax.ppermute(piece, 'dp', ring) for piece in pieces]]
    ppermute x3 -> x2, waiting for transfers between devices: 0.01 us -> 1.21 us  [per_device(): moved = [lax.ppermute(piece, 'dp', ring) for piece in pieces]]
    pallas_call x8 -> x7, Pallas kernels: 13.3 us -> 12.6 us  [the longest x4 5.23 us: project(): pl.pallas_call(functools.partial(project_kernel, count, tuple(places), st...]
    ppermute x20 -> x18, starting transfers between devices: 13.1 us -> 13.4 us  [the longest x6 7.06 us: across_chips(): lax.ppermute(block, 'group', [(i, i ^ m) for i in range(groups)])]
  transfers between devices with their start and end apart: 26 -> 23, of which waited for: 16 -> 13; matrix products, arithmetic and copies ran while one was open for 0% -> 0% of each run, Pallas kernels for 18% -> 17%
where the time goes in v3:
time: 52.8 us; the launch traced here: 52.7 us
  starting transfers between devices  20.3 us (38%)
  waiting for transfers between devices  17.7 us (34%)
  Pallas kernels  13.3 us (25%)
  between operations  0.74 us (1%)
  local copies, waits for them, and re-layouts  0.65 us (1%)
    ppermute x6, starting transfers between devices, across_chips(): lax.ppermute(block, 'group', [(i, i ^ m) for i in range(groups)])  7.06 us
    ppermute x6, waiting for transfers between devices, across_chips(): lax.ppermute(block, 'group', [(i, i ^ m) for i in range(groups)])  6.7 us
    ppermute x4, starting transfers between devices, per_device(): pieces = [lax.ppermute(piece, 'dp', ring) for piece in pieces]  5.63 us
    pallas_call x4, Pallas kernels, project(): pl.pallas_call(functools.partial(project_kernel, count, tuple(places), st...  5.23 us
    pallas_call x1, Pallas kernels, begin(): pl.pallas_call(functools.partial(begin_kernel, shards), in_specs=[IN_SMEM...  4.85 us
    ppermute x3, waiting for transfers between devices, per_device(): lax.ppermute(results[s], 'dp', [(i, (i - s) % shards) for i in range(shar...  4.53 us
    ppermute x2, starting transfers between devices, per_device(): moved = [lax.ppermute(piece, 'dp', ring) for piece in pieces]  4.37 us
    ppermute x4, waiting for transfers between devices, per_device(): pieces = [lax.ppermute(piece, 'dp', ring) for piece in pieces]  3.32 us
  transfers between devices with their start and end apart: 23, of which 13 were waited for; matrix products, arithmetic and copies ran while one was open for 0% of the time, Pallas kernels for 17%

profile of v3, /device:TPU:0, one launch (start us, length us, event | category | flops | bytes accessed | tf_op | source)
XLA Modules:
  0.0 52.7 jit_solution(6834660173985180030)
XLA Ops:
  0.7 1.6 %modulate.1 = (bf16[32,3072]{1,0:T(8,128)(2,1)S(1)}, bf16[32,3072]{1,0:T(8,128)(2,1)S(1)}) custom-call(s32[1]{0:T(128)S(6)} %copy.8.steps_ref, bf16[1,32,6144]{2,1,0:T(8,128)(2,1)} %x_hbm.1, f32[16,2,6144]{2,1,0:T(2,128)} %table_hbm.1), custom_call_target="tpu_custom_call" | custom-call | tf_op jit(solution)/shard_map/modulate/pallas_call | solution.py:56
  2.3 3.1 %collective-permute-start = (bf16[32,3072]{1,0:T(8,128)(2,1)S(1)}, bf16[32,3072]{1,0:T(8,128)(2,1)S(1)}, u32[]{:S(2)}, u32[]{:S(2)}) collective-permute-start(bf16[32,3072]{1,0:T(8,128)(2,1)S(1)} %get-tuple-element.40.refs_3_), channel_id=1, source_target_pairs={{0,1},{1,2},{2,3},{3,0},{4,5},{5,6},{6,7},{7,4},{8,9},{9,10},{10,1... | collective-permute-start | bytes 589832 | tf_op jit(solution)/shard_map/ppermute | solution.py:301
  5.3 1.6 %collective-permute-start.1 = (bf16[32,3072]{1,0:T(8,128)(2,1)S(1)}, bf16[32,3072]{1,0:T(8,128)(2,1)S(1)}, u32[]{:S(2)}, u32[]{:S(2)}) collective-permute-start(bf16[32,3072]{1,0:T(8,128)(2,1)S(1)} %get-tuple-element.41.refs_4_), channel_id=1, source_target_pairs={{0,1},{1,2},{2,3},{3,0},{4,5},{5,6},{6,7},{7,4},{8,9},{9,10},{10,1... | collective-permute-start | bytes 589832 | tf_op jit(solution)/shard_map/ppermute | solution.py:301
  6.9 0.7 %copy-done = s32[128]{0:T(128)S(1)} copy-done((s32[128]{0:T(128)S(1)}, s32[128]{0:T(128)}, u32[]{:S(2)}) %copy-start) | copy-done | bytes 536
  7.6 4.9 %begin.1 = (bf16[32,256]{1,0:T(8,128)(2,1)S(1)}, bf16[32,512]{1,0:T(8,128)(2,1)S(1)}, bf16[6144,256]{1,0:T(8,128)(2,1)S(1)}, bf16[6144,256]{1,0:T(8,128)(2,1)S(1...) custom-call(s32[1]{0:T(128)} %bitcast.place, s32[1,128]{1,0:T(1,128)S(1)} %bitcast.3, ...), custom_call_target="tpu_custom_call" | custom-call | tf_op jit(solution)/shard_map/begin/pallas_call | solution.py:119
  12.4 0.7 %collective-permute-done.refs_0_ = bf16[32,3072]{1,0:T(8,128)(2,1)S(1)} collective-permute-done((bf16[32,3072]{1,0:T(8,128)(2,1)S(1)}, bf16[32,3072]{1,0:T(8,128)(2,1)S(1)}, u32[]{:S(2)}, u32[]{:S(2)}) %collective-permute-start) | collective-permute-done | bytes 196640 | tf_op jit(solution)/shard_map/ppermute | solution.py:301
  13.1 1.0 %collective-permute-start.2 = (bf16[32,3072]{1,0:T(8,128)(2,1)S(1)}, bf16[32,3072]{1,0:T(8,128)(2,1)S(1)}, u32[]{:S(2)}, u32[]{:S(2)}) collective-permute-start(bf16[32,3072]{1,0:T(8,128)(2,1)S(1)} %collective-permute-done.refs_0_), channel_id=1, source_target_pairs={{0,1},{1,2},{2,3},{3,0},{4,5},{5,6},{6,7},{7,4},{8,9},{9,10},{10,1... | collective-permute-start | bytes 589832 | tf_op jit(solution)/shard_map/ppermute | solution.py:306
  14.1 2.7 %collective-permute-done.1.refs_1_ = bf16[32,3072]{1,0:T(8,128)(2,1)S(1)} collective-permute-done((bf16[32,3072]{1,0:T(8,128)(2,1)S(1)}, bf16[32,3072]{1,0:T(8,128)(2,1)S(1)}, u32[]{:S(2)}, u32[]{:S(2)}) %collective-permute-start.1) | collective-permute-done | bytes 196640 | tf_op jit(solution)/shard_map/ppermute | solution.py:301
  16.7 0.0 collective-permute-start.3
  16.7 1.7 %project.4 = (bf16[32,256]{1,0:T(8,128)(2,1)S(1)}, bf16[64,512]{1,0:T(8,128)(2,1)S(1)}) custom-call(bf16[32,3072]{1,0:T(8,128)(2,1)S(1)} %collective-permute-done.refs_0_, bf16[32,3072]{1,0:T(8,128)(2,1)S(1)} %collective-permute-done.1.refs_1_, bf16[6144,256]{1,0:T(8,128)(2,1)S(1)} %get-tuple-element.47.refs_2_.refs_1_, ...), custom_call_target="tpu_custom_call" | custom-call | tf_op jit(solution)/shard_map/project/pallas_call | solution.py:177
  18.4 1.5 %collective-permute-start.4 = (bf16[64,512]{1,0:T(8,128)(2,1)S(1)}, bf16[64,512]{1,0:T(8,128)(2,1)S(1)}, u32[]{:S(2)}, u32[]{:S(2)}) collective-permute-start(bf16[64,512]{1,0:T(8,128)(2,1)S(1)} %get-tuple-element.62.refs_4_), channel_id=1, source_target_pairs={{0,8},{4,12},{8,0},{12,4},{16,24},{20,28},{24,16},{28,20},{1,9},{5... | collective-permute-start | bytes 196616 | tf_op jit(solution)/shard_map/ppermute | solution.py:277
  20.0 1.5 %collective-permute-start.5 = (bf16[64,512]{1,0:T(8,128)(2,1)S(1)}, bf16[64,512]{1,0:T(8,128)(2,1)S(1)}, u32[]{:S(2)}, u32[]{:S(2)}) collective-permute-start(bf16[64,512]{1,0:T(8,128)(2,1)S(1)} %get-tuple-element.62.refs_4_), channel_id=1, source_target_pairs={{0,16},{4,20},{8,24},{12,28},{16,0},{20,4},{24,8},{28,12},{1,17},{... | collective-permute-start | bytes 196616 | tf_op jit(solution)/shard_map/ppermute | solution.py:277
  21.5 0.5 collective-permute-start.6
  22.0 2.2 %collective-permute-start.8 = (bf16[32,3072]{1,0:T(8,128)(2,1)S(1)}, bf16[32,3072]{1,0:T(8,128)(2,1)S(1)}, u32[]{:S(2)}, u32[]{:S(2)}) collective-permute-start(bf16[32,3072]{1,0:T(8,128)(2,1)S(1)} %collective-permute-done.2.refs_0_), channel_id=1, source_target_pairs={{0,1},{1,2},{2,3},{3,0},{4,5},{5,6},{6,7},{7,4},{8,9},{9,10},{10,1... | collective-permute-start | bytes 589832 | tf_op jit(solution)/shard_map/ppermute | solution.py:312
  24.1 0.0 collective-permute-done.4.refs_6_
  24.1 0.6 %collective-permute-done.5.refs_8_ = bf16[64,512]{1,0:T(8,128)(2,1)S(1)} collective-permute-done((bf16[64,512]{1,0:T(8,128)(2,1)S(1)}, bf16[64,512]{1,0:T(8,128)(2,1)S(1)}, u32[]{:S(2)}, u32[]{:S(2)}) %collective-permute-start.5) | collective-permute-done | bytes 65568 | tf_op jit(solution)/shard_map/ppermute | solution.py:277
  24.8 1.9 %collective-permute-done.6.refs_10_ = bf16[64,512]{1,0:T(8,128)(2,1)S(1)} collective-permute-done((bf16[64,512]{1,0:T(8,128)(2,1)S(1)}, bf16[64,512]{1,0:T(8,128)(2,1)S(1)}, u32[]{:S(2)}, u32[]{:S(2)}) %collective-permute-start.6) | collective-permute-done | bytes 65568 | tf_op jit(solution)/shard_map/ppermute | solution.py:277
  26.6 0.0 collective-permute-done.3.refs_1_
  26.6 2.2 %collective-permute-start.7 = (bf16[32,3072]{1,0:T(8,128)(2,1)S(1)}, bf16[32,3072]{1,0:T(8,128)(2,1)S(1)}, u32[]{:S(2)}, u32[]{:S(2)}) collective-permute-start(bf16[32,3072]{1,0:T(8,128)(2,1)S(1)} %collective-permute-done.3.refs_1_), channel_id=1, source_target_pairs={{0,1},{1,2},{2,3},{3,0},{4,5},{5,6},{6,7},{7,4},{8,9},{9,10},{10,1... | collective-permute-start | bytes 589832 | tf_op jit(solution)/shard_map/ppermute | solution.py:312
  28.8 0.5 collective-permute-start.10
  29.3 0.0 collective-permute-start.11
  29.3 0.7 %collective-permute-done.9.refs_5_ = bf16[64,512]{1,0:T(8,128)(2,1)S(1)} collective-permute-done((bf16[64,512]{1,0:T(8,128)(2,1)S(1)}, bf16[64,512]{1,0:T(8,128)(2,1)S(1)}, u32[]{:S(2)}, u32[]{:S(2)}) %collective-permute-start.9) | collective-permute-done | bytes 65568 | tf_op jit(solution)/shard_map/ppermute | solution.py:284
  30.1 0.2 collective-permute-start.12
  30.2 1.7 %project.5 = (bf16[32,256]{1,0:T(8,128)(2,1)S(1)}, bf16[32,512]{1,0:T(8,128)(2,1)S(1)}) custom-call(bf16[32,3072]{1,0:T(8,128)(2,1)S(1)} %collective-permute-done.2.refs_0_, bf16[32,3072]{1,0:T(8,128)(2,1)S(1)} %collective-permute-done.3.refs_1_, bf16[6144,256]{1,0:T(8,128)(2,1)S(1)} %get-tuple-element.47.refs_2_.refs_1_, ...), custom_call_target="tpu_custom_call" | custom-call | tf_op jit(solution)/shard_map/project/pallas_call | solution.py:177
  32.0 0.0 collective-permute-done.10.refs_7_
  32.0 0.0 collective-permute-done.11.refs_9_
  32.0 0.0 collective-permute-done.8.refs_0_
  32.0 0.9 %project.6.refs_4_ = f32[32,768]{1,0:T(8,128)S(1)} custom-call(bf16[32,3072]{1,0:T(8,128)(2,1)S(1)} %collective-permute-done.8.refs_0_, bf16[6144,256]{1,0:T(8,128)(2,1)S(1)} %get-tuple-element.47.refs_2_.refs_1_, bf16[6144,256]{1,0:T(8,128)(2,1)S(1)} %get-tuple-element.48.refs_3_.refs_2_, bf16[6144,256]{1,0:T(8,128)(2,1)S(1)} %get-tuple-element.49.refs_4_.refs_3_), custom_call_target="tpu_custom_call" | custom-call | tf_op jit(solution)/shard_map/project/pallas_call | solution.py:177
  32.9 1.2 %collective-permute-done.7.refs_0_ = bf16[32,3072]{1,0:T(8,128)(2,1)S(1)} collective-permute-done((bf16[32,3072]{1,0:T(8,128)(2,1)S(1)}, bf16[32,3072]{1,0:T(8,128)(2,1)S(1)}, u32[]{:S(2)}, u32[]{:S(2)}) %collective-permute-start.7) | collective-permute-done | bytes 196640 | tf_op jit(solution)/shard_map/ppermute | solution.py:312
  34.1 0.9 %project.7 = (bf16[32,256]{1,0:T(8,128)(2,1)S(1)}, bf16[64,512]{1,0:T(8,128)(2,1)S(1)}) custom-call(bf16[32,3072]{1,0:T(8,128)(2,1)S(1)} %collective-permute-done.7.refs_0_, bf16[6144,256]{1,0:T(8,128)(2,1)S(1)} %get-tuple-element.47.refs_2_.refs_1_, bf16[6144,256]{1,0:T(8,128)(2,1)S(1)} %get-tuple-element.48.refs_3_.refs_2_, ...), custom_call_target="tpu_custom_call" | custom-call | tf_op jit(solution)/shard_map/project/pallas_call | solution.py:177
  35.0 1.1 %collective-permute-start.14 = (bf16[64,512]{1,0:T(8,128)(2,1)S(1)}, bf16[64,512]{1,0:T(8,128)(2,1)S(1)}, u32[]{:S(2)}, u32[]{:S(2)}) collective-permute-start(bf16[64,512]{1,0:T(8,128)(2,1)S(1)} %get-tuple-element.70.refs_12_), channel_id=1, source_target_pairs={{0,8},{4,12},{8,0},{12,4},{16,24},{20,28},{24,16},{28,20},{1,9},{5... | collective-permute-start | bytes 196616 | tf_op jit(solution)/shard_map/ppermute | solution.py:277
  36.1 1.5 %collective-permute-start.16 = (bf16[64,512]{1,0:T(8,128)(2,1)S(1)}, bf16[64,512]{1,0:T(8,128)(2,1)S(1)}, u32[]{:S(2)}, u32[]{:S(2)}) collective-permute-start(bf16[64,512]{1,0:T(8,128)(2,1)S(1)} %get-tuple-element.70.refs_12_), channel_id=1, source_target_pairs={{0,16},{4,20},{8,24},{12,28},{16,0},{20,4},{24,8},{28,12},{1,17},{... | collective-permute-start | bytes 196616 | tf_op jit(solution)/shard_map/ppermute | solution.py:277
  37.6 1.0 %collective-permute-start.18 = (bf16[64,512]{1,0:T(8,128)(2,1)S(1)}, bf16[64,512]{1,0:T(8,128)(2,1)S(1)}, u32[]{:S(2)}, u32[]{:S(2)}) collective-permute-start(bf16[64,512]{1,0:T(8,128)(2,1)S(1)} %get-tuple-element.70.refs_12_), channel_id=1, source_target_pairs={{0,24},{4,28},{8,16},{12,20},{16,8},{20,12},{24,0},{28,4},{1,25},{... | collective-permute-start | bytes 196616 | tf_op jit(solution)/shard_map/ppermute | solution.py:277
  38.6 1.1 %collective-permute-done.14.refs_14_ = bf16[64,512]{1,0:T(8,128)(2,1)S(1)} collective-permute-done((bf16[64,512]{1,0:T(8,128)(2,1)S(1)}, bf16[64,512]{1,0:T(8,128)(2,1)S(1)}, u32[]{:S(2)}, u32[]{:S(2)}) %collective-permute-start.14) | collective-permute-done | bytes 65568 | tf_op jit(solution)/shard_map/ppermute | solution.py:277
  39.7 0.0 collective-permute-start.15
  39.7 1.0 %collective-permute-done.16.refs_16_ = bf16[64,512]{1,0:T(8,128)(2,1)S(1)} collective-permute-done((bf16[64,512]{1,0:T(8,128)(2,1)S(1)}, bf16[64,512]{1,0:T(8,128)(2,1)S(1)}, u32[]{:S(2)}, u32[]{:S(2)}) %collective-permute-start.16) | collective-permute-done | bytes 65568 | tf_op jit(solution)/shard_map/ppermute | solution.py:277
  40.7 0.0 collective-permute-start.17
  40.7 2.1 %collective-permute-done.18.refs_18_ = bf16[64,512]{1,0:T(8,128)(2,1)S(1)} collective-permute-done((bf16[64,512]{1,0:T(8,128)(2,1)S(1)}, bf16[64,512]{1,0:T(8,128)(2,1)S(1)}, u32[]{:S(2)}, u32[]{:S(2)}) %collective-permute-start.18) | collective-permute-done | bytes 65568 | tf_op jit(solution)/shard_map/ppermute | solution.py:277
  42.8 0.0 collective-permute-start.19
  42.8 0.0 collective-permute-done.13.refs_13_
  42.8 1.2 %collective-permute-done.19.refs_19_ = bf16[64,512]{1,0:T(8,128)(2,1)S(1)} collective-permute-done((bf16[64,512]{1,0:T(8,128)(2,1)S(1)}, bf16[64,512]{1,0:T(8,128)(2,1)S(1)}, u32[]{:S(2)}, u32[]{:S(2)}) %collective-permute-start.19) | collective-permute-done | bytes 65568 | tf_op jit(solution)/shard_map/ppermute | solution.py:284
  44.0 0.9 %attend.1 = (bf16[32,256]{1,0:T(8,128)(2,1)S(1)}, bf16[32,256]{1,0:T(8,128)(2,1)S(1)}, bf16[32,256]{1,0:T(8,128)(2,1)S(1)}, bf16[32,256]{1,0:T(8,128)(2,1)S(1)}) custom-call(s32[1]{0:T(128)} %bitcast.1.mine, s32[128,1]{1,0:T(8,128)S(1)} %get-tuple-element.42.seg_col, s32[1,128]{1,0:T(1,128)S(1)} %get-tuple-element.43.seg_row, ...), custom_call_target="tpu_custom_call" | custom-call | tf_op jit(solution)/shard_map/attend/pallas_call | solution.py:240
  45.0 1.5 %collective-permute-start.20 = (bf16[32,256]{1,0:T(8,128)(2,1)S(1)}, bf16[32,256]{1,0:T(8,128)(2,1)S(1)}, u32[]{:S(2)}, u32[]{:S(2)}) collective-permute-start(bf16[32,256]{1,0:T(8,128)(2,1)S(1)} %get-tuple-element.72), channel_id=1, source_target_pairs={{0,3},{1,0},{2,1},{3,2},{4,7},{5,4},{6,5},{7,6},{8,11},{9,8},{10,9... | collective-permute-start | bytes 49160 | tf_op jit(solution)/shard_map/ppermute | solution.py:324
  46.5 1.0 %collective-permute-start.22 = (bf16[32,256]{1,0:T(8,128)(2,1)S(1)}, bf16[32,256]{1,0:T(8,128)(2,1)S(1)}, u32[]{:S(2)}, u32[]{:S(2)}) collective-permute-start(bf16[32,256]{1,0:T(8,128)(2,1)S(1)} %get-tuple-element.74), channel_id=1, source_target_pairs={{0,1},{1,2},{2,3},{3,0},{4,5},{5,6},{6,7},{7,4},{8,9},{9,10},{10,1... | collective-permute-start | bytes 49160 | tf_op jit(solution)/shard_map/ppermute | solution.py:324
  47.5 1.3 %collective-permute-done.20.refs_1_ = bf16[32,256]{1,0:T(8,128)(2,1)S(1)} collective-permute-done((bf16[32,256]{1,0:T(8,128)(2,1)S(1)}, bf16[32,256]{1,0:T(8,128)(2,1)S(1)}, u32[]{:S(2)}, u32[]{:S(2)}) %collective-permute-start.20) | collective-permute-done | bytes 16416 | tf_op jit(solution)/shard_map/ppermute | solution.py:324
  48.8 2.5 %collective-permute-done.21.refs_2_ = bf16[32,256]{1,0:T(8,128)(2,1)S(1)} collective-permute-done((bf16[32,256]{1,0:T(8,128)(2,1)S(1)}, bf16[32,256]{1,0:T(8,128)(2,1)S(1)}, u32[]{:S(2)}, u32[]{:S(2)}) %collective-permute-start.21) | collective-permute-done | bytes 16416 | tf_op jit(solution)/shard_map/ppermute | solution.py:324
  51.3 0.7 %collective-permute-done.22.refs_3_ = bf16[32,256]{1,0:T(8,128)(2,1)S(1)} collective-permute-done((bf16[32,256]{1,0:T(8,128)(2,1)S(1)}, bf16[32,256]{1,0:T(8,128)(2,1)S(1)}, u32[]{:S(2)}, u32[]{:S(2)}) %collective-permute-start.22) | collective-permute-done | bytes 16416 | tf_op jit(solution)/shard_map/ppermute | solution.py:324
  52.0 0.6 %place.1 = bf16[1,32,1024]{2,1,0:T(8,128)(2,1)} custom-call(s32[1]{0:T(128)} %bitcast.place, bf16[32,256]{1,0:T(8,128)(2,1)S(1)} %get-tuple-element.71.refs_0_, bf16[32,256]{1,0:T(8,128)(2,1)S(1)} %collective-permute-done.20.refs_1_, bf16[32,256]{1,0:T(8,128)(2,1)S(1)} %collective-permute-done.21.refs_2_, bf16[32,256]{1,0:T(8,128)(2,1)S(1)} %collective-permute-done.22.refs_3_), custom_call_target="tpu_custom_call" | custom-call | tf_op jit(solution)/shard_map/place/pallas_call | solution.py:265
  (8 shorter events, 0.0 us)
Async XLA Ops:
  2.3 10.8 %collective-permute-start = (bf16[32,3072]{1,0:T(8,128)(2,1)S(1)}, bf16[32,3072]{1,0:T(8,128)(2,1)S(1)}, u32[]{:S(2)}, u32[]{:S(2)}) collective-permute-start(bf16[32,3072]{1,0:T(8,128)(2,1)S(1)} %get-tuple-element.40.refs_3_), channel_id=1, source_target_pairs={{0,1},{1,2},{2,3},{3,0},{4,5},{5,6},{6,7},{7,4},{8,9},{9,10},{10,1... | collective-permute-start | bytes 589832 | tf_op jit(solution)/shard_map/ppermute | solution.py:301
  5.3 11.4 %collective-permute-start.1 = (bf16[32,3072]{1,0:T(8,128)(2,1)S(1)}, bf16[32,3072]{1,0:T(8,128)(2,1)S(1)}, u32[]{:S(2)}, u32[]{:S(2)}) collective-permute-start(bf16[32,3072]{1,0:T(8,128)(2,1)S(1)} %get-tuple-element.41.refs_4_), channel_id=1, source_target_pairs={{0,1},{1,2},{2,3},{3,0},{4,5},{5,6},{6,7},{7,4},{8,9},{9,10},{10,1... | collective-permute-start | bytes 589832 | tf_op jit(solution)/shard_map/ppermute | solution.py:301
  6.9 0.7 %copy-start = (s32[128]{0:T(128)S(1)}, s32[128]{0:T(128)}, u32[]{:S(2)}) copy-start(s32[128]{0:T(128)} %param.9) | copy-start | bytes 1540
  13.1 8.9 %collective-permute-start.2 = (bf16[32,3072]{1,0:T(8,128)(2,1)S(1)}, bf16[32,3072]{1,0:T(8,128)(2,1)S(1)}, u32[]{:S(2)}, u32[]{:S(2)}) collective-permute-start(bf16[32,3072]{1,0:T(8,128)(2,1)S(1)} %collective-permute-done.refs_0_), channel_id=1, source_target_pairs={{0,1},{1,2},{2,3},{3,0},{4,5},{5,6},{6,7},{7,4},{8,9},{9,10},{10,1... | collective-permute-start | bytes 589832 | tf_op jit(solution)/shard_map/ppermute | solution.py:306
  16.7 9.9 %collective-permute-start.3 = (bf16[32,3072]{1,0:T(8,128)(2,1)S(1)}, bf16[32,3072]{1,0:T(8,128)(2,1)S(1)}, u32[]{:S(2)}, u32[]{:S(2)}) collective-permute-start(bf16[32,3072]{1,0:T(8,128)(2,1)S(1)} %collective-permute-done.1.refs_1_), channel_id=1, source_target_pairs={{0,1},{1,2},{2,3},{3,0},{4,5},{5,6},{6,7},{7,4},{8,9},{9,10},{10,1... | collective-permute-start | bytes 589832 | tf_op jit(solution)/shard_map/ppermute | solution.py:306
  18.4 5.7 %collective-permute-start.4 = (bf16[64,512]{1,0:T(8,128)(2,1)S(1)}, bf16[64,512]{1,0:T(8,128)(2,1)S(1)}, u32[]{:S(2)}, u32[]{:S(2)}) collective-permute-start(bf16[64,512]{1,0:T(8,128)(2,1)S(1)} %get-tuple-element.62.refs_4_), channel_id=1, source_target_pairs={{0,8},{4,12},{8,0},{12,4},{16,24},{20,28},{24,16},{28,20},{1,9},{5... | collective-permute-start | bytes 196616 | tf_op jit(solution)/shard_map/ppermute | solution.py:277
  20.0 4.8 %collective-permute-start.5 = (bf16[64,512]{1,0:T(8,128)(2,1)S(1)}, bf16[64,512]{1,0:T(8,128)(2,1)S(1)}, u32[]{:S(2)}, u32[]{:S(2)}) collective-permute-start(bf16[64,512]{1,0:T(8,128)(2,1)S(1)} %get-tuple-element.62.refs_4_), channel_id=1, source_target_pairs={{0,16},{4,20},{8,24},{12,28},{16,0},{20,4},{24,8},{28,12},{1,17},{... | collective-permute-start | bytes 196616 | tf_op jit(solution)/shard_map/ppermute | solution.py:277
  21.5 5.2 %collective-permute-start.6 = (bf16[64,512]{1,0:T(8,128)(2,1)S(1)}, bf16[64,512]{1,0:T(8,128)(2,1)S(1)}, u32[]{:S(2)}, u32[]{:S(2)}) collective-permute-start(bf16[64,512]{1,0:T(8,128)(2,1)S(1)} %get-tuple-element.62.refs_4_), channel_id=1, source_target_pairs={{0,24},{4,28},{8,16},{12,20},{16,8},{20,12},{24,0},{28,4},{1,25},{... | collective-permute-start | bytes 196616 | tf_op jit(solution)/shard_map/ppermute | solution.py:277
  22.0 10.0 %collective-permute-start.8 = (bf16[32,3072]{1,0:T(8,128)(2,1)S(1)}, bf16[32,3072]{1,0:T(8,128)(2,1)S(1)}, u32[]{:S(2)}, u32[]{:S(2)}) collective-permute-start(bf16[32,3072]{1,0:T(8,128)(2,1)S(1)} %collective-permute-done.2.refs_0_), channel_id=1, source_target_pairs={{0,1},{1,2},{2,3},{3,0},{4,5},{5,6},{6,7},{7,4},{8,9},{9,10},{10,1... | collective-permute-start | bytes 589832 | tf_op jit(solution)/shard_map/ppermute | solution.py:312
  26.6 7.5 %collective-permute-start.7 = (bf16[32,3072]{1,0:T(8,128)(2,1)S(1)}, bf16[32,3072]{1,0:T(8,128)(2,1)S(1)}, u32[]{:S(2)}, u32[]{:S(2)}) collective-permute-start(bf16[32,3072]{1,0:T(8,128)(2,1)S(1)} %collective-permute-done.3.refs_1_), channel_id=1, source_target_pairs={{0,1},{1,2},{2,3},{3,0},{4,5},{5,6},{6,7},{7,4},{8,9},{9,10},{10,1... | collective-permute-start | bytes 589832 | tf_op jit(solution)/shard_map/ppermute | solution.py:312
  28.8 1.3 %collective-permute-start.9 = (bf16[64,512]{1,0:T(8,128)(2,1)S(1)}, bf16[64,512]{1,0:T(8,128)(2,1)S(1)}, u32[]{:S(2)}, u32[]{:S(2)}) collective-permute-start(bf16[64,512]{1,0:T(8,128)(2,1)S(1)} %get-tuple-element.62.refs_4_), channel_id=1, source_target_pairs={{0,4},{4,0},{8,12},{12,8},{16,20},{20,16},{24,28},{28,24},{1,5},{5... | collective-permute-start | bytes 196616 | tf_op jit(solution)/shard_map/ppermute | solution.py:284
  28.8 3.1 %collective-permute-start.10 = (bf16[64,512]{1,0:T(8,128)(2,1)S(1)}, bf16[64,512]{1,0:T(8,128)(2,1)S(1)}, u32[]{:S(2)}, u32[]{:S(2)}) collective-permute-start(bf16[64,512]{1,0:T(8,128)(2,1)S(1)} %collective-permute-done.4.refs_6_), channel_id=1, source_target_pairs={{0,4},{4,0},{8,12},{12,8},{16,20},{20,16},{24,28},{28,24},{1,5},{5... | collective-permute-start | bytes 196616 | tf_op jit(solution)/shard_map/ppermute | solution.py:284
  29.3 2.6 %collective-permute-start.11 = (bf16[64,512]{1,0:T(8,128)(2,1)S(1)}, bf16[64,512]{1,0:T(8,128)(2,1)S(1)}, u32[]{:S(2)}, u32[]{:S(2)}) collective-permute-start(bf16[64,512]{1,0:T(8,128)(2,1)S(1)} %collective-permute-done.5.refs_8_), channel_id=1, source_target_pairs={{0,4},{4,0},{8,12},{12,8},{16,20},{20,16},{24,28},{28,24},{1,5},{5... | collective-permute-start | bytes 196616 | tf_op jit(solution)/shard_map/ppermute | solution.py:284
  30.1 1.9 %collective-permute-start.12 = (bf16[64,512]{1,0:T(8,128)(2,1)S(1)}, bf16[64,512]{1,0:T(8,128)(2,1)S(1)}, u32[]{:S(2)}, u32[]{:S(2)}) collective-permute-start(bf16[64,512]{1,0:T(8,128)(2,1)S(1)} %collective-permute-done.6.refs_10_), channel_id=1, source_target_pairs={{0,4},{4,0},{8,12},{12,8},{16,20},{20,16},{24,28},{28,24},{1,5},{5... | collective-permute-start | bytes 196616 | tf_op jit(solution)/shard_map/ppermute | solution.py:284
  35.0 4.7 %collective-permute-start.14 = (bf16[64,512]{1,0:T(8,128)(2,1)S(1)}, bf16[64,512]{1,0:T(8,128)(2,1)S(1)}, u32[]{:S(2)}, u32[]{:S(2)}) collective-permute-start(bf16[64,512]{1,0:T(8,128)(2,1)S(1)} %get-tuple-element.70.refs_12_), channel_id=1, source_target_pairs={{0,8},{4,12},{8,0},{12,4},{16,24},{20,28},{24,16},{28,20},{1,9},{5... | collective-permute-start | bytes 196616 | tf_op jit(solution)/shard_map/ppermute | solution.py:277
  36.1 4.5 %collective-permute-start.16 = (bf16[64,512]{1,0:T(8,128)(2,1)S(1)}, bf16[64,512]{1,0:T(8,128)(2,1)S(1)}, u32[]{:S(2)}, u32[]{:S(2)}) collective-permute-start(bf16[64,512]{1,0:T(8,128)(2,1)S(1)} %get-tuple-element.70.refs_12_), channel_id=1, source_target_pairs={{0,16},{4,20},{8,24},{12,28},{16,0},{20,4},{24,8},{28,12},{1,17},{... | collective-permute-start | bytes 196616 | tf_op jit(solution)/shard_map/ppermute | solution.py:277
  37.6 5.2 %collective-permute-start.18 = (bf16[64,512]{1,0:T(8,128)(2,1)S(1)}, bf16[64,512]{1,0:T(8,128)(2,1)S(1)}, u32[]{:S(2)}, u32[]{:S(2)}) collective-permute-start(bf16[64,512]{1,0:T(8,128)(2,1)S(1)} %get-tuple-element.70.refs_12_), channel_id=1, source_target_pairs={{0,24},{4,28},{8,16},{12,20},{16,8},{20,12},{24,0},{28,4},{1,25},{... | collective-permute-start | bytes 196616 | tf_op jit(solution)/shard_map/ppermute | solution.py:277
  38.6 4.2 %collective-permute-start.13 = (bf16[64,512]{1,0:T(8,128)(2,1)S(1)}, bf16[64,512]{1,0:T(8,128)(2,1)S(1)}, u32[]{:S(2)}, u32[]{:S(2)}) collective-permute-start(bf16[64,512]{1,0:T(8,128)(2,1)S(1)} %get-tuple-element.70.refs_12_), channel_id=1, source_target_pairs={{0,4},{4,0},{8,12},{12,8},{16,20},{20,16},{24,28},{28,24},{1,5},{5... | collective-permute-start | bytes 196616 | tf_op jit(solution)/shard_map/ppermute | solution.py:284
  39.7 3.1 %collective-permute-start.15 = (bf16[64,512]{1,0:T(8,128)(2,1)S(1)}, bf16[64,512]{1,0:T(8,128)(2,1)S(1)}, u32[]{:S(2)}, u32[]{:S(2)}) collective-permute-start(bf16[64,512]{1,0:T(8,128)(2,1)S(1)} %collective-permute-done.14.refs_14_), channel_id=1, source_target_pairs={{0,4},{4,0},{8,12},{12,8},{16,20},{20,16},{24,28},{28,24},{1,5},{5... | collective-permute-start | bytes 196616 | tf_op jit(solution)/shard_map/ppermute | solution.py:284
  40.7 2.2 %collective-permute-start.17 = (bf16[64,512]{1,0:T(8,128)(2,1)S(1)}, bf16[64,512]{1,0:T(8,128)(2,1)S(1)}, u32[]{:S(2)}, u32[]{:S(2)}) collective-permute-start(bf16[64,512]{1,0:T(8,128)(2,1)S(1)} %collective-permute-done.16.refs_16_), channel_id=1, source_target_pairs={{0,4},{4,0},{8,12},{12,8},{16,20},{20,16},{24,28},{28,24},{1,5},{5... | collective-permute-start | bytes 196616 | tf_op jit(solution)/shard_map/ppermute | solution.py:284
  42.8 1.3 %collective-permute-start.19 = (bf16[64,512]{1,0:T(8,128)(2,1)S(1)}, bf16[64,512]{1,0:T(8,128)(2,1)S(1)}, u32[]{:S(2)}, u32[]{:S(2)}) collective-permute-start(bf16[64,512]{1,0:T(8,128)(2,1)S(1)} %collective-permute-done.18.refs_18_), channel_id=1, source_target_pairs={{0,4},{4,0},{8,12},{12,8},{16,20},{20,16},{24,28},{28,24},{1,5},{5... | collective-permute-start | bytes 196616 | tf_op jit(solution)/shard_map/ppermute | solution.py:284
  45.0 3.8 %collective-permute-start.20 = (bf16[32,256]{1,0:T(8,128)(2,1)S(1)}, bf16[32,256]{1,0:T(8,128)(2,1)S(1)}, u32[]{:S(2)}, u32[]{:S(2)}) collective-permute-start(bf16[32,256]{1,0:T(8,128)(2,1)S(1)} %get-tuple-element.72), channel_id=1, source_target_pairs={{0,3},{1,0},{2,1},{3,2},{4,7},{5,4},{6,5},{7,6},{8,11},{9,8},{10,9... | collective-permute-start | bytes 49160 | tf_op jit(solution)/shard_map/ppermute | solution.py:324
  46.5 4.8 %collective-permute-start.21 = (bf16[32,256]{1,0:T(8,128)(2,1)S(1)}, bf16[32,256]{1,0:T(8,128)(2,1)S(1)}, u32[]{:S(2)}, u32[]{:S(2)}) collective-permute-start(bf16[32,256]{1,0:T(8,128)(2,1)S(1)} %get-tuple-element.73), channel_id=1, source_target_pairs={{0,2},{1,3},{2,0},{3,1},{4,6},{5,7},{6,4},{7,5},{8,10},{9,11},{10,... | collective-permute-start | bytes 49160 | tf_op jit(solution)/shard_map/ppermute | solution.py:324
  46.5 5.5 %collective-permute-start.22 = (bf16[32,256]{1,0:T(8,128)(2,1)S(1)}, bf16[32,256]{1,0:T(8,128)(2,1)S(1)}, u32[]{:S(2)}, u32[]{:S(2)}) collective-permute-start(bf16[32,256]{1,0:T(8,128)(2,1)S(1)} %get-tuple-element.74), channel_id=1, source_target_pairs={{0,1},{1,2},{2,3},{3,0},{4,5},{5,6},{6,7},{7,4},{8,9},{9,10},{10,1... | collective-permute-start | bytes 49160 | tf_op jit(solution)/shard_map/ppermute | solution.py:324

commit v4 on v3

--- a/solution.py
+++ b/solution.py
@@ -9,7 +9,10 @@
 from jax.sharding import PartitionSpec as P
 
 HD = 128
+LANES = 128
 CHUNKS = 2
+PARTS = 2
+AHEAD = 6
 VMEM = pltpu.MemorySpace.VMEM
 HBM = pltpu.MemorySpace.HBM
 SMEM = pltpu.MemorySpace.SMEM
@@ -30,63 +33,75 @@
     return [pltpu.with_memory_space_constraint(a, HBM) for a in arrays]
 
 
-def modulate_kernel(chunks, steps_ref, x_hbm, table_hbm, *refs):
-    outs, (x_ref, table, steps, sems) = refs[:chunks], refs[chunks:]
-    copies = [
-        pltpu.make_async_copy(x_hbm.at[0], x_ref, sems.at[0]),
-        pltpu.make_async_copy(table_hbm, table, sems.at[1]),
-        pltpu.make_async_copy(steps_ref, steps, sems.at[2]),
-    ]
-    for copy in copies:
-        copy.start()
-    for copy in copies:
-        copy.wait()
+def split_kernel(x_hbm, *refs):
+    outs, (x_ref, sem) = refs[:CHUNKS], refs[CHUNKS:]
+    copy = pltpu.make_async_copy(x_hbm.at[0], x_ref, sem)
+    copy.start()
+    copy.wait()
+    width = outs[-1].shape[1]
+    for index, out in enumerate(outs):
+        out[:, :width] = x_ref[:, index * width : (index + 1) * width]
     x = x_ref[...].astype(jnp.float32)
     scale = lax.rsqrt(jnp.mean(x * x, axis=-1, keepdims=True) + 1e-06)
-    mod = table[steps[0]]
-    rows = (x * scale * (1.0 + mod[0:1]) + mod[1:2]).astype(jnp.bfloat16)
-    width = outs[0].shape[1]
-    for index, out in enumerate(outs):
-        out[...] = rows[:, index * width : (index + 1) * width]
-
-
-def modulate(latents, steps, mod_table):
+    high = scale.astype(jnp.bfloat16).astype(jnp.float32)
+    middle = (scale - high).astype(jnp.bfloat16).astype(jnp.float32)
+    lane = lax.broadcasted_iota(jnp.int32, (x.shape[0], LANES), 1)
+    parts = jnp.where(lane == 0, high, jnp.where(lane == 1, middle, scale - high - middle))
+    outs[0][:, width:] = parts.astype(jnp.bfloat16)
+
+
+def split(latents):
     _, rows, depth = latents.shape
     width = depth // CHUNKS
     return pl.pallas_call(
-        functools.partial(modulate_kernel, CHUNKS),
-        in_specs=[IN_HBM, IN_HBM, IN_HBM],
+        split_kernel,
+        in_specs=[IN_HBM],
         out_specs=[IN_VMEM] * CHUNKS,
-        out_shape=[VMEM((rows, width), jnp.bfloat16)] * CHUNKS,
-        scratch_shapes=[
-            pltpu.VMEM((rows, depth), jnp.bfloat16),
-            pltpu.VMEM(mod_table.shape, jnp.float32),
-            pltpu.SMEM((1,), jnp.int32),
-            pltpu.SemaphoreType.DMA((3,)),
-        ],
+        out_shape=[VMEM((rows, width + (0 if k else LANES)), jnp.bfloat16) for k in range(CHUNKS)],
+        scratch_shapes=[pltpu.VMEM((rows, depth), jnp.bfloat16), pltpu.SemaphoreType.DMA],
         compiler_params=params(4),
-        name="modulate",
-    )(steps, *far(latents, mod_table))
-
-
-def begin_kernel(shards, place, segments, *refs):
+        name="split",
+    )(*far(latents))
+
+
+def scale_of(piece):
+    parts = piece[:, piece.shape[1] - LANES :].astype(jnp.float32)
+    return parts[:, 0:1] + (parts[:, 1:2] + parts[:, 2:3])
+
+
+def modulated(piece, scale, gain, k, width):
+    span = slice(k * width, (k + 1) * width)
+    x = piece[:, :width].astype(jnp.float32)
+    return (x * scale * gain[0:1, span] + gain[1:2, span]).astype(jnp.bfloat16)
+
+
+def begin_kernel(shards, place, steps, seg_hbm, table, *refs):
     sources, refs = refs[:3], refs[3:]
     pieces, refs = refs[:CHUNKS], refs[CHUNKS:]
     query, keyval = refs[:2]
-    outs, (seg_col, seg_row, sems) = refs[2:5], refs[5:]
-    depth = pieces[0].shape[1]
+    outs, (gain, seg_col, seg_row, segments, sems, small) = refs[2:5], refs[5:]
+    depth = pieces[-1].shape[1]
     width = query.shape[1]
-    spans = [slice(k * depth, (k + 1) * depth) for k in range(CHUNKS)]
+    reads = [
+        pltpu.make_async_copy(table.at[steps[0]], gain, small.at[0]),
+        pltpu.make_async_copy(seg_hbm, segments, small.at[1]),
+    ]
+    for copy in reads:
+        copy.start()
+    short = depth // PARTS
+    spans = [slice(k * short, (k + 1) * short) for k in range(CHUNKS * PARTS)]
     copies = [
-        [
-            pltpu.make_async_copy(sources[i].at[span], outs[i].at[span], sems.at[i, k])
-            for k, span in enumerate(spans)
-        ]
+        pltpu.make_async_copy(sources[i].at[span], outs[i].at[span], sems.at[i, k])
         for i in range(3)
+        for k, span in enumerate(spans)
     ]
-    for column in copies:
-        for copy in column:
-            copy.start()
+    for copy in copies[:AHEAD]:
+        copy.start()
+    for copy in reads:
+        copy.wait()
+    gain[0:1, :] = 1.0 + gain[0:1, :]
+    scale = scale_of(pieces[0])
+    own = [modulated(piece, scale, gain, k, depth) for k, piece in enumerate(pieces)]
     tokc = segments.shape[1]
     rows = tokc // shards
 
@@ -103,8 +118,16 @@
     for i in range(3):
         total = None
         for k, span in enumerate(spans):
-            copies[i][k].wait()
-            part = jnp.dot(pieces[k][...], outs[i][span], preferred_element_type=jnp.float32)
+            index = i * len(spans) + k
+            copies[index].wait()
+            if index + AHEAD < len(copies):
+                copies[index + AHEAD].start()
+            part = k % PARTS
+            part = jnp.dot(
+                own[k // PARTS][:, part * short : (part + 1) * short],
+                outs[i][span],
+                preferred_element_type=jnp.float32,
+            )
             total = part if total is None else total + part
         if i == 0:
             query[...] = total.astype(jnp.bfloat16)
@@ -112,36 +135,49 @@
             keyval[:, (i - 1) * width : i * width] = total.astype(jnp.bfloat16)
 
 
-def begin(weights, segments, pieces, place, shards):
+def begin(weights, segments, steps, mod_table, pieces, place, shards):
     tokc = segments.shape[0]
     rows = pieces[0].shape[0]
     width = weights[0].shape[1]
     return pl.pallas_call(
         functools.partial(begin_kernel, shards),
-        in_specs=[IN_SMEM, pl.BlockSpec((1, tokc))] + [IN_HBM] * 3 + [IN_VMEM] * CHUNKS,
-        out_specs=[IN_VMEM] * 7,
+        in_specs=[IN_SMEM] * 2 + [IN_HBM] * 5 + [IN_VMEM] * CHUNKS,
+        out_specs=[IN_VMEM] * 8,
         out_shape=[VMEM((rows, width), jnp.bfloat16), VMEM((rows, 2 * width), jnp.bfloat16)]
         + [VMEM(w.shape, w.dtype) for w in weights]
+        + [VMEM(mod_table.shape[1:], jnp.float32)]
         + [VMEM((tokc, 1), jnp.int32), VMEM((1, tokc), jnp.int32)],
-        scratch_shapes=[pltpu.SemaphoreType.DMA((3, CHUNKS))],
-        compiler_params=params(2 + tokc * tokc * 32 // 2**20),
+        scratch_shapes=[
+            pltpu.VMEM((1, tokc), jnp.int32),
+            pltpu.SemaphoreType.DMA((3, CHUNKS * PARTS)),
+            pltpu.SemaphoreType.DMA((2,)),
+        ],
+        compiler_params=params(4 + tokc * tokc * 32 // 2**20),
         name="begin",
-    )(place, segments[None], *far(*weights), *near(*pieces))
+    )(place, steps, *far(segments[None], mod_table, *weights), *near(*pieces))
 
 
 def project_kernel(count, places, first, last, older, *refs):
-    pieces, refs = refs[: count * len(places)], refs[count * len(places) :]
-    weights, refs = refs[:3], refs[3:]
+    known = len({0, *places})
+    pieces, refs = refs[: count * known], refs[count * known :]
+    gain, weights, refs = refs[0], refs[1:4], refs[4:]
     if not first:
         start, refs = refs[0], refs[1:]
     if older:
         before, refs = refs[0], refs[1:]
         refs[1][:older, :] = before[...]
     width = weights[0].shape[1]
-    depth = pieces[0].shape[1]
+    depth = weights[0].shape[0] // CHUNKS
+    scales = [scale_of(pieces[s * known]) for s in range(count)]
     stacked = [
-        jnp.concatenate([pieces[s * len(places) + k][...] for s in range(count)], axis=0)
-        for k in range(len(places))
+        jnp.concatenate(
+            [
+                modulated(pieces[s * known + known - len(places) + i], scales[s], gain, k, depth)
+                for s in range(count)
+            ],
+            axis=0,
+        )
+        for i, k in enumerate(places)
     ]
     for index, weight in enumerate(weights):
         total = None if first else start[:, index * width : (index + 1) * width]
@@ -160,7 +196,7 @@
             refs[1][older:, (index - 1) * width : index * width] = total.astype(jnp.bfloat16)
 
 
-def project(shard_pieces, places, weights, start, last, before=None):
+def project(shard_pieces, places, gain, weights, start, last, before=None):
     count = len(shard_pieces)
     rows = shard_pieces[0][0].shape[0] * count
     older = 0 if before is None else before.shape[0]
@@ -172,16 +208,16 @@
         ]
     else:
         shapes = [VMEM((rows, 3 * width), jnp.float32)]
-    pieces = [piece for shard in shard_pieces for piece in shard]
+    pieces = [shard[k] for shard in shard_pieces for k in sorted({0, *places})]
     extra = [array for array in (start, before) if array is not None]
     return pl.pallas_call(
         functools.partial(project_kernel, count, tuple(places), start is None, last, older),
-        in_specs=[IN_VMEM] * (len(pieces) + 3 + len(extra)),
+        in_specs=[IN_VMEM] * (len(pieces) + 4 + len(extra)),
         out_specs=[IN_VMEM] * len(shapes),
         out_shape=shapes,
-        compiler_params=params(3 + count),
+        compiler_params=params(4 + count * 2),
         name="project",
-    )(*near(*pieces, *weights, *extra))
+    )(*near(*pieces, gain, *weights, *extra))
 
 
 def attend_kernel(shards, parts, sources, mine, seg_col, seg_row, *refs):
@@ -251,25 +287,26 @@
     )(mine, *near(seg_col, seg_row, *queries, *early, *late))
 
 
-def place_kernel(place, *refs):
+def place_kernel(order, place, *refs):
     pieces, out = refs[:-1], refs[-1]
     width = pieces[0].shape[1]
     count = len(pieces)
-    for s, piece in enumerate(pieces):
+    for s, piece in zip(order, pieces):
         column = lax.rem(place[0] + s, count) * width
         out[0, :, pl.ds(pl.multiple_of(column, width), width)] = piece[...]
 
 
 def place_columns(place, pieces):
     rows, width = pieces[0].shape
-    return pl.pallas_call(
-        place_kernel,
+    order = [0, *range(2, len(pieces)), 1]
+    return pl.pallas_call(
+        functools.partial(place_kernel, order),
         in_specs=[IN_SMEM] + [IN_VMEM] * len(pieces),
         out_specs=IN_VMEM,
         out_shape=jax.ShapeDtypeStruct((1, rows, width * len(pieces)), jnp.bfloat16),
         compiler_params=params(2),
         name="place",
-    )(place, *near(*pieces))
+    )(place, *near(*[pieces[s] for s in order]))
 
 
 def across_chips(block, groups):
@@ -292,11 +329,11 @@
     mine = lax.axis_index("group").astype(jnp.int32)
     ring = [(i, (i + 1) % shards) for i in range(shards)]
 
-    pieces = list(modulate(latents, steps, mod_table))
+    pieces = list(split(latents))
     query, keyval, *rest = begin(
-        (w_query, w_key, w_value), segment_ids, pieces, place[None], shards
+        (w_query, w_key, w_value), segment_ids, steps, mod_table, pieces, place[None], shards
     )
-    weights, (seg_col, seg_row) = rest[:3], rest[3:]
+    weights, (gain, seg_col, seg_row) = rest[:3], rest[3:]
     queries = [query]
     pieces = [lax.ppermute(piece, "dp", ring) for piece in pieces]
     pieces[0], keyval = lax.optimization_barrier((pieces[0], keyval))
@@ -304,17 +341,17 @@
     for s in range(1, shards - 2):
         arrived.append(pieces)
         pieces = [lax.ppermute(piece, "dp", ring) for piece in pieces]
-    query, keyval = project(arrived, range(CHUNKS), weights, None, True, keyval)
+    query, keyval = project(arrived, range(CHUNKS), gain, weights, None, True, keyval)
     queries.append(query)
+    pieces[0], keyval = lax.optimization_barrier((pieces[0], keyval))
     early = across_chips(keyval, groups)
-    pieces[-1], early = lax.optimization_barrier((pieces[-1], early))
+    _, early = lax.optimization_barrier((pieces[-1], early))
     early = across_cores(early, groups)
     moved = [lax.ppermute(piece, "dp", ring) for piece in pieces]
     moved[0], early = lax.optimization_barrier((moved[0], early))
-    query, keyval = project([pieces], range(CHUNKS), weights, None, True)
-    queries.append(query)
-    start = project([moved[:-1]], range(CHUNKS - 1), weights, None, False)[0]
-    query, keyval = project([moved[-1:]], [CHUNKS - 1], weights, start, True, keyval)
+    both = [pieces, moved]
+    start = project(both, range(CHUNKS - 1), gain, weights, None, False)[0]
+    query, keyval = project(both, [CHUNKS - 1], gain, weights, start, True)
     queries.append(query)
     late = across_cores(across_chips(keyval, groups), groups)
     results = attend(shards, mine[None], seg_col, seg_row, queries, early, late)

time: 52.8 us -> 51.1 us (0.968)
  Pallas kernels: 13.3 us -> 12.4 us
  local copies, waits for them, and re-layouts: 0.65 us -> 0 us
    ppermute x2, starting transfers between devices: 4.37 us -> 1.4 us  [per_device(): moved = [lax.ppermute(piece, 'dp', ring) for piece in pieces]]
    ppermute x3, waiting for transfers between devices: 4.53 us -> 2 us  [per_device(): lax.ppermute(results[s], 'dp', [(i, (i - s) % shards) for i in range(shar...]
    ppermute x4, waiting for transfers between devices: 3.32 us -> 5.65 us  [per_device(): pieces = [lax.ppermute(piece, 'dp', ring) for piece in pieces]]
    ppermute x3, starting transfers between devices: 2.5 us -> 4.69 us  [per_device(): lax.ppermute(results[s], 'dp', [(i, (i - s) % shards) for i in range(shar...]
    ppermute x8, waiting for transfers between devices: 1.99 us -> 3.08 us  [across_cores(): lax.ppermute(block, 'group', swap)]
    pallas_call x4 -> x3, Pallas kernels: 5.23 us -> 4.17 us  [project(): pl.pallas_call(functools.partial(project_kernel, count, tuple(places), st...]
    ppermute x2, waiting for transfers between devices: 1.21 us -> 0.41 us  [per_device(): moved = [lax.ppermute(piece, 'dp', ring) for piece in pieces]]
    unnamed x2 -> x0, local copies, waits for them, and re-layouts: 0.65 us -> none
  transfers between devices with their start and end apart: 23 -> 23, of which waited for: 13 -> 18; matrix products, arithmetic and copies ran while one was open for 0% -> 0% of each run, Pallas kernels for 17% -> 17%
where the time goes in v4:
time: 51.1 us; the launch traced here: 50.9 us
  starting transfers between devices  19.9 us (39%)
  waiting for transfers between devices  17.9 us (35%)
  Pallas kernels  12.4 us (24%)
  between operations  0.71 us (1%)
    ppermute x6, starting transfers between devices, across_chips(): lax.ppermute(block, 'group', [(i, i ^ m) for i in range(groups)])  7.04 us
    ppermute x6, waiting for transfers between devices, across_chips(): lax.ppermute(block, 'group', [(i, i ^ m) for i in range(groups)])  6.72 us
    ppermute x4, starting transfers between devices, per_device(): pieces = [lax.ppermute(piece, 'dp', ring) for piece in pieces]  6.06 us
    ppermute x4, waiting for transfers between devices, per_device(): pieces = [lax.ppermute(piece, 'dp', ring) for piece in pieces]  5.65 us
    pallas_call x1, Pallas kernels, begin(): pl.pallas_call(functools.partial(begin_kernel, shards), in_specs=[IN_SMEM...  5.46 us
    ppermute x3, starting transfers between devices, per_device(): lax.ppermute(results[s], 'dp', [(i, (i - s) % shards) for i in range(shar...  4.69 us
    pallas_call x3, Pallas kernels, project(): pl.pallas_call(functools.partial(project_kernel, count, tuple(places), st...  4.17 us
    ppermute x8, waiting for transfers between devices, across_cores(): lax.ppermute(block, 'group', swap)  3.08 us
  transfers between devices with their start and end apart: 23, of which 18 were waited for; matrix products, arithmetic and copies ran while one was open for 0% of the time, Pallas kernels for 17%

profile of v4, /device:TPU:0, one launch (start us, length us, event | category | flops | bytes accessed | tf_op | source)
XLA Modules:
  0.0 50.9 jit_solution(38032472638143855)
XLA Ops:
  0.0 1.2 %split.1 = (bf16[32,3200]{1,0:T(8,128)(2,1)S(1)}, bf16[32,3072]{1,0:T(8,128)(2,1)S(1)}) custom-call(bf16[1,32,6144]{2,1,0:T(8,128)(2,1)} %x_hbm.1), custom_call_target="tpu_custom_call" | custom-call | tf_op jit(solution)/shard_map/split/pallas_call | solution.py:56
  1.2 3.1 %collective-permute-start = (bf16[32,3200]{1,0:T(8,128)(2,1)S(1)}, bf16[32,3200]{1,0:T(8,128)(2,1)S(1)}, u32[]{:S(2)}, u32[]{:S(2)}) collective-permute-start(bf16[32,3200]{1,0:T(8,128)(2,1)S(1)} %get-tuple-element.40.refs_3_), channel_id=1, source_target_pairs={{0,1},{1,2},{2,3},{3,0},{4,5},{5,6},{6,7},{7,4},{8,9},{9,10},{10,1... | collective-permute-start | bytes 614408 | tf_op jit(solution)/shard_map/ppermute | solution.py:338
  4.3 1.6 %collective-permute-start.1 = (bf16[32,3072]{1,0:T(8,128)(2,1)S(1)}, bf16[32,3072]{1,0:T(8,128)(2,1)S(1)}, u32[]{:S(2)}, u32[]{:S(2)}) collective-permute-start(bf16[32,3072]{1,0:T(8,128)(2,1)S(1)} %get-tuple-element.41.refs_4_), channel_id=1, source_target_pairs={{0,1},{1,2},{2,3},{3,0},{4,5},{5,6},{6,7},{7,4},{8,9},{9,10},{10,1... | collective-permute-start | bytes 589832 | tf_op jit(solution)/shard_map/ppermute | solution.py:338
  6.5 5.5 %begin.1 = (bf16[32,256]{1,0:T(8,128)(2,1)S(1)}, bf16[32,512]{1,0:T(8,128)(2,1)S(1)}, bf16[6144,256]{1,0:T(8,128)(2,1)S(1)}, bf16[6144,256]{1,0:T(8,128)(2,1)S(1...) custom-call(s32[1]{0:T(128)} %bitcast.place, ...), custom_call_target="tpu_custom_call" | custom-call | tf_op jit(solution)/shard_map/begin/pallas_call | solution.py:142
  12.0 0.2 collective-permute-done.refs_0_
  12.2 1.4 %collective-permute-start.2 = (bf16[32,3200]{1,0:T(8,128)(2,1)S(1)}, bf16[32,3200]{1,0:T(8,128)(2,1)S(1)}, u32[]{:S(2)}, u32[]{:S(2)}) collective-permute-start(bf16[32,3200]{1,0:T(8,128)(2,1)S(1)} %collective-permute-done.refs_0_), channel_id=1, source_target_pairs={{0,1},{1,2},{2,3},{3,0},{4,5},{5,6},{6,7},{7,4},{8,9},{9,10},{10,1... | collective-permute-start | bytes 614408 | tf_op jit(solution)/shard_map/ppermute | solution.py:343
  13.6 2.0 %collective-permute-done.1.refs_1_ = bf16[32,3072]{1,0:T(8,128)(2,1)S(1)} collective-permute-done((bf16[32,3072]{1,0:T(8,128)(2,1)S(1)}, bf16[32,3072]{1,0:T(8,128)(2,1)S(1)}, u32[]{:S(2)}, u32[]{:S(2)}) %collective-permute-start.1) | collective-permute-done | bytes 196640 | tf_op jit(solution)/shard_map/ppermute | solution.py:338
  15.6 0.0 collective-permute-start.3
  15.6 1.9 %project.3 = (bf16[32,256]{1,0:T(8,128)(2,1)S(1)}, bf16[64,512]{1,0:T(8,128)(2,1)S(1)}) custom-call(bf16[32,3200]{1,0:T(8,128)(2,1)S(1)} %collective-permute-done.refs_0_, bf16[32,3072]{1,0:T(8,128)(2,1)S(1)} %collective-permute-done.1.refs_1_, f32[2,6144]{1,0:T(2,128)S(1)} %get-tuple-element.47.refs_2_.refs_4_, ...), custom_call_target="tpu_custom_call" | custom-call | tf_op jit(solution)/shard_map/project/pallas_call | solution.py:213
  17.5 3.3 %collective-permute-done.2.refs_0_ = bf16[32,3200]{1,0:T(8,128)(2,1)S(1)} collective-permute-done((bf16[32,3200]{1,0:T(8,128)(2,1)S(1)}, bf16[32,3200]{1,0:T(8,128)(2,1)S(1)}, u32[]{:S(2)}, u32[]{:S(2)}) %collective-permute-start.2) | collective-permute-done | bytes 204832 | tf_op jit(solution)/shard_map/ppermute | solution.py:343
  20.9 0.8 %collective-permute-start.4 = (bf16[32,3200]{1,0:T(8,128)(2,1)S(1)}, bf16[32,3200]{1,0:T(8,128)(2,1)S(1)}, u32[]{:S(2)}, u32[]{:S(2)}) collective-permute-start(bf16[32,3200]{1,0:T(8,128)(2,1)S(1)} %collective-permute-done.2.refs_0_), channel_id=1, source_target_pairs={{0,1},{1,2},{2,3},{3,0},{4,5},{5,6},{6,7},{7,4},{8,9},{9,10},{10,1... | collective-permute-start | bytes 614408 | tf_op jit(solution)/shard_map/ppermute | solution.py:350
  21.6 2.4 %collective-permute-start.7 = (bf16[64,512]{1,0:T(8,128)(2,1)S(1)}, bf16[64,512]{1,0:T(8,128)(2,1)S(1)}, u32[]{:S(2)}, u32[]{:S(2)}) collective-permute-start(bf16[64,512]{1,0:T(8,128)(2,1)S(1)} %get-tuple-element.62.refs_3_), channel_id=1, source_target_pairs={{0,24},{4,28},{8,16},{12,20},{16,8},{20,12},{24,0},{28,4},{1,25},{... | collective-permute-start | bytes 196616 | tf_op jit(solution)/shard_map/ppermute | solution.py:314
  24.1 0.5 collective-permute-start.6
  24.6 0.5 %collective-permute-start.5 = (bf16[64,512]{1,0:T(8,128)(2,1)S(1)}, bf16[64,512]{1,0:T(8,128)(2,1)S(1)}, u32[]{:S(2)}, u32[]{:S(2)}) collective-permute-start(bf16[64,512]{1,0:T(8,128)(2,1)S(1)} %get-tuple-element.62.refs_3_), channel_id=1, source_target_pairs={{0,8},{4,12},{8,0},{12,4},{16,24},{20,28},{24,16},{28,20},{1,9},{5... | collective-permute-start | bytes 196616 | tf_op jit(solution)/shard_map/ppermute | solution.py:314
  25.1 0.1 collective-permute-done.3.refs_1_
  25.2 0.6 %collective-permute-start.12 = (bf16[32,3072]{1,0:T(8,128)(2,1)S(1)}, bf16[32,3072]{1,0:T(8,128)(2,1)S(1)}, u32[]{:S(2)}, u32[]{:S(2)}) collective-permute-start(bf16[32,3072]{1,0:T(8,128)(2,1)S(1)} %collective-permute-done.3.refs_1_), channel_id=1, source_target_pairs={{0,1},{1,2},{2,3},{3,0},{4,5},{5,6},{6,7},{7,4},{8,9},{9,10},{10,1... | collective-permute-start | bytes 589832 | tf_op jit(solution)/shard_map/ppermute | solution.py:350
  25.9 1.0 %collective-permute-done.7.refs_9_ = bf16[64,512]{1,0:T(8,128)(2,1)S(1)} collective-permute-done((bf16[64,512]{1,0:T(8,128)(2,1)S(1)}, bf16[64,512]{1,0:T(8,128)(2,1)S(1)}, u32[]{:S(2)}, u32[]{:S(2)}) %collective-permute-start.7) | collective-permute-done | bytes 65568 | tf_op jit(solution)/shard_map/ppermute | solution.py:314
  26.8 1.5 %collective-permute-done.6.refs_7_ = bf16[64,512]{1,0:T(8,128)(2,1)S(1)} collective-permute-done((bf16[64,512]{1,0:T(8,128)(2,1)S(1)}, bf16[64,512]{1,0:T(8,128)(2,1)S(1)}, u32[]{:S(2)}, u32[]{:S(2)}) %collective-permute-start.6) | collective-permute-done | bytes 65568 | tf_op jit(solution)/shard_map/ppermute | solution.py:314
  28.4 0.5 collective-permute-done.5.refs_5_
  28.9 0.0 collective-permute-start.8
  28.9 0.5 collective-permute-start.9
  29.4 0.0 collective-permute-start.10
  29.4 0.7 %collective-permute-done.8.refs_4_ = bf16[64,512]{1,0:T(8,128)(2,1)S(1)} collective-permute-done((bf16[64,512]{1,0:T(8,128)(2,1)S(1)}, bf16[64,512]{1,0:T(8,128)(2,1)S(1)}, u32[]{:S(2)}, u32[]{:S(2)}) %collective-permute-start.8) | collective-permute-done | bytes 65568 | tf_op jit(solution)/shard_map/ppermute | solution.py:321
  30.1 0.2 collective-permute-start.11
  30.3 0.0 collective-permute-done.9.refs_6_
  30.3 0.3 collective-permute-done.10.refs_8_
  30.6 0.7 %collective-permute-done.11.refs_10_ = bf16[64,512]{1,0:T(8,128)(2,1)S(1)} collective-permute-done((bf16[64,512]{1,0:T(8,128)(2,1)S(1)}, bf16[64,512]{1,0:T(8,128)(2,1)S(1)}, u32[]{:S(2)}, u32[]{:S(2)}) %collective-permute-start.11) | collective-permute-done | bytes 65568 | tf_op jit(solution)/shard_map/ppermute | solution.py:321
  31.4 0.0 collective-permute-done.4.refs_1_.refs_2_
  31.4 1.1 %project.4.refs_8_ = f32[64,768]{1,0:T(8,128)S(1)} custom-call(bf16[32,3200]{1,0:T(8,128)(2,1)S(1)} %collective-permute-done.2.refs_0_, bf16[32,3200]{1,0:T(8,128)(2,1)S(1)} %collective-permute-done.4.refs_1_.refs_2_, f32[2,6144]{1,0:T(2,128)S(1)} %get-tuple-element.47.refs_2_.refs_4_, bf16[6144,256]{1,0:T(8,128)(2,1)S(1)} %get-tuple-element.48.refs_3_.refs_5_, ...), custom_call_target="tpu_custom_call" | custom-call | tf_op jit(solution)/shard_map/project/pallas_call | solution.py:213
  32.5 0.4 collective-permute-done.12.refs_3_
  32.9 1.1 %project.5 = (bf16[64,256]{1,0:T(8,128)(2,1)S(1)}, bf16[64,512]{1,0:T(8,128)(2,1)S(1)}) custom-call(bf16[32,3200]{1,0:T(8,128)(2,1)S(1)} %collective-permute-done.2.refs_0_, bf16[32,3072]{1,0:T(8,128)(2,1)S(1)} %collective-permute-done.3.refs_1_, bf16[32,3200]{1,0:T(8,128)(2,1)S(1)} %collective-permute-done.4.refs_1_.refs_2_, ...), custom_call_target="tpu_custom_call" | custom-call | tf_op jit(solution)/shard_map/project/pallas_call | solution.py:213
  34.1 2.5 %collective-permute-start.18 = (bf16[64,512]{1,0:T(8,128)(2,1)S(1)}, bf16[64,512]{1,0:T(8,128)(2,1)S(1)}, u32[]{:S(2)}, u32[]{:S(2)}) collective-permute-start(bf16[64,512]{1,0:T(8,128)(2,1)S(1)} %get-tuple-element.70.refs_11_), channel_id=1, source_target_pairs={{0,24},{4,28},{8,16},{12,20},{16,8},{20,12},{24,0},{28,4},{1,25},{... | collective-permute-start | bytes 196616 | tf_op jit(solution)/shard_map/ppermute | solution.py:314
  36.6 0.5 collective-permute-start.16
  37.1 0.5 %collective-permute-start.14 = (bf16[64,512]{1,0:T(8,128)(2,1)S(1)}, bf16[64,512]{1,0:T(8,128)(2,1)S(1)}, u32[]{:S(2)}, u32[]{:S(2)}) collective-permute-start(bf16[64,512]{1,0:T(8,128)(2,1)S(1)} %get-tuple-element.70.refs_11_), channel_id=1, source_target_pairs={{0,8},{4,12},{8,0},{12,4},{16,24},{20,28},{24,16},{28,20},{1,9},{5... | collective-permute-start | bytes 196616 | tf_op jit(solution)/shard_map/ppermute | solution.py:314
  37.6 2.1 %collective-permute-done.18.refs_17_ = bf16[64,512]{1,0:T(8,128)(2,1)S(1)} collective-permute-done((bf16[64,512]{1,0:T(8,128)(2,1)S(1)}, bf16[64,512]{1,0:T(8,128)(2,1)S(1)}, u32[]{:S(2)}, u32[]{:S(2)}) %collective-permute-start.18) | collective-permute-done | bytes 65568 | tf_op jit(solution)/shard_map/ppermute | solution.py:314
  39.7 1.1 %collective-permute-done.16.refs_15_ = bf16[64,512]{1,0:T(8,128)(2,1)S(1)} collective-permute-done((bf16[64,512]{1,0:T(8,128)(2,1)S(1)}, bf16[64,512]{1,0:T(8,128)(2,1)S(1)}, u32[]{:S(2)}, u32[]{:S(2)}) %collective-permute-start.16) | collective-permute-done | bytes 65568 | tf_op jit(solution)/shard_map/ppermute | solution.py:314
  40.8 0.5 collective-permute-done.14.refs_13_
  41.3 0.0 collective-permute-start.15
  41.4 0.7 %collective-permute-done.17.refs_16_ = bf16[64,512]{1,0:T(8,128)(2,1)S(1)} collective-permute-done((bf16[64,512]{1,0:T(8,128)(2,1)S(1)}, bf16[64,512]{1,0:T(8,128)(2,1)S(1)}, u32[]{:S(2)}, u32[]{:S(2)}) %collective-permute-start.17) | collective-permute-done | bytes 65568 | tf_op jit(solution)/shard_map/ppermute | solution.py:321
  42.1 0.5 collective-permute-done.15.refs_14_
  42.6 0.9 %attend.1 = (bf16[32,256]{1,0:T(8,128)(2,1)S(1)}, bf16[32,256]{1,0:T(8,128)(2,1)S(1)}, bf16[32,256]{1,0:T(8,128)(2,1)S(1)}, bf16[32,256]{1,0:T(8,128)(2,1)S(1)}) custom-call(s32[1]{0:T(128)} %bitcast.1.mine, s32[128,1]{1,0:T(8,128)S(1)} %get-tuple-element.42.seg_col, s32[1,128]{1,0:T(1,128)S(1)} %get-tuple-element.43.seg_row, ...), custom_call_target="tpu_custom_call" | custom-call | tf_op jit(solution)/shard_map/attend/pallas_call | solution.py:276
  43.6 0.9 %collective-permute-start.20 = (bf16[32,256]{1,0:T(8,128)(2,1)S(1)}, bf16[32,256]{1,0:T(8,128)(2,1)S(1)}, u32[]{:S(2)}, u32[]{:S(2)}) collective-permute-start(bf16[32,256]{1,0:T(8,128)(2,1)S(1)} %get-tuple-element.72), channel_id=1, source_target_pairs={{0,2},{1,3},{2,0},{3,1},{4,6},{5,7},{6,4},{7,5},{8,10},{9,11},{10,... | collective-permute-start | bytes 49160 | tf_op jit(solution)/shard_map/ppermute | solution.py:361
  44.4 2.1 %collective-permute-start.21 = (bf16[32,256]{1,0:T(8,128)(2,1)S(1)}, bf16[32,256]{1,0:T(8,128)(2,1)S(1)}, u32[]{:S(2)}, u32[]{:S(2)}) collective-permute-start(bf16[32,256]{1,0:T(8,128)(2,1)S(1)} %get-tuple-element.73), channel_id=1, source_target_pairs={{0,1},{1,2},{2,3},{3,0},{4,5},{5,6},{6,7},{7,4},{8,9},{9,10},{10,1... | collective-permute-start | bytes 49160 | tf_op jit(solution)/shard_map/ppermute | solution.py:361
  46.5 1.7 %collective-permute-start.22 = (bf16[32,256]{1,0:T(8,128)(2,1)S(1)}, bf16[32,256]{1,0:T(8,128)(2,1)S(1)}, u32[]{:S(2)}, u32[]{:S(2)}) collective-permute-start(bf16[32,256]{1,0:T(8,128)(2,1)S(1)} %get-tuple-element.74), channel_id=1, source_target_pairs={{0,3},{1,0},{2,1},{3,2},{4,7},{5,4},{6,5},{7,6},{8,11},{9,8},{10,9... | collective-permute-start | bytes 49160 | tf_op jit(solution)/shard_map/ppermute | solution.py:361
  48.2 0.0 collective-permute-done.20.refs_1_
  48.3 1.7 %collective-permute-done.21.refs_2_ = bf16[32,256]{1,0:T(8,128)(2,1)S(1)} collective-permute-done((bf16[32,256]{1,0:T(8,128)(2,1)S(1)}, bf16[32,256]{1,0:T(8,128)(2,1)S(1)}, u32[]{:S(2)}, u32[]{:S(2)}) %collective-permute-start.21) | collective-permute-done | bytes 16416 | tf_op jit(solution)/shard_map/ppermute | solution.py:361
  50.0 0.3 collective-permute-done.22.refs_3_
  50.3 0.6 %place.1 = bf16[1,32,1024]{2,1,0:T(8,128)(2,1)} custom-call(s32[1]{0:T(128)} %bitcast.place, bf16[32,256]{1,0:T(8,128)(2,1)S(1)} %get-tuple-element.71.refs_0_, bf16[32,256]{1,0:T(8,128)(2,1)S(1)} %collective-permute-done.20.refs_1_, bf16[32,256]{1,0:T(8,128)(2,1)S(1)} %collective-permute-done.21.refs_2_, bf16[32,256]{1,0:T(8,128)(2,1)S(1)} %collective-permute-done.22.refs_3_), custom_call_target="tpu_custom_call" | custom-call | tf_op jit(solution)/shard_map/place/pallas_call | solution.py:302
  (5 shorter events, 0.0 us)
Async XLA Ops:
  1.2 11.0 %collective-permute-start = (bf16[32,3200]{1,0:T(8,128)(2,1)S(1)}, bf16[32,3200]{1,0:T(8,128)(2,1)S(1)}, u32[]{:S(2)}, u32[]{:S(2)}) collective-permute-start(bf16[32,3200]{1,0:T(8,128)(2,1)S(1)} %get-tuple-element.40.refs_3_), channel_id=1, source_target_pairs={{0,1},{1,2},{2,3},{3,0},{4,5},{5,6},{6,7},{7,4},{8,9},{9,10},{10,1... | collective-permute-start | bytes 614408 | tf_op jit(solution)/shard_map/ppermute | solution.py:338
  4.3 11.3 %collective-permute-start.1 = (bf16[32,3072]{1,0:T(8,128)(2,1)S(1)}, bf16[32,3072]{1,0:T(8,128)(2,1)S(1)}, u32[]{:S(2)}, u32[]{:S(2)}) collective-permute-start(bf16[32,3072]{1,0:T(8,128)(2,1)S(1)} %get-tuple-element.41.refs_4_), channel_id=1, source_target_pairs={{0,1},{1,2},{2,3},{3,0},{4,5},{5,6},{6,7},{7,4},{8,9},{9,10},{10,1... | collective-permute-start | bytes 589832 | tf_op jit(solution)/shard_map/ppermute | solution.py:338
  12.2 8.6 %collective-permute-start.2 = (bf16[32,3200]{1,0:T(8,128)(2,1)S(1)}, bf16[32,3200]{1,0:T(8,128)(2,1)S(1)}, u32[]{:S(2)}, u32[]{:S(2)}) collective-permute-start(bf16[32,3200]{1,0:T(8,128)(2,1)S(1)} %collective-permute-done.refs_0_), channel_id=1, source_target_pairs={{0,1},{1,2},{2,3},{3,0},{4,5},{5,6},{6,7},{7,4},{8,9},{9,10},{10,1... | collective-permute-start | bytes 614408 | tf_op jit(solution)/shard_map/ppermute | solution.py:343
  15.6 9.6 %collective-permute-start.3 = (bf16[32,3072]{1,0:T(8,128)(2,1)S(1)}, bf16[32,3072]{1,0:T(8,128)(2,1)S(1)}, u32[]{:S(2)}, u32[]{:S(2)}) collective-permute-start(bf16[32,3072]{1,0:T(8,128)(2,1)S(1)} %collective-permute-done.1.refs_1_), channel_id=1, source_target_pairs={{0,1},{1,2},{2,3},{3,0},{4,5},{5,6},{6,7},{7,4},{8,9},{9,10},{10,1... | collective-permute-start | bytes 589832 | tf_op jit(solution)/shard_map/ppermute | solution.py:343
  20.9 10.5 %collective-permute-start.4 = (bf16[32,3200]{1,0:T(8,128)(2,1)S(1)}, bf16[32,3200]{1,0:T(8,128)(2,1)S(1)}, u32[]{:S(2)}, u32[]{:S(2)}) collective-permute-start(bf16[32,3200]{1,0:T(8,128)(2,1)S(1)} %collective-permute-done.2.refs_0_), channel_id=1, source_target_pairs={{0,1},{1,2},{2,3},{3,0},{4,5},{5,6},{6,7},{7,4},{8,9},{9,10},{10,1... | collective-permute-start | bytes 614408 | tf_op jit(solution)/shard_map/ppermute | solution.py:350
  21.6 5.2 %collective-permute-start.7 = (bf16[64,512]{1,0:T(8,128)(2,1)S(1)}, bf16[64,512]{1,0:T(8,128)(2,1)S(1)}, u32[]{:S(2)}, u32[]{:S(2)}) collective-permute-start(bf16[64,512]{1,0:T(8,128)(2,1)S(1)} %get-tuple-element.62.refs_3_), channel_id=1, source_target_pairs={{0,24},{4,28},{8,16},{12,20},{16,8},{20,12},{24,0},{28,4},{1,25},{... | collective-permute-start | bytes 196616 | tf_op jit(solution)/shard_map/ppermute | solution.py:314
  24.1 4.3 %collective-permute-start.6 = (bf16[64,512]{1,0:T(8,128)(2,1)S(1)}, bf16[64,512]{1,0:T(8,128)(2,1)S(1)}, u32[]{:S(2)}, u32[]{:S(2)}) collective-permute-start(bf16[64,512]{1,0:T(8,128)(2,1)S(1)} %get-tuple-element.62.refs_3_), channel_id=1, source_target_pairs={{0,16},{4,20},{8,24},{12,28},{16,0},{20,4},{24,8},{28,12},{1,17},{... | collective-permute-start | bytes 196616 | tf_op jit(solution)/shard_map/ppermute | solution.py:314
  24.6 4.3 %collective-permute-start.5 = (bf16[64,512]{1,0:T(8,128)(2,1)S(1)}, bf16[64,512]{1,0:T(8,128)(2,1)S(1)}, u32[]{:S(2)}, u32[]{:S(2)}) collective-permute-start(bf16[64,512]{1,0:T(8,128)(2,1)S(1)} %get-tuple-element.62.refs_3_), channel_id=1, source_target_pairs={{0,8},{4,12},{8,0},{12,4},{16,24},{20,28},{24,16},{28,20},{1,9},{5... | collective-permute-start | bytes 196616 | tf_op jit(solution)/shard_map/ppermute | solution.py:314
  25.2 7.7 %collective-permute-start.12 = (bf16[32,3072]{1,0:T(8,128)(2,1)S(1)}, bf16[32,3072]{1,0:T(8,128)(2,1)S(1)}, u32[]{:S(2)}, u32[]{:S(2)}) collective-permute-start(bf16[32,3072]{1,0:T(8,128)(2,1)S(1)} %collective-permute-done.3.refs_1_), channel_id=1, source_target_pairs={{0,1},{1,2},{2,3},{3,0},{4,5},{5,6},{6,7},{7,4},{8,9},{9,10},{10,1... | collective-permute-start | bytes 589832 | tf_op jit(solution)/shard_map/ppermute | solution.py:350
  28.9 1.3 %collective-permute-start.8 = (bf16[64,512]{1,0:T(8,128)(2,1)S(1)}, bf16[64,512]{1,0:T(8,128)(2,1)S(1)}, u32[]{:S(2)}, u32[]{:S(2)}) collective-permute-start(bf16[64,512]{1,0:T(8,128)(2,1)S(1)} %get-tuple-element.62.refs_3_), channel_id=1, source_target_pairs={{0,4},{4,0},{8,12},{12,8},{16,20},{20,16},{24,28},{28,24},{1,5},{5... | collective-permute-start | bytes 196616 | tf_op jit(solution)/shard_map/ppermute | solution.py:321
  28.9 1.4 %collective-permute-start.9 = (bf16[64,512]{1,0:T(8,128)(2,1)S(1)}, bf16[64,512]{1,0:T(8,128)(2,1)S(1)}, u32[]{:S(2)}, u32[]{:S(2)}) collective-permute-start(bf16[64,512]{1,0:T(8,128)(2,1)S(1)} %collective-permute-done.5.refs_5_), channel_id=1, source_target_pairs={{0,4},{4,0},{8,12},{12,8},{16,20},{20,16},{24,28},{28,24},{1,5},{5... | collective-permute-start | bytes 196616 | tf_op jit(solution)/shard_map/ppermute | solution.py:321
  29.4 1.3 %collective-permute-start.10 = (bf16[64,512]{1,0:T(8,128)(2,1)S(1)}, bf16[64,512]{1,0:T(8,128)(2,1)S(1)}, u32[]{:S(2)}, u32[]{:S(2)}) collective-permute-start(bf16[64,512]{1,0:T(8,128)(2,1)S(1)} %collective-permute-done.6.refs_7_), channel_id=1, source_target_pairs={{0,4},{4,0},{8,12},{12,8},{16,20},{20,16},{24,28},{28,24},{1,5},{5... | collective-permute-start | bytes 196616 | tf_op jit(solution)/shard_map/ppermute | solution.py:321
  30.1 1.3 %collective-permute-start.11 = (bf16[64,512]{1,0:T(8,128)(2,1)S(1)}, bf16[64,512]{1,0:T(8,128)(2,1)S(1)}, u32[]{:S(2)}, u32[]{:S(2)}) collective-permute-start(bf16[64,512]{1,0:T(8,128)(2,1)S(1)} %collective-permute-done.7.refs_9_), channel_id=1, source_target_pairs={{0,4},{4,0},{8,12},{12,8},{16,20},{20,16},{24,28},{28,24},{1,5},{5... | collective-permute-start | bytes 196616 | tf_op jit(solution)/shard_map/ppermute | solution.py:321
  34.1 5.6 %collective-permute-start.18 = (bf16[64,512]{1,0:T(8,128)(2,1)S(1)}, bf16[64,512]{1,0:T(8,128)(2,1)S(1)}, u32[]{:S(2)}, u32[]{:S(2)}) collective-permute-start(bf16[64,512]{1,0:T(8,128)(2,1)S(1)} %get-tuple-element.70.refs_11_), channel_id=1, source_target_pairs={{0,24},{4,28},{8,16},{12,20},{16,8},{20,12},{24,0},{28,4},{1,25},{... | collective-permute-start | bytes 196616 | tf_op jit(solution)/shard_map/ppermute | solution.py:314
  36.6 4.3 %collective-permute-start.16 = (bf16[64,512]{1,0:T(8,128)(2,1)S(1)}, bf16[64,512]{1,0:T(8,128)(2,1)S(1)}, u32[]{:S(2)}, u32[]{:S(2)}) collective-permute-start(bf16[64,512]{1,0:T(8,128)(2,1)S(1)} %get-tuple-element.70.refs_11_), channel_id=1, source_target_pairs={{0,16},{4,20},{8,24},{12,28},{16,0},{20,4},{24,8},{28,12},{1,17},{... | collective-permute-start | bytes 196616 | tf_op jit(solution)/shard_map/ppermute | solution.py:314
  37.1 4.3 %collective-permute-start.14 = (bf16[64,512]{1,0:T(8,128)(2,1)S(1)}, bf16[64,512]{1,0:T(8,128)(2,1)S(1)}, u32[]{:S(2)}, u32[]{:S(2)}) collective-permute-start(bf16[64,512]{1,0:T(8,128)(2,1)S(1)} %get-tuple-element.70.refs_11_), channel_id=1, source_target_pairs={{0,8},{4,12},{8,0},{12,4},{16,24},{20,28},{24,16},{28,20},{1,9},{5... | collective-permute-start | bytes 196616 | tf_op jit(solution)/shard_map/ppermute | solution.py:314
  37.6 3.7 %collective-permute-start.13 = (bf16[64,512]{1,0:T(8,128)(2,1)S(1)}, bf16[64,512]{1,0:T(8,128)(2,1)S(1)}, u32[]{:S(2)}, u32[]{:S(2)}) collective-permute-start(bf16[64,512]{1,0:T(8,128)(2,1)S(1)} %get-tuple-element.70.refs_11_), channel_id=1, source_target_pairs={{0,4},{4,0},{8,12},{12,8},{16,20},{20,16},{24,28},{28,24},{1,5},{5... | collective-permute-start | bytes 196616 | tf_op jit(solution)/shard_map/ppermute | solution.py:321
  39.7 1.7 %collective-permute-start.19 = (bf16[64,512]{1,0:T(8,128)(2,1)S(1)}, bf16[64,512]{1,0:T(8,128)(2,1)S(1)}, u32[]{:S(2)}, u32[]{:S(2)}) collective-permute-start(bf16[64,512]{1,0:T(8,128)(2,1)S(1)} %collective-permute-done.18.refs_17_), channel_id=1, source_target_pairs={{0,4},{4,0},{8,12},{12,8},{16,20},{20,16},{24,28},{28,24},{1,5},{5... | collective-permute-start | bytes 196616 | tf_op jit(solution)/shard_map/ppermute | solution.py:321
  40.8 1.3 %collective-permute-start.17 = (bf16[64,512]{1,0:T(8,128)(2,1)S(1)}, bf16[64,512]{1,0:T(8,128)(2,1)S(1)}, u32[]{:S(2)}, u32[]{:S(2)}) collective-permute-start(bf16[64,512]{1,0:T(8,128)(2,1)S(1)} %collective-permute-done.16.refs_15_), channel_id=1, source_target_pairs={{0,4},{4,0},{8,12},{12,8},{16,20},{20,16},{24,28},{28,24},{1,5},{5... | collective-permute-start | bytes 196616 | tf_op jit(solution)/shard_map/ppermute | solution.py:321
  41.3 1.3 %collective-permute-start.15 = (bf16[64,512]{1,0:T(8,128)(2,1)S(1)}, bf16[64,512]{1,0:T(8,128)(2,1)S(1)}, u32[]{:S(2)}, u32[]{:S(2)}) collective-permute-start(bf16[64,512]{1,0:T(8,128)(2,1)S(1)} %collective-permute-done.14.refs_13_), channel_id=1, source_target_pairs={{0,4},{4,0},{8,12},{12,8},{16,20},{20,16},{24,28},{28,24},{1,5},{5... | collective-permute-start | bytes 196616 | tf_op jit(solution)/shard_map/ppermute | solution.py:321
  43.6 4.7 %collective-permute-start.20 = (bf16[32,256]{1,0:T(8,128)(2,1)S(1)}, bf16[32,256]{1,0:T(8,128)(2,1)S(1)}, u32[]{:S(2)}, u32[]{:S(2)}) collective-permute-start(bf16[32,256]{1,0:T(8,128)(2,1)S(1)} %get-tuple-element.72), channel_id=1, source_target_pairs={{0,2},{1,3},{2,0},{3,1},{4,6},{5,7},{6,4},{7,5},{8,10},{9,11},{10,... | collective-permute-start | bytes 49160 | tf_op jit(solution)/shard_map/ppermute | solution.py:361
  44.4 5.5 %collective-permute-start.21 = (bf16[32,256]{1,0:T(8,128)(2,1)S(1)}, bf16[32,256]{1,0:T(8,128)(2,1)S(1)}, u32[]{:S(2)}, u32[]{:S(2)}) collective-permute-start(bf16[32,256]{1,0:T(8,128)(2,1)S(1)} %get-tuple-element.73), channel_id=1, source_target_pairs={{0,1},{1,2},{2,3},{3,0},{4,5},{5,6},{6,7},{7,4},{8,9},{9,10},{10,1... | collective-permute-start | bytes 49160 | tf_op jit(solution)/shard_map/ppermute | solution.py:361
  46.5 3.7 %collective-permute-start.22 = (bf16[32,256]{1,0:T(8,128)(2,1)S(1)}, bf16[32,256]{1,0:T(8,128)(2,1)S(1)}, u32[]{:S(2)}, u32[]{:S(2)}) collective-permute-start(bf16[32,256]{1,0:T(8,128)(2,1)S(1)} %get-tuple-element.74), channel_id=1, source_target_pairs={{0,3},{1,0},{2,1},{3,2},{4,7},{5,4},{6,5},{7,6},{8,11},{9,8},{10,9... | collective-permute-start | bytes 49160 | tf_op jit(solution)/shard_map/ppermute | solution.py:361

commit v5 on v4

v5 whole, which is shorter than its diff:
```python
import functools
import math

import jax
import jax.numpy as jnp
from jax import lax
from jax.experimental import pallas as pl
from jax.experimental.pallas import tpu as pltpu
from jax.sharding import PartitionSpec as P

HD = 128
LANES = 128
EDGES = (0, 1, 2)
CHUNKS = len(EDGES) - 1
PARTS = 4
AHEAD = 6
VMEM = pltpu.MemorySpace.VMEM
HBM = pltpu.MemorySpace.HBM
SMEM = pltpu.MemorySpace.SMEM
IN_VMEM = pl.BlockSpec(memory_space=VMEM)
IN_HBM = pl.BlockSpec(memory_space=HBM)
IN_SMEM = pl.BlockSpec(memory_space=SMEM)


def spans_of(depth):
    edges = [depth * edge // EDGES[-1] for edge in EDGES]
    return [slice(low, high) for low, high in zip(edges, edges[1:])]


def params(mebibytes):
    return pltpu.CompilerParams(vmem_limit_bytes=mebibytes * 1024 * 1024)


def near(*arrays):
    return [pltpu.with_memory_space_constraint(a, VMEM) for a in arrays]


def far(*arrays):
    return [pltpu.with_memory_space_constraint(a, HBM) for a in arrays]


def split_kernel(x_hbm, *refs):
    outs, (x_ref, sem) = refs[:CHUNKS], refs[CHUNKS:]
    copy = pltpu.make_async_copy(x_hbm.at[0], x_ref, sem)
    copy.start()
    copy.wait()
    for span, out in zip(spans_of(x_ref.shape[1]), outs):
        out[:, : span.stop - span.start] = x_ref[:, span]
    x = x_ref[...].astype(jnp.float32)
    scale = lax.rsqrt(jnp.mean(x * x, axis=-1, keepdims=True) + 1e-06)
    high = scale.astype(jnp.bfloat16).astype(jnp.float32)
    middle = (scale - high).astype(jnp.bfloat16).astype(jnp.float32)
    lane = lax.broadcasted_iota(jnp.int32, (x.shape[0], LANES), 1)
    parts = jnp.where(lane == 0, high, jnp.where(lane == 1, middle, scale - high - middle))
    outs[0][:, outs[0].shape[1] - LANES :] = parts.astype(jnp.bfloat16)


def split(latents):
    _, rows, depth = latents.shape
    widths = [span.stop - span.start for span in spans_of(depth)]
    widths[0] += LANES
    return pl.pallas_call(
        split_kernel,
        in_specs=[IN_HBM],
        out_specs=[IN_VMEM] * CHUNKS,
        out_shape=[VMEM((rows, width), jnp.bfloat16) for width in widths],
        scratch_shapes=[pltpu.VMEM((rows, depth), jnp.bfloat16), pltpu.SemaphoreType.DMA],
        compiler_params=params(1),
        name="split",
    )(*far(latents))


def scale_of(piece):
    parts = piece[:, piece.shape[1] - LANES :].astype(jnp.float32)
    return parts[:, 0:1] + (parts[:, 1:2] + parts[:, 2:3])


def modulated(piece, scale, gain, span):
    x = piece[:, : span.stop - span.start].astype(jnp.float32)
    return (x * scale * gain[0:1, span] + gain[1:2, span]).astype(jnp.bfloat16)


def begin_kernel(shards, place, steps, seg_hbm, table, *refs):
    sources, refs = refs[:3], refs[3:]
    pieces, refs = refs[:CHUNKS], refs[CHUNKS:]
    query, keyval = refs[:2]
    outs, (gain, seg_col, seg_row, segments, sems, small) = refs[2:5], refs[5:]
    depth = outs[0].shape[0]
    width = query.shape[1]
    chunks = spans_of(depth)
    reads = [
        pltpu.make_async_copy(table.at[steps[0]], gain, small.at[0]),
        pltpu.make_async_copy(seg_hbm, segments, small.at[1]),
    ]
    for copy in reads:
        copy.start()
    short = depth // PARTS
    spans = [slice(k * short, (k + 1) * short) for k in range(PARTS)]
    copies = [
        pltpu.make_async_copy(sources[i].at[span], outs[i].at[span], sems.at[i, k])
        for i in range(3)
        for k, span in enumerate(spans)
    ]
    for copy in copies[:AHEAD]:
        copy.start()
    for copy in reads:
        copy.wait()
    gain[0:1, :] = 1.0 + gain[0:1, :]
    scale = scale_of(pieces[0])
    own = jnp.concatenate(
        [modulated(piece, scale, gain, chunk) for piece, chunk in zip(pieces, chunks)], axis=1
    )
    tokc = segments.shape[1]
    rows = tokc // shards

    def owner(position):
        shard = place[0] - position // rows
        return jnp.where(shard < 0, shard + shards, shard) * rows + position % rows

    down = lax.broadcasted_iota(jnp.int32, (tokc, tokc), 0)
    across = lax.broadcasted_iota(jnp.int32, (tokc, tokc), 1)
    natural = segments[...]
    column = jnp.sum(jnp.where(down == across, natural, 0), axis=1, keepdims=True)
    seg_col[...] = jnp.sum(jnp.where(owner(down) == across, natural, 0), axis=1, keepdims=True)
    seg_row[...] = jnp.sum(jnp.where(owner(across) == down, column, 0), axis=0, keepdims=True)
    for i in range(3):
        total = None
        for k, span in enumerate(spans):
            index = i * len(spans) + k
            copies[index].wait()
            if index + AHEAD < len(copies):
                copies[index + AHEAD].start()
            part = jnp.dot(own[:, span], outs[i][span], preferred_element_type=jnp.float32)
            total = part if total is None else total + part
        if i == 0:
            query[...] = total.astype(jnp.bfloat16)
        else:
            keyval[:, (i - 1) * width : i * width] = total.astype(jnp.bfloat16)


def begin(weights, segments, steps, mod_table, pieces, place, shards):
    tokc = segments.shape[0]
    rows = pieces[0].shape[0]
    width = weights[0].shape[1]
    return pl.pallas_call(
        functools.partial(begin_kernel, shards),
        in_specs=[IN_SMEM] * 2 + [IN_HBM] * 5 + [IN_VMEM] * CHUNKS,
        out_specs=[IN_VMEM] * 8,
        out_shape=[VMEM((rows, width), jnp.bfloat16), VMEM((rows, 2 * width), jnp.bfloat16)]
        + [VMEM(w.shape, w.dtype) for w in weights]
        + [VMEM(mod_table.shape[1:], jnp.float32)]
        + [VMEM((tokc, 1), jnp.int32), VMEM((1, tokc), jnp.int32)],
        scratch_shapes=[
            pltpu.VMEM((1, tokc), jnp.int32),
            pltpu.SemaphoreType.DMA((3, PARTS)),
            pltpu.SemaphoreType.DMA((2,)),
        ],
        compiler_params=params(2 + tokc * tokc * 32 // 2**20),
        name="begin",
    )(place, steps, *far(segments[None], mod_table, *weights), *near(*pieces))


def project_kernel(count, places, kinds, first, last, older, *refs):
    known = len({0, *places})
    pieces, refs = refs[: count * known], refs[count * known :]
    gain, weights, refs = refs[0], refs[1 : 1 + len(kinds)], refs[1 + len(kinds) :]
    if not first:
        start, refs = refs[0], refs[1:]
    if older:
        before, refs = refs[0], refs[1:]
        refs[-1][:older, :] = before[...]
    width = weights[0].shape[1]
    chunks = spans_of(weights[0].shape[0])
    scales = [scale_of(pieces[s * known]) for s in range(count)]
    stacked = [
        jnp.concatenate(
            [
                modulated(pieces[s * known + known - len(places) + i], scales[s], gain, chunks[k])
                for s in range(count)
            ],
            axis=0,
        )
        for i, k in enumerate(places)
    ]
    for index, (kind, weight) in enumerate(zip(kinds, weights)):
        total = None if first else start[:, index * width : (index + 1) * width]
        for k, place in enumerate(places):
            part = jnp.dot(
                stacked[k],
                weight[chunks[place], :],
                preferred_element_type=jnp.float32,
            )
            total = part if total is None else total + part
        if not last:
            refs[0][:, index * width : (index + 1) * width] = total
        elif kind == 0:
            refs[0][...] = total.astype(jnp.bfloat16)
        else:
            refs[-1][older:, (kind - 1) * width : kind * width] = total.astype(jnp.bfloat16)


def project(shard_pieces, places, gain, weights, kinds, start, last, before=None):
    count = len(shard_pieces)
    rows = shard_pieces[0][0].shape[0] * count
    older = 0 if before is None else before.shape[0]
    width = weights[0].shape[1]
    if last:
        shapes = [VMEM((rows, width), jnp.bfloat16)] if 0 in kinds else []
        if 1 in kinds:
            shapes.append(VMEM((older + rows, 2 * width), jnp.bfloat16))
    else:
        shapes = [VMEM((rows, len(kinds) * width), jnp.float32)]
    pieces = [shard[k] for shard in shard_pieces for k in sorted({0, *places})]
    extra = [array for array in (start, before) if array is not None]
    used = [weights[kind] for kind in kinds]
    return pl.pallas_call(
        functools.partial(
            project_kernel, count, tuple(places), tuple(kinds), start is None, last, older
        ),
        in_specs=[IN_VMEM] * (len(pieces) + 1 + len(used) + len(extra)),
        out_specs=[IN_VMEM] * len(shapes),
        out_shape=shapes,
        compiler_params=params(1 + count // 2),
        name="project",
    )(*near(*pieces, gain, *used, *extra))


def bias_of(sources, mine, seg_col, seg_row):
    here = mine[0]
    clip = jnp.concatenate(
        [seg_row + jnp.where((here ^ m) <= here, 0, 1000) for m in range(sources)], axis=1
    )
    return jnp.where(seg_col == clip, 0.0, -1e30)


def stack(blocks, out):
    many = blocks[0].shape[0]
    for m, block in enumerate(blocks):
        out[m * many : (m + 1) * many, :] = block[...]


def blocks_of(tokc):
    block = min(tokc, 128)
    return [slice(start, start + block) for start in range(0, tokc, block)]


def weigh(queries, keys, values, bias, floors):
    scores = [
        lax.dot_general(q, k, (((1,), (1,)), ((), ())), preferred_element_type=jnp.float32)
        for q, k in zip(queries, keys)
    ]
    scores = [s * (1.0 / math.sqrt(HD)) + bias for s in scores]
    bests = [jnp.max(s, axis=-1, keepdims=True) for s in scores]
    if floors is not None:
        bests = [jnp.maximum(best, floor) for best, floor in zip(bests, floors)]
    weights = [jnp.exp(s - best) for s, best in zip(scores, bests)]
    sums = [
        jnp.dot(w.astype(jnp.bfloat16), v, preferred_element_type=jnp.float32)
        for w, v in zip(weights, values)
    ]
    totals = [jnp.sum(w, axis=-1, keepdims=True) for w in weights]
    return bests, totals, sums


def columns(ref, span, count, start=0):
    return [ref[span, start + h * HD : start + (h + 1) * HD] for h in range(count)]


def attend_early_kernel(parts, sources, mine, seg_col, seg_row, *refs):
    queries, refs = refs[:parts], refs[parts:]
    early, refs = refs[:sources], refs[sources:]
    q_all, sums, bests, totals, bias_late, kv_all = refs
    filled = 0
    for query in queries:
        q_all[filled : filled + query.shape[0], :] = query[...]
        filled += query.shape[0]
    stack(early, kv_all)
    many = early[0].shape[0]
    heads = q_all.shape[1] // HD
    every = slice(0, kv_all.shape[0])
    for span in blocks_of(q_all.shape[0]):
        bias = bias_of(sources, mine, seg_col[span, :], seg_row[:, :many])
        state = weigh(
            columns(q_all, span, heads),
            columns(kv_all, every, heads),
            columns(kv_all, every, heads, heads * HD),
            bias,
            None,
        )
        for h, (best, total, summed) in enumerate(zip(*state)):
            bests[span, h * HD : (h + 1) * HD] = jnp.broadcast_to(best, summed.shape)
            totals[span, h * HD : (h + 1) * HD] = jnp.broadcast_to(total, summed.shape)
            sums[span, h * HD : (h + 1) * HD] = summed
        bias_late[span, :] = bias_of(sources, mine, seg_col[span, :], seg_row[:, many:])


def attend_early(mine, seg_col, seg_row, queries, early):
    sources, many = len(early), early[0].shape[0]
    tokc, width = seg_col.shape[0], queries[0].shape[1]
    return pl.pallas_call(
        functools.partial(attend_early_kernel, len(queries), sources),
        in_specs=[IN_SMEM] + [IN_VMEM] * (2 + len(queries) + sources),
        out_specs=[IN_VMEM] * 5,
        out_shape=[VMEM((tokc, width), jnp.bfloat16)]
        + [VMEM((tokc, width), jnp.float32)] * 3
        + [VMEM((tokc, sources * (tokc - many)), jnp.float32)],
        scratch_shapes=[pltpu.VMEM((sources * many, 2 * width), jnp.bfloat16)],
        compiler_params=params(3 * (sources * tokc // 1024)),
        name="attend_early",
    )(mine, *near(seg_col, seg_row, *queries, *early))


def attend_kernel(shards, sources, q_all, sums, bests, totals, bias, *refs):
    late, outs, kv_all = refs[:sources], refs[sources:-1], refs[-1]
    tokc, width = q_all.shape
    rows = tokc // shards
    heads = width // HD
    stack(late, kv_all)
    every = slice(0, kv_all.shape[0])
    for span in blocks_of(tokc):
        floors = [floor[:, 0:1] for floor in columns(bests, span, heads)]
        state = weigh(
            columns(q_all, span, heads),
            columns(kv_all, every, heads),
            columns(kv_all, every, heads, heads * HD),
            bias[span, :],
            floors,
        )
        before = zip(floors, columns(totals, span, heads), columns(sums, span, heads))
        for h, (best, total, summed) in enumerate(zip(*state)):
            floor, old_total, old_sum = next(before)
            fade = jnp.exp(floor - best)
            scale = 1.0 / (total + old_total[:, 0:1] * fade)
            result = ((summed + old_sum * fade) * scale).astype(jnp.bfloat16)
            for s in range(span.start // rows, span.stop // rows):
                outs[s][:, h * HD : (h + 1) * HD] = result[
                    s * rows - span.start : (s + 1) * rows - span.start
                ]


def attend(shards, state, late):
    sources, many = len(late), late[0].shape[0]
    tokc, width = state[0].shape
    rows = tokc // shards
    return pl.pallas_call(
        functools.partial(attend_kernel, shards, sources),
        in_specs=[IN_VMEM] * (len(state) + sources),
        out_specs=[IN_VMEM] * shards,
        out_shape=[VMEM((rows, width), jnp.bfloat16)] * shards,
        scratch_shapes=[pltpu.VMEM((sources * many, 2 * width), jnp.bfloat16)],
        compiler_params=params(3 * (sources * tokc // 1024)),
        name="attend",
    )(*near(*state, *late))


def place_kernel(order, place, *refs):
    pieces, out = refs[:-1], refs[-1]
    width = pieces[0].shape[1]
    count = len(pieces)
    for s, piece in zip(order, pieces):
        column = lax.rem(place[0] + s, count) * width
        out[0, :, pl.ds(pl.multiple_of(column, width), width)] = piece[...]


def place_columns(place, pieces):
    rows, width = pieces[0].shape
    order = [0, *range(2, len(pieces)), 1]
    return pl.pallas_call(
        functools.partial(place_kernel, order),
        in_specs=[IN_SMEM] + [IN_VMEM] * len(pieces),
        out_specs=IN_VMEM,
        out_shape=jax.ShapeDtypeStruct((1, rows, width * len(pieces)), jnp.bfloat16),
        compiler_params=params(1),
        name="place",
    )(place, *near(*[pieces[s] for s in order]))


def across_chips(block, groups):
    return [block] + [
        lax.ppermute(block, "group", [(i, i ^ m) for i in range(groups)])
        for m in range(2, groups, 2)
    ]


def across_cores(held, groups):
    swap = [(i, i ^ 1) for i in range(groups)]
    return [each for block in held for each in (block, lax.ppermute(block, "group", swap))]


def per_device(latents, steps, segment_ids, mod_table, w_query, w_key, w_value):
    shards = lax.axis_size("dp")
    groups = lax.axis_size("group")
    rows = latents.shape[1]
    place = lax.axis_index("dp").astype(jnp.int32)
    mine = lax.axis_index("group").astype(jnp.int32)
    ring = [(i, (i + 1) % shards) for i in range(shards)]

    latents, place, mine = lax.optimization_barrier((latents, place[None], mine[None]))
    pieces = list(split(latents))
    query, keyval, *rest = begin(
        (w_query, w_key, w_value), segment_ids, steps, mod_table, pieces, place, shards
    )
    weights, (gain, seg_col, seg_row) = rest[:3], rest[3:]
    queries = [query]
    pieces = [lax.ppermute(piece, "dp", ring) for piece in pieces]
    pieces[0], keyval = lax.optimization_barrier((pieces[0], keyval))
    arrived = []
    for s in range(1, shards - 2):
        arrived.append(pieces)
        pieces = [lax.ppermute(piece, "dp", ring) for piece in pieces]
    query, keyval = project(arrived, range(CHUNKS), gain, weights, (0, 1, 2), None, True, keyval)
    queries.append(query)
    pieces[0], keyval = lax.optimization_barrier((pieces[0], keyval))
    early = across_chips(keyval, groups)
    _, early = lax.optimization_barrier((pieces[-1], early))
    early = across_cores(early, groups)
    moved = [lax.ppermute(piece, "dp", ring) for piece in pieces]
    moved[0], early = lax.optimization_barrier((moved[0], early))
    both = [pieces, moved]
    start = project(both, range(CHUNKS - 1), gain, weights, (1, 2), None, False)[0]
    keyval = project(both, [CHUNKS - 1], gain, weights, (1, 2), start, True)[0]
    gain, keyval = lax.optimization_barrier((gain, keyval))
    late = across_chips(keyval, groups)
    query = project(both, range(CHUNKS), gain, weights, (0,), None, True)[0]
    queries.append(query)
    state = attend_early(mine, seg_col, seg_row, queries, early)
    late[1:], state = lax.optimization_barrier((late[1:], state))
    late = across_cores(late, groups)
    results = attend(shards, state, late)
    landed = [results[0]]
    for s in range(1, shards):
        landed.append(
            lax.ppermute(results[s], "dp", [(i, (i - s) % shards) for i in range(shards)])
        )
    return place_columns(place, landed)


def solution(mesh):
    placed = (
        P("group", "dp", None),
        P("group"),
        P(),
        P(),
        P(None, "dp"),
        P(None, "dp"),
        P(None, "dp"),
    )
    return jax.shard_map(
        per_device, mesh=mesh, in_specs=placed, out_specs=P("group", "dp", None), check_vma=False
    )
```

time: 51.1 us -> 50.6 us (level)
  waiting for transfers between devices: 17.9 us -> 16.7 us
    ppermute x6, waiting for transfers between devices: 6.72 us -> 5.36 us  [across_chips(): lax.ppermute(block, 'group', [(i, i ^ m) for i in range(groups)])]
    pallas_call x4 -> x6, Pallas kernels: 5.12 us -> 5.58 us  [the longest x4 4.47 us: project(): pl.pallas_call(functools.partial(project_kernel, count, tuple(places), tu...]
  transfers between devices with their start and end apart: 23 -> 23, of which waited for: 18 -> 20; matrix products, arithmetic and copies ran while one was open for 0% -> 0% of each run, Pallas kernels for 17% -> 19%
where the time goes in v5:
time: 50.6 us; the launch traced here: 50.5 us
  starting transfers between devices  20.2 us (40%)
  waiting for transfers between devices  16.7 us (33%)
  Pallas kernels  12.9 us (25%)
  between operations  0.73 us (1%)
    ppermute x6, starting transfers between devices, across_chips(): lax.ppermute(block, 'group', [(i, i ^ m) for i in range(groups)])  7.04 us
    ppermute x4, starting transfers between devices, per_device(): pieces = [lax.ppermute(piece, 'dp', ring) for piece in pieces]  6.06 us
    ppermute x4, waiting for transfers between devices, per_device(): pieces = [lax.ppermute(piece, 'dp', ring) for piece in pieces]  5.66 us
    pallas_call x1, Pallas kernels, begin(): pl.pallas_call(functools.partial(begin_kernel, shards), in_specs=[IN_SMEM...  5.46 us
    ppermute x6, waiting for transfers between devices, across_chips(): lax.ppermute(block, 'group', [(i, i ^ m) for i in range(groups)])  5.36 us
    ppermute x3, starting transfers between devices, per_device(): lax.ppermute(results[s], 'dp', [(i, (i - s) % shards) for i in range(shar...  4.5 us
    pallas_call x4, Pallas kernels, project(): pl.pallas_call(functools.partial(project_kernel, count, tuple(places), tu...  4.47 us
    ppermute x8, waiting for transfers between devices, across_cores(): lax.ppermute(block, 'group', swap)  3.08 us
  transfers between devices with their start and end apart: 23, of which 20 were waited for; matrix products, arithmetic and copies ran while one was open for 0% of the time, Pallas kernels for 19%

profile of v5, /device:TPU:0, one launch (start us, length us, event | category | flops | bytes accessed | tf_op | source)
XLA Modules:
  0.0 50.5 jit_solution(8638169332764838100)
XLA Ops:
  0.0 1.2 %split.1 = (bf16[32,3200]{1,0:T(8,128)(2,1)S(1)}, bf16[32,3072]{1,0:T(8,128)(2,1)S(1)}) custom-call(bf16[1,32,6144]{2,1,0:T(8,128)(2,1)} %x_hbm), custom_call_target="tpu_custom_call" | custom-call | tf_op jit(solution)/shard_map/split/pallas_call | solution.py:62
  1.2 3.1 %collective-permute-start = (bf16[32,3200]{1,0:T(8,128)(2,1)S(1)}, bf16[32,3200]{1,0:T(8,128)(2,1)S(1)}, u32[]{:S(2)}, u32[]{:S(2)}) collective-permute-start(bf16[32,3200]{1,0:T(8,128)(2,1)S(1)} %get-tuple-element.58.refs_3_), channel_id=1, source_target_pairs={{0,1},{1,2},{2,3},{3,0},{4,5},{5,6},{6,7},{7,4},{8,9},{9,10},{10,1... | collective-permute-start | bytes 614408 | tf_op jit(solution)/shard_map/ppermute | solution.py:405
  4.3 1.6 %collective-permute-start.2 = (bf16[32,3072]{1,0:T(8,128)(2,1)S(1)}, bf16[32,3072]{1,0:T(8,128)(2,1)S(1)}, u32[]{:S(2)}, u32[]{:S(2)}) collective-permute-start(bf16[32,3072]{1,0:T(8,128)(2,1)S(1)} %get-tuple-element.59.refs_4_), channel_id=1, source_target_pairs={{0,1},{1,2},{2,3},{3,0},{4,5},{5,6},{6,7},{7,4},{8,9},{9,10},{10,1... | collective-permute-start | bytes 589832 | tf_op jit(solution)/shard_map/ppermute | solution.py:405
  6.5 5.5 %begin.1 = (bf16[32,256]{1,0:T(8,128)(2,1)S(1)}, bf16[32,512]{1,0:T(8,128)(2,1)S(1)}, bf16[6144,256]{1,0:T(8,128)(2,1)S(1)}, bf16[6144,256]{1,0:T(8,128)(2,1)S(1...) custom-call(s32[1]{0:T(128)} %bitcast.place, ...), custom_call_target="tpu_custom_call" | custom-call | tf_op jit(solution)/shard_map/begin/pallas_call | solution.py:145
  12.0 0.2 collective-permute-done.refs_0_
  12.2 1.4 %collective-permute-start.1 = (bf16[32,3200]{1,0:T(8,128)(2,1)S(1)}, bf16[32,3200]{1,0:T(8,128)(2,1)S(1)}, u32[]{:S(2)}, u32[]{:S(2)}) collective-permute-start(bf16[32,3200]{1,0:T(8,128)(2,1)S(1)} %collective-permute-done.refs_0_), channel_id=1, source_target_pairs={{0,1},{1,2},{2,3},{3,0},{4,5},{5,6},{6,7},{7,4},{8,9},{9,10},{10,1... | collective-permute-start | bytes 614408 | tf_op jit(solution)/shard_map/ppermute | solution.py:410
  13.6 2.0 %collective-permute-done.2.refs_1_ = bf16[32,3072]{1,0:T(8,128)(2,1)S(1)} collective-permute-done((bf16[32,3072]{1,0:T(8,128)(2,1)S(1)}, bf16[32,3072]{1,0:T(8,128)(2,1)S(1)}, u32[]{:S(2)}, u32[]{:S(2)}) %collective-permute-start.2) | collective-permute-done | bytes 196640 | tf_op jit(solution)/shard_map/ppermute | solution.py:405
  15.6 1.9 %project.4 = (bf16[32,256]{1,0:T(8,128)(2,1)S(1)}, bf16[64,512]{1,0:T(8,128)(2,1)S(1)}) custom-call(bf16[32,3200]{1,0:T(8,128)(2,1)S(1)} %collective-permute-done.refs_0_, bf16[32,3072]{1,0:T(8,128)(2,1)S(1)} %collective-permute-done.2.refs_1_, f32[2,6144]{1,0:T(2,128)S(1)} %get-tuple-element.81.refs_2_.refs_4_, ...), custom_call_target="tpu_custom_call" | custom-call | tf_op jit(solution)/shard_map/project/pallas_call | solution.py:216
  17.5 3.3 %collective-permute-done.1.refs_0_ = bf16[32,3200]{1,0:T(8,128)(2,1)S(1)} collective-permute-done((bf16[32,3200]{1,0:T(8,128)(2,1)S(1)}, bf16[32,3200]{1,0:T(8,128)(2,1)S(1)}, u32[]{:S(2)}, u32[]{:S(2)}) %collective-permute-start.1) | collective-permute-done | bytes 204832 | tf_op jit(solution)/shard_map/ppermute | solution.py:410
  20.9 0.8 %collective-permute-start.4 = (bf16[32,3200]{1,0:T(8,128)(2,1)S(1)}, bf16[32,3200]{1,0:T(8,128)(2,1)S(1)}, u32[]{:S(2)}, u32[]{:S(2)}) collective-permute-start(bf16[32,3200]{1,0:T(8,128)(2,1)S(1)} %collective-permute-done.1.refs_0_), channel_id=1, source_target_pairs={{0,1},{1,2},{2,3},{3,0},{4,5},{5,6},{6,7},{7,4},{8,9},{9,10},{10,1... | collective-permute-start | bytes 614408 | tf_op jit(solution)/shard_map/ppermute | solution.py:417
  21.6 2.4 %collective-permute-start.7 = (bf16[64,512]{1,0:T(8,128)(2,1)S(1)}, bf16[64,512]{1,0:T(8,128)(2,1)S(1)}, u32[]{:S(2)}, u32[]{:S(2)}) collective-permute-start(bf16[64,512]{1,0:T(8,128)(2,1)S(1)} %get-tuple-element.82.refs_3_), channel_id=1, source_target_pairs={{0,24},{4,28},{8,16},{12,20},{16,8},{20,12},{24,0},{28,4},{1,25},{... | collective-permute-start | bytes 196616 | tf_op jit(solution)/shard_map/ppermute | solution.py:380
  24.1 0.5 %collective-permute-start.6 = (bf16[64,512]{1,0:T(8,128)(2,1)S(1)}, bf16[64,512]{1,0:T(8,128)(2,1)S(1)}, u32[]{:S(2)}, u32[]{:S(2)}) collective-permute-start(bf16[64,512]{1,0:T(8,128)(2,1)S(1)} %get-tuple-element.82.refs_3_), channel_id=1, source_target_pairs={{0,16},{4,20},{8,24},{12,28},{16,0},{20,4},{24,8},{28,12},{1,17},{... | collective-permute-start | bytes 196616 | tf_op jit(solution)/shard_map/ppermute | solution.py:380
  24.6 0.5 %collective-permute-start.5 = (bf16[64,512]{1,0:T(8,128)(2,1)S(1)}, bf16[64,512]{1,0:T(8,128)(2,1)S(1)}, u32[]{:S(2)}, u32[]{:S(2)}) collective-permute-start(bf16[64,512]{1,0:T(8,128)(2,1)S(1)} %get-tuple-element.82.refs_3_), channel_id=1, source_target_pairs={{0,8},{4,12},{8,0},{12,4},{16,24},{20,28},{24,16},{28,20},{1,9},{5... | collective-permute-start | bytes 196616 | tf_op jit(solution)/shard_map/ppermute | solution.py:380
  25.1 0.1 collective-permute-done.3.refs_1_
  25.2 0.6 %collective-permute-start.12 = (bf16[32,3072]{1,0:T(8,128)(2,1)S(1)}, bf16[32,3072]{1,0:T(8,128)(2,1)S(1)}, u32[]{:S(2)}, u32[]{:S(2)}) collective-permute-start(bf16[32,3072]{1,0:T(8,128)(2,1)S(1)} %collective-permute-done.3.refs_1_), channel_id=1, source_target_pairs={{0,1},{1,2},{2,3},{3,0},{4,5},{5,6},{6,7},{7,4},{8,9},{9,10},{10,1... | collective-permute-start | bytes 589832 | tf_op jit(solution)/shard_map/ppermute | solution.py:417
  25.9 1.0 %collective-permute-done.7.refs_9_ = bf16[64,512]{1,0:T(8,128)(2,1)S(1)} collective-permute-done((bf16[64,512]{1,0:T(8,128)(2,1)S(1)}, bf16[64,512]{1,0:T(8,128)(2,1)S(1)}, u32[]{:S(2)}, u32[]{:S(2)}) %collective-permute-start.7) | collective-permute-done | bytes 65568 | tf_op jit(solution)/shard_map/ppermute | solution.py:380
  26.8 1.5 %collective-permute-done.6.refs_7_ = bf16[64,512]{1,0:T(8,128)(2,1)S(1)} collective-permute-done((bf16[64,512]{1,0:T(8,128)(2,1)S(1)}, bf16[64,512]{1,0:T(8,128)(2,1)S(1)}, u32[]{:S(2)}, u32[]{:S(2)}) %collective-permute-start.6) | collective-permute-done | bytes 65568 | tf_op jit(solution)/shard_map/ppermute | solution.py:380
  28.4 0.5 %collective-permute-done.5.refs_5_ = bf16[64,512]{1,0:T(8,128)(2,1)S(1)} collective-permute-done((bf16[64,512]{1,0:T(8,128)(2,1)S(1)}, bf16[64,512]{1,0:T(8,128)(2,1)S(1)}, u32[]{:S(2)}, u32[]{:S(2)}) %collective-permute-start.5) | collective-permute-done | bytes 65568 | tf_op jit(solution)/shard_map/ppermute | solution.py:380
  28.9 0.5 %collective-permute-start.9 = (bf16[64,512]{1,0:T(8,128)(2,1)S(1)}, bf16[64,512]{1,0:T(8,128)(2,1)S(1)}, u32[]{:S(2)}, u32[]{:S(2)}) collective-permute-start(bf16[64,512]{1,0:T(8,128)(2,1)S(1)} %collective-permute-done.5.refs_5_), channel_id=1, source_target_pairs={{0,4},{4,0},{8,12},{12,8},{16,20},{20,16},{24,28},{28,24},{1,5},{5... | collective-permute-start | bytes 196616 | tf_op jit(solution)/shard_map/ppermute | solution.py:387
  29.4 0.0 collective-permute-start.10
  29.4 0.7 %collective-permute-done.8.refs_4_ = bf16[64,512]{1,0:T(8,128)(2,1)S(1)} collective-permute-done((bf16[64,512]{1,0:T(8,128)(2,1)S(1)}, bf16[64,512]{1,0:T(8,128)(2,1)S(1)}, u32[]{:S(2)}, u32[]{:S(2)}) %collective-permute-start.8) | collective-permute-done | bytes 65568 | tf_op jit(solution)/shard_map/ppermute | solution.py:387
  30.1 0.2 collective-permute-start.11
  30.3 0.3 collective-permute-done.10.refs_8_
  30.6 0.7 %collective-permute-done.11.refs_10_ = bf16[64,512]{1,0:T(8,128)(2,1)S(1)} collective-permute-done((bf16[64,512]{1,0:T(8,128)(2,1)S(1)}, bf16[64,512]{1,0:T(8,128)(2,1)S(1)}, u32[]{:S(2)}, u32[]{:S(2)}) %collective-permute-start.11) | collective-permute-done | bytes 65568 | tf_op jit(solution)/shard_map/ppermute | solution.py:387
  31.4 0.8 %project.5.refs_7_ = f32[64,512]{1,0:T(8,128)S(1)} custom-call(bf16[32,3200]{1,0:T(8,128)(2,1)S(1)} %collective-permute-done.1.refs_0_, bf16[32,3200]{1,0:T(8,128)(2,1)S(1)} %collective-permute-done.4.refs_1_.refs_2_, f32[2,6144]{1,0:T(2,128)S(1)} %get-tuple-element.81.refs_2_.refs_4_, bf16[6144,256]{1,0:T(8,128)(2,1)S(1)} %get-tuple-element.64.refs_4_.refs_3_.refs_5_, ...), custom_call_target="tpu_custom_call" | custom-call | tf_op jit(solution)/shard_map/project/pallas_call | solution.py:216
  32.2 0.7 %collective-permute-done.12.refs_3_ = bf16[32,3072]{1,0:T(8,128)(2,1)S(1)} collective-permute-done((bf16[32,3072]{1,0:T(8,128)(2,1)S(1)}, bf16[32,3072]{1,0:T(8,128)(2,1)S(1)}, u32[]{:S(2)}, u32[]{:S(2)}) %collective-permute-start.12) | collective-permute-done | bytes 196640 | tf_op jit(solution)/shard_map/ppermute | solution.py:417
  32.9 0.9 %project.6.refs_0_ = bf16[64,512]{1,0:T(8,128)(2,1)S(1)} custom-call(bf16[32,3200]{1,0:T(8,128)(2,1)S(1)} %collective-permute-done.1.refs_0_, bf16[32,3072]{1,0:T(8,128)(2,1)S(1)} %collective-permute-done.3.refs_1_, bf16[32,3200]{1,0:T(8,128)(2,1)S(1)} %collective-permute-done.4.refs_1_.refs_2_, bf16[32,3072]{1,0:T(8,128)(2,1)S(1)} %collective-permute-done.12.refs_3_, ...), custom_call_target="tpu_custom_call" | custom-call | tf_op jit(solution)/shard_map/project/pallas_call | solution.py:216
  33.8 2.5 %collective-permute-start.15 = (bf16[64,512]{1,0:T(8,128)(2,1)S(1)}, bf16[64,512]{1,0:T(8,128)(2,1)S(1)}, u32[]{:S(2)}, u32[]{:S(2)}) collective-permute-start(bf16[64,512]{1,0:T(8,128)(2,1)S(1)} %project.6.refs_0_), channel_id=1, source_target_pairs={{0,24},{4,28},{8,16},{12,20},{16,8},{20,12},{24,0},{28,4},{1,25},{... | collective-permute-start | bytes 196616 | tf_op jit(solution)/shard_map/ppermute | solution.py:380
  36.3 0.5 %collective-permute-start.14 = (bf16[64,512]{1,0:T(8,128)(2,1)S(1)}, bf16[64,512]{1,0:T(8,128)(2,1)S(1)}, u32[]{:S(2)}, u32[]{:S(2)}) collective-permute-start(bf16[64,512]{1,0:T(8,128)(2,1)S(1)} %project.6.refs_0_), channel_id=1, source_target_pairs={{0,16},{4,20},{8,24},{12,28},{16,0},{20,4},{24,8},{28,12},{1,17},{... | collective-permute-start | bytes 196616 | tf_op jit(solution)/shard_map/ppermute | solution.py:380
  36.8 0.5 %collective-permute-start.13 = (bf16[64,512]{1,0:T(8,128)(2,1)S(1)}, bf16[64,512]{1,0:T(8,128)(2,1)S(1)}, u32[]{:S(2)}, u32[]{:S(2)}) collective-permute-start(bf16[64,512]{1,0:T(8,128)(2,1)S(1)} %project.6.refs_0_), channel_id=1, source_target_pairs={{0,8},{4,12},{8,0},{12,4},{16,24},{20,28},{24,16},{28,20},{1,9},{5... | collective-permute-start | bytes 196616 | tf_op jit(solution)/shard_map/ppermute | solution.py:380
  37.3 0.9 %project.7.refs_2_ = bf16[64,256]{1,0:T(8,128)(2,1)S(1)} custom-call(bf16[32,3200]{1,0:T(8,128)(2,1)S(1)} %collective-permute-done.1.refs_0_, bf16[32,3072]{1,0:T(8,128)(2,1)S(1)} %collective-permute-done.3.refs_1_, bf16[32,3200]{1,0:T(8,128)(2,1)S(1)} %collective-permute-done.4.refs_1_.refs_2_, bf16[32,3072]{1,0:T(8,128)(2,1)S(1)} %collective-permute-done.12.refs_3_, ...), custom_call_target="tpu_custom_call" | custom-call | tf_op jit(solution)/shard_map/project/pallas_call | solution.py:216
  38.2 0.5 attend_early.1
  38.7 1.0 %collective-permute-done.15.refs_6_ = bf16[64,512]{1,0:T(8,128)(2,1)S(1)} collective-permute-done((bf16[64,512]{1,0:T(8,128)(2,1)S(1)}, bf16[64,512]{1,0:T(8,128)(2,1)S(1)}, u32[]{:S(2)}, u32[]{:S(2)}) %collective-permute-start.15) | collective-permute-done | bytes 65568 | tf_op jit(solution)/shard_map/ppermute | solution.py:380
  39.7 0.9 %collective-permute-done.14.refs_4_ = bf16[64,512]{1,0:T(8,128)(2,1)S(1)} collective-permute-done((bf16[64,512]{1,0:T(8,128)(2,1)S(1)}, bf16[64,512]{1,0:T(8,128)(2,1)S(1)}, u32[]{:S(2)}, u32[]{:S(2)}) %collective-permute-start.14) | collective-permute-done | bytes 65568 | tf_op jit(solution)/shard_map/ppermute | solution.py:380
  40.6 0.5 %collective-permute-done.13.refs_2_ = bf16[64,512]{1,0:T(8,128)(2,1)S(1)} collective-permute-done((bf16[64,512]{1,0:T(8,128)(2,1)S(1)}, bf16[64,512]{1,0:T(8,128)(2,1)S(1)}, u32[]{:S(2)}, u32[]{:S(2)}) %collective-permute-start.13) | collective-permute-done | bytes 65568 | tf_op jit(solution)/shard_map/ppermute | solution.py:380
  41.1 0.5 %collective-permute-start.18 = (bf16[64,512]{1,0:T(8,128)(2,1)S(1)}, bf16[64,512]{1,0:T(8,128)(2,1)S(1)}, u32[]{:S(2)}, u32[]{:S(2)}) collective-permute-start(bf16[64,512]{1,0:T(8,128)(2,1)S(1)} %collective-permute-done.14.refs_4_), channel_id=1, source_target_pairs={{0,4},{4,0},{8,12},{12,8},{16,20},{20,16},{24,28},{28,24},{1,5},{5... | collective-permute-start | bytes 196616 | tf_op jit(solution)/shard_map/ppermute | solution.py:387
  41.6 0.0 collective-permute-start.19
  41.6 0.7 %collective-permute-done.17.refs_3_ = bf16[64,512]{1,0:T(8,128)(2,1)S(1)} collective-permute-done((bf16[64,512]{1,0:T(8,128)(2,1)S(1)}, bf16[64,512]{1,0:T(8,128)(2,1)S(1)}, u32[]{:S(2)}, u32[]{:S(2)}) %collective-permute-start.17) | collective-permute-done | bytes 65568 | tf_op jit(solution)/shard_map/ppermute | solution.py:387
  42.3 0.2 collective-permute-done.18.refs_5_
  42.5 0.4 collective-permute-done.19.refs_7_
  42.8 0.6 %attend.1 = (bf16[32,256]{1,0:T(8,128)(2,1)S(1)}, bf16[32,256]{1,0:T(8,128)(2,1)S(1)}, bf16[32,256]{1,0:T(8,128)(2,1)S(1)}, bf16[32,256]{1,0:T(8,128)(2,1)S(1)}) custom-call(bf16[128,256]{1,0:T(8,128)(2,1)S(1)} %get-tuple-element.95.q_all, f32[128,256]{1,0:T(8,128)S(1)} %get-tuple-element.96.sums, f32[128,256]{1,0:T(8,128)S(1)} %get-tuple-element.97.bests, ...), custom_call_target="tpu_custom_call" | custom-call | tf_op jit(solution)/shard_map/attend/pallas_call | solution.py:345
  43.5 0.7 %collective-permute-start.20 = (bf16[32,256]{1,0:T(8,128)(2,1)S(1)}, bf16[32,256]{1,0:T(8,128)(2,1)S(1)}, u32[]{:S(2)}, u32[]{:S(2)}) collective-permute-start(bf16[32,256]{1,0:T(8,128)(2,1)S(1)} %get-tuple-element.104), channel_id=1, source_target_pairs={{0,2},{1,3},{2,0},{3,1},{4,6},{5,7},{6,4},{7,5},{8,10},{9,11},{10,... | collective-permute-start | bytes 49160 | tf_op jit(solution)/shard_map/ppermute | solution.py:433
  44.1 1.9 %collective-permute-start.21 = (bf16[32,256]{1,0:T(8,128)(2,1)S(1)}, bf16[32,256]{1,0:T(8,128)(2,1)S(1)}, u32[]{:S(2)}, u32[]{:S(2)}) collective-permute-start(bf16[32,256]{1,0:T(8,128)(2,1)S(1)} %get-tuple-element.105), channel_id=1, source_target_pairs={{0,1},{1,2},{2,3},{3,0},{4,5},{5,6},{6,7},{7,4},{8,9},{9,10},{10,1... | collective-permute-start | bytes 49160 | tf_op jit(solution)/shard_map/ppermute | solution.py:433
  46.0 1.9 %collective-permute-start.22 = (bf16[32,256]{1,0:T(8,128)(2,1)S(1)}, bf16[32,256]{1,0:T(8,128)(2,1)S(1)}, u32[]{:S(2)}, u32[]{:S(2)}) collective-permute-start(bf16[32,256]{1,0:T(8,128)(2,1)S(1)} %get-tuple-element.106), channel_id=1, source_target_pairs={{0,3},{1,0},{2,1},{3,2},{4,7},{5,4},{6,5},{7,6},{8,11},{9,8},{10,9... | collective-permute-start | bytes 49160 | tf_op jit(solution)/shard_map/ppermute | solution.py:433
  48.0 0.2 collective-permute-done.20.refs_1_
  48.2 1.5 %collective-permute-done.21.refs_2_ = bf16[32,256]{1,0:T(8,128)(2,1)S(1)} collective-permute-done((bf16[32,256]{1,0:T(8,128)(2,1)S(1)}, bf16[32,256]{1,0:T(8,128)(2,1)S(1)}, u32[]{:S(2)}, u32[]{:S(2)}) %collective-permute-start.21) | collective-permute-done | bytes 16416 | tf_op jit(solution)/shard_map/ppermute | solution.py:433
  49.7 0.2 collective-permute-done.22.refs_3_
  49.8 0.6 %place.1 = bf16[1,32,1024]{2,1,0:T(8,128)(2,1)} custom-call(s32[1]{0:T(128)} %bitcast.place, bf16[32,256]{1,0:T(8,128)(2,1)S(1)} %get-tuple-element.103.refs_0_, bf16[32,256]{1,0:T(8,128)(2,1)S(1)} %collective-permute-done.20.refs_1_, bf16[32,256]{1,0:T(8,128)(2,1)S(1)} %collective-permute-done.21.refs_2_, bf16[32,256]{1,0:T(8,128)(2,1)S(1)} %collective-permute-done.22.refs_3_), custom_call_target="tpu_custom_call" | custom-call | tf_op jit(solution)/shard_map/place/pallas_call | solution.py:368
  (7 shorter events, 0.0 us)
Async XLA Ops:
  1.2 11.0 %collective-permute-start = (bf16[32,3200]{1,0:T(8,128)(2,1)S(1)}, bf16[32,3200]{1,0:T(8,128)(2,1)S(1)}, u32[]{:S(2)}, u32[]{:S(2)}) collective-permute-start(bf16[32,3200]{1,0:T(8,128)(2,1)S(1)} %get-tuple-element.58.refs_3_), channel_id=1, source_target_pairs={{0,1},{1,2},{2,3},{3,0},{4,5},{5,6},{6,7},{7,4},{8,9},{9,10},{10,1... | collective-permute-start | bytes 614408 | tf_op jit(solution)/shard_map/ppermute | solution.py:405
  4.3 11.3 %collective-permute-start.2 = (bf16[32,3072]{1,0:T(8,128)(2,1)S(1)}, bf16[32,3072]{1,0:T(8,128)(2,1)S(1)}, u32[]{:S(2)}, u32[]{:S(2)}) collective-permute-start(bf16[32,3072]{1,0:T(8,128)(2,1)S(1)} %get-tuple-element.59.refs_4_), channel_id=1, source_target_pairs={{0,1},{1,2},{2,3},{3,0},{4,5},{5,6},{6,7},{7,4},{8,9},{9,10},{10,1... | collective-permute-start | bytes 589832 | tf_op jit(solution)/shard_map/ppermute | solution.py:405
  12.2 8.6 %collective-permute-start.1 = (bf16[32,3200]{1,0:T(8,128)(2,1)S(1)}, bf16[32,3200]{1,0:T(8,128)(2,1)S(1)}, u32[]{:S(2)}, u32[]{:S(2)}) collective-permute-start(bf16[32,3200]{1,0:T(8,128)(2,1)S(1)} %collective-permute-done.refs_0_), channel_id=1, source_target_pairs={{0,1},{1,2},{2,3},{3,0},{4,5},{5,6},{6,7},{7,4},{8,9},{9,10},{10,1... | collective-permute-start | bytes 614408 | tf_op jit(solution)/shard_map/ppermute | solution.py:410
  15.6 9.6 %collective-permute-start.3 = (bf16[32,3072]{1,0:T(8,128)(2,1)S(1)}, bf16[32,3072]{1,0:T(8,128)(2,1)S(1)}, u32[]{:S(2)}, u32[]{:S(2)}) collective-permute-start(bf16[32,3072]{1,0:T(8,128)(2,1)S(1)} %collective-permute-done.2.refs_1_), channel_id=1, source_target_pairs={{0,1},{1,2},{2,3},{3,0},{4,5},{5,6},{6,7},{7,4},{8,9},{9,10},{10,1... | collective-permute-start | bytes 589832 | tf_op jit(solution)/shard_map/ppermute | solution.py:410
  20.9 10.5 %collective-permute-start.4 = (bf16[32,3200]{1,0:T(8,128)(2,1)S(1)}, bf16[32,3200]{1,0:T(8,128)(2,1)S(1)}, u32[]{:S(2)}, u32[]{:S(2)}) collective-permute-start(bf16[32,3200]{1,0:T(8,128)(2,1)S(1)} %collective-permute-done.1.refs_0_), channel_id=1, source_target_pairs={{0,1},{1,2},{2,3},{3,0},{4,5},{5,6},{6,7},{7,4},{8,9},{9,10},{10,1... | collective-permute-start | bytes 614408 | tf_op jit(solution)/shard_map/ppermute | solution.py:417
  21.6 5.2 %collective-permute-start.7 = (bf16[64,512]{1,0:T(8,128)(2,1)S(1)}, bf16[64,512]{1,0:T(8,128)(2,1)S(1)}, u32[]{:S(2)}, u32[]{:S(2)}) collective-permute-start(bf16[64,512]{1,0:T(8,128)(2,1)S(1)} %get-tuple-element.82.refs_3_), channel_id=1, source_target_pairs={{0,24},{4,28},{8,16},{12,20},{16,8},{20,12},{24,0},{28,4},{1,25},{... | collective-permute-start | bytes 196616 | tf_op jit(solution)/shard_map/ppermute | solution.py:380
  24.1 4.3 %collective-permute-start.6 = (bf16[64,512]{1,0:T(8,128)(2,1)S(1)}, bf16[64,512]{1,0:T(8,128)(2,1)S(1)}, u32[]{:S(2)}, u32[]{:S(2)}) collective-permute-start(bf16[64,512]{1,0:T(8,128)(2,1)S(1)} %get-tuple-element.82.refs_3_), channel_id=1, source_target_pairs={{0,16},{4,20},{8,24},{12,28},{16,0},{20,4},{24,8},{28,12},{1,17},{... | collective-permute-start | bytes 196616 | tf_op jit(solution)/shard_map/ppermute | solution.py:380
  24.6 4.3 %collective-permute-start.5 = (bf16[64,512]{1,0:T(8,128)(2,1)S(1)}, bf16[64,512]{1,0:T(8,128)(2,1)S(1)}, u32[]{:S(2)}, u32[]{:S(2)}) collective-permute-start(bf16[64,512]{1,0:T(8,128)(2,1)S(1)} %get-tuple-element.82.refs_3_), channel_id=1, source_target_pairs={{0,8},{4,12},{8,0},{12,4},{16,24},{20,28},{24,16},{28,20},{1,9},{5... | collective-permute-start | bytes 196616 | tf_op jit(solution)/shard_map/ppermute | solution.py:380
  25.2 7.7 %collective-permute-start.12 = (bf16[32,3072]{1,0:T(8,128)(2,1)S(1)}, bf16[32,3072]{1,0:T(8,128)(2,1)S(1)}, u32[]{:S(2)}, u32[]{:S(2)}) collective-permute-start(bf16[32,3072]{1,0:T(8,128)(2,1)S(1)} %collective-permute-done.3.refs_1_), channel_id=1, source_target_pairs={{0,1},{1,2},{2,3},{3,0},{4,5},{5,6},{6,7},{7,4},{8,9},{9,10},{10,1... | collective-permute-start | bytes 589832 | tf_op jit(solution)/shard_map/ppermute | solution.py:417
  28.9 1.3 %collective-permute-start.8 = (bf16[64,512]{1,0:T(8,128)(2,1)S(1)}, bf16[64,512]{1,0:T(8,128)(2,1)S(1)}, u32[]{:S(2)}, u32[]{:S(2)}) collective-permute-start(bf16[64,512]{1,0:T(8,128)(2,1)S(1)} %get-tuple-element.82.refs_3_), channel_id=1, source_target_pairs={{0,4},{4,0},{8,12},{12,8},{16,20},{20,16},{24,28},{28,24},{1,5},{5... | collective-permute-start | bytes 196616 | tf_op jit(solution)/shard_map/ppermute | solution.py:387
  28.9 1.4 %collective-permute-start.9 = (bf16[64,512]{1,0:T(8,128)(2,1)S(1)}, bf16[64,512]{1,0:T(8,128)(2,1)S(1)}, u32[]{:S(2)}, u32[]{:S(2)}) collective-permute-start(bf16[64,512]{1,0:T(8,128)(2,1)S(1)} %collective-permute-done.5.refs_5_), channel_id=1, source_target_pairs={{0,4},{4,0},{8,12},{12,8},{16,20},{20,16},{24,28},{28,24},{1,5},{5... | collective-permute-start | bytes 196616 | tf_op jit(solution)/shard_map/ppermute | solution.py:387
  29.4 1.3 %collective-permute-start.10 = (bf16[64,512]{1,0:T(8,128)(2,1)S(1)}, bf16[64,512]{1,0:T(8,128)(2,1)S(1)}, u32[]{:S(2)}, u32[]{:S(2)}) collective-permute-start(bf16[64,512]{1,0:T(8,128)(2,1)S(1)} %collective-permute-done.6.refs_7_), channel_id=1, source_target_pairs={{0,4},{4,0},{8,12},{12,8},{16,20},{20,16},{24,28},{28,24},{1,5},{5... | collective-permute-start | bytes 196616 | tf_op jit(solution)/shard_map/ppermute | solution.py:387
  30.1 1.3 %collective-permute-start.11 = (bf16[64,512]{1,0:T(8,128)(2,1)S(1)}, bf16[64,512]{1,0:T(8,128)(2,1)S(1)}, u32[]{:S(2)}, u32[]{:S(2)}) collective-permute-start(bf16[64,512]{1,0:T(8,128)(2,1)S(1)} %collective-permute-done.7.refs_9_), channel_id=1, source_target_pairs={{0,4},{4,0},{8,12},{12,8},{16,20},{20,16},{24,28},{28,24},{1,5},{5... | collective-permute-start | bytes 196616 | tf_op jit(solution)/shard_map/ppermute | solution.py:387
  33.8 5.9 %collective-permute-start.15 = (bf16[64,512]{1,0:T(8,128)(2,1)S(1)}, bf16[64,512]{1,0:T(8,128)(2,1)S(1)}, u32[]{:S(2)}, u32[]{:S(2)}) collective-permute-start(bf16[64,512]{1,0:T(8,128)(2,1)S(1)} %project.6.refs_0_), channel_id=1, source_target_pairs={{0,24},{4,28},{8,16},{12,20},{16,8},{20,12},{24,0},{28,4},{1,25},{... | collective-permute-start | bytes 196616 | tf_op jit(solution)/shard_map/ppermute | solution.py:380
  36.3 4.3 %collective-permute-start.14 = (bf16[64,512]{1,0:T(8,128)(2,1)S(1)}, bf16[64,512]{1,0:T(8,128)(2,1)S(1)}, u32[]{:S(2)}, u32[]{:S(2)}) collective-permute-start(bf16[64,512]{1,0:T(8,128)(2,1)S(1)} %project.6.refs_0_), channel_id=1, source_target_pairs={{0,16},{4,20},{8,24},{12,28},{16,0},{20,4},{24,8},{28,12},{1,17},{... | collective-permute-start | bytes 196616 | tf_op jit(solution)/shard_map/ppermute | solution.py:380
  36.8 4.3 %collective-permute-start.13 = (bf16[64,512]{1,0:T(8,128)(2,1)S(1)}, bf16[64,512]{1,0:T(8,128)(2,1)S(1)}, u32[]{:S(2)}, u32[]{:S(2)}) collective-permute-start(bf16[64,512]{1,0:T(8,128)(2,1)S(1)} %project.6.refs_0_), channel_id=1, source_target_pairs={{0,8},{4,12},{8,0},{12,4},{16,24},{20,28},{24,16},{28,20},{1,9},{5... | collective-permute-start | bytes 196616 | tf_op jit(solution)/shard_map/ppermute | solution.py:380
  37.3 4.2 %collective-permute-start.16 = (bf16[64,512]{1,0:T(8,128)(2,1)S(1)}, bf16[64,512]{1,0:T(8,128)(2,1)S(1)}, u32[]{:S(2)}, u32[]{:S(2)}) collective-permute-start(bf16[64,512]{1,0:T(8,128)(2,1)S(1)} %project.6.refs_0_), channel_id=1, source_target_pairs={{0,4},{4,0},{8,12},{12,8},{16,20},{20,16},{24,28},{28,24},{1,5},{5... | collective-permute-start | bytes 196616 | tf_op jit(solution)/shard_map/ppermute | solution.py:387
  41.1 1.3 %collective-permute-start.17 = (bf16[64,512]{1,0:T(8,128)(2,1)S(1)}, bf16[64,512]{1,0:T(8,128)(2,1)S(1)}, u32[]{:S(2)}, u32[]{:S(2)}) collective-permute-start(bf16[64,512]{1,0:T(8,128)(2,1)S(1)} %collective-permute-done.13.refs_2_), channel_id=1, source_target_pairs={{0,4},{4,0},{8,12},{12,8},{16,20},{20,16},{24,28},{28,24},{1,5},{5... | collective-permute-start | bytes 196616 | tf_op jit(solution)/shard_map/ppermute | solution.py:387
  41.1 1.4 %collective-permute-start.18 = (bf16[64,512]{1,0:T(8,128)(2,1)S(1)}, bf16[64,512]{1,0:T(8,128)(2,1)S(1)}, u32[]{:S(2)}, u32[]{:S(2)}) collective-permute-start(bf16[64,512]{1,0:T(8,128)(2,1)S(1)} %collective-permute-done.14.refs_4_), channel_id=1, source_target_pairs={{0,4},{4,0},{8,12},{12,8},{16,20},{20,16},{24,28},{28,24},{1,5},{5... | collective-permute-start | bytes 196616 | tf_op jit(solution)/shard_map/ppermute | solution.py:387
  41.6 1.3 %collective-permute-start.19 = (bf16[64,512]{1,0:T(8,128)(2,1)S(1)}, bf16[64,512]{1,0:T(8,128)(2,1)S(1)}, u32[]{:S(2)}, u32[]{:S(2)}) collective-permute-start(bf16[64,512]{1,0:T(8,128)(2,1)S(1)} %collective-permute-done.15.refs_6_), channel_id=1, source_target_pairs={{0,4},{4,0},{8,12},{12,8},{16,20},{20,16},{24,28},{28,24},{1,5},{5... | collective-permute-start | bytes 196616 | tf_op jit(solution)/shard_map/ppermute | solution.py:387
  43.5 4.7 %collective-permute-start.20 = (bf16[32,256]{1,0:T(8,128)(2,1)S(1)}, bf16[32,256]{1,0:T(8,128)(2,1)S(1)}, u32[]{:S(2)}, u32[]{:S(2)}) collective-permute-start(bf16[32,256]{1,0:T(8,128)(2,1)S(1)} %get-tuple-element.104), channel_id=1, source_target_pairs={{0,2},{1,3},{2,0},{3,1},{4,6},{5,7},{6,4},{7,5},{8,10},{9,11},{10,... | collective-permute-start | bytes 49160 | tf_op jit(solution)/shard_map/ppermute | solution.py:433
  44.1 5.5 %collective-permute-start.21 = (bf16[32,256]{1,0:T(8,128)(2,1)S(1)}, bf16[32,256]{1,0:T(8,128)(2,1)S(1)}, u32[]{:S(2)}, u32[]{:S(2)}) collective-permute-start(bf16[32,256]{1,0:T(8,128)(2,1)S(1)} %get-tuple-element.105), channel_id=1, source_target_pairs={{0,1},{1,2},{2,3},{3,0},{4,5},{5,6},{6,7},{7,4},{8,9},{9,10},{10,1... | collective-permute-start | bytes 49160 | tf_op jit(solution)/shard_map/ppermute | solution.py:433
  46.0 3.8 %collective-permute-start.22 = (bf16[32,256]{1,0:T(8,128)(2,1)S(1)}, bf16[32,256]{1,0:T(8,128)(2,1)S(1)}, u32[]{:S(2)}, u32[]{:S(2)}) collective-permute-start(bf16[32,256]{1,0:T(8,128)(2,1)S(1)} %get-tuple-element.106), channel_id=1, source_target_pairs={{0,3},{1,0},{2,1},{3,2},{4,7},{5,4},{6,5},{7,6},{8,11},{9,8},{10,9... | collective-permute-start | bytes 49160 | tf_op jit(solution)/shard_map/ppermute | solution.py:433

commit v6 on v5

--- a/solution.py
+++ b/solution.py
@@ -10,7 +10,8 @@
 
 HD = 128
 LANES = 128
-EDGES = (0, 1, 2)
+EXTRA = 16
+EDGES = (0, 25, 48)
 CHUNKS = len(EDGES) - 1
 PARTS = 4
 AHEAD = 6
@@ -40,43 +41,47 @@
 
 
 def split_kernel(x_hbm, *refs):
-    outs, (x_ref, sem) = refs[:CHUNKS], refs[CHUNKS:]
-    copy = pltpu.make_async_copy(x_hbm.at[0], x_ref, sem)
-    copy.start()
-    copy.wait()
-    for span, out in zip(spans_of(x_ref.shape[1]), outs):
-        out[:, : span.stop - span.start] = x_ref[:, span]
-    x = x_ref[...].astype(jnp.float32)
-    scale = lax.rsqrt(jnp.mean(x * x, axis=-1, keepdims=True) + 1e-06)
-    high = scale.astype(jnp.bfloat16).astype(jnp.float32)
-    middle = (scale - high).astype(jnp.bfloat16).astype(jnp.float32)
-    lane = lax.broadcasted_iota(jnp.int32, (x.shape[0], LANES), 1)
-    parts = jnp.where(lane == 0, high, jnp.where(lane == 1, middle, scale - high - middle))
-    outs[0][:, outs[0].shape[1] - LANES :] = parts.astype(jnp.bfloat16)
+    outs, sems = refs[:CHUNKS], refs[CHUNKS]
+    copies = [
+        pltpu.make_async_copy(x_hbm.at[0, :, span], out, sems.at[k])
+        for k, (span, out) in enumerate(zip(spans_of(x_hbm.shape[2]), outs))
+    ]
+    for copy in copies:
+        copy.start()
+    for copy in copies:
+        copy.wait()
 
 
 def split(latents):
     _, rows, depth = latents.shape
     widths = [span.stop - span.start for span in spans_of(depth)]
-    widths[0] += LANES
     return pl.pallas_call(
         split_kernel,
         in_specs=[IN_HBM],
         out_specs=[IN_VMEM] * CHUNKS,
         out_shape=[VMEM((rows, width), jnp.bfloat16) for width in widths],
-        scratch_shapes=[pltpu.VMEM((rows, depth), jnp.bfloat16), pltpu.SemaphoreType.DMA],
+        scratch_shapes=[pltpu.SemaphoreType.DMA((CHUNKS,))],
         compiler_params=params(1),
         name="split",
     )(*far(latents))
 
 
-def scale_of(piece):
-    parts = piece[:, piece.shape[1] - LANES :].astype(jnp.float32)
-    return parts[:, 0:1] + (parts[:, 1:2] + parts[:, 2:3])
+def squares(piece):
+    x = piece[...].astype(jnp.float32)
+    return jnp.sum(x * x, axis=-1, keepdims=True)
+
+
+def scale_from(total, depth):
+    return lax.rsqrt(total * (1.0 / depth) + 1e-06)
+
+
+def scale_of(pieces):
+    depth = sum(piece.shape[1] for piece in pieces)
+    return scale_from(sum(squares(piece) for piece in pieces), depth)
 
 
 def modulated(piece, scale, gain, span):
-    x = piece[:, : span.stop - span.start].astype(jnp.float32)
+    x = piece[...].astype(jnp.float32)
     return (x * scale * gain[0:1, span] + gain[1:2, span]).astype(jnp.bfloat16)
 
 
@@ -106,7 +111,7 @@
     for copy in reads:
         copy.wait()
     gain[0:1, :] = 1.0 + gain[0:1, :]
-    scale = scale_of(pieces[0])
+    scale = scale_of(pieces)
     own = jnp.concatenate(
         [modulated(piece, scale, gain, chunk) for piece, chunk in zip(pieces, chunks)], axis=1
     )
@@ -160,69 +165,140 @@
     )(place, steps, *far(segments[None], mod_table, *weights), *near(*pieces))
 
 
-def project_kernel(count, places, kinds, first, last, older, *refs):
-    known = len({0, *places})
-    pieces, refs = refs[: count * known], refs[count * known :]
+def project_kernel(count, kinds, older, *refs):
+    pieces, refs = refs[: count * CHUNKS], refs[count * CHUNKS :]
     gain, weights, refs = refs[0], refs[1 : 1 + len(kinds)], refs[1 + len(kinds) :]
-    if not first:
-        start, refs = refs[0], refs[1:]
     if older:
         before, refs = refs[0], refs[1:]
         refs[-1][:older, :] = before[...]
     width = weights[0].shape[1]
     chunks = spans_of(weights[0].shape[0])
-    scales = [scale_of(pieces[s * known]) for s in range(count)]
+    shards = [pieces[s * CHUNKS : (s + 1) * CHUNKS] for s in range(count)]
+    scales = [scale_of(shard) for shard in shards]
     stacked = [
         jnp.concatenate(
-            [
-                modulated(pieces[s * known + known - len(places) + i], scales[s], gain, chunks[k])
-                for s in range(count)
-            ],
+            [modulated(shard[k], scale, gain, chunk) for shard, scale in zip(shards, scales)],
             axis=0,
         )
-        for i, k in enumerate(places)
-    ]
-    for index, (kind, weight) in enumerate(zip(kinds, weights)):
-        total = None if first else start[:, index * width : (index + 1) * width]
-        for k, place in enumerate(places):
-            part = jnp.dot(
-                stacked[k],
-                weight[chunks[place], :],
-                preferred_element_type=jnp.float32,
-            )
+        for k, chunk in enumerate(chunks)
+    ]
+    for kind, weight in zip(kinds, weights):
+        total = None
+        for rows, chunk in zip(stacked, chunks):
+            part = jnp.dot(rows, weight[chunk, :], preferred_element_type=jnp.float32)
             total = part if total is None else total + part
-        if not last:
-            refs[0][:, index * width : (index + 1) * width] = total
-        elif kind == 0:
+        if kind == 0:
             refs[0][...] = total.astype(jnp.bfloat16)
         else:
             refs[-1][older:, (kind - 1) * width : kind * width] = total.astype(jnp.bfloat16)
 
 
-def project(shard_pieces, places, gain, weights, kinds, start, last, before=None):
-    count = len(shard_pieces)
-    rows = shard_pieces[0][0].shape[0] * count
+def project(shards, gain, weights, kinds, before=None):
+    count = len(shards)
+    rows = shards[0][0].shape[0] * count
     older = 0 if before is None else before.shape[0]
     width = weights[0].shape[1]
-    if last:
-        shapes = [VMEM((rows, width), jnp.bfloat16)] if 0 in kinds else []
-        if 1 in kinds:
-            shapes.append(VMEM((older + rows, 2 * width), jnp.bfloat16))
-    else:
-        shapes = [VMEM((rows, len(kinds) * width), jnp.float32)]
-    pieces = [shard[k] for shard in shard_pieces for k in sorted({0, *places})]
-    extra = [array for array in (start, before) if array is not None]
+    shapes = [VMEM((rows, width), jnp.bfloat16)] if 0 in kinds else []
+    if 1 in kinds:
+        shapes.append(VMEM((older + rows, 2 * width), jnp.bfloat16))
+    pieces = [piece for shard in shards for piece in shard]
+    extra = [] if before is None else [before]
     used = [weights[kind] for kind in kinds]
     return pl.pallas_call(
-        functools.partial(
-            project_kernel, count, tuple(places), tuple(kinds), start is None, last, older
-        ),
+        functools.partial(project_kernel, count, tuple(kinds), older),
         in_specs=[IN_VMEM] * (len(pieces) + 1 + len(used) + len(extra)),
         out_specs=[IN_VMEM] * len(shapes),
         out_shape=shapes,
-        compiler_params=params(1 + count // 2),
+        compiler_params=params(max(1, 2 * count - 2)),
         name="project",
     )(*near(*pieces, gain, *used, *extra))
+
+
+def lead_kernel(*refs):
+    whole, refs = refs[:CHUNKS], refs[CHUNKS:]
+    parts, refs = refs[: CHUNKS - 1], refs[CHUNKS - 1 :]
+    gain, weights, out = refs[0], refs[1:-1], refs[-1]
+    width = weights[0].shape[1]
+    chunks = spans_of(weights[0].shape[0])
+    rows = whole[0].shape[0]
+    scale = scale_of(whole)
+    row = lax.broadcasted_iota(jnp.int32, (EXTRA, 1), 0)
+    stacked = []
+    for k, piece in enumerate(parts):
+        shift = gain[1:2, chunks[k]]
+        high = shift.astype(jnp.bfloat16).astype(jnp.float32)
+        added = jnp.where(row == 0, high, jnp.where(row == 1, shift - high, 0.0))
+        unscaled = piece[...].astype(jnp.float32) * gain[0:1, chunks[k]]
+        stacked.append(
+            jnp.concatenate(
+                [
+                    modulated(whole[k], scale, gain, chunks[k]),
+                    unscaled.astype(jnp.bfloat16),
+                    added.astype(jnp.bfloat16),
+                ],
+                axis=0,
+            )
+        )
+    for index, weight in enumerate(weights):
+        total = sum(
+            jnp.dot(lines, weight[chunk, :], preferred_element_type=jnp.float32)
+            for lines, chunk in zip(stacked, chunks)
+        )
+        out[:, index * width : (index + 1) * width] = total
+    seen = sum(squares(piece) for piece in parts)
+    last = slice(len(weights) * width, len(weights) * width + LANES)
+    out[:rows, last] = jnp.broadcast_to(scale, (rows, LANES))
+    out[rows : 2 * rows, last] = jnp.broadcast_to(seen, (rows, LANES))
+
+
+def lead(whole, parts, gain, weights):
+    rows = whole[0].shape[0]
+    width = weights[0].shape[1]
+    return pl.pallas_call(
+        lead_kernel,
+        in_specs=[IN_VMEM] * (2 * CHUNKS + len(weights)),
+        out_specs=IN_VMEM,
+        out_shape=VMEM((2 * rows + EXTRA, len(weights) * width + LANES), jnp.float32),
+        compiler_params=params(2),
+        name="lead",
+    )(*near(*whole, *parts, gain, *weights))
+
+
+def finish_kernel(whole, piece, gain, *refs):
+    weights, (start, out) = refs[:-2], refs[-2:]
+    width = weights[0].shape[1]
+    depth = weights[0].shape[0]
+    chunk = spans_of(depth)[-1]
+    rows = whole.shape[0]
+    last = len(weights) * width
+    scale = scale_from(start[rows : 2 * rows, last : last + 1] + squares(piece), depth)
+    lines = jnp.concatenate(
+        [
+            modulated(whole, start[:rows, last : last + 1], gain, chunk),
+            modulated(piece, scale, gain, chunk),
+        ],
+        axis=0,
+    )
+    for index, weight in enumerate(weights):
+        cols = slice(index * width, (index + 1) * width)
+        shift = start[2 * rows : 2 * rows + 1, cols] + start[2 * rows + 1 : 2 * rows + 2, cols]
+        total = jnp.dot(lines, weight[chunk, :], preferred_element_type=jnp.float32)
+        out[:rows, cols] = (total[:rows] + start[:rows, cols]).astype(jnp.bfloat16)
+        known = start[rows : 2 * rows, cols] * scale + shift
+        out[rows:, cols] = (total[rows:] + known).astype(jnp.bfloat16)
+
+
+def finish(whole, piece, gain, weights, start):
+    rows = whole.shape[0]
+    width = weights[0].shape[1]
+    return pl.pallas_call(
+        finish_kernel,
+        in_specs=[IN_VMEM] * (4 + len(weights)),
+        out_specs=IN_VMEM,
+        out_shape=VMEM((2 * rows, len(weights) * width), jnp.bfloat16),
+        compiler_params=params(2),
+        name="finish",
+    )(*near(whole, piece, gain, *weights, start))
 
 
 def bias_of(sources, mine, seg_col, seg_row):
@@ -310,8 +386,8 @@
     )(mine, *near(seg_col, seg_row, *queries, *early))
 
 
-def attend_kernel(shards, sources, q_all, sums, bests, totals, bias, *refs):
-    late, outs, kv_all = refs[:sources], refs[sources:-1], refs[-1]
+def attend_kernel(shards, sources, place, q_all, sums, bests, totals, bias, *refs):
+    late, outs, kv_all, held = refs[:sources], refs[sources:-2], refs[-2], refs[-1]
     tokc, width = q_all.shape
     rows = tokc // shards
     heads = width // HD
@@ -332,25 +408,28 @@
             fade = jnp.exp(floor - best)
             scale = 1.0 / (total + old_total[:, 0:1] * fade)
             result = ((summed + old_sum * fade) * scale).astype(jnp.bfloat16)
-            for s in range(span.start // rows, span.stop // rows):
-                outs[s][:, h * HD : (h + 1) * HD] = result[
-                    s * rows - span.start : (s + 1) * rows - span.start
-                ]
-
-
-def attend(shards, state, late):
+            held[span, h * HD : (h + 1) * HD] = result
+    for m, out in enumerate(outs):
+        spot = lax.rem(place[0] - (place[0] ^ m) + shards, shards) * rows
+        out[...] = held[pl.ds(pl.multiple_of(spot, rows), rows), :]
+
+
+def attend(shards, place, state, late):
     sources, many = len(late), late[0].shape[0]
     tokc, width = state[0].shape
     rows = tokc // shards
     return pl.pallas_call(
         functools.partial(attend_kernel, shards, sources),
-        in_specs=[IN_VMEM] * (len(state) + sources),
+        in_specs=[IN_SMEM] + [IN_VMEM] * (len(state) + sources),
         out_specs=[IN_VMEM] * shards,
         out_shape=[VMEM((rows, width), jnp.bfloat16)] * shards,
-        scratch_shapes=[pltpu.VMEM((sources * many, 2 * width), jnp.bfloat16)],
+        scratch_shapes=[
+            pltpu.VMEM((sources * many, 2 * width), jnp.bfloat16),
+            pltpu.VMEM((tokc, width), jnp.bfloat16),
+        ],
         compiler_params=params(3 * (sources * tokc // 1024)),
         name="attend",
-    )(*near(*state, *late))
+    )(place, *near(*state, *late))
 
 
 def place_kernel(order, place, *refs):
@@ -358,7 +437,7 @@
     width = pieces[0].shape[1]
     count = len(pieces)
     for s, piece in zip(order, pieces):
-        column = lax.rem(place[0] + s, count) * width
+        column = (place[0] ^ s) * width
         out[0, :, pl.ds(pl.multiple_of(column, width), width)] = piece[...]
 
 
@@ -408,7 +487,7 @@
     for s in range(1, shards - 2):
         arrived.append(pieces)
         pieces = [lax.ppermute(piece, "dp", ring) for piece in pieces]
-    query, keyval = project(arrived, range(CHUNKS), gain, weights, (0, 1, 2), None, True, keyval)
+    query, keyval = project(arrived, gain, weights, (0, 1, 2), keyval)
     queries.append(query)
     pieces[0], keyval = lax.optimization_barrier((pieces[0], keyval))
     early = across_chips(keyval, groups)
@@ -417,20 +496,20 @@
     moved = [lax.ppermute(piece, "dp", ring) for piece in pieces]
     moved[0], early = lax.optimization_barrier((moved[0], early))
     both = [pieces, moved]
-    start = project(both, range(CHUNKS - 1), gain, weights, (1, 2), None, False)[0]
-    keyval = project(both, [CHUNKS - 1], gain, weights, (1, 2), start, True)[0]
+    start = lead(pieces, moved[:-1], gain, weights[1:])
+    keyval = finish(pieces[-1], moved[-1], gain, weights[1:], start)
     gain, keyval = lax.optimization_barrier((gain, keyval))
     late = across_chips(keyval, groups)
-    query = project(both, range(CHUNKS), gain, weights, (0,), None, True)[0]
+    query = project(both, gain, weights, (0,))[0]
     queries.append(query)
     state = attend_early(mine, seg_col, seg_row, queries, early)
     late[1:], state = lax.optimization_barrier((late[1:], state))
     late = across_cores(late, groups)
-    results = attend(shards, state, late)
+    results = attend(shards, place, state, late)
     landed = [results[0]]
     for s in range(1, shards):
         landed.append(
-            lax.ppermute(results[s], "dp", [(i, (i - s) % shards) for i in range(shards)])
+            lax.ppermute(results[s], "dp", [(i, i ^ s) for i in range(shards)])
         )
     return place_columns(place, landed)
 

time: 50.6 us -> 49.9 us (0.986)
  starting transfers between devices: 20.2 us -> 19 us
  waiting for transfers between devices: 16.7 us -> 17.7 us
  Pallas kernels: 12.9 us -> 12.3 us
    ppermute x3, starting transfers between devices: 4.5 us -> 3.55 us  [per_device(): lax.ppermute(results[s], 'dp', [(i, i ^ s) for i in range(shards)])]
    ppermute x3, waiting for transfers between devices: 1.89 us -> 2.47 us  [per_device(): lax.ppermute(results[s], 'dp', [(i, i ^ s) for i in range(shards)])]
  transfers between devices with their start and end apart: 23 -> 23, of which waited for: 20 -> 19; matrix products, arithmetic and copies ran while one was open for 0% -> 0% of each run, Pallas kernels for 19% -> 19%
where the time goes in v6:
time: 49.9 us; the launch traced here: 49.8 us
  starting transfers between devices  19 us (38%)
  waiting for transfers between devices  17.7 us (35%)
  Pallas kernels  12.3 us (25%)
  between operations  0.72 us (1%)
    ppermute x6, starting transfers between devices, across_chips(): lax.ppermute(block, 'group', [(i, i ^ m) for i in range(groups)])  7.04 us
    ppermute x4, waiting for transfers between devices, per_device(): pieces = [lax.ppermute(piece, 'dp', ring) for piece in pieces]  6.03 us
    ppermute x4, starting transfers between devices, per_device(): pieces = [lax.ppermute(piece, 'dp', ring) for piece in pieces]  5.99 us
    ppermute x6, waiting for transfers between devices, across_chips(): lax.ppermute(block, 'group', [(i, i ^ m) for i in range(groups)])  5.78 us
    pallas_call x1, Pallas kernels, begin(): pl.pallas_call(functools.partial(begin_kernel, shards), in_specs=[IN_SMEM...  5.39 us
    ppermute x3, starting transfers between devices, per_device(): lax.ppermute(results[s], 'dp', [(i, i ^ s) for i in range(shards)])  3.55 us
    ppermute x8, waiting for transfers between devices, across_cores(): lax.ppermute(block, 'group', swap)  3.08 us
    pallas_call x2, Pallas kernels, project(): pl.pallas_call(functools.partial(project_kernel, count, tuple(kinds), old...  2.51 us
  transfers between devices with their start and end apart: 23, of which 19 were waited for; matrix products, arithmetic and copies ran while one was open for 0% of the time, Pallas kernels for 19%

profile of v6, /device:TPU:0, one launch (start us, length us, event | category | flops | bytes accessed | tf_op | source)
XLA Modules:
  0.0 49.8 jit_solution(2238971751529129549)
XLA Ops:
  0.0 1.0 %split.1 = (bf16[32,3200]{1,0:T(8,128)(2,1)S(1)}, bf16[32,2944]{1,0:T(8,128)(2,1)S(1)}) custom-call(bf16[1,32,6144]{2,1,0:T(8,128)(2,1)} %x_hbm), custom_call_target="tpu_custom_call" | custom-call | tf_op jit(solution)/shard_map/split/pallas_call | solution.py:58
  1.0 3.1 %collective-permute-start.3 = (bf16[32,3200]{1,0:T(8,128)(2,1)S(1)}, bf16[32,3200]{1,0:T(8,128)(2,1)S(1)}, u32[]{:S(2)}, u32[]{:S(2)}) collective-permute-start(bf16[32,3200]{1,0:T(8,128)(2,1)S(1)} %get-tuple-element.58.refs_3_), channel_id=1, source_target_pairs={{0,1},{1,2},{2,3},{3,0},{4,5},{5,6},{6,7},{7,4},{8,9},{9,10},{10,1... | collective-permute-start | bytes 614408 | tf_op jit(solution)/shard_map/ppermute | solution.py:484
  4.1 1.6 %collective-permute-start = (bf16[32,2944]{1,0:T(8,128)(2,1)S(1)}, bf16[32,2944]{1,0:T(8,128)(2,1)S(1)}, u32[]{:S(2)}, u32[]{:S(2)}) collective-permute-start(bf16[32,2944]{1,0:T(8,128)(2,1)S(1)} %get-tuple-element.59.refs_4_), channel_id=1, source_target_pairs={{0,1},{1,2},{2,3},{3,0},{4,5},{5,6},{6,7},{7,4},{8,9},{9,10},{10,1... | collective-permute-start | bytes 565256 | tf_op jit(solution)/shard_map/ppermute | solution.py:484
  6.4 5.4 %begin.1 = (bf16[32,256]{1,0:T(8,128)(2,1)S(1)}, bf16[32,512]{1,0:T(8,128)(2,1)S(1)}, bf16[6144,256]{1,0:T(8,128)(2,1)S(1)}, bf16[6144,256]{1,0:T(8,128)(2,1)S(1...) custom-call(s32[1]{0:T(128)} %bitcast.place, ...), custom_call_target="tpu_custom_call" | custom-call | tf_op jit(solution)/shard_map/begin/pallas_call | solution.py:150
  11.7 0.3 collective-permute-done.3.refs_0_
  12.1 1.3 %collective-permute-start.4 = (bf16[32,3200]{1,0:T(8,128)(2,1)S(1)}, bf16[32,3200]{1,0:T(8,128)(2,1)S(1)}, u32[]{:S(2)}, u32[]{:S(2)}) collective-permute-start(bf16[32,3200]{1,0:T(8,128)(2,1)S(1)} %collective-permute-done.3.refs_0_), channel_id=1, source_target_pairs={{0,1},{1,2},{2,3},{3,0},{4,5},{5,6},{6,7},{7,4},{8,9},{9,10},{10,1... | collective-permute-start | bytes 614408 | tf_op jit(solution)/shard_map/ppermute | solution.py:489
  13.4 1.9 %collective-permute-done.refs_1_ = bf16[32,2944]{1,0:T(8,128)(2,1)S(1)} collective-permute-done((bf16[32,2944]{1,0:T(8,128)(2,1)S(1)}, bf16[32,2944]{1,0:T(8,128)(2,1)S(1)}, u32[]{:S(2)}, u32[]{:S(2)}) %collective-permute-start) | collective-permute-done | bytes 188448 | tf_op jit(solution)/shard_map/ppermute | solution.py:484
  15.3 1.6 %project.2 = (bf16[32,256]{1,0:T(8,128)(2,1)S(1)}, bf16[64,512]{1,0:T(8,128)(2,1)S(1)}) custom-call(bf16[32,3200]{1,0:T(8,128)(2,1)S(1)} %collective-permute-done.3.refs_0_, bf16[32,2944]{1,0:T(8,128)(2,1)S(1)} %collective-permute-done.refs_1_, f32[2,6144]{1,0:T(2,128)S(1)} %get-tuple-element.81.refs_2_.refs_3_.gain.refs_4_, ...), custom_call_target="tpu_custom_call" | custom-call | tf_op jit(solution)/shard_map/project/pallas_call | solution.py:207
  16.9 3.8 %collective-permute-done.4.refs_0_ = bf16[32,3200]{1,0:T(8,128)(2,1)S(1)} collective-permute-done((bf16[32,3200]{1,0:T(8,128)(2,1)S(1)}, bf16[32,3200]{1,0:T(8,128)(2,1)S(1)}, u32[]{:S(2)}, u32[]{:S(2)}) %collective-permute-start.4) | collective-permute-done | bytes 204832 | tf_op jit(solution)/shard_map/ppermute | solution.py:489
  20.7 0.7 %collective-permute-start.5 = (bf16[32,3200]{1,0:T(8,128)(2,1)S(1)}, bf16[32,3200]{1,0:T(8,128)(2,1)S(1)}, u32[]{:S(2)}, u32[]{:S(2)}) collective-permute-start(bf16[32,3200]{1,0:T(8,128)(2,1)S(1)} %collective-permute-done.4.refs_0_), channel_id=1, source_target_pairs={{0,1},{1,2},{2,3},{3,0},{4,5},{5,6},{6,7},{7,4},{8,9},{9,10},{10,1... | collective-permute-start | bytes 614408 | tf_op jit(solution)/shard_map/ppermute | solution.py:496
  21.4 2.4 %collective-permute-start.8 = (bf16[64,512]{1,0:T(8,128)(2,1)S(1)}, bf16[64,512]{1,0:T(8,128)(2,1)S(1)}, u32[]{:S(2)}, u32[]{:S(2)}) collective-permute-start(bf16[64,512]{1,0:T(8,128)(2,1)S(1)} %get-tuple-element.82.refs_3_), channel_id=1, source_target_pairs={{0,24},{4,28},{8,16},{12,20},{16,8},{20,12},{24,0},{28,4},{1,25},{... | collective-permute-start | bytes 196616 | tf_op jit(solution)/shard_map/ppermute | solution.py:459
  23.9 0.5 %collective-permute-start.7 = (bf16[64,512]{1,0:T(8,128)(2,1)S(1)}, bf16[64,512]{1,0:T(8,128)(2,1)S(1)}, u32[]{:S(2)}, u32[]{:S(2)}) collective-permute-start(bf16[64,512]{1,0:T(8,128)(2,1)S(1)} %get-tuple-element.82.refs_3_), channel_id=1, source_target_pairs={{0,16},{4,20},{8,24},{12,28},{16,0},{20,4},{24,8},{28,12},{1,17},{... | collective-permute-start | bytes 196616 | tf_op jit(solution)/shard_map/ppermute | solution.py:459
  24.4 0.5 %collective-permute-start.6 = (bf16[64,512]{1,0:T(8,128)(2,1)S(1)}, bf16[64,512]{1,0:T(8,128)(2,1)S(1)}, u32[]{:S(2)}, u32[]{:S(2)}) collective-permute-start(bf16[64,512]{1,0:T(8,128)(2,1)S(1)} %get-tuple-element.82.refs_3_), channel_id=1, source_target_pairs={{0,8},{4,12},{8,0},{12,4},{16,24},{20,28},{24,16},{28,20},{1,9},{5... | collective-permute-start | bytes 196616 | tf_op jit(solution)/shard_map/ppermute | solution.py:459
  24.9 0.5 %collective-permute-start.2 = (bf16[32,2944]{1,0:T(8,128)(2,1)S(1)}, bf16[32,2944]{1,0:T(8,128)(2,1)S(1)}, u32[]{:S(2)}, u32[]{:S(2)}) collective-permute-start(bf16[32,2944]{1,0:T(8,128)(2,1)S(1)} %collective-permute-done.1.refs_1_.whole), channel_id=1, source_target_pairs={{0,1},{1,2},{2,3},{3,0},{4,5},{5,6},{6,7},{7,4},{8,9},{9,10},{10,1... | collective-permute-start | bytes 565256 | tf_op jit(solution)/shard_map/ppermute | solution.py:496
  25.4 1.1 %collective-permute-done.8.refs_9_ = bf16[64,512]{1,0:T(8,128)(2,1)S(1)} collective-permute-done((bf16[64,512]{1,0:T(8,128)(2,1)S(1)}, bf16[64,512]{1,0:T(8,128)(2,1)S(1)}, u32[]{:S(2)}, u32[]{:S(2)}) %collective-permute-start.8) | collective-permute-done | bytes 65568 | tf_op jit(solution)/shard_map/ppermute | solution.py:459
  26.6 1.5 %collective-permute-done.7.refs_7_ = bf16[64,512]{1,0:T(8,128)(2,1)S(1)} collective-permute-done((bf16[64,512]{1,0:T(8,128)(2,1)S(1)}, bf16[64,512]{1,0:T(8,128)(2,1)S(1)}, u32[]{:S(2)}, u32[]{:S(2)}) %collective-permute-start.7) | collective-permute-done | bytes 65568 | tf_op jit(solution)/shard_map/ppermute | solution.py:459
  28.1 0.5 %collective-permute-done.6.refs_5_ = bf16[64,512]{1,0:T(8,128)(2,1)S(1)} collective-permute-done((bf16[64,512]{1,0:T(8,128)(2,1)S(1)}, bf16[64,512]{1,0:T(8,128)(2,1)S(1)}, u32[]{:S(2)}, u32[]{:S(2)}) %collective-permute-start.6) | collective-permute-done | bytes 65568 | tf_op jit(solution)/shard_map/ppermute | solution.py:459
  28.6 0.5 %collective-permute-start.10 = (bf16[64,512]{1,0:T(8,128)(2,1)S(1)}, bf16[64,512]{1,0:T(8,128)(2,1)S(1)}, u32[]{:S(2)}, u32[]{:S(2)}) collective-permute-start(bf16[64,512]{1,0:T(8,128)(2,1)S(1)} %collective-permute-done.6.refs_5_), channel_id=1, source_target_pairs={{0,4},{4,0},{8,12},{12,8},{16,20},{20,16},{24,28},{28,24},{1,5},{5... | collective-permute-start | bytes 196616 | tf_op jit(solution)/shard_map/ppermute | solution.py:466
  29.1 0.0 collective-permute-start.11
  29.1 0.7 %collective-permute-done.9.refs_4_ = bf16[64,512]{1,0:T(8,128)(2,1)S(1)} collective-permute-done((bf16[64,512]{1,0:T(8,128)(2,1)S(1)}, bf16[64,512]{1,0:T(8,128)(2,1)S(1)}, u32[]{:S(2)}, u32[]{:S(2)}) %collective-permute-start.9) | collective-permute-done | bytes 65568 | tf_op jit(solution)/shard_map/ppermute | solution.py:466
  29.9 0.2 collective-permute-start.12
  30.0 0.0 collective-permute-done.10.refs_6_
  30.0 0.3 collective-permute-done.11.refs_8_
  30.4 0.7 %collective-permute-done.12.refs_10_ = bf16[64,512]{1,0:T(8,128)(2,1)S(1)} collective-permute-done((bf16[64,512]{1,0:T(8,128)(2,1)S(1)}, bf16[64,512]{1,0:T(8,128)(2,1)S(1)}, u32[]{:S(2)}, u32[]{:S(2)}) %collective-permute-start.12) | collective-permute-done | bytes 65568 | tf_op jit(solution)/shard_map/ppermute | solution.py:466
  31.1 0.9 %lead.1.refs_2_ = f32[80,640]{1,0:T(8,128)S(1)} custom-call(bf16[32,3200]{1,0:T(8,128)(2,1)S(1)} %collective-permute-done.4.refs_0_, bf16[32,2944]{1,0:T(8,128)(2,1)S(1)} %collective-permute-done.1.refs_1_.whole, bf16[32,3200]{1,0:T(8,128)(2,1)S(1)} %collective-permute-done.5.refs_2_, f32[2,6144]{1,0:T(2,128)S(1)} %get-tuple-element.81.refs_2_.refs_3_.gain.refs_4_, ...), custom_call_target="tpu_custom_call" | custom-call | tf_op jit(solution)/shard_map/lead/pallas_call | solution.py:257
  32.0 0.3 collective-permute-done.2.piece.refs_3_
  32.3 0.8 %finish.1.refs_0_ = bf16[64,512]{1,0:T(8,128)(2,1)S(1)} custom-call(bf16[32,2944]{1,0:T(8,128)(2,1)S(1)} %collective-permute-done.1.refs_1_.whole, bf16[32,2944]{1,0:T(8,128)(2,1)S(1)} %collective-permute-done.2.piece.refs_3_, f32[2,6144]{1,0:T(2,128)S(1)} %get-tuple-element.81.refs_2_.refs_3_.gain.refs_4_, ...), custom_call_target="tpu_custom_call" | custom-call | tf_op jit(solution)/shard_map/finish/pallas_call | solution.py:294
  33.1 2.8 %collective-permute-start.15 = (bf16[64,512]{1,0:T(8,128)(2,1)S(1)}, bf16[64,512]{1,0:T(8,128)(2,1)S(1)}, u32[]{:S(2)}, u32[]{:S(2)}) collective-permute-start(bf16[64,512]{1,0:T(8,128)(2,1)S(1)} %finish.1.refs_0_), channel_id=1, source_target_pairs={{0,24},{4,28},{8,16},{12,20},{16,8},{20,12},{24,0},{28,4},{1,25},{... | collective-permute-start | bytes 196616 | tf_op jit(solution)/shard_map/ppermute | solution.py:459
  35.9 0.5 %collective-permute-start.14 = (bf16[64,512]{1,0:T(8,128)(2,1)S(1)}, bf16[64,512]{1,0:T(8,128)(2,1)S(1)}, u32[]{:S(2)}, u32[]{:S(2)}) collective-permute-start(bf16[64,512]{1,0:T(8,128)(2,1)S(1)} %finish.1.refs_0_), channel_id=1, source_target_pairs={{0,16},{4,20},{8,24},{12,28},{16,0},{20,4},{24,8},{28,12},{1,17},{... | collective-permute-start | bytes 196616 | tf_op jit(solution)/shard_map/ppermute | solution.py:459
  36.4 0.2 collective-permute-start.13
  36.7 0.9 %project.3.refs_2_ = bf16[64,256]{1,0:T(8,128)(2,1)S(1)} custom-call(bf16[32,3200]{1,0:T(8,128)(2,1)S(1)} %collective-permute-done.4.refs_0_, bf16[32,2944]{1,0:T(8,128)(2,1)S(1)} %collective-permute-done.1.refs_1_.whole, bf16[32,3200]{1,0:T(8,128)(2,1)S(1)} %collective-permute-done.5.refs_2_, bf16[32,2944]{1,0:T(8,128)(2,1)S(1)} %collective-permute-done.2.piece.refs_3_, ...), custom_call_target="tpu_custom_call" | custom-call | tf_op jit(solution)/shard_map/project/pallas_call | solution.py:207
  37.6 0.5 %attend_early.1 = (bf16[128,256]{1,0:T(8,128)(2,1)S(1)}, f32[128,256]{1,0:T(8,128)S(1)}, f32[128,256]{1,0:T(8,128)S(1)}, f32[128,256]{1,0:T(8,128)S(1)}, f32[128,512]{1,0:T(8,128)S(1)}) custom-call(s32[1]{0:T(128)} %bitcast.1.mine, s32[128,1]{1,0:T(8,128)S(1)} %get-tuple-element.77.seg_col, s32[1,128]{1,0:T(1,128)S(1)} %get-tuple-element.78.seg_row, ...), custom_call_target="tpu_custom_call" | custom-call | tf_op jit(solution)/shard_map/attend_early/pallas_call | solution.py:376
  38.1 0.7 %collective-permute-done.15.refs_6_ = bf16[64,512]{1,0:T(8,128)(2,1)S(1)} collective-permute-done((bf16[64,512]{1,0:T(8,128)(2,1)S(1)}, bf16[64,512]{1,0:T(8,128)(2,1)S(1)}, u32[]{:S(2)}, u32[]{:S(2)}) %collective-permute-start.15) | collective-permute-done | bytes 65568 | tf_op jit(solution)/shard_map/ppermute | solution.py:459
  38.8 1.4 %collective-permute-done.14.refs_4_ = bf16[64,512]{1,0:T(8,128)(2,1)S(1)} collective-permute-done((bf16[64,512]{1,0:T(8,128)(2,1)S(1)}, bf16[64,512]{1,0:T(8,128)(2,1)S(1)}, u32[]{:S(2)}, u32[]{:S(2)}) %collective-permute-start.14) | collective-permute-done | bytes 65568 | tf_op jit(solution)/shard_map/ppermute | solution.py:459
  40.2 0.5 %collective-permute-done.13.refs_2_ = bf16[64,512]{1,0:T(8,128)(2,1)S(1)} collective-permute-done((bf16[64,512]{1,0:T(8,128)(2,1)S(1)}, bf16[64,512]{1,0:T(8,128)(2,1)S(1)}, u32[]{:S(2)}, u32[]{:S(2)}) %collective-permute-start.13) | collective-permute-done | bytes 65568 | tf_op jit(solution)/shard_map/ppermute | solution.py:459
  40.7 0.5 %collective-permute-start.18 = (bf16[64,512]{1,0:T(8,128)(2,1)S(1)}, bf16[64,512]{1,0:T(8,128)(2,1)S(1)}, u32[]{:S(2)}, u32[]{:S(2)}) collective-permute-start(bf16[64,512]{1,0:T(8,128)(2,1)S(1)} %collective-permute-done.14.refs_4_), channel_id=1, source_target_pairs={{0,4},{4,0},{8,12},{12,8},{16,20},{20,16},{24,28},{28,24},{1,5},{5... | collective-permute-start | bytes 196616 | tf_op jit(solution)/shard_map/ppermute | solution.py:466
  41.2 0.0 collective-permute-start.19
  41.2 0.7 %collective-permute-done.17.refs_3_ = bf16[64,512]{1,0:T(8,128)(2,1)S(1)} collective-permute-done((bf16[64,512]{1,0:T(8,128)(2,1)S(1)}, bf16[64,512]{1,0:T(8,128)(2,1)S(1)}, u32[]{:S(2)}, u32[]{:S(2)}) %collective-permute-start.17) | collective-permute-done | bytes 65568 | tf_op jit(solution)/shard_map/ppermute | solution.py:466
  42.0 0.2 collective-permute-done.18.refs_5_
  42.1 0.4 collective-permute-done.19.refs_7_
  42.5 0.6 %attend.1 = (bf16[32,256]{1,0:T(8,128)(2,1)S(1)}, bf16[32,256]{1,0:T(8,128)(2,1)S(1)}, bf16[32,256]{1,0:T(8,128)(2,1)S(1)}, bf16[32,256]{1,0:T(8,128)(2,1)S(1)}) custom-call(s32[1]{0:T(128)} %bitcast.place, bf16[128,256]{1,0:T(8,128)(2,1)S(1)} %get-tuple-element.95.q_all, f32[128,256]{1,0:T(8,128)S(1)} %get-tuple-element.96.sums, ...), custom_call_target="tpu_custom_call" | custom-call | tf_op jit(solution)/shard_map/attend/pallas_call | solution.py:421
  43.1 0.3 collective-permute-start.20
  43.4 2.0 %collective-permute-start.21 = (bf16[32,256]{1,0:T(8,128)(2,1)S(1)}, bf16[32,256]{1,0:T(8,128)(2,1)S(1)}, u32[]{:S(2)}, u32[]{:S(2)}) collective-permute-start(bf16[32,256]{1,0:T(8,128)(2,1)S(1)} %get-tuple-element.105), channel_id=1, source_target_pairs={{0,3},{1,2},{2,1},{3,0},{4,7},{5,6},{6,5},{7,4},{8,11},{9,10},{10,... | collective-permute-start | bytes 49160 | tf_op jit(solution)/shard_map/ppermute | solution.py:512
  45.4 1.3 %collective-permute-start.22 = (bf16[32,256]{1,0:T(8,128)(2,1)S(1)}, bf16[32,256]{1,0:T(8,128)(2,1)S(1)}, u32[]{:S(2)}, u32[]{:S(2)}) collective-permute-start(bf16[32,256]{1,0:T(8,128)(2,1)S(1)} %get-tuple-element.106), channel_id=1, source_target_pairs={{0,1},{1,0},{2,3},{3,2},{4,5},{5,4},{6,7},{7,6},{8,9},{9,8},{10,11... | collective-permute-start | bytes 49160 | tf_op jit(solution)/shard_map/ppermute | solution.py:512
  46.6 1.2 %collective-permute-done.20.refs_1_ = bf16[32,256]{1,0:T(8,128)(2,1)S(1)} collective-permute-done((bf16[32,256]{1,0:T(8,128)(2,1)S(1)}, bf16[32,256]{1,0:T(8,128)(2,1)S(1)}, u32[]{:S(2)}, u32[]{:S(2)}) %collective-permute-start.20) | collective-permute-done | bytes 16416 | tf_op jit(solution)/shard_map/ppermute | solution.py:512
  47.8 1.1 %collective-permute-done.21.refs_2_ = bf16[32,256]{1,0:T(8,128)(2,1)S(1)} collective-permute-done((bf16[32,256]{1,0:T(8,128)(2,1)S(1)}, bf16[32,256]{1,0:T(8,128)(2,1)S(1)}, u32[]{:S(2)}, u32[]{:S(2)}) %collective-permute-start.21) | collective-permute-done | bytes 16416 | tf_op jit(solution)/shard_map/ppermute | solution.py:512
  48.9 0.2 collective-permute-done.22.refs_3_
  49.1 0.6 %place.1 = bf16[1,32,1024]{2,1,0:T(8,128)(2,1)} custom-call(s32[1]{0:T(128)} %bitcast.place, bf16[32,256]{1,0:T(8,128)(2,1)S(1)} %get-tuple-element.103.refs_0_, bf16[32,256]{1,0:T(8,128)(2,1)S(1)} %collective-permute-done.20.refs_1_, bf16[32,256]{1,0:T(8,128)(2,1)S(1)} %collective-permute-done.21.refs_2_, bf16[32,256]{1,0:T(8,128)(2,1)S(1)} %collective-permute-done.22.refs_3_), custom_call_target="tpu_custom_call" | custom-call | tf_op jit(solution)/shard_map/place/pallas_call | solution.py:447
  (7 shorter events, 0.0 us)
Async XLA Ops:
  1.0 11.0 %collective-permute-start.3 = (bf16[32,3200]{1,0:T(8,128)(2,1)S(1)}, bf16[32,3200]{1,0:T(8,128)(2,1)S(1)}, u32[]{:S(2)}, u32[]{:S(2)}) collective-permute-start(bf16[32,3200]{1,0:T(8,128)(2,1)S(1)} %get-tuple-element.58.refs_3_), channel_id=1, source_target_pairs={{0,1},{1,2},{2,3},{3,0},{4,5},{5,6},{6,7},{7,4},{8,9},{9,10},{10,1... | collective-permute-start | bytes 614408 | tf_op jit(solution)/shard_map/ppermute | solution.py:484
  4.1 11.1 %collective-permute-start = (bf16[32,2944]{1,0:T(8,128)(2,1)S(1)}, bf16[32,2944]{1,0:T(8,128)(2,1)S(1)}, u32[]{:S(2)}, u32[]{:S(2)}) collective-permute-start(bf16[32,2944]{1,0:T(8,128)(2,1)S(1)} %get-tuple-element.59.refs_4_), channel_id=1, source_target_pairs={{0,1},{1,2},{2,3},{3,0},{4,5},{5,6},{6,7},{7,4},{8,9},{9,10},{10,1... | collective-permute-start | bytes 565256 | tf_op jit(solution)/shard_map/ppermute | solution.py:484
  12.1 8.7 %collective-permute-start.4 = (bf16[32,3200]{1,0:T(8,128)(2,1)S(1)}, bf16[32,3200]{1,0:T(8,128)(2,1)S(1)}, u32[]{:S(2)}, u32[]{:S(2)}) collective-permute-start(bf16[32,3200]{1,0:T(8,128)(2,1)S(1)} %collective-permute-done.3.refs_0_), channel_id=1, source_target_pairs={{0,1},{1,2},{2,3},{3,0},{4,5},{5,6},{6,7},{7,4},{8,9},{9,10},{10,1... | collective-permute-start | bytes 614408 | tf_op jit(solution)/shard_map/ppermute | solution.py:489
  15.3 9.6 %collective-permute-start.1 = (bf16[32,2944]{1,0:T(8,128)(2,1)S(1)}, bf16[32,2944]{1,0:T(8,128)(2,1)S(1)}, u32[]{:S(2)}, u32[]{:S(2)}) collective-permute-start(bf16[32,2944]{1,0:T(8,128)(2,1)S(1)} %collective-permute-done.refs_1_), channel_id=1, source_target_pairs={{0,1},{1,2},{2,3},{3,0},{4,5},{5,6},{6,7},{7,4},{8,9},{9,10},{10,1... | collective-permute-start | bytes 565256 | tf_op jit(solution)/shard_map/ppermute | solution.py:489
  20.7 10.4 %collective-permute-start.5 = (bf16[32,3200]{1,0:T(8,128)(2,1)S(1)}, bf16[32,3200]{1,0:T(8,128)(2,1)S(1)}, u32[]{:S(2)}, u32[]{:S(2)}) collective-permute-start(bf16[32,3200]{1,0:T(8,128)(2,1)S(1)} %collective-permute-done.4.refs_0_), channel_id=1, source_target_pairs={{0,1},{1,2},{2,3},{3,0},{4,5},{5,6},{6,7},{7,4},{8,9},{9,10},{10,1... | collective-permute-start | bytes 614408 | tf_op jit(solution)/shard_map/ppermute | solution.py:496
  21.4 5.2 %collective-permute-start.8 = (bf16[64,512]{1,0:T(8,128)(2,1)S(1)}, bf16[64,512]{1,0:T(8,128)(2,1)S(1)}, u32[]{:S(2)}, u32[]{:S(2)}) collective-permute-start(bf16[64,512]{1,0:T(8,128)(2,1)S(1)} %get-tuple-element.82.refs_3_), channel_id=1, source_target_pairs={{0,24},{4,28},{8,16},{12,20},{16,8},{20,12},{24,0},{28,4},{1,25},{... | collective-permute-start | bytes 196616 | tf_op jit(solution)/shard_map/ppermute | solution.py:459
  23.9 4.3 %collective-permute-start.7 = (bf16[64,512]{1,0:T(8,128)(2,1)S(1)}, bf16[64,512]{1,0:T(8,128)(2,1)S(1)}, u32[]{:S(2)}, u32[]{:S(2)}) collective-permute-start(bf16[64,512]{1,0:T(8,128)(2,1)S(1)} %get-tuple-element.82.refs_3_), channel_id=1, source_target_pairs={{0,16},{4,20},{8,24},{12,28},{16,0},{20,4},{24,8},{28,12},{1,17},{... | collective-permute-start | bytes 196616 | tf_op jit(solution)/shard_map/ppermute | solution.py:459
  24.4 4.3 %collective-permute-start.6 = (bf16[64,512]{1,0:T(8,128)(2,1)S(1)}, bf16[64,512]{1,0:T(8,128)(2,1)S(1)}, u32[]{:S(2)}, u32[]{:S(2)}) collective-permute-start(bf16[64,512]{1,0:T(8,128)(2,1)S(1)} %get-tuple-element.82.refs_3_), channel_id=1, source_target_pairs={{0,8},{4,12},{8,0},{12,4},{16,24},{20,28},{24,16},{28,20},{1,9},{5... | collective-permute-start | bytes 196616 | tf_op jit(solution)/shard_map/ppermute | solution.py:459
  24.9 7.4 %collective-permute-start.2 = (bf16[32,2944]{1,0:T(8,128)(2,1)S(1)}, bf16[32,2944]{1,0:T(8,128)(2,1)S(1)}, u32[]{:S(2)}, u32[]{:S(2)}) collective-permute-start(bf16[32,2944]{1,0:T(8,128)(2,1)S(1)} %collective-permute-done.1.refs_1_.whole), channel_id=1, source_target_pairs={{0,1},{1,2},{2,3},{3,0},{4,5},{5,6},{6,7},{7,4},{8,9},{9,10},{10,1... | collective-permute-start | bytes 565256 | tf_op jit(solution)/shard_map/ppermute | solution.py:496
  28.6 1.3 %collective-permute-start.9 = (bf16[64,512]{1,0:T(8,128)(2,1)S(1)}, bf16[64,512]{1,0:T(8,128)(2,1)S(1)}, u32[]{:S(2)}, u32[]{:S(2)}) collective-permute-start(bf16[64,512]{1,0:T(8,128)(2,1)S(1)} %get-tuple-element.82.refs_3_), channel_id=1, source_target_pairs={{0,4},{4,0},{8,12},{12,8},{16,20},{20,16},{24,28},{28,24},{1,5},{5... | collective-permute-start | bytes 196616 | tf_op jit(solution)/shard_map/ppermute | solution.py:466
  28.6 1.4 %collective-permute-start.10 = (bf16[64,512]{1,0:T(8,128)(2,1)S(1)}, bf16[64,512]{1,0:T(8,128)(2,1)S(1)}, u32[]{:S(2)}, u32[]{:S(2)}) collective-permute-start(bf16[64,512]{1,0:T(8,128)(2,1)S(1)} %collective-permute-done.6.refs_5_), channel_id=1, source_target_pairs={{0,4},{4,0},{8,12},{12,8},{16,20},{20,16},{24,28},{28,24},{1,5},{5... | collective-permute-start | bytes 196616 | tf_op jit(solution)/shard_map/ppermute | solution.py:466
  29.1 1.3 %collective-permute-start.11 = (bf16[64,512]{1,0:T(8,128)(2,1)S(1)}, bf16[64,512]{1,0:T(8,128)(2,1)S(1)}, u32[]{:S(2)}, u32[]{:S(2)}) collective-permute-start(bf16[64,512]{1,0:T(8,128)(2,1)S(1)} %collective-permute-done.7.refs_7_), channel_id=1, source_target_pairs={{0,4},{4,0},{8,12},{12,8},{16,20},{20,16},{24,28},{28,24},{1,5},{5... | collective-permute-start | bytes 196616 | tf_op jit(solution)/shard_map/ppermute | solution.py:466
  29.9 1.3 %collective-permute-start.12 = (bf16[64,512]{1,0:T(8,128)(2,1)S(1)}, bf16[64,512]{1,0:T(8,128)(2,1)S(1)}, u32[]{:S(2)}, u32[]{:S(2)}) collective-permute-start(bf16[64,512]{1,0:T(8,128)(2,1)S(1)} %collective-permute-done.8.refs_9_), channel_id=1, source_target_pairs={{0,4},{4,0},{8,12},{12,8},{16,20},{20,16},{24,28},{28,24},{1,5},{5... | collective-permute-start | bytes 196616 | tf_op jit(solution)/shard_map/ppermute | solution.py:466
  33.1 5.7 %collective-permute-start.15 = (bf16[64,512]{1,0:T(8,128)(2,1)S(1)}, bf16[64,512]{1,0:T(8,128)(2,1)S(1)}, u32[]{:S(2)}, u32[]{:S(2)}) collective-permute-start(bf16[64,512]{1,0:T(8,128)(2,1)S(1)} %finish.1.refs_0_), channel_id=1, source_target_pairs={{0,24},{4,28},{8,16},{12,20},{16,8},{20,12},{24,0},{28,4},{1,25},{... | collective-permute-start | bytes 196616 | tf_op jit(solution)/shard_map/ppermute | solution.py:459
  35.9 4.3 %collective-permute-start.14 = (bf16[64,512]{1,0:T(8,128)(2,1)S(1)}, bf16[64,512]{1,0:T(8,128)(2,1)S(1)}, u32[]{:S(2)}, u32[]{:S(2)}) collective-permute-start(bf16[64,512]{1,0:T(8,128)(2,1)S(1)} %finish.1.refs_0_), channel_id=1, source_target_pairs={{0,16},{4,20},{8,24},{12,28},{16,0},{20,4},{24,8},{28,12},{1,17},{... | collective-permute-start | bytes 196616 | tf_op jit(solution)/shard_map/ppermute | solution.py:459
  36.4 4.3 %collective-permute-start.13 = (bf16[64,512]{1,0:T(8,128)(2,1)S(1)}, bf16[64,512]{1,0:T(8,128)(2,1)S(1)}, u32[]{:S(2)}, u32[]{:S(2)}) collective-permute-start(bf16[64,512]{1,0:T(8,128)(2,1)S(1)} %finish.1.refs_0_), channel_id=1, source_target_pairs={{0,8},{4,12},{8,0},{12,4},{16,24},{20,28},{24,16},{28,20},{1,9},{5... | collective-permute-start | bytes 196616 | tf_op jit(solution)/shard_map/ppermute | solution.py:459
  36.7 4.5 %collective-permute-start.16 = (bf16[64,512]{1,0:T(8,128)(2,1)S(1)}, bf16[64,512]{1,0:T(8,128)(2,1)S(1)}, u32[]{:S(2)}, u32[]{:S(2)}) collective-permute-start(bf16[64,512]{1,0:T(8,128)(2,1)S(1)} %finish.1.refs_0_), channel_id=1, source_target_pairs={{0,4},{4,0},{8,12},{12,8},{16,20},{20,16},{24,28},{28,24},{1,5},{5... | collective-permute-start | bytes 196616 | tf_op jit(solution)/shard_map/ppermute | solution.py:466
  40.7 1.3 %collective-permute-start.17 = (bf16[64,512]{1,0:T(8,128)(2,1)S(1)}, bf16[64,512]{1,0:T(8,128)(2,1)S(1)}, u32[]{:S(2)}, u32[]{:S(2)}) collective-permute-start(bf16[64,512]{1,0:T(8,128)(2,1)S(1)} %collective-permute-done.13.refs_2_), channel_id=1, source_target_pairs={{0,4},{4,0},{8,12},{12,8},{16,20},{20,16},{24,28},{28,24},{1,5},{5... | collective-permute-start | bytes 196616 | tf_op jit(solution)/shard_map/ppermute | solution.py:466
  40.7 1.4 %collective-permute-start.18 = (bf16[64,512]{1,0:T(8,128)(2,1)S(1)}, bf16[64,512]{1,0:T(8,128)(2,1)S(1)}, u32[]{:S(2)}, u32[]{:S(2)}) collective-permute-start(bf16[64,512]{1,0:T(8,128)(2,1)S(1)} %collective-permute-done.14.refs_4_), channel_id=1, source_target_pairs={{0,4},{4,0},{8,12},{12,8},{16,20},{20,16},{24,28},{28,24},{1,5},{5... | collective-permute-start | bytes 196616 | tf_op jit(solution)/shard_map/ppermute | solution.py:466
  41.2 1.3 %collective-permute-start.19 = (bf16[64,512]{1,0:T(8,128)(2,1)S(1)}, bf16[64,512]{1,0:T(8,128)(2,1)S(1)}, u32[]{:S(2)}, u32[]{:S(2)}) collective-permute-start(bf16[64,512]{1,0:T(8,128)(2,1)S(1)} %collective-permute-done.15.refs_6_), channel_id=1, source_target_pairs={{0,4},{4,0},{8,12},{12,8},{16,20},{20,16},{24,28},{28,24},{1,5},{5... | collective-permute-start | bytes 196616 | tf_op jit(solution)/shard_map/ppermute | solution.py:466
  43.1 4.7 %collective-permute-start.20 = (bf16[32,256]{1,0:T(8,128)(2,1)S(1)}, bf16[32,256]{1,0:T(8,128)(2,1)S(1)}, u32[]{:S(2)}, u32[]{:S(2)}) collective-permute-start(bf16[32,256]{1,0:T(8,128)(2,1)S(1)} %get-tuple-element.104), channel_id=1, source_target_pairs={{0,2},{1,3},{2,0},{3,1},{4,6},{5,7},{6,4},{7,5},{8,10},{9,11},{10,... | collective-permute-start | bytes 49160 | tf_op jit(solution)/shard_map/ppermute | solution.py:512
  43.4 5.5 %collective-permute-start.21 = (bf16[32,256]{1,0:T(8,128)(2,1)S(1)}, bf16[32,256]{1,0:T(8,128)(2,1)S(1)}, u32[]{:S(2)}, u32[]{:S(2)}) collective-permute-start(bf16[32,256]{1,0:T(8,128)(2,1)S(1)} %get-tuple-element.105), channel_id=1, source_target_pairs={{0,3},{1,2},{2,1},{3,0},{4,7},{5,6},{6,5},{7,4},{8,11},{9,10},{10,... | collective-permute-start | bytes 49160 | tf_op jit(solution)/shard_map/ppermute | solution.py:512
  45.4 3.7 %collective-permute-start.22 = (bf16[32,256]{1,0:T(8,128)(2,1)S(1)}, bf16[32,256]{1,0:T(8,128)(2,1)S(1)}, u32[]{:S(2)}, u32[]{:S(2)}) collective-permute-start(bf16[32,256]{1,0:T(8,128)(2,1)S(1)} %get-tuple-element.106), channel_id=1, source_target_pairs={{0,1},{1,0},{2,3},{3,2},{4,5},{5,4},{6,7},{7,6},{8,9},{9,8},{10,11... | collective-permute-start | bytes 49160 | tf_op jit(solution)/shard_map/ppermute | solution.py:512

commit v7 on v6

--- a/solution.py
+++ b/solution.py
@@ -503,7 +503,7 @@
     query = project(both, gain, weights, (0,))[0]
     queries.append(query)
     state = attend_early(mine, seg_col, seg_row, queries, early)
-    late[1:], state = lax.optimization_barrier((late[1:], state))
+    late[1:] = [lax.optimization_barrier((block, state[0]))[0] for block in late[1:]]
     late = across_cores(late, groups)
     results = attend(shards, place, state, late)
     landed = [results[0]]

time: 49.9 us -> 49.5 us (level)
  starting transfers between devices: 19 us -> 18.5 us
  transfers between devices with their start and end apart: 23 -> 23, of which waited for: 19 -> 18; matrix products, arithmetic and copies ran while one was open for 0% -> 0% of each run, Pallas kernels for 19% -> 19%
where the time goes in v7:
time: 49.5 us; the launch traced here: 49.3 us
  starting transfers between devices  18.5 us (37%)
  waiting for transfers between devices  17.8 us (36%)
  Pallas kernels  12.3 us (25%)
  between operations  0.72 us (1%)
    ppermute x6, starting transfers between devices, across_chips(): lax.ppermute(block, 'group', [(i, i ^ m) for i in range(groups)])  7.04 us
    ppermute x4, waiting for transfers between devices, per_device(): pieces = [lax.ppermute(piece, 'dp', ring) for piece in pieces]  6.03 us
    ppermute x4, starting transfers between devices, per_device(): pieces = [lax.ppermute(piece, 'dp', ring) for piece in pieces]  5.99 us
    ppermute x6, waiting for transfers between devices, across_chips(): lax.ppermute(block, 'group', [(i, i ^ m) for i in range(groups)])  5.78 us
    pallas_call x1, Pallas kernels, begin(): pl.pallas_call(functools.partial(begin_kernel, shards), in_specs=[IN_SMEM...  5.39 us
    ppermute x3, starting transfers between devices, per_device(): lax.ppermute(results[s], 'dp', [(i, i ^ s) for i in range(shards)])  3.55 us
    ppermute x8, waiting for transfers between devices, across_cores(): lax.ppermute(block, 'group', swap)  3.08 us
    ppermute x3, waiting for transfers between devices, per_device(): lax.ppermute(results[s], 'dp', [(i, i ^ s) for i in range(shards)])  2.57 us
  transfers between devices with their start and end apart: 23, of which 18 were waited for; matrix products, arithmetic and copies ran while one was open for 0% of the time, Pallas kernels for 19%

profile of v7, /device:TPU:0, one launch (start us, length us, event | category | flops | bytes accessed | tf_op | source)
XLA Modules:
  0.0 49.3 jit_solution(9518317471162344265)
XLA Ops:
  0.0 1.0 %split.1 = (bf16[32,3200]{1,0:T(8,128)(2,1)S(1)}, bf16[32,2944]{1,0:T(8,128)(2,1)S(1)}) custom-call(bf16[1,32,6144]{2,1,0:T(8,128)(2,1)} %x_hbm), custom_call_target="tpu_custom_call" | custom-call | tf_op jit(solution)/shard_map/split/pallas_call | solution.py:58
  1.0 3.1 %collective-permute-start = (bf16[32,3200]{1,0:T(8,128)(2,1)S(1)}, bf16[32,3200]{1,0:T(8,128)(2,1)S(1)}, u32[]{:S(2)}, u32[]{:S(2)}) collective-permute-start(bf16[32,3200]{1,0:T(8,128)(2,1)S(1)} %get-tuple-element.54.refs_3_), channel_id=1, source_target_pairs={{0,1},{1,2},{2,3},{3,0},{4,5},{5,6},{6,7},{7,4},{8,9},{9,10},{10,1... | collective-permute-start | bytes 614408 | tf_op jit(solution)/shard_map/ppermute | solution.py:484
  4.1 1.6 %collective-permute-start.1 = (bf16[32,2944]{1,0:T(8,128)(2,1)S(1)}, bf16[32,2944]{1,0:T(8,128)(2,1)S(1)}, u32[]{:S(2)}, u32[]{:S(2)}) collective-permute-start(bf16[32,2944]{1,0:T(8,128)(2,1)S(1)} %get-tuple-element.55.refs_4_), channel_id=1, source_target_pairs={{0,1},{1,2},{2,3},{3,0},{4,5},{5,6},{6,7},{7,4},{8,9},{9,10},{10,1... | collective-permute-start | bytes 565256 | tf_op jit(solution)/shard_map/ppermute | solution.py:484
  6.4 5.4 %begin.1 = (bf16[32,256]{1,0:T(8,128)(2,1)S(1)}, bf16[32,512]{1,0:T(8,128)(2,1)S(1)}, bf16[6144,256]{1,0:T(8,128)(2,1)S(1)}, bf16[6144,256]{1,0:T(8,128)(2,1)S(1...) custom-call(s32[1]{0:T(128)} %bitcast.place, ...), custom_call_target="tpu_custom_call" | custom-call | tf_op jit(solution)/shard_map/begin/pallas_call | solution.py:150
  11.7 0.3 collective-permute-done.refs_0_
  12.1 1.3 %collective-permute-start.2 = (bf16[32,3200]{1,0:T(8,128)(2,1)S(1)}, bf16[32,3200]{1,0:T(8,128)(2,1)S(1)}, u32[]{:S(2)}, u32[]{:S(2)}) collective-permute-start(bf16[32,3200]{1,0:T(8,128)(2,1)S(1)} %collective-permute-done.refs_0_), channel_id=1, source_target_pairs={{0,1},{1,2},{2,3},{3,0},{4,5},{5,6},{6,7},{7,4},{8,9},{9,10},{10,1... | collective-permute-start | bytes 614408 | tf_op jit(solution)/shard_map/ppermute | solution.py:489
  13.4 1.9 %collective-permute-done.1.refs_1_ = bf16[32,2944]{1,0:T(8,128)(2,1)S(1)} collective-permute-done((bf16[32,2944]{1,0:T(8,128)(2,1)S(1)}, bf16[32,2944]{1,0:T(8,128)(2,1)S(1)}, u32[]{:S(2)}, u32[]{:S(2)}) %collective-permute-start.1) | collective-permute-done | bytes 188448 | tf_op jit(solution)/shard_map/ppermute | solution.py:484
  15.3 1.6 %project.2 = (bf16[32,256]{1,0:T(8,128)(2,1)S(1)}, bf16[64,512]{1,0:T(8,128)(2,1)S(1)}) custom-call(bf16[32,3200]{1,0:T(8,128)(2,1)S(1)} %collective-permute-done.refs_0_, bf16[32,2944]{1,0:T(8,128)(2,1)S(1)} %collective-permute-done.1.refs_1_, f32[2,6144]{1,0:T(2,128)S(1)} %get-tuple-element.75.refs_2_.refs_3_.gain.refs_4_, ...), custom_call_target="tpu_custom_call" | custom-call | tf_op jit(solution)/shard_map/project/pallas_call | solution.py:207
  16.9 3.8 %collective-permute-done.2.refs_0_ = bf16[32,3200]{1,0:T(8,128)(2,1)S(1)} collective-permute-done((bf16[32,3200]{1,0:T(8,128)(2,1)S(1)}, bf16[32,3200]{1,0:T(8,128)(2,1)S(1)}, u32[]{:S(2)}, u32[]{:S(2)}) %collective-permute-start.2) | collective-permute-done | bytes 204832 | tf_op jit(solution)/shard_map/ppermute | solution.py:489
  20.7 0.7 %collective-permute-start.4 = (bf16[32,3200]{1,0:T(8,128)(2,1)S(1)}, bf16[32,3200]{1,0:T(8,128)(2,1)S(1)}, u32[]{:S(2)}, u32[]{:S(2)}) collective-permute-start(bf16[32,3200]{1,0:T(8,128)(2,1)S(1)} %collective-permute-done.2.refs_0_), channel_id=1, source_target_pairs={{0,1},{1,2},{2,3},{3,0},{4,5},{5,6},{6,7},{7,4},{8,9},{9,10},{10,1... | collective-permute-start | bytes 614408 | tf_op jit(solution)/shard_map/ppermute | solution.py:496
  21.4 2.4 %collective-permute-start.7 = (bf16[64,512]{1,0:T(8,128)(2,1)S(1)}, bf16[64,512]{1,0:T(8,128)(2,1)S(1)}, u32[]{:S(2)}, u32[]{:S(2)}) collective-permute-start(bf16[64,512]{1,0:T(8,128)(2,1)S(1)} %get-tuple-element.76.refs_3_), channel_id=1, source_target_pairs={{0,24},{4,28},{8,16},{12,20},{16,8},{20,12},{24,0},{28,4},{1,25},{... | collective-permute-start | bytes 196616 | tf_op jit(solution)/shard_map/ppermute | solution.py:459
  23.9 0.5 %collective-permute-start.6 = (bf16[64,512]{1,0:T(8,128)(2,1)S(1)}, bf16[64,512]{1,0:T(8,128)(2,1)S(1)}, u32[]{:S(2)}, u32[]{:S(2)}) collective-permute-start(bf16[64,512]{1,0:T(8,128)(2,1)S(1)} %get-tuple-element.76.refs_3_), channel_id=1, source_target_pairs={{0,16},{4,20},{8,24},{12,28},{16,0},{20,4},{24,8},{28,12},{1,17},{... | collective-permute-start | bytes 196616 | tf_op jit(solution)/shard_map/ppermute | solution.py:459
  24.4 0.5 %collective-permute-start.5 = (bf16[64,512]{1,0:T(8,128)(2,1)S(1)}, bf16[64,512]{1,0:T(8,128)(2,1)S(1)}, u32[]{:S(2)}, u32[]{:S(2)}) collective-permute-start(bf16[64,512]{1,0:T(8,128)(2,1)S(1)} %get-tuple-element.76.refs_3_), channel_id=1, source_target_pairs={{0,8},{4,12},{8,0},{12,4},{16,24},{20,28},{24,16},{28,20},{1,9},{5... | collective-permute-start | bytes 196616 | tf_op jit(solution)/shard_map/ppermute | solution.py:459
  24.9 0.5 %collective-permute-start.12 = (bf16[32,2944]{1,0:T(8,128)(2,1)S(1)}, bf16[32,2944]{1,0:T(8,128)(2,1)S(1)}, u32[]{:S(2)}, u32[]{:S(2)}) collective-permute-start(bf16[32,2944]{1,0:T(8,128)(2,1)S(1)} %collective-permute-done.3.refs_1_.whole), channel_id=1, source_target_pairs={{0,1},{1,2},{2,3},{3,0},{4,5},{5,6},{6,7},{7,4},{8,9},{9,10},{10,1... | collective-permute-start | bytes 565256 | tf_op jit(solution)/shard_map/ppermute | solution.py:496
  25.4 1.1 %collective-permute-done.7.refs_9_ = bf16[64,512]{1,0:T(8,128)(2,1)S(1)} collective-permute-done((bf16[64,512]{1,0:T(8,128)(2,1)S(1)}, bf16[64,512]{1,0:T(8,128)(2,1)S(1)}, u32[]{:S(2)}, u32[]{:S(2)}) %collective-permute-start.7) | collective-permute-done | bytes 65568 | tf_op jit(solution)/shard_map/ppermute | solution.py:459
  26.6 1.5 %collective-permute-done.6.refs_7_ = bf16[64,512]{1,0:T(8,128)(2,1)S(1)} collective-permute-done((bf16[64,512]{1,0:T(8,128)(2,1)S(1)}, bf16[64,512]{1,0:T(8,128)(2,1)S(1)}, u32[]{:S(2)}, u32[]{:S(2)}) %collective-permute-start.6) | collective-permute-done | bytes 65568 | tf_op jit(solution)/shard_map/ppermute | solution.py:459
  28.1 0.5 %collective-permute-done.5.refs_5_ = bf16[64,512]{1,0:T(8,128)(2,1)S(1)} collective-permute-done((bf16[64,512]{1,0:T(8,128)(2,1)S(1)}, bf16[64,512]{1,0:T(8,128)(2,1)S(1)}, u32[]{:S(2)}, u32[]{:S(2)}) %collective-permute-start.5) | collective-permute-done | bytes 65568 | tf_op jit(solution)/shard_map/ppermute | solution.py:459
  28.6 0.0 collective-permute-start.8
  28.6 0.5 %collective-permute-start.9 = (bf16[64,512]{1,0:T(8,128)(2,1)S(1)}, bf16[64,512]{1,0:T(8,128)(2,1)S(1)}, u32[]{:S(2)}, u32[]{:S(2)}) collective-permute-start(bf16[64,512]{1,0:T(8,128)(2,1)S(1)} %collective-permute-done.5.refs_5_), channel_id=1, source_target_pairs={{0,4},{4,0},{8,12},{12,8},{16,20},{20,16},{24,28},{28,24},{1,5},{5... | collective-permute-start | bytes 196616 | tf_op jit(solution)/shard_map/ppermute | solution.py:466
  29.1 0.0 collective-permute-start.10
  29.1 0.7 %collective-permute-done.8.refs_4_ = bf16[64,512]{1,0:T(8,128)(2,1)S(1)} collective-permute-done((bf16[64,512]{1,0:T(8,128)(2,1)S(1)}, bf16[64,512]{1,0:T(8,128)(2,1)S(1)}, u32[]{:S(2)}, u32[]{:S(2)}) %collective-permute-start.8) | collective-permute-done | bytes 65568 | tf_op jit(solution)/shard_map/ppermute | solution.py:466
  29.9 0.2 collective-permute-start.11
  30.0 0.0 collective-permute-done.9.refs_6_
  30.0 0.3 collective-permute-done.10.refs_8_
  30.4 0.7 %collective-permute-done.11.refs_10_ = bf16[64,512]{1,0:T(8,128)(2,1)S(1)} collective-permute-done((bf16[64,512]{1,0:T(8,128)(2,1)S(1)}, bf16[64,512]{1,0:T(8,128)(2,1)S(1)}, u32[]{:S(2)}, u32[]{:S(2)}) %collective-permute-start.11) | collective-permute-done | bytes 65568 | tf_op jit(solution)/shard_map/ppermute | solution.py:466
  31.1 0.0 collective-permute-done.4.refs_2_
  31.1 0.9 %lead.1.refs_2_ = f32[80,640]{1,0:T(8,128)S(1)} custom-call(bf16[32,3200]{1,0:T(8,128)(2,1)S(1)} %collective-permute-done.2.refs_0_, bf16[32,2944]{1,0:T(8,128)(2,1)S(1)} %collective-permute-done.3.refs_1_.whole, bf16[32,3200]{1,0:T(8,128)(2,1)S(1)} %collective-permute-done.4.refs_2_, f32[2,6144]{1,0:T(2,128)S(1)} %get-tuple-element.75.refs_2_.refs_3_.gain.refs_4_, ...), custom_call_target="tpu_custom_call" | custom-call | tf_op jit(solution)/shard_map/lead/pallas_call | solution.py:257
  32.0 0.3 collective-permute-done.12.piece.refs_3_
  32.3 0.8 %finish.1.refs_0_ = bf16[64,512]{1,0:T(8,128)(2,1)S(1)} custom-call(bf16[32,2944]{1,0:T(8,128)(2,1)S(1)} %collective-permute-done.3.refs_1_.whole, bf16[32,2944]{1,0:T(8,128)(2,1)S(1)} %collective-permute-done.12.piece.refs_3_, f32[2,6144]{1,0:T(2,128)S(1)} %get-tuple-element.75.refs_2_.refs_3_.gain.refs_4_, ...), custom_call_target="tpu_custom_call" | custom-call | tf_op jit(solution)/shard_map/finish/pallas_call | solution.py:294
  33.1 2.8 %collective-permute-start.18 = (bf16[64,512]{1,0:T(8,128)(2,1)S(1)}, bf16[64,512]{1,0:T(8,128)(2,1)S(1)}, u32[]{:S(2)}, u32[]{:S(2)}) collective-permute-start(bf16[64,512]{1,0:T(8,128)(2,1)S(1)} %finish.1.refs_0_), channel_id=1, source_target_pairs={{0,24},{4,28},{8,16},{12,20},{16,8},{20,12},{24,0},{28,4},{1,25},{... | collective-permute-start | bytes 196616 | tf_op jit(solution)/shard_map/ppermute | solution.py:459
  35.9 0.5 %collective-permute-start.16 = (bf16[64,512]{1,0:T(8,128)(2,1)S(1)}, bf16[64,512]{1,0:T(8,128)(2,1)S(1)}, u32[]{:S(2)}, u32[]{:S(2)}) collective-permute-start(bf16[64,512]{1,0:T(8,128)(2,1)S(1)} %finish.1.refs_0_), channel_id=1, source_target_pairs={{0,16},{4,20},{8,24},{12,28},{16,0},{20,4},{24,8},{28,12},{1,17},{... | collective-permute-start | bytes 196616 | tf_op jit(solution)/shard_map/ppermute | solution.py:459
  36.4 0.2 collective-permute-start.14
  36.7 0.9 %project.3.refs_2_ = bf16[64,256]{1,0:T(8,128)(2,1)S(1)} custom-call(bf16[32,3200]{1,0:T(8,128)(2,1)S(1)} %collective-permute-done.2.refs_0_, bf16[32,2944]{1,0:T(8,128)(2,1)S(1)} %collective-permute-done.3.refs_1_.whole, bf16[32,3200]{1,0:T(8,128)(2,1)S(1)} %collective-permute-done.4.refs_2_, bf16[32,2944]{1,0:T(8,128)(2,1)S(1)} %collective-permute-done.12.piece.refs_3_, ...), custom_call_target="tpu_custom_call" | custom-call | tf_op jit(solution)/shard_map/project/pallas_call | solution.py:207
  37.6 0.5 %attend_early.1 = (bf16[128,256]{1,0:T(8,128)(2,1)S(1)}, f32[128,256]{1,0:T(8,128)S(1)}, f32[128,256]{1,0:T(8,128)S(1)}, f32[128,256]{1,0:T(8,128)S(1)}, f32[128,512]{1,0:T(8,128)S(1)}) custom-call(s32[1]{0:T(128)} %bitcast.1.mine, s32[128,1]{1,0:T(8,128)S(1)} %get-tuple-element.56.seg_col, s32[1,128]{1,0:T(1,128)S(1)} %get-tuple-element.57.seg_row, ...), custom_call_target="tpu_custom_call" | custom-call | tf_op jit(solution)/shard_map/attend_early/pallas_call | solution.py:376
  38.1 0.7 %collective-permute-done.18.refs_6_ = bf16[64,512]{1,0:T(8,128)(2,1)S(1)} collective-permute-done((bf16[64,512]{1,0:T(8,128)(2,1)S(1)}, bf16[64,512]{1,0:T(8,128)(2,1)S(1)}, u32[]{:S(2)}, u32[]{:S(2)}) %collective-permute-start.18) | collective-permute-done | bytes 65568 | tf_op jit(solution)/shard_map/ppermute | solution.py:459
  38.8 1.4 %collective-permute-done.16.refs_4_ = bf16[64,512]{1,0:T(8,128)(2,1)S(1)} collective-permute-done((bf16[64,512]{1,0:T(8,128)(2,1)S(1)}, bf16[64,512]{1,0:T(8,128)(2,1)S(1)}, u32[]{:S(2)}, u32[]{:S(2)}) %collective-permute-start.16) | collective-permute-done | bytes 65568 | tf_op jit(solution)/shard_map/ppermute | solution.py:459
  40.2 0.5 %collective-permute-done.14.refs_2_ = bf16[64,512]{1,0:T(8,128)(2,1)S(1)} collective-permute-done((bf16[64,512]{1,0:T(8,128)(2,1)S(1)}, bf16[64,512]{1,0:T(8,128)(2,1)S(1)}, u32[]{:S(2)}, u32[]{:S(2)}) %collective-permute-start.14) | collective-permute-done | bytes 65568 | tf_op jit(solution)/shard_map/ppermute | solution.py:459
  40.7 0.0 collective-permute-start.15
  40.7 0.7 %collective-permute-done.17.refs_5_ = bf16[64,512]{1,0:T(8,128)(2,1)S(1)} collective-permute-done((bf16[64,512]{1,0:T(8,128)(2,1)S(1)}, bf16[64,512]{1,0:T(8,128)(2,1)S(1)}, u32[]{:S(2)}, u32[]{:S(2)}) %collective-permute-start.17) | collective-permute-done | bytes 65568 | tf_op jit(solution)/shard_map/ppermute | solution.py:466
  41.5 0.5 %collective-permute-done.15.refs_3_ = bf16[64,512]{1,0:T(8,128)(2,1)S(1)} collective-permute-done((bf16[64,512]{1,0:T(8,128)(2,1)S(1)}, bf16[64,512]{1,0:T(8,128)(2,1)S(1)}, u32[]{:S(2)}, u32[]{:S(2)}) %collective-permute-start.15) | collective-permute-done | bytes 65568 | tf_op jit(solution)/shard_map/ppermute | solution.py:466
  42.0 0.6 %attend.1 = (bf16[32,256]{1,0:T(8,128)(2,1)S(1)}, bf16[32,256]{1,0:T(8,128)(2,1)S(1)}, bf16[32,256]{1,0:T(8,128)(2,1)S(1)}, bf16[32,256]{1,0:T(8,128)(2,1)S(1)}) custom-call(s32[1]{0:T(128)} %bitcast.place, bf16[128,256]{1,0:T(8,128)(2,1)S(1)} %get-tuple-element.84.q_all, f32[128,256]{1,0:T(8,128)S(1)} %get-tuple-element.85.sums, ...), custom_call_target="tpu_custom_call" | custom-call | tf_op jit(solution)/shard_map/attend/pallas_call | solution.py:421
  42.6 0.4 collective-permute-start.20
  43.0 2.0 %collective-permute-start.21 = (bf16[32,256]{1,0:T(8,128)(2,1)S(1)}, bf16[32,256]{1,0:T(8,128)(2,1)S(1)}, u32[]{:S(2)}, u32[]{:S(2)}) collective-permute-start(bf16[32,256]{1,0:T(8,128)(2,1)S(1)} %get-tuple-element.95), channel_id=1, source_target_pairs={{0,3},{1,2},{2,1},{3,0},{4,7},{5,6},{6,5},{7,4},{8,11},{9,10},{10,... | collective-permute-start | bytes 49160 | tf_op jit(solution)/shard_map/ppermute | solution.py:512
  45.0 1.2 %collective-permute-start.22 = (bf16[32,256]{1,0:T(8,128)(2,1)S(1)}, bf16[32,256]{1,0:T(8,128)(2,1)S(1)}, u32[]{:S(2)}, u32[]{:S(2)}) collective-permute-start(bf16[32,256]{1,0:T(8,128)(2,1)S(1)} %get-tuple-element.96), channel_id=1, source_target_pairs={{0,1},{1,0},{2,3},{3,2},{4,5},{5,4},{6,7},{7,6},{8,9},{9,8},{10,11... | collective-permute-start | bytes 49160 | tf_op jit(solution)/shard_map/ppermute | solution.py:512
  46.1 1.1 %collective-permute-done.20.refs_1_ = bf16[32,256]{1,0:T(8,128)(2,1)S(1)} collective-permute-done((bf16[32,256]{1,0:T(8,128)(2,1)S(1)}, bf16[32,256]{1,0:T(8,128)(2,1)S(1)}, u32[]{:S(2)}, u32[]{:S(2)}) %collective-permute-start.20) | collective-permute-done | bytes 16416 | tf_op jit(solution)/shard_map/ppermute | solution.py:512
  47.3 1.3 %collective-permute-done.21.refs_2_ = bf16[32,256]{1,0:T(8,128)(2,1)S(1)} collective-permute-done((bf16[32,256]{1,0:T(8,128)(2,1)S(1)}, bf16[32,256]{1,0:T(8,128)(2,1)S(1)}, u32[]{:S(2)}, u32[]{:S(2)}) %collective-permute-start.21) | collective-permute-done | bytes 16416 | tf_op jit(solution)/shard_map/ppermute | solution.py:512
  48.5 0.2 collective-permute-done.22.refs_3_
  48.7 0.6 %place.1 = bf16[1,32,1024]{2,1,0:T(8,128)(2,1)} custom-call(s32[1]{0:T(128)} %bitcast.place, bf16[32,256]{1,0:T(8,128)(2,1)S(1)} %get-tuple-element.93.refs_0_, bf16[32,256]{1,0:T(8,128)(2,1)S(1)} %collective-permute-done.20.refs_1_, bf16[32,256]{1,0:T(8,128)(2,1)S(1)} %collective-permute-done.21.refs_2_, bf16[32,256]{1,0:T(8,128)(2,1)S(1)} %collective-permute-done.22.refs_3_), custom_call_target="tpu_custom_call" | custom-call | tf_op jit(solution)/shard_map/place/pallas_call | solution.py:447
  (7 shorter events, 0.0 us)
Async XLA Ops:
  1.0 11.0 %collective-permute-start = (bf16[32,3200]{1,0:T(8,128)(2,1)S(1)}, bf16[32,3200]{1,0:T(8,128)(2,1)S(1)}, u32[]{:S(2)}, u32[]{:S(2)}) collective-permute-start(bf16[32,3200]{1,0:T(8,128)(2,1)S(1)} %get-tuple-element.54.refs_3_), channel_id=1, source_target_pairs={{0,1},{1,2},{2,3},{3,0},{4,5},{5,6},{6,7},{7,4},{8,9},{9,10},{10,1... | collective-permute-start | bytes 614408 | tf_op jit(solution)/shard_map/ppermute | solution.py:484
  4.1 11.1 %collective-permute-start.1 = (bf16[32,2944]{1,0:T(8,128)(2,1)S(1)}, bf16[32,2944]{1,0:T(8,128)(2,1)S(1)}, u32[]{:S(2)}, u32[]{:S(2)}) collective-permute-start(bf16[32,2944]{1,0:T(8,128)(2,1)S(1)} %get-tuple-element.55.refs_4_), channel_id=1, source_target_pairs={{0,1},{1,2},{2,3},{3,0},{4,5},{5,6},{6,7},{7,4},{8,9},{9,10},{10,1... | collective-permute-start | bytes 565256 | tf_op jit(solution)/shard_map/ppermute | solution.py:484
  12.1 8.7 %collective-permute-start.2 = (bf16[32,3200]{1,0:T(8,128)(2,1)S(1)}, bf16[32,3200]{1,0:T(8,128)(2,1)S(1)}, u32[]{:S(2)}, u32[]{:S(2)}) collective-permute-start(bf16[32,3200]{1,0:T(8,128)(2,1)S(1)} %collective-permute-done.refs_0_), channel_id=1, source_target_pairs={{0,1},{1,2},{2,3},{3,0},{4,5},{5,6},{6,7},{7,4},{8,9},{9,10},{10,1... | collective-permute-start | bytes 614408 | tf_op jit(solution)/shard_map/ppermute | solution.py:489
  15.3 9.6 %collective-permute-start.3 = (bf16[32,2944]{1,0:T(8,128)(2,1)S(1)}, bf16[32,2944]{1,0:T(8,128)(2,1)S(1)}, u32[]{:S(2)}, u32[]{:S(2)}) collective-permute-start(bf16[32,2944]{1,0:T(8,128)(2,1)S(1)} %collective-permute-done.1.refs_1_), channel_id=1, source_target_pairs={{0,1},{1,2},{2,3},{3,0},{4,5},{5,6},{6,7},{7,4},{8,9},{9,10},{10,1... | collective-permute-start | bytes 565256 | tf_op jit(solution)/shard_map/ppermute | solution.py:489
  20.7 10.4 %collective-permute-start.4 = (bf16[32,3200]{1,0:T(8,128)(2,1)S(1)}, bf16[32,3200]{1,0:T(8,128)(2,1)S(1)}, u32[]{:S(2)}, u32[]{:S(2)}) collective-permute-start(bf16[32,3200]{1,0:T(8,128)(2,1)S(1)} %collective-permute-done.2.refs_0_), channel_id=1, source_target_pairs={{0,1},{1,2},{2,3},{3,0},{4,5},{5,6},{6,7},{7,4},{8,9},{9,10},{10,1... | collective-permute-start | bytes 614408 | tf_op jit(solution)/shard_map/ppermute | solution.py:496
  21.4 5.2 %collective-permute-start.7 = (bf16[64,512]{1,0:T(8,128)(2,1)S(1)}, bf16[64,512]{1,0:T(8,128)(2,1)S(1)}, u32[]{:S(2)}, u32[]{:S(2)}) collective-permute-start(bf16[64,512]{1,0:T(8,128)(2,1)S(1)} %get-tuple-element.76.refs_3_), channel_id=1, source_target_pairs={{0,24},{4,28},{8,16},{12,20},{16,8},{20,12},{24,0},{28,4},{1,25},{... | collective-permute-start | bytes 196616 | tf_op jit(solution)/shard_map/ppermute | solution.py:459
  23.9 4.3 %collective-permute-start.6 = (bf16[64,512]{1,0:T(8,128)(2,1)S(1)}, bf16[64,512]{1,0:T(8,128)(2,1)S(1)}, u32[]{:S(2)}, u32[]{:S(2)}) collective-permute-start(bf16[64,512]{1,0:T(8,128)(2,1)S(1)} %get-tuple-element.76.refs_3_), channel_id=1, source_target_pairs={{0,16},{4,20},{8,24},{12,28},{16,0},{20,4},{24,8},{28,12},{1,17},{... | collective-permute-start | bytes 196616 | tf_op jit(solution)/shard_map/ppermute | solution.py:459
  24.4 4.3 %collective-permute-start.5 = (bf16[64,512]{1,0:T(8,128)(2,1)S(1)}, bf16[64,512]{1,0:T(8,128)(2,1)S(1)}, u32[]{:S(2)}, u32[]{:S(2)}) collective-permute-start(bf16[64,512]{1,0:T(8,128)(2,1)S(1)} %get-tuple-element.76.refs_3_), channel_id=1, source_target_pairs={{0,8},{4,12},{8,0},{12,4},{16,24},{20,28},{24,16},{28,20},{1,9},{5... | collective-permute-start | bytes 196616 | tf_op jit(solution)/shard_map/ppermute | solution.py:459
  24.9 7.4 %collective-permute-start.12 = (bf16[32,2944]{1,0:T(8,128)(2,1)S(1)}, bf16[32,2944]{1,0:T(8,128)(2,1)S(1)}, u32[]{:S(2)}, u32[]{:S(2)}) collective-permute-start(bf16[32,2944]{1,0:T(8,128)(2,1)S(1)} %collective-permute-done.3.refs_1_.whole), channel_id=1, source_target_pairs={{0,1},{1,2},{2,3},{3,0},{4,5},{5,6},{6,7},{7,4},{8,9},{9,10},{10,1... | collective-permute-start | bytes 565256 | tf_op jit(solution)/shard_map/ppermute | solution.py:496
  28.6 1.3 %collective-permute-start.8 = (bf16[64,512]{1,0:T(8,128)(2,1)S(1)}, bf16[64,512]{1,0:T(8,128)(2,1)S(1)}, u32[]{:S(2)}, u32[]{:S(2)}) collective-permute-start(bf16[64,512]{1,0:T(8,128)(2,1)S(1)} %get-tuple-element.76.refs_3_), channel_id=1, source_target_pairs={{0,4},{4,0},{8,12},{12,8},{16,20},{20,16},{24,28},{28,24},{1,5},{5... | collective-permute-start | bytes 196616 | tf_op jit(solution)/shard_map/ppermute | solution.py:466
  28.6 1.4 %collective-permute-start.9 = (bf16[64,512]{1,0:T(8,128)(2,1)S(1)}, bf16[64,512]{1,0:T(8,128)(2,1)S(1)}, u32[]{:S(2)}, u32[]{:S(2)}) collective-permute-start(bf16[64,512]{1,0:T(8,128)(2,1)S(1)} %collective-permute-done.5.refs_5_), channel_id=1, source_target_pairs={{0,4},{4,0},{8,12},{12,8},{16,20},{20,16},{24,28},{28,24},{1,5},{5... | collective-permute-start | bytes 196616 | tf_op jit(solution)/shard_map/ppermute | solution.py:466
  29.1 1.3 %collective-permute-start.10 = (bf16[64,512]{1,0:T(8,128)(2,1)S(1)}, bf16[64,512]{1,0:T(8,128)(2,1)S(1)}, u32[]{:S(2)}, u32[]{:S(2)}) collective-permute-start(bf16[64,512]{1,0:T(8,128)(2,1)S(1)} %collective-permute-done.6.refs_7_), channel_id=1, source_target_pairs={{0,4},{4,0},{8,12},{12,8},{16,20},{20,16},{24,28},{28,24},{1,5},{5... | collective-permute-start | bytes 196616 | tf_op jit(solution)/shard_map/ppermute | solution.py:466
  29.9 1.3 %collective-permute-start.11 = (bf16[64,512]{1,0:T(8,128)(2,1)S(1)}, bf16[64,512]{1,0:T(8,128)(2,1)S(1)}, u32[]{:S(2)}, u32[]{:S(2)}) collective-permute-start(bf16[64,512]{1,0:T(8,128)(2,1)S(1)} %collective-permute-done.7.refs_9_), channel_id=1, source_target_pairs={{0,4},{4,0},{8,12},{12,8},{16,20},{20,16},{24,28},{28,24},{1,5},{5... | collective-permute-start | bytes 196616 | tf_op jit(solution)/shard_map/ppermute | solution.py:466
  33.1 5.7 %collective-permute-start.18 = (bf16[64,512]{1,0:T(8,128)(2,1)S(1)}, bf16[64,512]{1,0:T(8,128)(2,1)S(1)}, u32[]{:S(2)}, u32[]{:S(2)}) collective-permute-start(bf16[64,512]{1,0:T(8,128)(2,1)S(1)} %finish.1.refs_0_), channel_id=1, source_target_pairs={{0,24},{4,28},{8,16},{12,20},{16,8},{20,12},{24,0},{28,4},{1,25},{... | collective-permute-start | bytes 196616 | tf_op jit(solution)/shard_map/ppermute | solution.py:459
  35.9 4.3 %collective-permute-start.16 = (bf16[64,512]{1,0:T(8,128)(2,1)S(1)}, bf16[64,512]{1,0:T(8,128)(2,1)S(1)}, u32[]{:S(2)}, u32[]{:S(2)}) collective-permute-start(bf16[64,512]{1,0:T(8,128)(2,1)S(1)} %finish.1.refs_0_), channel_id=1, source_target_pairs={{0,16},{4,20},{8,24},{12,28},{16,0},{20,4},{24,8},{28,12},{1,17},{... | collective-permute-start | bytes 196616 | tf_op jit(solution)/shard_map/ppermute | solution.py:459
  36.4 4.3 %collective-permute-start.14 = (bf16[64,512]{1,0:T(8,128)(2,1)S(1)}, bf16[64,512]{1,0:T(8,128)(2,1)S(1)}, u32[]{:S(2)}, u32[]{:S(2)}) collective-permute-start(bf16[64,512]{1,0:T(8,128)(2,1)S(1)} %finish.1.refs_0_), channel_id=1, source_target_pairs={{0,8},{4,12},{8,0},{12,4},{16,24},{20,28},{24,16},{28,20},{1,9},{5... | collective-permute-start | bytes 196616 | tf_op jit(solution)/shard_map/ppermute | solution.py:459
  36.7 4.0 %collective-permute-start.13 = (bf16[64,512]{1,0:T(8,128)(2,1)S(1)}, bf16[64,512]{1,0:T(8,128)(2,1)S(1)}, u32[]{:S(2)}, u32[]{:S(2)}) collective-permute-start(bf16[64,512]{1,0:T(8,128)(2,1)S(1)} %finish.1.refs_0_), channel_id=1, source_target_pairs={{0,4},{4,0},{8,12},{12,8},{16,20},{20,16},{24,28},{28,24},{1,5},{5... | collective-permute-start | bytes 196616 | tf_op jit(solution)/shard_map/ppermute | solution.py:466
  38.8 1.9 %collective-permute-start.19 = (bf16[64,512]{1,0:T(8,128)(2,1)S(1)}, bf16[64,512]{1,0:T(8,128)(2,1)S(1)}, u32[]{:S(2)}, u32[]{:S(2)}) collective-permute-start(bf16[64,512]{1,0:T(8,128)(2,1)S(1)} %collective-permute-done.18.refs_6_), channel_id=1, source_target_pairs={{0,4},{4,0},{8,12},{12,8},{16,20},{20,16},{24,28},{28,24},{1,5},{5... | collective-permute-start | bytes 196616 | tf_op jit(solution)/shard_map/ppermute | solution.py:466
  40.2 1.3 %collective-permute-start.17 = (bf16[64,512]{1,0:T(8,128)(2,1)S(1)}, bf16[64,512]{1,0:T(8,128)(2,1)S(1)}, u32[]{:S(2)}, u32[]{:S(2)}) collective-permute-start(bf16[64,512]{1,0:T(8,128)(2,1)S(1)} %collective-permute-done.16.refs_4_), channel_id=1, source_target_pairs={{0,4},{4,0},{8,12},{12,8},{16,20},{20,16},{24,28},{28,24},{1,5},{5... | collective-permute-start | bytes 196616 | tf_op jit(solution)/shard_map/ppermute | solution.py:466
  40.7 1.3 %collective-permute-start.15 = (bf16[64,512]{1,0:T(8,128)(2,1)S(1)}, bf16[64,512]{1,0:T(8,128)(2,1)S(1)}, u32[]{:S(2)}, u32[]{:S(2)}) collective-permute-start(bf16[64,512]{1,0:T(8,128)(2,1)S(1)} %collective-permute-done.14.refs_2_), channel_id=1, source_target_pairs={{0,4},{4,0},{8,12},{12,8},{16,20},{20,16},{24,28},{28,24},{1,5},{5... | collective-permute-start | bytes 196616 | tf_op jit(solution)/shard_map/ppermute | solution.py:466
  42.6 4.7 %collective-permute-start.20 = (bf16[32,256]{1,0:T(8,128)(2,1)S(1)}, bf16[32,256]{1,0:T(8,128)(2,1)S(1)}, u32[]{:S(2)}, u32[]{:S(2)}) collective-permute-start(bf16[32,256]{1,0:T(8,128)(2,1)S(1)} %get-tuple-element.94), channel_id=1, source_target_pairs={{0,2},{1,3},{2,0},{3,1},{4,6},{5,7},{6,4},{7,5},{8,10},{9,11},{10,... | collective-permute-start | bytes 49160 | tf_op jit(solution)/shard_map/ppermute | solution.py:512
  43.0 5.5 %collective-permute-start.21 = (bf16[32,256]{1,0:T(8,128)(2,1)S(1)}, bf16[32,256]{1,0:T(8,128)(2,1)S(1)}, u32[]{:S(2)}, u32[]{:S(2)}) collective-permute-start(bf16[32,256]{1,0:T(8,128)(2,1)S(1)} %get-tuple-element.95), channel_id=1, source_target_pairs={{0,3},{1,2},{2,1},{3,0},{4,7},{5,6},{6,5},{7,4},{8,11},{9,10},{10,... | collective-permute-start | bytes 49160 | tf_op jit(solution)/shard_map/ppermute | solution.py:512
  45.0 3.7 %collective-permute-start.22 = (bf16[32,256]{1,0:T(8,128)(2,1)S(1)}, bf16[32,256]{1,0:T(8,128)(2,1)S(1)}, u32[]{:S(2)}, u32[]{:S(2)}) collective-permute-start(bf16[32,256]{1,0:T(8,128)(2,1)S(1)} %get-tuple-element.96), channel_id=1, source_target_pairs={{0,1},{1,0},{2,3},{3,2},{4,5},{5,4},{6,7},{7,6},{8,9},{9,8},{10,11... | collective-permute-start | bytes 49160 | tf_op jit(solution)/shard_map/ppermute | solution.py:512

commit v8 on v7

--- a/solution.py
+++ b/solution.py
@@ -11,7 +11,7 @@
 HD = 128
 LANES = 128
 EXTRA = 16
-EDGES = (0, 25, 48)
+EDGES = (0, 1, 2)
 CHUNKS = len(EDGES) - 1
 PARTS = 4
 AHEAD = 6
@@ -489,7 +489,7 @@
         pieces = [lax.ppermute(piece, "dp", ring) for piece in pieces]
     query, keyval = project(arrived, gain, weights, (0, 1, 2), keyval)
     queries.append(query)
-    pieces[0], keyval = lax.optimization_barrier((pieces[0], keyval))
+    pieces[0], _ = lax.optimization_barrier((pieces[0], keyval))
     early = across_chips(keyval, groups)
     _, early = lax.optimization_barrier((pieces[-1], early))
     early = across_cores(early, groups)

time: 49.5 us -> 49.3 us (level)
  waiting for transfers between devices: 17.8 us -> 15.5 us
  starting transfers between devices: 18.5 us -> 20.4 us
    ppermute x2, waiting for transfers between devices: 0.34 us -> 3.99 us  [per_device(): moved = [lax.ppermute(piece, 'dp', ring) for piece in pieces]]
    ppermute x6, waiting for transfers between devices: 5.78 us -> 2.34 us  [across_chips(): lax.ppermute(block, 'group', [(i, i ^ m) for i in range(groups)])]
    ppermute x4, waiting for transfers between devices: 6.03 us -> 3.47 us  [per_device(): pieces = [lax.ppermute(piece, 'dp', ring) for piece in pieces]]
    ppermute x2, starting transfers between devices: 1.23 us -> 2.84 us  [per_device(): moved = [lax.ppermute(piece, 'dp', ring) for piece in pieces]]
  transfers between devices with their start and end apart: 23 -> 23, of which waited for: 18 -> 15; matrix products, arithmetic and copies ran while one was open for 0% -> 0% of each run, Pallas kernels for 19% -> 19%
where the time goes in v8:
time: 49.3 us; the launch traced here: 49.2 us
  starting transfers between devices  20.4 us (41%)
  waiting for transfers between devices  15.5 us (31%)
  Pallas kernels  12.5 us (25%)
  between operations  0.71 us (1%)
    ppermute x6, starting transfers between devices, across_chips(): lax.ppermute(block, 'group', [(i, i ^ m) for i in range(groups)])  7.06 us
    ppermute x4, starting transfers between devices, per_device(): pieces = [lax.ppermute(piece, 'dp', ring) for piece in pieces]  6.16 us
    pallas_call x1, Pallas kernels, begin(): pl.pallas_call(functools.partial(begin_kernel, shards), in_specs=[IN_SMEM...  5.38 us
    ppermute x2, waiting for transfers between devices, per_device(): moved = [lax.ppermute(piece, 'dp', ring) for piece in pieces]  3.99 us
    ppermute x3, starting transfers between devices, per_device(): lax.ppermute(results[s], 'dp', [(i, i ^ s) for i in range(shards)])  3.55 us
    ppermute x4, waiting for transfers between devices, per_device(): pieces = [lax.ppermute(piece, 'dp', ring) for piece in pieces]  3.47 us
    ppermute x8, waiting for transfers between devices, across_cores(): lax.ppermute(block, 'group', swap)  3 us
    ppermute x2, starting transfers between devices, per_device(): moved = [lax.ppermute(piece, 'dp', ring) for piece in pieces]  2.84 us
  transfers between devices with their start and end apart: 23, of which 15 were waited for; matrix products, arithmetic and copies ran while one was open for 0% of the time, Pallas kernels for 19%

profile of v8, /device:TPU:0, one launch (start us, length us, event | category | flops | bytes accessed | tf_op | source)
XLA Modules:
  0.0 49.2 jit_solution(12903129567133784471)
XLA Ops:
  0.0 1.0 %split.1 = (bf16[32,3072]{1,0:T(8,128)(2,1)S(1)}, bf16[32,3072]{1,0:T(8,128)(2,1)S(1)}) custom-call(bf16[1,32,6144]{2,1,0:T(8,128)(2,1)} %x_hbm), custom_call_target="tpu_custom_call" | custom-call | tf_op jit(solution)/shard_map/split/pallas_call | solution.py:58
  1.0 3.1 %collective-permute-start = (bf16[32,3072]{1,0:T(8,128)(2,1)S(1)}, bf16[32,3072]{1,0:T(8,128)(2,1)S(1)}, u32[]{:S(2)}, u32[]{:S(2)}) collective-permute-start(bf16[32,3072]{1,0:T(8,128)(2,1)S(1)} %get-tuple-element.53.refs_3_), channel_id=1, source_target_pairs={{0,1},{1,2},{2,3},{3,0},{4,5},{5,6},{6,7},{7,4},{8,9},{9,10},{10,1... | collective-permute-start | bytes 589832 | tf_op jit(solution)/shard_map/ppermute | solution.py:484
  4.1 1.6 %collective-permute-start.1 = (bf16[32,3072]{1,0:T(8,128)(2,1)S(1)}, bf16[32,3072]{1,0:T(8,128)(2,1)S(1)}, u32[]{:S(2)}, u32[]{:S(2)}) collective-permute-start(bf16[32,3072]{1,0:T(8,128)(2,1)S(1)} %get-tuple-element.54.refs_4_), channel_id=1, source_target_pairs={{0,1},{1,2},{2,3},{3,0},{4,5},{5,6},{6,7},{7,4},{8,9},{9,10},{10,1... | collective-permute-start | bytes 589832 | tf_op jit(solution)/shard_map/ppermute | solution.py:484
  6.3 5.4 %begin.1 = (bf16[32,256]{1,0:T(8,128)(2,1)S(1)}, bf16[32,512]{1,0:T(8,128)(2,1)S(1)}, bf16[6144,256]{1,0:T(8,128)(2,1)S(1)}, bf16[6144,256]{1,0:T(8,128)(2,1)S(1...) custom-call(s32[1]{0:T(128)} %bitcast.place, ...), custom_call_target="tpu_custom_call" | custom-call | tf_op jit(solution)/shard_map/begin/pallas_call | solution.py:150
  11.7 0.1 collective-permute-done.refs_0_
  11.9 1.5 %collective-permute-start.2 = (bf16[32,3072]{1,0:T(8,128)(2,1)S(1)}, bf16[32,3072]{1,0:T(8,128)(2,1)S(1)}, u32[]{:S(2)}, u32[]{:S(2)}) collective-permute-start(bf16[32,3072]{1,0:T(8,128)(2,1)S(1)} %collective-permute-done.refs_0_), channel_id=1, source_target_pairs={{0,1},{1,2},{2,3},{3,0},{4,5},{5,6},{6,7},{7,4},{8,9},{9,10},{10,1... | collective-permute-start | bytes 589832 | tf_op jit(solution)/shard_map/ppermute | solution.py:489
  13.4 1.9 %collective-permute-done.1.refs_1_ = bf16[32,3072]{1,0:T(8,128)(2,1)S(1)} collective-permute-done((bf16[32,3072]{1,0:T(8,128)(2,1)S(1)}, bf16[32,3072]{1,0:T(8,128)(2,1)S(1)}, u32[]{:S(2)}, u32[]{:S(2)}) %collective-permute-start.1) | collective-permute-done | bytes 196640 | tf_op jit(solution)/shard_map/ppermute | solution.py:484
  15.3 0.0 collective-permute-start.3
  15.3 1.9 %project.2 = (bf16[32,256]{1,0:T(8,128)(2,1)S(1)}, bf16[64,512]{1,0:T(8,128)(2,1)S(1)}) custom-call(bf16[32,3072]{1,0:T(8,128)(2,1)S(1)} %collective-permute-done.refs_0_, bf16[32,3072]{1,0:T(8,128)(2,1)S(1)} %collective-permute-done.1.refs_1_, f32[2,6144]{1,0:T(2,128)S(1)} %get-tuple-element.73.refs_2_.refs_3_.gain.refs_4_, ...), custom_call_target="tpu_custom_call" | custom-call | tf_op jit(solution)/shard_map/project/pallas_call | solution.py:207
  17.1 2.5 %collective-permute-start.7 = (bf16[64,512]{1,0:T(8,128)(2,1)S(1)}, bf16[64,512]{1,0:T(8,128)(2,1)S(1)}, u32[]{:S(2)}, u32[]{:S(2)}) collective-permute-start(bf16[64,512]{1,0:T(8,128)(2,1)S(1)} %get-tuple-element.74.refs_3_), channel_id=1, source_target_pairs={{0,24},{4,28},{8,16},{12,20},{16,8},{20,12},{24,0},{28,4},{1,25},{... | collective-permute-start | bytes 196616 | tf_op jit(solution)/shard_map/ppermute | solution.py:459
  19.6 0.5 %collective-permute-start.6 = (bf16[64,512]{1,0:T(8,128)(2,1)S(1)}, bf16[64,512]{1,0:T(8,128)(2,1)S(1)}, u32[]{:S(2)}, u32[]{:S(2)}) collective-permute-start(bf16[64,512]{1,0:T(8,128)(2,1)S(1)} %get-tuple-element.74.refs_3_), channel_id=1, source_target_pairs={{0,16},{4,20},{8,24},{12,28},{16,0},{20,4},{24,8},{28,12},{1,17},{... | collective-permute-start | bytes 196616 | tf_op jit(solution)/shard_map/ppermute | solution.py:459
  20.1 0.5 %collective-permute-start.5 = (bf16[64,512]{1,0:T(8,128)(2,1)S(1)}, bf16[64,512]{1,0:T(8,128)(2,1)S(1)}, u32[]{:S(2)}, u32[]{:S(2)}) collective-permute-start(bf16[64,512]{1,0:T(8,128)(2,1)S(1)} %get-tuple-element.74.refs_3_), channel_id=1, source_target_pairs={{0,8},{4,12},{8,0},{12,4},{16,24},{20,28},{24,16},{28,20},{1,9},{5... | collective-permute-start | bytes 196616 | tf_op jit(solution)/shard_map/ppermute | solution.py:459
  20.6 2.2 %collective-permute-start.4 = (bf16[32,3072]{1,0:T(8,128)(2,1)S(1)}, bf16[32,3072]{1,0:T(8,128)(2,1)S(1)}, u32[]{:S(2)}, u32[]{:S(2)}) collective-permute-start(bf16[32,3072]{1,0:T(8,128)(2,1)S(1)} %collective-permute-done.2.refs_0_), channel_id=1, source_target_pairs={{0,1},{1,2},{2,3},{3,0},{4,5},{5,6},{6,7},{7,4},{8,9},{9,10},{10,1... | collective-permute-start | bytes 589832 | tf_op jit(solution)/shard_map/ppermute | solution.py:496
  22.8 1.5 %collective-permute-done.3.refs_1_.whole = bf16[32,3072]{1,0:T(8,128)(2,1)S(1)} collective-permute-done((bf16[32,3072]{1,0:T(8,128)(2,1)S(1)}, bf16[32,3072]{1,0:T(8,128)(2,1)S(1)}, u32[]{:S(2)}, u32[]{:S(2)}) %collective-permute-start.3) | collective-permute-done | bytes 196640 | tf_op jit(solution)/shard_map/ppermute | solution.py:489
  24.3 0.7 %collective-permute-start.12 = (bf16[32,3072]{1,0:T(8,128)(2,1)S(1)}, bf16[32,3072]{1,0:T(8,128)(2,1)S(1)}, u32[]{:S(2)}, u32[]{:S(2)}) collective-permute-start(bf16[32,3072]{1,0:T(8,128)(2,1)S(1)} %collective-permute-done.3.refs_1_.whole), channel_id=1, source_target_pairs={{0,1},{1,2},{2,3},{3,0},{4,5},{5,6},{6,7},{7,4},{8,9},{9,10},{10,1... | collective-permute-start | bytes 589832 | tf_op jit(solution)/shard_map/ppermute | solution.py:496
  24.9 0.0 collective-permute-done.7.refs_9_
  24.9 0.1 collective-permute-start.8
  25.0 0.5 %collective-permute-start.9 = (bf16[64,512]{1,0:T(8,128)(2,1)S(1)}, bf16[64,512]{1,0:T(8,128)(2,1)S(1)}, u32[]{:S(2)}, u32[]{:S(2)}) collective-permute-start(bf16[64,512]{1,0:T(8,128)(2,1)S(1)} %collective-permute-done.5.refs_5_), channel_id=1, source_target_pairs={{0,4},{4,0},{8,12},{12,8},{16,20},{20,16},{24,28},{28,24},{1,5},{5... | collective-permute-start | bytes 196616 | tf_op jit(solution)/shard_map/ppermute | solution.py:466
  25.5 0.1 collective-permute-start.10
  25.6 0.7 %collective-permute-done.8.refs_4_ = bf16[64,512]{1,0:T(8,128)(2,1)S(1)} collective-permute-done((bf16[64,512]{1,0:T(8,128)(2,1)S(1)}, bf16[64,512]{1,0:T(8,128)(2,1)S(1)}, u32[]{:S(2)}, u32[]{:S(2)}) %collective-permute-start.8) | collective-permute-done | bytes 65568 | tf_op jit(solution)/shard_map/ppermute | solution.py:466
  26.3 0.2 collective-permute-start.11
  26.4 0.3 collective-permute-done.10.refs_8_
  26.8 0.7 %collective-permute-done.11.refs_10_ = bf16[64,512]{1,0:T(8,128)(2,1)S(1)} collective-permute-done((bf16[64,512]{1,0:T(8,128)(2,1)S(1)}, bf16[64,512]{1,0:T(8,128)(2,1)S(1)}, u32[]{:S(2)}, u32[]{:S(2)}) %collective-permute-start.11) | collective-permute-done | bytes 65568 | tf_op jit(solution)/shard_map/ppermute | solution.py:466
  27.5 1.3 %collective-permute-done.4.refs_2_ = bf16[32,3072]{1,0:T(8,128)(2,1)S(1)} collective-permute-done((bf16[32,3072]{1,0:T(8,128)(2,1)S(1)}, bf16[32,3072]{1,0:T(8,128)(2,1)S(1)}, u32[]{:S(2)}, u32[]{:S(2)}) %collective-permute-start.4) | collective-permute-done | bytes 196640 | tf_op jit(solution)/shard_map/ppermute | solution.py:496
  28.8 0.8 %lead.1.refs_2_ = f32[80,640]{1,0:T(8,128)S(1)} custom-call(bf16[32,3072]{1,0:T(8,128)(2,1)S(1)} %collective-permute-done.2.refs_0_, bf16[32,3072]{1,0:T(8,128)(2,1)S(1)} %collective-permute-done.3.refs_1_.whole, bf16[32,3072]{1,0:T(8,128)(2,1)S(1)} %collective-permute-done.4.refs_2_, f32[2,6144]{1,0:T(2,128)S(1)} %get-tuple-element.73.refs_2_.refs_3_.gain.refs_4_, ...), custom_call_target="tpu_custom_call" | custom-call | tf_op jit(solution)/shard_map/lead/pallas_call | solution.py:257
  29.6 2.7 %collective-permute-done.12.piece.refs_3_ = bf16[32,3072]{1,0:T(8,128)(2,1)S(1)} collective-permute-done((bf16[32,3072]{1,0:T(8,128)(2,1)S(1)}, bf16[32,3072]{1,0:T(8,128)(2,1)S(1)}, u32[]{:S(2)}, u32[]{:S(2)}) %collective-permute-start.12) | collective-permute-done | bytes 196640 | tf_op jit(solution)/shard_map/ppermute | solution.py:496
  32.3 0.8 %finish.1.refs_0_ = bf16[64,512]{1,0:T(8,128)(2,1)S(1)} custom-call(bf16[32,3072]{1,0:T(8,128)(2,1)S(1)} %collective-permute-done.3.refs_1_.whole, bf16[32,3072]{1,0:T(8,128)(2,1)S(1)} %collective-permute-done.12.piece.refs_3_, f32[2,6144]{1,0:T(2,128)S(1)} %get-tuple-element.73.refs_2_.refs_3_.gain.refs_4_, ...), custom_call_target="tpu_custom_call" | custom-call | tf_op jit(solution)/shard_map/finish/pallas_call | solution.py:294
  33.1 2.5 %collective-permute-start.18 = (bf16[64,512]{1,0:T(8,128)(2,1)S(1)}, bf16[64,512]{1,0:T(8,128)(2,1)S(1)}, u32[]{:S(2)}, u32[]{:S(2)}) collective-permute-start(bf16[64,512]{1,0:T(8,128)(2,1)S(1)} %finish.1.refs_0_), channel_id=1, source_target_pairs={{0,24},{4,28},{8,16},{12,20},{16,8},{20,12},{24,0},{28,4},{1,25},{... | collective-permute-start | bytes 196616 | tf_op jit(solution)/shard_map/ppermute | solution.py:459
  35.7 0.5 %collective-permute-start.16 = (bf16[64,512]{1,0:T(8,128)(2,1)S(1)}, bf16[64,512]{1,0:T(8,128)(2,1)S(1)}, u32[]{:S(2)}, u32[]{:S(2)}) collective-permute-start(bf16[64,512]{1,0:T(8,128)(2,1)S(1)} %finish.1.refs_0_), channel_id=1, source_target_pairs={{0,16},{4,20},{8,24},{12,28},{16,0},{20,4},{24,8},{28,12},{1,17},{... | collective-permute-start | bytes 196616 | tf_op jit(solution)/shard_map/ppermute | solution.py:459
  36.2 0.5 %collective-permute-start.14 = (bf16[64,512]{1,0:T(8,128)(2,1)S(1)}, bf16[64,512]{1,0:T(8,128)(2,1)S(1)}, u32[]{:S(2)}, u32[]{:S(2)}) collective-permute-start(bf16[64,512]{1,0:T(8,128)(2,1)S(1)} %finish.1.refs_0_), channel_id=1, source_target_pairs={{0,8},{4,12},{8,0},{12,4},{16,24},{20,28},{24,16},{28,20},{1,9},{5... | collective-permute-start | bytes 196616 | tf_op jit(solution)/shard_map/ppermute | solution.py:459
  36.7 0.0 collective-permute-start.13
  36.7 0.9 %project.3.refs_2_ = bf16[64,256]{1,0:T(8,128)(2,1)S(1)} custom-call(bf16[32,3072]{1,0:T(8,128)(2,1)S(1)} %collective-permute-done.2.refs_0_, bf16[32,3072]{1,0:T(8,128)(2,1)S(1)} %collective-permute-done.3.refs_1_.whole, bf16[32,3072]{1,0:T(8,128)(2,1)S(1)} %collective-permute-done.4.refs_2_, bf16[32,3072]{1,0:T(8,128)(2,1)S(1)} %collective-permute-done.12.piece.refs_3_, ...), custom_call_target="tpu_custom_call" | custom-call | tf_op jit(solution)/shard_map/project/pallas_call | solution.py:207
  37.6 0.5 %attend_early.1 = (bf16[128,256]{1,0:T(8,128)(2,1)S(1)}, f32[128,256]{1,0:T(8,128)S(1)}, f32[128,256]{1,0:T(8,128)S(1)}, f32[128,256]{1,0:T(8,128)S(1)}, f32[128,512]{1,0:T(8,128)S(1)}) custom-call(s32[1]{0:T(128)} %bitcast.1.mine, s32[128,1]{1,0:T(8,128)S(1)} %get-tuple-element.55.seg_col, s32[1,128]{1,0:T(1,128)S(1)} %get-tuple-element.56.seg_row, ...), custom_call_target="tpu_custom_call" | custom-call | tf_op jit(solution)/shard_map/attend_early/pallas_call | solution.py:376
  38.1 0.8 %collective-permute-done.18.refs_6_ = bf16[64,512]{1,0:T(8,128)(2,1)S(1)} collective-permute-done((bf16[64,512]{1,0:T(8,128)(2,1)S(1)}, bf16[64,512]{1,0:T(8,128)(2,1)S(1)}, u32[]{:S(2)}, u32[]{:S(2)}) %collective-permute-start.18) | collective-permute-done | bytes 65568 | tf_op jit(solution)/shard_map/ppermute | solution.py:459
  38.8 0.0 collective-permute-start.19
  38.9 1.1 %collective-permute-done.16.refs_4_ = bf16[64,512]{1,0:T(8,128)(2,1)S(1)} collective-permute-done((bf16[64,512]{1,0:T(8,128)(2,1)S(1)}, bf16[64,512]{1,0:T(8,128)(2,1)S(1)}, u32[]{:S(2)}, u32[]{:S(2)}) %collective-permute-start.16) | collective-permute-done | bytes 65568 | tf_op jit(solution)/shard_map/ppermute | solution.py:459
  39.9 0.5 %collective-permute-done.14.refs_2_ = bf16[64,512]{1,0:T(8,128)(2,1)S(1)} collective-permute-done((bf16[64,512]{1,0:T(8,128)(2,1)S(1)}, bf16[64,512]{1,0:T(8,128)(2,1)S(1)}, u32[]{:S(2)}, u32[]{:S(2)}) %collective-permute-start.14) | collective-permute-done | bytes 65568 | tf_op jit(solution)/shard_map/ppermute | solution.py:459
  40.4 0.0 collective-permute-start.15
  40.4 0.7 %collective-permute-done.17.refs_5_ = bf16[64,512]{1,0:T(8,128)(2,1)S(1)} collective-permute-done((bf16[64,512]{1,0:T(8,128)(2,1)S(1)}, bf16[64,512]{1,0:T(8,128)(2,1)S(1)}, u32[]{:S(2)}, u32[]{:S(2)}) %collective-permute-start.17) | collective-permute-done | bytes 65568 | tf_op jit(solution)/shard_map/ppermute | solution.py:466
  41.2 0.5 %collective-permute-done.15.refs_3_ = bf16[64,512]{1,0:T(8,128)(2,1)S(1)} collective-permute-done((bf16[64,512]{1,0:T(8,128)(2,1)S(1)}, bf16[64,512]{1,0:T(8,128)(2,1)S(1)}, u32[]{:S(2)}, u32[]{:S(2)}) %collective-permute-start.15) | collective-permute-done | bytes 65568 | tf_op jit(solution)/shard_map/ppermute | solution.py:466
  41.7 0.6 %attend.1 = (bf16[32,256]{1,0:T(8,128)(2,1)S(1)}, bf16[32,256]{1,0:T(8,128)(2,1)S(1)}, bf16[32,256]{1,0:T(8,128)(2,1)S(1)}, bf16[32,256]{1,0:T(8,128)(2,1)S(1)}) custom-call(s32[1]{0:T(128)} %bitcast.place, bf16[128,256]{1,0:T(8,128)(2,1)S(1)} %get-tuple-element.82.q_all, f32[128,256]{1,0:T(8,128)S(1)} %get-tuple-element.83.sums, ...), custom_call_target="tpu_custom_call" | custom-call | tf_op jit(solution)/shard_map/attend/pallas_call | solution.py:421
  42.3 0.6 %collective-permute-start.20 = (bf16[32,256]{1,0:T(8,128)(2,1)S(1)}, bf16[32,256]{1,0:T(8,128)(2,1)S(1)}, u32[]{:S(2)}, u32[]{:S(2)}) collective-permute-start(bf16[32,256]{1,0:T(8,128)(2,1)S(1)} %get-tuple-element.92), channel_id=1, source_target_pairs={{0,2},{1,3},{2,0},{3,1},{4,6},{5,7},{6,4},{7,5},{8,10},{9,11},{10,... | collective-permute-start | bytes 49160 | tf_op jit(solution)/shard_map/ppermute | solution.py:512
  42.9 1.8 %collective-permute-start.21 = (bf16[32,256]{1,0:T(8,128)(2,1)S(1)}, bf16[32,256]{1,0:T(8,128)(2,1)S(1)}, u32[]{:S(2)}, u32[]{:S(2)}) collective-permute-start(bf16[32,256]{1,0:T(8,128)(2,1)S(1)} %get-tuple-element.93), channel_id=1, source_target_pairs={{0,3},{1,2},{2,1},{3,0},{4,7},{5,6},{6,5},{7,4},{8,11},{9,10},{10,... | collective-permute-start | bytes 49160 | tf_op jit(solution)/shard_map/ppermute | solution.py:512
  44.6 1.2 %collective-permute-start.22 = (bf16[32,256]{1,0:T(8,128)(2,1)S(1)}, bf16[32,256]{1,0:T(8,128)(2,1)S(1)}, u32[]{:S(2)}, u32[]{:S(2)}) collective-permute-start(bf16[32,256]{1,0:T(8,128)(2,1)S(1)} %get-tuple-element.94), channel_id=1, source_target_pairs={{0,1},{1,0},{2,3},{3,2},{4,5},{5,4},{6,7},{7,6},{8,9},{9,8},{10,11... | collective-permute-start | bytes 49160 | tf_op jit(solution)/shard_map/ppermute | solution.py:512
  45.9 1.3 %collective-permute-done.20.refs_1_ = bf16[32,256]{1,0:T(8,128)(2,1)S(1)} collective-permute-done((bf16[32,256]{1,0:T(8,128)(2,1)S(1)}, bf16[32,256]{1,0:T(8,128)(2,1)S(1)}, u32[]{:S(2)}, u32[]{:S(2)}) %collective-permute-start.20) | collective-permute-done | bytes 16416 | tf_op jit(solution)/shard_map/ppermute | solution.py:512
  47.1 1.4 %collective-permute-done.21.refs_2_ = bf16[32,256]{1,0:T(8,128)(2,1)S(1)} collective-permute-done((bf16[32,256]{1,0:T(8,128)(2,1)S(1)}, bf16[32,256]{1,0:T(8,128)(2,1)S(1)}, u32[]{:S(2)}, u32[]{:S(2)}) %collective-permute-start.21) | collective-permute-done | bytes 16416 | tf_op jit(solution)/shard_map/ppermute | solution.py:512
  48.5 0.0 collective-permute-done.22.refs_3_
  48.6 0.6 %place.1 = bf16[1,32,1024]{2,1,0:T(8,128)(2,1)} custom-call(s32[1]{0:T(128)} %bitcast.place, bf16[32,256]{1,0:T(8,128)(2,1)S(1)} %get-tuple-element.91.refs_0_, bf16[32,256]{1,0:T(8,128)(2,1)S(1)} %collective-permute-done.20.refs_1_, bf16[32,256]{1,0:T(8,128)(2,1)S(1)} %collective-permute-done.21.refs_2_, bf16[32,256]{1,0:T(8,128)(2,1)S(1)} %collective-permute-done.22.refs_3_), custom_call_target="tpu_custom_call" | custom-call | tf_op jit(solution)/shard_map/place/pallas_call | solution.py:447
  (7 shorter events, 0.0 us)
Async XLA Ops:
  1.0 10.8 %collective-permute-start = (bf16[32,3072]{1,0:T(8,128)(2,1)S(1)}, bf16[32,3072]{1,0:T(8,128)(2,1)S(1)}, u32[]{:S(2)}, u32[]{:S(2)}) collective-permute-start(bf16[32,3072]{1,0:T(8,128)(2,1)S(1)} %get-tuple-element.53.refs_3_), channel_id=1, source_target_pairs={{0,1},{1,2},{2,3},{3,0},{4,5},{5,6},{6,7},{7,4},{8,9},{9,10},{10,1... | collective-permute-start | bytes 589832 | tf_op jit(solution)/shard_map/ppermute | solution.py:484
  4.1 11.1 %collective-permute-start.1 = (bf16[32,3072]{1,0:T(8,128)(2,1)S(1)}, bf16[32,3072]{1,0:T(8,128)(2,1)S(1)}, u32[]{:S(2)}, u32[]{:S(2)}) collective-permute-start(bf16[32,3072]{1,0:T(8,128)(2,1)S(1)} %get-tuple-element.54.refs_4_), channel_id=1, source_target_pairs={{0,1},{1,2},{2,3},{3,0},{4,5},{5,6},{6,7},{7,4},{8,9},{9,10},{10,1... | collective-permute-start | bytes 589832 | tf_op jit(solution)/shard_map/ppermute | solution.py:484
  11.9 8.8 %collective-permute-start.2 = (bf16[32,3072]{1,0:T(8,128)(2,1)S(1)}, bf16[32,3072]{1,0:T(8,128)(2,1)S(1)}, u32[]{:S(2)}, u32[]{:S(2)}) collective-permute-start(bf16[32,3072]{1,0:T(8,128)(2,1)S(1)} %collective-permute-done.refs_0_), channel_id=1, source_target_pairs={{0,1},{1,2},{2,3},{3,0},{4,5},{5,6},{6,7},{7,4},{8,9},{9,10},{10,1... | collective-permute-start | bytes 589832 | tf_op jit(solution)/shard_map/ppermute | solution.py:489
  15.3 9.0 %collective-permute-start.3 = (bf16[32,3072]{1,0:T(8,128)(2,1)S(1)}, bf16[32,3072]{1,0:T(8,128)(2,1)S(1)}, u32[]{:S(2)}, u32[]{:S(2)}) collective-permute-start(bf16[32,3072]{1,0:T(8,128)(2,1)S(1)} %collective-permute-done.1.refs_1_), channel_id=1, source_target_pairs={{0,1},{1,2},{2,3},{3,0},{4,5},{5,6},{6,7},{7,4},{8,9},{9,10},{10,1... | collective-permute-start | bytes 589832 | tf_op jit(solution)/shard_map/ppermute | solution.py:489
  17.1 7.8 %collective-permute-start.7 = (bf16[64,512]{1,0:T(8,128)(2,1)S(1)}, bf16[64,512]{1,0:T(8,128)(2,1)S(1)}, u32[]{:S(2)}, u32[]{:S(2)}) collective-permute-start(bf16[64,512]{1,0:T(8,128)(2,1)S(1)} %get-tuple-element.74.refs_3_), channel_id=1, source_target_pairs={{0,24},{4,28},{8,16},{12,20},{16,8},{20,12},{24,0},{28,4},{1,25},{... | collective-permute-start | bytes 196616 | tf_op jit(solution)/shard_map/ppermute | solution.py:459
  19.6 5.4 %collective-permute-start.6 = (bf16[64,512]{1,0:T(8,128)(2,1)S(1)}, bf16[64,512]{1,0:T(8,128)(2,1)S(1)}, u32[]{:S(2)}, u32[]{:S(2)}) collective-permute-start(bf16[64,512]{1,0:T(8,128)(2,1)S(1)} %get-tuple-element.74.refs_3_), channel_id=1, source_target_pairs={{0,16},{4,20},{8,24},{12,28},{16,0},{20,4},{24,8},{28,12},{1,17},{... | collective-permute-start | bytes 196616 | tf_op jit(solution)/shard_map/ppermute | solution.py:459
  20.1 4.8 %collective-permute-start.5 = (bf16[64,512]{1,0:T(8,128)(2,1)S(1)}, bf16[64,512]{1,0:T(8,128)(2,1)S(1)}, u32[]{:S(2)}, u32[]{:S(2)}) collective-permute-start(bf16[64,512]{1,0:T(8,128)(2,1)S(1)} %get-tuple-element.74.refs_3_), channel_id=1, source_target_pairs={{0,8},{4,12},{8,0},{12,4},{16,24},{20,28},{24,16},{28,20},{1,9},{5... | collective-permute-start | bytes 196616 | tf_op jit(solution)/shard_map/ppermute | solution.py:459
  20.6 8.1 %collective-permute-start.4 = (bf16[32,3072]{1,0:T(8,128)(2,1)S(1)}, bf16[32,3072]{1,0:T(8,128)(2,1)S(1)}, u32[]{:S(2)}, u32[]{:S(2)}) collective-permute-start(bf16[32,3072]{1,0:T(8,128)(2,1)S(1)} %collective-permute-done.2.refs_0_), channel_id=1, source_target_pairs={{0,1},{1,2},{2,3},{3,0},{4,5},{5,6},{6,7},{7,4},{8,9},{9,10},{10,1... | collective-permute-start | bytes 589832 | tf_op jit(solution)/shard_map/ppermute | solution.py:496
  24.3 8.1 %collective-permute-start.12 = (bf16[32,3072]{1,0:T(8,128)(2,1)S(1)}, bf16[32,3072]{1,0:T(8,128)(2,1)S(1)}, u32[]{:S(2)}, u32[]{:S(2)}) collective-permute-start(bf16[32,3072]{1,0:T(8,128)(2,1)S(1)} %collective-permute-done.3.refs_1_.whole), channel_id=1, source_target_pairs={{0,1},{1,2},{2,3},{3,0},{4,5},{5,6},{6,7},{7,4},{8,9},{9,10},{10,1... | collective-permute-start | bytes 589832 | tf_op jit(solution)/shard_map/ppermute | solution.py:496
  24.9 1.3 %collective-permute-start.8 = (bf16[64,512]{1,0:T(8,128)(2,1)S(1)}, bf16[64,512]{1,0:T(8,128)(2,1)S(1)}, u32[]{:S(2)}, u32[]{:S(2)}) collective-permute-start(bf16[64,512]{1,0:T(8,128)(2,1)S(1)} %get-tuple-element.74.refs_3_), channel_id=1, source_target_pairs={{0,4},{4,0},{8,12},{12,8},{16,20},{20,16},{24,28},{28,24},{1,5},{5... | collective-permute-start | bytes 196616 | tf_op jit(solution)/shard_map/ppermute | solution.py:466
  25.0 1.4 %collective-permute-start.9 = (bf16[64,512]{1,0:T(8,128)(2,1)S(1)}, bf16[64,512]{1,0:T(8,128)(2,1)S(1)}, u32[]{:S(2)}, u32[]{:S(2)}) collective-permute-start(bf16[64,512]{1,0:T(8,128)(2,1)S(1)} %collective-permute-done.5.refs_5_), channel_id=1, source_target_pairs={{0,4},{4,0},{8,12},{12,8},{16,20},{20,16},{24,28},{28,24},{1,5},{5... | collective-permute-start | bytes 196616 | tf_op jit(solution)/shard_map/ppermute | solution.py:466
  25.5 1.3 %collective-permute-start.10 = (bf16[64,512]{1,0:T(8,128)(2,1)S(1)}, bf16[64,512]{1,0:T(8,128)(2,1)S(1)}, u32[]{:S(2)}, u32[]{:S(2)}) collective-permute-start(bf16[64,512]{1,0:T(8,128)(2,1)S(1)} %collective-permute-done.6.refs_7_), channel_id=1, source_target_pairs={{0,4},{4,0},{8,12},{12,8},{16,20},{20,16},{24,28},{28,24},{1,5},{5... | collective-permute-start | bytes 196616 | tf_op jit(solution)/shard_map/ppermute | solution.py:466
  26.3 1.3 %collective-permute-start.11 = (bf16[64,512]{1,0:T(8,128)(2,1)S(1)}, bf16[64,512]{1,0:T(8,128)(2,1)S(1)}, u32[]{:S(2)}, u32[]{:S(2)}) collective-permute-start(bf16[64,512]{1,0:T(8,128)(2,1)S(1)} %collective-permute-done.7.refs_9_), channel_id=1, source_target_pairs={{0,4},{4,0},{8,12},{12,8},{16,20},{20,16},{24,28},{28,24},{1,5},{5... | collective-permute-start | bytes 196616 | tf_op jit(solution)/shard_map/ppermute | solution.py:466
  33.1 5.7 %collective-permute-start.18 = (bf16[64,512]{1,0:T(8,128)(2,1)S(1)}, bf16[64,512]{1,0:T(8,128)(2,1)S(1)}, u32[]{:S(2)}, u32[]{:S(2)}) collective-permute-start(bf16[64,512]{1,0:T(8,128)(2,1)S(1)} %finish.1.refs_0_), channel_id=1, source_target_pairs={{0,24},{4,28},{8,16},{12,20},{16,8},{20,12},{24,0},{28,4},{1,25},{... | collective-permute-start | bytes 196616 | tf_op jit(solution)/shard_map/ppermute | solution.py:459
  35.7 4.3 %collective-permute-start.16 = (bf16[64,512]{1,0:T(8,128)(2,1)S(1)}, bf16[64,512]{1,0:T(8,128)(2,1)S(1)}, u32[]{:S(2)}, u32[]{:S(2)}) collective-permute-start(bf16[64,512]{1,0:T(8,128)(2,1)S(1)} %finish.1.refs_0_), channel_id=1, source_target_pairs={{0,16},{4,20},{8,24},{12,28},{16,0},{20,4},{24,8},{28,12},{1,17},{... | collective-permute-start | bytes 196616 | tf_op jit(solution)/shard_map/ppermute | solution.py:459
  36.2 4.3 %collective-permute-start.14 = (bf16[64,512]{1,0:T(8,128)(2,1)S(1)}, bf16[64,512]{1,0:T(8,128)(2,1)S(1)}, u32[]{:S(2)}, u32[]{:S(2)}) collective-permute-start(bf16[64,512]{1,0:T(8,128)(2,1)S(1)} %finish.1.refs_0_), channel_id=1, source_target_pairs={{0,8},{4,12},{8,0},{12,4},{16,24},{20,28},{24,16},{28,20},{1,9},{5... | collective-permute-start | bytes 196616 | tf_op jit(solution)/shard_map/ppermute | solution.py:459
  36.7 3.8 %collective-permute-start.13 = (bf16[64,512]{1,0:T(8,128)(2,1)S(1)}, bf16[64,512]{1,0:T(8,128)(2,1)S(1)}, u32[]{:S(2)}, u32[]{:S(2)}) collective-permute-start(bf16[64,512]{1,0:T(8,128)(2,1)S(1)} %finish.1.refs_0_), channel_id=1, source_target_pairs={{0,4},{4,0},{8,12},{12,8},{16,20},{20,16},{24,28},{28,24},{1,5},{5... | collective-permute-start | bytes 196616 | tf_op jit(solution)/shard_map/ppermute | solution.py:466
  38.8 1.6 %collective-permute-start.19 = (bf16[64,512]{1,0:T(8,128)(2,1)S(1)}, bf16[64,512]{1,0:T(8,128)(2,1)S(1)}, u32[]{:S(2)}, u32[]{:S(2)}) collective-permute-start(bf16[64,512]{1,0:T(8,128)(2,1)S(1)} %collective-permute-done.18.refs_6_), channel_id=1, source_target_pairs={{0,4},{4,0},{8,12},{12,8},{16,20},{20,16},{24,28},{28,24},{1,5},{5... | collective-permute-start | bytes 196616 | tf_op jit(solution)/shard_map/ppermute | solution.py:466
  39.9 1.3 %collective-permute-start.17 = (bf16[64,512]{1,0:T(8,128)(2,1)S(1)}, bf16[64,512]{1,0:T(8,128)(2,1)S(1)}, u32[]{:S(2)}, u32[]{:S(2)}) collective-permute-start(bf16[64,512]{1,0:T(8,128)(2,1)S(1)} %collective-permute-done.16.refs_4_), channel_id=1, source_target_pairs={{0,4},{4,0},{8,12},{12,8},{16,20},{20,16},{24,28},{28,24},{1,5},{5... | collective-permute-start | bytes 196616 | tf_op jit(solution)/shard_map/ppermute | solution.py:466
  40.4 1.3 %collective-permute-start.15 = (bf16[64,512]{1,0:T(8,128)(2,1)S(1)}, bf16[64,512]{1,0:T(8,128)(2,1)S(1)}, u32[]{:S(2)}, u32[]{:S(2)}) collective-permute-start(bf16[64,512]{1,0:T(8,128)(2,1)S(1)} %collective-permute-done.14.refs_2_), channel_id=1, source_target_pairs={{0,4},{4,0},{8,12},{12,8},{16,20},{20,16},{24,28},{28,24},{1,5},{5... | collective-permute-start | bytes 196616 | tf_op jit(solution)/shard_map/ppermute | solution.py:466
  42.3 4.8 %collective-permute-start.20 = (bf16[32,256]{1,0:T(8,128)(2,1)S(1)}, bf16[32,256]{1,0:T(8,128)(2,1)S(1)}, u32[]{:S(2)}, u32[]{:S(2)}) collective-permute-start(bf16[32,256]{1,0:T(8,128)(2,1)S(1)} %get-tuple-element.92), channel_id=1, source_target_pairs={{0,2},{1,3},{2,0},{3,1},{4,6},{5,7},{6,4},{7,5},{8,10},{9,11},{10,... | collective-permute-start | bytes 49160 | tf_op jit(solution)/shard_map/ppermute | solution.py:512
  42.9 5.6 %collective-permute-start.21 = (bf16[32,256]{1,0:T(8,128)(2,1)S(1)}, bf16[32,256]{1,0:T(8,128)(2,1)S(1)}, u32[]{:S(2)}, u32[]{:S(2)}) collective-permute-start(bf16[32,256]{1,0:T(8,128)(2,1)S(1)} %get-tuple-element.93), channel_id=1, source_target_pairs={{0,3},{1,2},{2,1},{3,0},{4,7},{5,6},{6,5},{7,4},{8,11},{9,10},{10,... | collective-permute-start | bytes 49160 | tf_op jit(solution)/shard_map/ppermute | solution.py:512
  44.6 3.9 %collective-permute-start.22 = (bf16[32,256]{1,0:T(8,128)(2,1)S(1)}, bf16[32,256]{1,0:T(8,128)(2,1)S(1)}, u32[]{:S(2)}, u32[]{:S(2)}) collective-permute-start(bf16[32,256]{1,0:T(8,128)(2,1)S(1)} %get-tuple-element.94), channel_id=1, source_target_pairs={{0,1},{1,0},{2,3},{3,2},{4,5},{5,4},{6,7},{7,6},{8,9},{9,8},{10,11... | collective-permute-start | bytes 49160 | tf_op jit(solution)/shard_map/ppermute | solution.py:512

commit v9 on v8

--- a/solution.py
+++ b/solution.py
@@ -228,7 +228,7 @@
         shift = gain[1:2, chunks[k]]
         high = shift.astype(jnp.bfloat16).astype(jnp.float32)
         added = jnp.where(row == 0, high, jnp.where(row == 1, shift - high, 0.0))
-        unscaled = piece[...].astype(jnp.float32) * gain[0:1, chunks[k]]
+        unscaled = piece[...].astype(jnp.float32) * (gain[0:1, chunks[k]] * 0.125)
         stacked.append(
             jnp.concatenate(
                 [
@@ -284,7 +284,7 @@
         shift = start[2 * rows : 2 * rows + 1, cols] + start[2 * rows + 1 : 2 * rows + 2, cols]
         total = jnp.dot(lines, weight[chunk, :], preferred_element_type=jnp.float32)
         out[:rows, cols] = (total[:rows] + start[:rows, cols]).astype(jnp.bfloat16)
-        known = start[rows : 2 * rows, cols] * scale + shift
+        known = start[rows : 2 * rows, cols] * (scale * 8.0) + shift
         out[rows:, cols] = (total[rows:] + known).astype(jnp.bfloat16)
 
 
@@ -301,12 +301,12 @@
     )(*near(whole, piece, gain, *weights, start))
 
 
-def bias_of(sources, mine, seg_col, seg_row):
+def barred_of(sources, mine, seg_col, seg_row):
     here = mine[0]
     clip = jnp.concatenate(
         [seg_row + jnp.where((here ^ m) <= here, 0, 1000) for m in range(sources)], axis=1
     )
-    return jnp.where(seg_col == clip, 0.0, -1e30)
+    return jnp.where(seg_col == clip, 0.0, 1.0)
 
 
 def stack(blocks, out):
@@ -320,16 +320,17 @@
     return [slice(start, start + block) for start in range(0, tokc, block)]
 
 
-def weigh(queries, keys, values, bias, floors):
+def weigh(queries, keys, values, barred, floors):
     scores = [
         lax.dot_general(q, k, (((1,), (1,)), ((), ())), preferred_element_type=jnp.float32)
         for q, k in zip(queries, keys)
     ]
-    scores = [s * (1.0 / math.sqrt(HD)) + bias for s in scores]
+    allowed = barred == 0.0
+    scores = [jnp.where(allowed, s * (1.0 / math.sqrt(HD)), -1e30) for s in scores]
     bests = [jnp.max(s, axis=-1, keepdims=True) for s in scores]
     if floors is not None:
         bests = [jnp.maximum(best, floor) for best, floor in zip(bests, floors)]
-    weights = [jnp.exp(s - best) for s, best in zip(scores, bests)]
+    weights = [jnp.where(allowed, jnp.exp(s - best), 0.0) for s, best in zip(scores, bests)]
     sums = [
         jnp.dot(w.astype(jnp.bfloat16), v, preferred_element_type=jnp.float32)
         for w, v in zip(weights, values)
@@ -345,7 +346,7 @@
 def attend_early_kernel(parts, sources, mine, seg_col, seg_row, *refs):
     queries, refs = refs[:parts], refs[parts:]
     early, refs = refs[:sources], refs[sources:]
-    q_all, sums, bests, totals, bias_late, kv_all = refs
+    q_all, sums, bests, totals, barred_late, kv_all = refs
     filled = 0
     for query in queries:
         q_all[filled : filled + query.shape[0], :] = query[...]
@@ -355,19 +356,19 @@
     heads = q_all.shape[1] // HD
     every = slice(0, kv_all.shape[0])
     for span in blocks_of(q_all.shape[0]):
-        bias = bias_of(sources, mine, seg_col[span, :], seg_row[:, :many])
+        barred = barred_of(sources, mine, seg_col[span, :], seg_row[:, :many])
         state = weigh(
             columns(q_all, span, heads),
             columns(kv_all, every, heads),
             columns(kv_all, every, heads, heads * HD),
-            bias,
+            barred,
             None,
         )
         for h, (best, total, summed) in enumerate(zip(*state)):
             bests[span, h * HD : (h + 1) * HD] = jnp.broadcast_to(best, summed.shape)
             totals[span, h * HD : (h + 1) * HD] = jnp.broadcast_to(total, summed.shape)
             sums[span, h * HD : (h + 1) * HD] = summed
-        bias_late[span, :] = bias_of(sources, mine, seg_col[span, :], seg_row[:, many:])
+        barred_late[span, :] = barred_of(sources, mine, seg_col[span, :], seg_row[:, many:])
 
 
 def attend_early(mine, seg_col, seg_row, queries, early):
@@ -386,7 +387,7 @@
     )(mine, *near(seg_col, seg_row, *queries, *early))
 
 
-def attend_kernel(shards, sources, place, q_all, sums, bests, totals, bias, *refs):
+def attend_kernel(shards, sources, place, q_all, sums, bests, totals, barred, *refs):
     late, outs, kv_all, held = refs[:sources], refs[sources:-2], refs[-2], refs[-1]
     tokc, width = q_all.shape
     rows = tokc // shards
@@ -399,7 +400,7 @@
             columns(q_all, span, heads),
             columns(kv_all, every, heads),
             columns(kv_all, every, heads, heads * HD),
-            bias[span, :],
+            barred[span, :],
             floors,
         )
         before = zip(floors, columns(totals, span, heads), columns(sums, span, heads))

time: 49.3 us -> 49.4 us (level)
  no operation moved by 1% of the time
where the time goes in v9:
time: 49.4 us; the launch traced here: 49.2 us
  starting transfers between devices  20.4 us (41%)
  waiting for transfers between devices  15.5 us (31%)
  Pallas kernels  12.6 us (26%)
  between operations  0.71 us (1%)
    ppermute x6, starting transfers between devices, across_chips(): lax.ppermute(block, 'group', [(i, i ^ m) for i in range(groups)])  7.06 us
    ppermute x4, starting transfers between devices, per_device(): pieces = [lax.ppermute(piece, 'dp', ring) for piece in pieces]  6.16 us
    pallas_call x1, Pallas kernels, begin(): pl.pallas_call(functools.partial(begin_kernel, shards), in_specs=[IN_SMEM...  5.38 us
    ppermute x2, waiting for transfers between devices, per_device(): moved = [lax.ppermute(piece, 'dp', ring) for piece in pieces]  4 us
    ppermute x3, starting transfers between devices, per_device(): lax.ppermute(results[s], 'dp', [(i, i ^ s) for i in range(shards)])  3.55 us
    ppermute x4, waiting for transfers between devices, per_device(): pieces = [lax.ppermute(piece, 'dp', ring) for piece in pieces]  3.47 us
    ppermute x8, waiting for transfers between devices, across_cores(): lax.ppermute(block, 'group', swap)  3.01 us
    ppermute x2, starting transfers between devices, per_device(): moved = [lax.ppermute(piece, 'dp', ring) for piece in pieces]  2.84 us
  transfers between devices with their start and end apart: 23, of which 15 were waited for; matrix products, arithmetic and copies ran while one was open for 0% of the time, Pallas kernels for 19%

profile of v9, /device:TPU:0, one launch (start us, length us, event | category | flops | bytes accessed | tf_op | source)
XLA Modules:
  0.0 49.2 jit_solution(5852937486014960524)
XLA Ops:
  0.0 1.0 %split.1 = (bf16[32,3072]{1,0:T(8,128)(2,1)S(1)}, bf16[32,3072]{1,0:T(8,128)(2,1)S(1)}) custom-call(bf16[1,32,6144]{2,1,0:T(8,128)(2,1)} %x_hbm), custom_call_target="tpu_custom_call" | custom-call | tf_op jit(solution)/shard_map/split/pallas_call | solution.py:58
  1.0 3.1 %collective-permute-start = (bf16[32,3072]{1,0:T(8,128)(2,1)S(1)}, bf16[32,3072]{1,0:T(8,128)(2,1)S(1)}, u32[]{:S(2)}, u32[]{:S(2)}) collective-permute-start(bf16[32,3072]{1,0:T(8,128)(2,1)S(1)} %get-tuple-element.53.refs_3_), channel_id=1, source_target_pairs={{0,1},{1,2},{2,3},{3,0},{4,5},{5,6},{6,7},{7,4},{8,9},{9,10},{10,1... | collective-permute-start | bytes 589832 | tf_op jit(solution)/shard_map/ppermute | solution.py:485
  4.1 1.6 %collective-permute-start.1 = (bf16[32,3072]{1,0:T(8,128)(2,1)S(1)}, bf16[32,3072]{1,0:T(8,128)(2,1)S(1)}, u32[]{:S(2)}, u32[]{:S(2)}) collective-permute-start(bf16[32,3072]{1,0:T(8,128)(2,1)S(1)} %get-tuple-element.54.refs_4_), channel_id=1, source_target_pairs={{0,1},{1,2},{2,3},{3,0},{4,5},{5,6},{6,7},{7,4},{8,9},{9,10},{10,1... | collective-permute-start | bytes 589832 | tf_op jit(solution)/shard_map/ppermute | solution.py:485
  6.3 5.4 %begin.1 = (bf16[32,256]{1,0:T(8,128)(2,1)S(1)}, bf16[32,512]{1,0:T(8,128)(2,1)S(1)}, bf16[6144,256]{1,0:T(8,128)(2,1)S(1)}, bf16[6144,256]{1,0:T(8,128)(2,1)S(1...) custom-call(s32[1]{0:T(128)} %bitcast.place, ...), custom_call_target="tpu_custom_call" | custom-call | tf_op jit(solution)/shard_map/begin/pallas_call | solution.py:150
  11.7 0.1 collective-permute-done.refs_0_
  11.9 1.5 %collective-permute-start.2 = (bf16[32,3072]{1,0:T(8,128)(2,1)S(1)}, bf16[32,3072]{1,0:T(8,128)(2,1)S(1)}, u32[]{:S(2)}, u32[]{:S(2)}) collective-permute-start(bf16[32,3072]{1,0:T(8,128)(2,1)S(1)} %collective-permute-done.refs_0_), channel_id=1, source_target_pairs={{0,1},{1,2},{2,3},{3,0},{4,5},{5,6},{6,7},{7,4},{8,9},{9,10},{10,1... | collective-permute-start | bytes 589832 | tf_op jit(solution)/shard_map/ppermute | solution.py:490
  13.4 1.9 %collective-permute-done.1.refs_1_ = bf16[32,3072]{1,0:T(8,128)(2,1)S(1)} collective-permute-done((bf16[32,3072]{1,0:T(8,128)(2,1)S(1)}, bf16[32,3072]{1,0:T(8,128)(2,1)S(1)}, u32[]{:S(2)}, u32[]{:S(2)}) %collective-permute-start.1) | collective-permute-done | bytes 196640 | tf_op jit(solution)/shard_map/ppermute | solution.py:485
  15.3 1.9 %project.2 = (bf16[32,256]{1,0:T(8,128)(2,1)S(1)}, bf16[64,512]{1,0:T(8,128)(2,1)S(1)}) custom-call(bf16[32,3072]{1,0:T(8,128)(2,1)S(1)} %collective-permute-done.refs_0_, bf16[32,3072]{1,0:T(8,128)(2,1)S(1)} %collective-permute-done.1.refs_1_, f32[2,6144]{1,0:T(2,128)S(1)} %get-tuple-element.73.refs_2_.refs_3_.gain.refs_4_, ...), custom_call_target="tpu_custom_call" | custom-call | tf_op jit(solution)/shard_map/project/pallas_call | solution.py:207
  17.1 2.5 %collective-permute-start.7 = (bf16[64,512]{1,0:T(8,128)(2,1)S(1)}, bf16[64,512]{1,0:T(8,128)(2,1)S(1)}, u32[]{:S(2)}, u32[]{:S(2)}) collective-permute-start(bf16[64,512]{1,0:T(8,128)(2,1)S(1)} %get-tuple-element.74.refs_3_), channel_id=1, source_target_pairs={{0,24},{4,28},{8,16},{12,20},{16,8},{20,12},{24,0},{28,4},{1,25},{... | collective-permute-start | bytes 196616 | tf_op jit(solution)/shard_map/ppermute | solution.py:460
  19.6 0.5 %collective-permute-start.6 = (bf16[64,512]{1,0:T(8,128)(2,1)S(1)}, bf16[64,512]{1,0:T(8,128)(2,1)S(1)}, u32[]{:S(2)}, u32[]{:S(2)}) collective-permute-start(bf16[64,512]{1,0:T(8,128)(2,1)S(1)} %get-tuple-element.74.refs_3_), channel_id=1, source_target_pairs={{0,16},{4,20},{8,24},{12,28},{16,0},{20,4},{24,8},{28,12},{1,17},{... | collective-permute-start | bytes 196616 | tf_op jit(solution)/shard_map/ppermute | solution.py:460
  20.1 0.5 %collective-permute-start.5 = (bf16[64,512]{1,0:T(8,128)(2,1)S(1)}, bf16[64,512]{1,0:T(8,128)(2,1)S(1)}, u32[]{:S(2)}, u32[]{:S(2)}) collective-permute-start(bf16[64,512]{1,0:T(8,128)(2,1)S(1)} %get-tuple-element.74.refs_3_), channel_id=1, source_target_pairs={{0,8},{4,12},{8,0},{12,4},{16,24},{20,28},{24,16},{28,20},{1,9},{5... | collective-permute-start | bytes 196616 | tf_op jit(solution)/shard_map/ppermute | solution.py:460
  20.6 2.2 %collective-permute-start.4 = (bf16[32,3072]{1,0:T(8,128)(2,1)S(1)}, bf16[32,3072]{1,0:T(8,128)(2,1)S(1)}, u32[]{:S(2)}, u32[]{:S(2)}) collective-permute-start(bf16[32,3072]{1,0:T(8,128)(2,1)S(1)} %collective-permute-done.2.refs_0_), channel_id=1, source_target_pairs={{0,1},{1,2},{2,3},{3,0},{4,5},{5,6},{6,7},{7,4},{8,9},{9,10},{10,1... | collective-permute-start | bytes 589832 | tf_op jit(solution)/shard_map/ppermute | solution.py:497
  22.8 1.5 %collective-permute-done.3.refs_1_.whole = bf16[32,3072]{1,0:T(8,128)(2,1)S(1)} collective-permute-done((bf16[32,3072]{1,0:T(8,128)(2,1)S(1)}, bf16[32,3072]{1,0:T(8,128)(2,1)S(1)}, u32[]{:S(2)}, u32[]{:S(2)}) %collective-permute-start.3) | collective-permute-done | bytes 196640 | tf_op jit(solution)/shard_map/ppermute | solution.py:490
  24.3 0.7 %collective-permute-start.12 = (bf16[32,3072]{1,0:T(8,128)(2,1)S(1)}, bf16[32,3072]{1,0:T(8,128)(2,1)S(1)}, u32[]{:S(2)}, u32[]{:S(2)}) collective-permute-start(bf16[32,3072]{1,0:T(8,128)(2,1)S(1)} %collective-permute-done.3.refs_1_.whole), channel_id=1, source_target_pairs={{0,1},{1,2},{2,3},{3,0},{4,5},{5,6},{6,7},{7,4},{8,9},{9,10},{10,1... | collective-permute-start | bytes 589832 | tf_op jit(solution)/shard_map/ppermute | solution.py:497
  24.9 0.0 collective-permute-done.7.refs_9_
  24.9 0.0 collective-permute-done.6.refs_7_
  24.9 0.0 collective-permute-done.5.refs_5_
  24.9 0.1 collective-permute-start.8
  25.0 0.5 %collective-permute-start.9 = (bf16[64,512]{1,0:T(8,128)(2,1)S(1)}, bf16[64,512]{1,0:T(8,128)(2,1)S(1)}, u32[]{:S(2)}, u32[]{:S(2)}) collective-permute-start(bf16[64,512]{1,0:T(8,128)(2,1)S(1)} %collective-permute-done.5.refs_5_), channel_id=1, source_target_pairs={{0,4},{4,0},{8,12},{12,8},{16,20},{20,16},{24,28},{28,24},{1,5},{5... | collective-permute-start | bytes 196616 | tf_op jit(solution)/shard_map/ppermute | solution.py:467
  25.5 0.1 collective-permute-start.10
  25.6 0.7 %collective-permute-done.8.refs_4_ = bf16[64,512]{1,0:T(8,128)(2,1)S(1)} collective-permute-done((bf16[64,512]{1,0:T(8,128)(2,1)S(1)}, bf16[64,512]{1,0:T(8,128)(2,1)S(1)}, u32[]{:S(2)}, u32[]{:S(2)}) %collective-permute-start.8) | collective-permute-done | bytes 65568 | tf_op jit(solution)/shard_map/ppermute | solution.py:467
  26.3 0.2 collective-permute-start.11
  26.4 0.3 collective-permute-done.10.refs_8_
  26.8 0.7 %collective-permute-done.11.refs_10_ = bf16[64,512]{1,0:T(8,128)(2,1)S(1)} collective-permute-done((bf16[64,512]{1,0:T(8,128)(2,1)S(1)}, bf16[64,512]{1,0:T(8,128)(2,1)S(1)}, u32[]{:S(2)}, u32[]{:S(2)}) %collective-permute-start.11) | collective-permute-done | bytes 65568 | tf_op jit(solution)/shard_map/ppermute | solution.py:467
  27.5 1.3 %collective-permute-done.4.refs_2_ = bf16[32,3072]{1,0:T(8,128)(2,1)S(1)} collective-permute-done((bf16[32,3072]{1,0:T(8,128)(2,1)S(1)}, bf16[32,3072]{1,0:T(8,128)(2,1)S(1)}, u32[]{:S(2)}, u32[]{:S(2)}) %collective-permute-start.4) | collective-permute-done | bytes 196640 | tf_op jit(solution)/shard_map/ppermute | solution.py:497
  28.8 0.8 %lead.1.refs_2_ = f32[80,640]{1,0:T(8,128)S(1)} custom-call(bf16[32,3072]{1,0:T(8,128)(2,1)S(1)} %collective-permute-done.2.refs_0_, bf16[32,3072]{1,0:T(8,128)(2,1)S(1)} %collective-permute-done.3.refs_1_.whole, bf16[32,3072]{1,0:T(8,128)(2,1)S(1)} %collective-permute-done.4.refs_2_, f32[2,6144]{1,0:T(2,128)S(1)} %get-tuple-element.73.refs_2_.refs_3_.gain.refs_4_, ...), custom_call_target="tpu_custom_call" | custom-call | tf_op jit(solution)/shard_map/lead/pallas_call | solution.py:257
  29.6 2.7 %collective-permute-done.12.piece.refs_3_ = bf16[32,3072]{1,0:T(8,128)(2,1)S(1)} collective-permute-done((bf16[32,3072]{1,0:T(8,128)(2,1)S(1)}, bf16[32,3072]{1,0:T(8,128)(2,1)S(1)}, u32[]{:S(2)}, u32[]{:S(2)}) %collective-permute-start.12) | collective-permute-done | bytes 196640 | tf_op jit(solution)/shard_map/ppermute | solution.py:497
  32.3 0.8 %finish.1.refs_0_ = bf16[64,512]{1,0:T(8,128)(2,1)S(1)} custom-call(bf16[32,3072]{1,0:T(8,128)(2,1)S(1)} %collective-permute-done.3.refs_1_.whole, bf16[32,3072]{1,0:T(8,128)(2,1)S(1)} %collective-permute-done.12.piece.refs_3_, f32[2,6144]{1,0:T(2,128)S(1)} %get-tuple-element.73.refs_2_.refs_3_.gain.refs_4_, ...), custom_call_target="tpu_custom_call" | custom-call | tf_op jit(solution)/shard_map/finish/pallas_call | solution.py:294
  33.1 2.5 %collective-permute-start.18 = (bf16[64,512]{1,0:T(8,128)(2,1)S(1)}, bf16[64,512]{1,0:T(8,128)(2,1)S(1)}, u32[]{:S(2)}, u32[]{:S(2)}) collective-permute-start(bf16[64,512]{1,0:T(8,128)(2,1)S(1)} %finish.1.refs_0_), channel_id=1, source_target_pairs={{0,24},{4,28},{8,16},{12,20},{16,8},{20,12},{24,0},{28,4},{1,25},{... | collective-permute-start | bytes 196616 | tf_op jit(solution)/shard_map/ppermute | solution.py:460
  35.7 0.5 %collective-permute-start.16 = (bf16[64,512]{1,0:T(8,128)(2,1)S(1)}, bf16[64,512]{1,0:T(8,128)(2,1)S(1)}, u32[]{:S(2)}, u32[]{:S(2)}) collective-permute-start(bf16[64,512]{1,0:T(8,128)(2,1)S(1)} %finish.1.refs_0_), channel_id=1, source_target_pairs={{0,16},{4,20},{8,24},{12,28},{16,0},{20,4},{24,8},{28,12},{1,17},{... | collective-permute-start | bytes 196616 | tf_op jit(solution)/shard_map/ppermute | solution.py:460
  36.2 0.5 %collective-permute-start.14 = (bf16[64,512]{1,0:T(8,128)(2,1)S(1)}, bf16[64,512]{1,0:T(8,128)(2,1)S(1)}, u32[]{:S(2)}, u32[]{:S(2)}) collective-permute-start(bf16[64,512]{1,0:T(8,128)(2,1)S(1)} %finish.1.refs_0_), channel_id=1, source_target_pairs={{0,8},{4,12},{8,0},{12,4},{16,24},{20,28},{24,16},{28,20},{1,9},{5... | collective-permute-start | bytes 196616 | tf_op jit(solution)/shard_map/ppermute | solution.py:460
  36.7 0.9 %project.3.refs_2_ = bf16[64,256]{1,0:T(8,128)(2,1)S(1)} custom-call(bf16[32,3072]{1,0:T(8,128)(2,1)S(1)} %collective-permute-done.2.refs_0_, bf16[32,3072]{1,0:T(8,128)(2,1)S(1)} %collective-permute-done.3.refs_1_.whole, bf16[32,3072]{1,0:T(8,128)(2,1)S(1)} %collective-permute-done.4.refs_2_, bf16[32,3072]{1,0:T(8,128)(2,1)S(1)} %collective-permute-done.12.piece.refs_3_, ...), custom_call_target="tpu_custom_call" | custom-call | tf_op jit(solution)/shard_map/project/pallas_call | solution.py:207
  37.6 0.5 %attend_early.1 = (bf16[128,256]{1,0:T(8,128)(2,1)S(1)}, f32[128,256]{1,0:T(8,128)S(1)}, f32[128,256]{1,0:T(8,128)S(1)}, f32[128,256]{1,0:T(8,128)S(1)}, f32[128,512]{1,0:T(8,128)S(1)}) custom-call(s32[1]{0:T(128)} %bitcast.1.mine, s32[128,1]{1,0:T(8,128)S(1)} %get-tuple-element.55.seg_col, s32[1,128]{1,0:T(1,128)S(1)} %get-tuple-element.56.seg_row, ...), custom_call_target="tpu_custom_call" | custom-call | tf_op jit(solution)/shard_map/attend_early/pallas_call | solution.py:377
  38.1 0.7 %collective-permute-done.18.refs_6_ = bf16[64,512]{1,0:T(8,128)(2,1)S(1)} collective-permute-done((bf16[64,512]{1,0:T(8,128)(2,1)S(1)}, bf16[64,512]{1,0:T(8,128)(2,1)S(1)}, u32[]{:S(2)}, u32[]{:S(2)}) %collective-permute-start.18) | collective-permute-done | bytes 65568 | tf_op jit(solution)/shard_map/ppermute | solution.py:460
  38.8 0.0 collective-permute-start.19
  38.9 1.1 %collective-permute-done.16.refs_4_ = bf16[64,512]{1,0:T(8,128)(2,1)S(1)} collective-permute-done((bf16[64,512]{1,0:T(8,128)(2,1)S(1)}, bf16[64,512]{1,0:T(8,128)(2,1)S(1)}, u32[]{:S(2)}, u32[]{:S(2)}) %collective-permute-start.16) | collective-permute-done | bytes 65568 | tf_op jit(solution)/shard_map/ppermute | solution.py:460
  39.9 0.5 %collective-permute-done.14.refs_2_ = bf16[64,512]{1,0:T(8,128)(2,1)S(1)} collective-permute-done((bf16[64,512]{1,0:T(8,128)(2,1)S(1)}, bf16[64,512]{1,0:T(8,128)(2,1)S(1)}, u32[]{:S(2)}, u32[]{:S(2)}) %collective-permute-start.14) | collective-permute-done | bytes 65568 | tf_op jit(solution)/shard_map/ppermute | solution.py:460
  40.4 0.0 collective-permute-start.15
  40.4 0.7 %collective-permute-done.17.refs_5_ = bf16[64,512]{1,0:T(8,128)(2,1)S(1)} collective-permute-done((bf16[64,512]{1,0:T(8,128)(2,1)S(1)}, bf16[64,512]{1,0:T(8,128)(2,1)S(1)}, u32[]{:S(2)}, u32[]{:S(2)}) %collective-permute-start.17) | collective-permute-done | bytes 65568 | tf_op jit(solution)/shard_map/ppermute | solution.py:467
  41.2 0.5 %collective-permute-done.15.refs_3_ = bf16[64,512]{1,0:T(8,128)(2,1)S(1)} collective-permute-done((bf16[64,512]{1,0:T(8,128)(2,1)S(1)}, bf16[64,512]{1,0:T(8,128)(2,1)S(1)}, u32[]{:S(2)}, u32[]{:S(2)}) %collective-permute-start.15) | collective-permute-done | bytes 65568 | tf_op jit(solution)/shard_map/ppermute | solution.py:467
  41.7 0.7 %attend.1 = (bf16[32,256]{1,0:T(8,128)(2,1)S(1)}, bf16[32,256]{1,0:T(8,128)(2,1)S(1)}, bf16[32,256]{1,0:T(8,128)(2,1)S(1)}, bf16[32,256]{1,0:T(8,128)(2,1)S(1)}) custom-call(s32[1]{0:T(128)} %bitcast.place, bf16[128,256]{1,0:T(8,128)(2,1)S(1)} %get-tuple-element.82.q_all, f32[128,256]{1,0:T(8,128)S(1)} %get-tuple-element.83.sums, ...), custom_call_target="tpu_custom_call" | custom-call | tf_op jit(solution)/shard_map/attend/pallas_call | solution.py:422
  42.3 0.6 %collective-permute-start.20 = (bf16[32,256]{1,0:T(8,128)(2,1)S(1)}, bf16[32,256]{1,0:T(8,128)(2,1)S(1)}, u32[]{:S(2)}, u32[]{:S(2)}) collective-permute-start(bf16[32,256]{1,0:T(8,128)(2,1)S(1)} %get-tuple-element.92), channel_id=1, source_target_pairs={{0,2},{1,3},{2,0},{3,1},{4,6},{5,7},{6,4},{7,5},{8,10},{9,11},{10,... | collective-permute-start | bytes 49160 | tf_op jit(solution)/shard_map/ppermute | solution.py:513
  42.9 1.8 %collective-permute-start.21 = (bf16[32,256]{1,0:T(8,128)(2,1)S(1)}, bf16[32,256]{1,0:T(8,128)(2,1)S(1)}, u32[]{:S(2)}, u32[]{:S(2)}) collective-permute-start(bf16[32,256]{1,0:T(8,128)(2,1)S(1)} %get-tuple-element.93), channel_id=1, source_target_pairs={{0,3},{1,2},{2,1},{3,0},{4,7},{5,6},{6,5},{7,4},{8,11},{9,10},{10,... | collective-permute-start | bytes 49160 | tf_op jit(solution)/shard_map/ppermute | solution.py:513
  44.7 1.2 %collective-permute-start.22 = (bf16[32,256]{1,0:T(8,128)(2,1)S(1)}, bf16[32,256]{1,0:T(8,128)(2,1)S(1)}, u32[]{:S(2)}, u32[]{:S(2)}) collective-permute-start(bf16[32,256]{1,0:T(8,128)(2,1)S(1)} %get-tuple-element.94), channel_id=1, source_target_pairs={{0,1},{1,0},{2,3},{3,2},{4,5},{5,4},{6,7},{7,6},{8,9},{9,8},{10,11... | collective-permute-start | bytes 49160 | tf_op jit(solution)/shard_map/ppermute | solution.py:513
  45.9 1.3 %collective-permute-done.20.refs_1_ = bf16[32,256]{1,0:T(8,128)(2,1)S(1)} collective-permute-done((bf16[32,256]{1,0:T(8,128)(2,1)S(1)}, bf16[32,256]{1,0:T(8,128)(2,1)S(1)}, u32[]{:S(2)}, u32[]{:S(2)}) %collective-permute-start.20) | collective-permute-done | bytes 16416 | tf_op jit(solution)/shard_map/ppermute | solution.py:513
  47.2 1.4 %collective-permute-done.21.refs_2_ = bf16[32,256]{1,0:T(8,128)(2,1)S(1)} collective-permute-done((bf16[32,256]{1,0:T(8,128)(2,1)S(1)}, bf16[32,256]{1,0:T(8,128)(2,1)S(1)}, u32[]{:S(2)}, u32[]{:S(2)}) %collective-permute-start.21) | collective-permute-done | bytes 16416 | tf_op jit(solution)/shard_map/ppermute | solution.py:513
  48.6 0.0 collective-permute-done.22.refs_3_
  48.6 0.6 %place.1 = bf16[1,32,1024]{2,1,0:T(8,128)(2,1)} custom-call(s32[1]{0:T(128)} %bitcast.place, bf16[32,256]{1,0:T(8,128)(2,1)S(1)} %get-tuple-element.91.refs_0_, bf16[32,256]{1,0:T(8,128)(2,1)S(1)} %collective-permute-done.20.refs_1_, bf16[32,256]{1,0:T(8,128)(2,1)S(1)} %collective-permute-done.21.refs_2_, bf16[32,256]{1,0:T(8,128)(2,1)S(1)} %collective-permute-done.22.refs_3_), custom_call_target="tpu_custom_call" | custom-call | tf_op jit(solution)/shard_map/place/pallas_call | solution.py:448
  (7 shorter events, 0.0 us)
Async XLA Ops:
  1.0 10.8 %collective-permute-start = (bf16[32,3072]{1,0:T(8,128)(2,1)S(1)}, bf16[32,3072]{1,0:T(8,128)(2,1)S(1)}, u32[]{:S(2)}, u32[]{:S(2)}) collective-permute-start(bf16[32,3072]{1,0:T(8,128)(2,1)S(1)} %get-tuple-element.53.refs_3_), channel_id=1, source_target_pairs={{0,1},{1,2},{2,3},{3,0},{4,5},{5,6},{6,7},{7,4},{8,9},{9,10},{10,1... | collective-permute-start | bytes 589832 | tf_op jit(solution)/shard_map/ppermute | solution.py:485
  4.1 11.1 %collective-permute-start.1 = (bf16[32,3072]{1,0:T(8,128)(2,1)S(1)}, bf16[32,3072]{1,0:T(8,128)(2,1)S(1)}, u32[]{:S(2)}, u32[]{:S(2)}) collective-permute-start(bf16[32,3072]{1,0:T(8,128)(2,1)S(1)} %get-tuple-element.54.refs_4_), channel_id=1, source_target_pairs={{0,1},{1,2},{2,3},{3,0},{4,5},{5,6},{6,7},{7,4},{8,9},{9,10},{10,1... | collective-permute-start | bytes 589832 | tf_op jit(solution)/shard_map/ppermute | solution.py:485
  11.9 8.8 %collective-permute-start.2 = (bf16[32,3072]{1,0:T(8,128)(2,1)S(1)}, bf16[32,3072]{1,0:T(8,128)(2,1)S(1)}, u32[]{:S(2)}, u32[]{:S(2)}) collective-permute-start(bf16[32,3072]{1,0:T(8,128)(2,1)S(1)} %collective-permute-done.refs_0_), channel_id=1, source_target_pairs={{0,1},{1,2},{2,3},{3,0},{4,5},{5,6},{6,7},{7,4},{8,9},{9,10},{10,1... | collective-permute-start | bytes 589832 | tf_op jit(solution)/shard_map/ppermute | solution.py:490
  15.3 9.0 %collective-permute-start.3 = (bf16[32,3072]{1,0:T(8,128)(2,1)S(1)}, bf16[32,3072]{1,0:T(8,128)(2,1)S(1)}, u32[]{:S(2)}, u32[]{:S(2)}) collective-permute-start(bf16[32,3072]{1,0:T(8,128)(2,1)S(1)} %collective-permute-done.1.refs_1_), channel_id=1, source_target_pairs={{0,1},{1,2},{2,3},{3,0},{4,5},{5,6},{6,7},{7,4},{8,9},{9,10},{10,1... | collective-permute-start | bytes 589832 | tf_op jit(solution)/shard_map/ppermute | solution.py:490
  17.1 7.8 %collective-permute-start.7 = (bf16[64,512]{1,0:T(8,128)(2,1)S(1)}, bf16[64,512]{1,0:T(8,128)(2,1)S(1)}, u32[]{:S(2)}, u32[]{:S(2)}) collective-permute-start(bf16[64,512]{1,0:T(8,128)(2,1)S(1)} %get-tuple-element.74.refs_3_), channel_id=1, source_target_pairs={{0,24},{4,28},{8,16},{12,20},{16,8},{20,12},{24,0},{28,4},{1,25},{... | collective-permute-start | bytes 196616 | tf_op jit(solution)/shard_map/ppermute | solution.py:460
  19.6 5.4 %collective-permute-start.6 = (bf16[64,512]{1,0:T(8,128)(2,1)S(1)}, bf16[64,512]{1,0:T(8,128)(2,1)S(1)}, u32[]{:S(2)}, u32[]{:S(2)}) collective-permute-start(bf16[64,512]{1,0:T(8,128)(2,1)S(1)} %get-tuple-element.74.refs_3_), channel_id=1, source_target_pairs={{0,16},{4,20},{8,24},{12,28},{16,0},{20,4},{24,8},{28,12},{1,17},{... | collective-permute-start | bytes 196616 | tf_op jit(solution)/shard_map/ppermute | solution.py:460
  20.1 4.8 %collective-permute-start.5 = (bf16[64,512]{1,0:T(8,128)(2,1)S(1)}, bf16[64,512]{1,0:T(8,128)(2,1)S(1)}, u32[]{:S(2)}, u32[]{:S(2)}) collective-permute-start(bf16[64,512]{1,0:T(8,128)(2,1)S(1)} %get-tuple-element.74.refs_3_), channel_id=1, source_target_pairs={{0,8},{4,12},{8,0},{12,4},{16,24},{20,28},{24,16},{28,20},{1,9},{5... | collective-permute-start | bytes 196616 | tf_op jit(solution)/shard_map/ppermute | solution.py:460
  20.6 8.1 %collective-permute-start.4 = (bf16[32,3072]{1,0:T(8,128)(2,1)S(1)}, bf16[32,3072]{1,0:T(8,128)(2,1)S(1)}, u32[]{:S(2)}, u32[]{:S(2)}) collective-permute-start(bf16[32,3072]{1,0:T(8,128)(2,1)S(1)} %collective-permute-done.2.refs_0_), channel_id=1, source_target_pairs={{0,1},{1,2},{2,3},{3,0},{4,5},{5,6},{6,7},{7,4},{8,9},{9,10},{10,1... | collective-permute-start | bytes 589832 | tf_op jit(solution)/shard_map/ppermute | solution.py:497
  24.3 8.1 %collective-permute-start.12 = (bf16[32,3072]{1,0:T(8,128)(2,1)S(1)}, bf16[32,3072]{1,0:T(8,128)(2,1)S(1)}, u32[]{:S(2)}, u32[]{:S(2)}) collective-permute-start(bf16[32,3072]{1,0:T(8,128)(2,1)S(1)} %collective-permute-done.3.refs_1_.whole), channel_id=1, source_target_pairs={{0,1},{1,2},{2,3},{3,0},{4,5},{5,6},{6,7},{7,4},{8,9},{9,10},{10,1... | collective-permute-start | bytes 589832 | tf_op jit(solution)/shard_map/ppermute | solution.py:497
  24.9 1.3 %collective-permute-start.8 = (bf16[64,512]{1,0:T(8,128)(2,1)S(1)}, bf16[64,512]{1,0:T(8,128)(2,1)S(1)}, u32[]{:S(2)}, u32[]{:S(2)}) collective-permute-start(bf16[64,512]{1,0:T(8,128)(2,1)S(1)} %get-tuple-element.74.refs_3_), channel_id=1, source_target_pairs={{0,4},{4,0},{8,12},{12,8},{16,20},{20,16},{24,28},{28,24},{1,5},{5... | collective-permute-start | bytes 196616 | tf_op jit(solution)/shard_map/ppermute | solution.py:467
  25.0 1.4 %collective-permute-start.9 = (bf16[64,512]{1,0:T(8,128)(2,1)S(1)}, bf16[64,512]{1,0:T(8,128)(2,1)S(1)}, u32[]{:S(2)}, u32[]{:S(2)}) collective-permute-start(bf16[64,512]{1,0:T(8,128)(2,1)S(1)} %collective-permute-done.5.refs_5_), channel_id=1, source_target_pairs={{0,4},{4,0},{8,12},{12,8},{16,20},{20,16},{24,28},{28,24},{1,5},{5... | collective-permute-start | bytes 196616 | tf_op jit(solution)/shard_map/ppermute | solution.py:467
  25.5 1.3 %collective-permute-start.10 = (bf16[64,512]{1,0:T(8,128)(2,1)S(1)}, bf16[64,512]{1,0:T(8,128)(2,1)S(1)}, u32[]{:S(2)}, u32[]{:S(2)}) collective-permute-start(bf16[64,512]{1,0:T(8,128)(2,1)S(1)} %collective-permute-done.6.refs_7_), channel_id=1, source_target_pairs={{0,4},{4,0},{8,12},{12,8},{16,20},{20,16},{24,28},{28,24},{1,5},{5... | collective-permute-start | bytes 196616 | tf_op jit(solution)/shard_map/ppermute | solution.py:467
  26.3 1.3 %collective-permute-start.11 = (bf16[64,512]{1,0:T(8,128)(2,1)S(1)}, bf16[64,512]{1,0:T(8,128)(2,1)S(1)}, u32[]{:S(2)}, u32[]{:S(2)}) collective-permute-start(bf16[64,512]{1,0:T(8,128)(2,1)S(1)} %collective-permute-done.7.refs_9_), channel_id=1, source_target_pairs={{0,4},{4,0},{8,12},{12,8},{16,20},{20,16},{24,28},{28,24},{1,5},{5... | collective-permute-start | bytes 196616 | tf_op jit(solution)/shard_map/ppermute | solution.py:467
  33.1 5.7 %collective-permute-start.18 = (bf16[64,512]{1,0:T(8,128)(2,1)S(1)}, bf16[64,512]{1,0:T(8,128)(2,1)S(1)}, u32[]{:S(2)}, u32[]{:S(2)}) collective-permute-start(bf16[64,512]{1,0:T(8,128)(2,1)S(1)} %finish.1.refs_0_), channel_id=1, source_target_pairs={{0,24},{4,28},{8,16},{12,20},{16,8},{20,12},{24,0},{28,4},{1,25},{... | collective-permute-start | bytes 196616 | tf_op jit(solution)/shard_map/ppermute | solution.py:460
  35.7 4.3 %collective-permute-start.16 = (bf16[64,512]{1,0:T(8,128)(2,1)S(1)}, bf16[64,512]{1,0:T(8,128)(2,1)S(1)}, u32[]{:S(2)}, u32[]{:S(2)}) collective-permute-start(bf16[64,512]{1,0:T(8,128)(2,1)S(1)} %finish.1.refs_0_), channel_id=1, source_target_pairs={{0,16},{4,20},{8,24},{12,28},{16,0},{20,4},{24,8},{28,12},{1,17},{... | collective-permute-start | bytes 196616 | tf_op jit(solution)/shard_map/ppermute | solution.py:460
  36.2 4.3 %collective-permute-start.14 = (bf16[64,512]{1,0:T(8,128)(2,1)S(1)}, bf16[64,512]{1,0:T(8,128)(2,1)S(1)}, u32[]{:S(2)}, u32[]{:S(2)}) collective-permute-start(bf16[64,512]{1,0:T(8,128)(2,1)S(1)} %finish.1.refs_0_), channel_id=1, source_target_pairs={{0,8},{4,12},{8,0},{12,4},{16,24},{20,28},{24,16},{28,20},{1,9},{5... | collective-permute-start | bytes 196616 | tf_op jit(solution)/shard_map/ppermute | solution.py:460
  36.7 3.7 %collective-permute-start.13 = (bf16[64,512]{1,0:T(8,128)(2,1)S(1)}, bf16[64,512]{1,0:T(8,128)(2,1)S(1)}, u32[]{:S(2)}, u32[]{:S(2)}) collective-permute-start(bf16[64,512]{1,0:T(8,128)(2,1)S(1)} %finish.1.refs_0_), channel_id=1, source_target_pairs={{0,4},{4,0},{8,12},{12,8},{16,20},{20,16},{24,28},{28,24},{1,5},{5... | collective-permute-start | bytes 196616 | tf_op jit(solution)/shard_map/ppermute | solution.py:467
  38.8 1.6 %collective-permute-start.19 = (bf16[64,512]{1,0:T(8,128)(2,1)S(1)}, bf16[64,512]{1,0:T(8,128)(2,1)S(1)}, u32[]{:S(2)}, u32[]{:S(2)}) collective-permute-start(bf16[64,512]{1,0:T(8,128)(2,1)S(1)} %collective-permute-done.18.refs_6_), channel_id=1, source_target_pairs={{0,4},{4,0},{8,12},{12,8},{16,20},{20,16},{24,28},{28,24},{1,5},{5... | collective-permute-start | bytes 196616 | tf_op jit(solution)/shard_map/ppermute | solution.py:467
  39.9 1.3 %collective-permute-start.17 = (bf16[64,512]{1,0:T(8,128)(2,1)S(1)}, bf16[64,512]{1,0:T(8,128)(2,1)S(1)}, u32[]{:S(2)}, u32[]{:S(2)}) collective-permute-start(bf16[64,512]{1,0:T(8,128)(2,1)S(1)} %collective-permute-done.16.refs_4_), channel_id=1, source_target_pairs={{0,4},{4,0},{8,12},{12,8},{16,20},{20,16},{24,28},{28,24},{1,5},{5... | collective-permute-start | bytes 196616 | tf_op jit(solution)/shard_map/ppermute | solution.py:467
  40.4 1.3 %collective-permute-start.15 = (bf16[64,512]{1,0:T(8,128)(2,1)S(1)}, bf16[64,512]{1,0:T(8,128)(2,1)S(1)}, u32[]{:S(2)}, u32[]{:S(2)}) collective-permute-start(bf16[64,512]{1,0:T(8,128)(2,1)S(1)} %collective-permute-done.14.refs_2_), channel_id=1, source_target_pairs={{0,4},{4,0},{8,12},{12,8},{16,20},{20,16},{24,28},{28,24},{1,5},{5... | collective-permute-start | bytes 196616 | tf_op jit(solution)/shard_map/ppermute | solution.py:467
  42.3 4.8 %collective-permute-start.20 = (bf16[32,256]{1,0:T(8,128)(2,1)S(1)}, bf16[32,256]{1,0:T(8,128)(2,1)S(1)}, u32[]{:S(2)}, u32[]{:S(2)}) collective-permute-start(bf16[32,256]{1,0:T(8,128)(2,1)S(1)} %get-tuple-element.92), channel_id=1, source_target_pairs={{0,2},{1,3},{2,0},{3,1},{4,6},{5,7},{6,4},{7,5},{8,10},{9,11},{10,... | collective-permute-start | bytes 49160 | tf_op jit(solution)/shard_map/ppermute | solution.py:513
  42.9 5.6 %collective-permute-start.21 = (bf16[32,256]{1,0:T(8,128)(2,1)S(1)}, bf16[32,256]{1,0:T(8,128)(2,1)S(1)}, u32[]{:S(2)}, u32[]{:S(2)}) collective-permute-start(bf16[32,256]{1,0:T(8,128)(2,1)S(1)} %get-tuple-element.93), channel_id=1, source_target_pairs={{0,3},{1,2},{2,1},{3,0},{4,7},{5,6},{6,5},{7,4},{8,11},{9,10},{10,... | collective-permute-start | bytes 49160 | tf_op jit(solution)/shard_map/ppermute | solution.py:513
  44.7 3.9 %collective-permute-start.22 = (bf16[32,256]{1,0:T(8,128)(2,1)S(1)}, bf16[32,256]{1,0:T(8,128)(2,1)S(1)}, u32[]{:S(2)}, u32[]{:S(2)}) collective-permute-start(bf16[32,256]{1,0:T(8,128)(2,1)S(1)} %get-tuple-element.94), channel_id=1, source_target_pairs={{0,1},{1,0},{2,3},{3,2},{4,5},{5,4},{6,7},{7,6},{8,9},{9,8},{10,11... | collective-permute-start | bytes 49160 | tf_op jit(solution)/shard_map/ppermute | solution.py:513

commit v10 on v9

--- a/solution.py
+++ b/solution.py
@@ -504,7 +504,8 @@
     query = project(both, gain, weights, (0,))[0]
     queries.append(query)
     state = attend_early(mine, seg_col, seg_row, queries, early)
-    late[1:] = [lax.optimization_barrier((block, state[0]))[0] for block in late[1:]]
+    tail = [lax.optimization_barrier((block, state[0]))[0] for block in late[:0:-1]]
+    late[1:] = tail[::-1]
     late = across_cores(late, groups)
     results = attend(shards, place, state, late)
     landed = [results[0]]

time: 49.4 us -> 49.4 us (level)
  no operation moved by 1% of the time
where the time goes in v10:
time: 49.4 us; the launch traced here: 49.2 us
  starting transfers between devices  20.4 us (41%)
  waiting for transfers between devices  15.5 us (31%)
  Pallas kernels  12.6 us (26%)
  between operations  0.71 us (1%)
    ppermute x6, starting transfers between devices, across_chips(): lax.ppermute(block, 'group', [(i, i ^ m) for i in range(groups)])  7.06 us
    ppermute x4, starting transfers between devices, per_device(): pieces = [lax.ppermute(piece, 'dp', ring) for piece in pieces]  6.16 us
    pallas_call x1, Pallas kernels, begin(): pl.pallas_call(functools.partial(begin_kernel, shards), in_specs=[IN_SMEM...  5.38 us
    ppermute x2, waiting for transfers between devices, per_device(): moved = [lax.ppermute(piece, 'dp', ring) for piece in pieces]  4 us
    ppermute x3, starting transfers between devices, per_device(): lax.ppermute(results[s], 'dp', [(i, i ^ s) for i in range(shards)])  3.55 us
    ppermute x4, waiting for transfers between devices, per_device(): pieces = [lax.ppermute(piece, 'dp', ring) for piece in pieces]  3.47 us
    ppermute x8, waiting for transfers between devices, across_cores(): lax.ppermute(block, 'group', swap)  3.01 us
    ppermute x2, starting transfers between devices, per_device(): moved = [lax.ppermute(piece, 'dp', ring) for piece in pieces]  2.84 us
  transfers between devices with their start and end apart: 23, of which 15 were waited for; matrix products, arithmetic and copies ran while one was open for 0% of the time, Pallas kernels for 19%

profile of v10, /device:TPU:0, one launch (start us, length us, event | category | flops | bytes accessed | tf_op | source)
XLA Modules:
  0.0 49.2 jit_solution(5852937486014960524)
XLA Ops:
  0.0 1.0 %split.1 = (bf16[32,3072]{1,0:T(8,128)(2,1)S(1)}, bf16[32,3072]{1,0:T(8,128)(2,1)S(1)}) custom-call(bf16[1,32,6144]{2,1,0:T(8,128)(2,1)} %x_hbm), custom_call_target="tpu_custom_call" | custom-call | tf_op jit(solution)/shard_map/split/pallas_call | solution.py:58
  1.0 3.1 %collective-permute-start = (bf16[32,3072]{1,0:T(8,128)(2,1)S(1)}, bf16[32,3072]{1,0:T(8,128)(2,1)S(1)}, u32[]{:S(2)}, u32[]{:S(2)}) collective-permute-start(bf16[32,3072]{1,0:T(8,128)(2,1)S(1)} %get-tuple-element.53.refs_3_), channel_id=1, source_target_pairs={{0,1},{1,2},{2,3},{3,0},{4,5},{5,6},{6,7},{7,4},{8,9},{9,10},{10,1... | collective-permute-start | bytes 589832 | tf_op jit(solution)/shard_map/ppermute | solution.py:485
  4.1 1.6 %collective-permute-start.1 = (bf16[32,3072]{1,0:T(8,128)(2,1)S(1)}, bf16[32,3072]{1,0:T(8,128)(2,1)S(1)}, u32[]{:S(2)}, u32[]{:S(2)}) collective-permute-start(bf16[32,3072]{1,0:T(8,128)(2,1)S(1)} %get-tuple-element.54.refs_4_), channel_id=1, source_target_pairs={{0,1},{1,2},{2,3},{3,0},{4,5},{5,6},{6,7},{7,4},{8,9},{9,10},{10,1... | collective-permute-start | bytes 589832 | tf_op jit(solution)/shard_map/ppermute | solution.py:485
  6.3 5.4 %begin.1 = (bf16[32,256]{1,0:T(8,128)(2,1)S(1)}, bf16[32,512]{1,0:T(8,128)(2,1)S(1)}, bf16[6144,256]{1,0:T(8,128)(2,1)S(1)}, bf16[6144,256]{1,0:T(8,128)(2,1)S(1...) custom-call(s32[1]{0:T(128)} %bitcast.place, ...), custom_call_target="tpu_custom_call" | custom-call | tf_op jit(solution)/shard_map/begin/pallas_call | solution.py:150
  11.7 0.1 collective-permute-done.refs_0_
  11.9 1.5 %collective-permute-start.2 = (bf16[32,3072]{1,0:T(8,128)(2,1)S(1)}, bf16[32,3072]{1,0:T(8,128)(2,1)S(1)}, u32[]{:S(2)}, u32[]{:S(2)}) collective-permute-start(bf16[32,3072]{1,0:T(8,128)(2,1)S(1)} %collective-permute-done.refs_0_), channel_id=1, source_target_pairs={{0,1},{1,2},{2,3},{3,0},{4,5},{5,6},{6,7},{7,4},{8,9},{9,10},{10,1... | collective-permute-start | bytes 589832 | tf_op jit(solution)/shard_map/ppermute | solution.py:490
  13.4 1.9 %collective-permute-done.1.refs_1_ = bf16[32,3072]{1,0:T(8,128)(2,1)S(1)} collective-permute-done((bf16[32,3072]{1,0:T(8,128)(2,1)S(1)}, bf16[32,3072]{1,0:T(8,128)(2,1)S(1)}, u32[]{:S(2)}, u32[]{:S(2)}) %collective-permute-start.1) | collective-permute-done | bytes 196640 | tf_op jit(solution)/shard_map/ppermute | solution.py:485
  15.3 1.9 %project.2 = (bf16[32,256]{1,0:T(8,128)(2,1)S(1)}, bf16[64,512]{1,0:T(8,128)(2,1)S(1)}) custom-call(bf16[32,3072]{1,0:T(8,128)(2,1)S(1)} %collective-permute-done.refs_0_, bf16[32,3072]{1,0:T(8,128)(2,1)S(1)} %collective-permute-done.1.refs_1_, f32[2,6144]{1,0:T(2,128)S(1)} %get-tuple-element.73.refs_2_.refs_3_.gain.refs_4_, ...), custom_call_target="tpu_custom_call" | custom-call | tf_op jit(solution)/shard_map/project/pallas_call | solution.py:207
  17.1 2.5 %collective-permute-start.7 = (bf16[64,512]{1,0:T(8,128)(2,1)S(1)}, bf16[64,512]{1,0:T(8,128)(2,1)S(1)}, u32[]{:S(2)}, u32[]{:S(2)}) collective-permute-start(bf16[64,512]{1,0:T(8,128)(2,1)S(1)} %get-tuple-element.74.refs_3_), channel_id=1, source_target_pairs={{0,24},{4,28},{8,16},{12,20},{16,8},{20,12},{24,0},{28,4},{1,25},{... | collective-permute-start | bytes 196616 | tf_op jit(solution)/shard_map/ppermute | solution.py:460
  19.6 0.5 %collective-permute-start.6 = (bf16[64,512]{1,0:T(8,128)(2,1)S(1)}, bf16[64,512]{1,0:T(8,128)(2,1)S(1)}, u32[]{:S(2)}, u32[]{:S(2)}) collective-permute-start(bf16[64,512]{1,0:T(8,128)(2,1)S(1)} %get-tuple-element.74.refs_3_), channel_id=1, source_target_pairs={{0,16},{4,20},{8,24},{12,28},{16,0},{20,4},{24,8},{28,12},{1,17},{... | collective-permute-start | bytes 196616 | tf_op jit(solution)/shard_map/ppermute | solution.py:460
  20.1 0.5 %collective-permute-start.5 = (bf16[64,512]{1,0:T(8,128)(2,1)S(1)}, bf16[64,512]{1,0:T(8,128)(2,1)S(1)}, u32[]{:S(2)}, u32[]{:S(2)}) collective-permute-start(bf16[64,512]{1,0:T(8,128)(2,1)S(1)} %get-tuple-element.74.refs_3_), channel_id=1, source_target_pairs={{0,8},{4,12},{8,0},{12,4},{16,24},{20,28},{24,16},{28,20},{1,9},{5... | collective-permute-start | bytes 196616 | tf_op jit(solution)/shard_map/ppermute | solution.py:460
  20.6 2.2 %collective-permute-start.4 = (bf16[32,3072]{1,0:T(8,128)(2,1)S(1)}, bf16[32,3072]{1,0:T(8,128)(2,1)S(1)}, u32[]{:S(2)}, u32[]{:S(2)}) collective-permute-start(bf16[32,3072]{1,0:T(8,128)(2,1)S(1)} %collective-permute-done.2.refs_0_), channel_id=1, source_target_pairs={{0,1},{1,2},{2,3},{3,0},{4,5},{5,6},{6,7},{7,4},{8,9},{9,10},{10,1... | collective-permute-start | bytes 589832 | tf_op jit(solution)/shard_map/ppermute | solution.py:497
  22.8 1.5 %collective-permute-done.3.refs_1_.whole = bf16[32,3072]{1,0:T(8,128)(2,1)S(1)} collective-permute-done((bf16[32,3072]{1,0:T(8,128)(2,1)S(1)}, bf16[32,3072]{1,0:T(8,128)(2,1)S(1)}, u32[]{:S(2)}, u32[]{:S(2)}) %collective-permute-start.3) | collective-permute-done | bytes 196640 | tf_op jit(solution)/shard_map/ppermute | solution.py:490
  24.3 0.7 %collective-permute-start.12 = (bf16[32,3072]{1,0:T(8,128)(2,1)S(1)}, bf16[32,3072]{1,0:T(8,128)(2,1)S(1)}, u32[]{:S(2)}, u32[]{:S(2)}) collective-permute-start(bf16[32,3072]{1,0:T(8,128)(2,1)S(1)} %collective-permute-done.3.refs_1_.whole), channel_id=1, source_target_pairs={{0,1},{1,2},{2,3},{3,0},{4,5},{5,6},{6,7},{7,4},{8,9},{9,10},{10,1... | collective-permute-start | bytes 589832 | tf_op jit(solution)/shard_map/ppermute | solution.py:497
  24.9 0.0 collective-permute-done.7.refs_9_
  24.9 0.0 collective-permute-done.6.refs_7_
  24.9 0.0 collective-permute-done.5.refs_5_
  24.9 0.1 collective-permute-start.8
  25.0 0.5 %collective-permute-start.9 = (bf16[64,512]{1,0:T(8,128)(2,1)S(1)}, bf16[64,512]{1,0:T(8,128)(2,1)S(1)}, u32[]{:S(2)}, u32[]{:S(2)}) collective-permute-start(bf16[64,512]{1,0:T(8,128)(2,1)S(1)} %collective-permute-done.5.refs_5_), channel_id=1, source_target_pairs={{0,4},{4,0},{8,12},{12,8},{16,20},{20,16},{24,28},{28,24},{1,5},{5... | collective-permute-start | bytes 196616 | tf_op jit(solution)/shard_map/ppermute | solution.py:467
  25.5 0.1 collective-permute-start.10
  25.6 0.7 %collective-permute-done.8.refs_4_ = bf16[64,512]{1,0:T(8,128)(2,1)S(1)} collective-permute-done((bf16[64,512]{1,0:T(8,128)(2,1)S(1)}, bf16[64,512]{1,0:T(8,128)(2,1)S(1)}, u32[]{:S(2)}, u32[]{:S(2)}) %collective-permute-start.8) | collective-permute-done | bytes 65568 | tf_op jit(solution)/shard_map/ppermute | solution.py:467
  26.3 0.2 collective-permute-start.11
  26.4 0.3 collective-permute-done.10.refs_8_
  26.8 0.7 %collective-permute-done.11.refs_10_ = bf16[64,512]{1,0:T(8,128)(2,1)S(1)} collective-permute-done((bf16[64,512]{1,0:T(8,128)(2,1)S(1)}, bf16[64,512]{1,0:T(8,128)(2,1)S(1)}, u32[]{:S(2)}, u32[]{:S(2)}) %collective-permute-start.11) | collective-permute-done | bytes 65568 | tf_op jit(solution)/shard_map/ppermute | solution.py:467
  27.5 1.3 %collective-permute-done.4.refs_2_ = bf16[32,3072]{1,0:T(8,128)(2,1)S(1)} collective-permute-done((bf16[32,3072]{1,0:T(8,128)(2,1)S(1)}, bf16[32,3072]{1,0:T(8,128)(2,1)S(1)}, u32[]{:S(2)}, u32[]{:S(2)}) %collective-permute-start.4) | collective-permute-done | bytes 196640 | tf_op jit(solution)/shard_map/ppermute | solution.py:497
  28.8 0.8 %lead.1.refs_2_ = f32[80,640]{1,0:T(8,128)S(1)} custom-call(bf16[32,3072]{1,0:T(8,128)(2,1)S(1)} %collective-permute-done.2.refs_0_, bf16[32,3072]{1,0:T(8,128)(2,1)S(1)} %collective-permute-done.3.refs_1_.whole, bf16[32,3072]{1,0:T(8,128)(2,1)S(1)} %collective-permute-done.4.refs_2_, f32[2,6144]{1,0:T(2,128)S(1)} %get-tuple-element.73.refs_2_.refs_3_.gain.refs_4_, ...), custom_call_target="tpu_custom_call" | custom-call | tf_op jit(solution)/shard_map/lead/pallas_call | solution.py:257
  29.6 2.7 %collective-permute-done.12.piece.refs_3_ = bf16[32,3072]{1,0:T(8,128)(2,1)S(1)} collective-permute-done((bf16[32,3072]{1,0:T(8,128)(2,1)S(1)}, bf16[32,3072]{1,0:T(8,128)(2,1)S(1)}, u32[]{:S(2)}, u32[]{:S(2)}) %collective-permute-start.12) | collective-permute-done | bytes 196640 | tf_op jit(solution)/shard_map/ppermute | solution.py:497
  32.3 0.8 %finish.1.refs_0_ = bf16[64,512]{1,0:T(8,128)(2,1)S(1)} custom-call(bf16[32,3072]{1,0:T(8,128)(2,1)S(1)} %collective-permute-done.3.refs_1_.whole, bf16[32,3072]{1,0:T(8,128)(2,1)S(1)} %collective-permute-done.12.piece.refs_3_, f32[2,6144]{1,0:T(2,128)S(1)} %get-tuple-element.73.refs_2_.refs_3_.gain.refs_4_, ...), custom_call_target="tpu_custom_call" | custom-call | tf_op jit(solution)/shard_map/finish/pallas_call | solution.py:294
  33.1 2.5 %collective-permute-start.18 = (bf16[64,512]{1,0:T(8,128)(2,1)S(1)}, bf16[64,512]{1,0:T(8,128)(2,1)S(1)}, u32[]{:S(2)}, u32[]{:S(2)}) collective-permute-start(bf16[64,512]{1,0:T(8,128)(2,1)S(1)} %finish.1.refs_0_), channel_id=1, source_target_pairs={{0,24},{4,28},{8,16},{12,20},{16,8},{20,12},{24,0},{28,4},{1,25},{... | collective-permute-start | bytes 196616 | tf_op jit(solution)/shard_map/ppermute | solution.py:460
  35.7 0.5 %collective-permute-start.16 = (bf16[64,512]{1,0:T(8,128)(2,1)S(1)}, bf16[64,512]{1,0:T(8,128)(2,1)S(1)}, u32[]{:S(2)}, u32[]{:S(2)}) collective-permute-start(bf16[64,512]{1,0:T(8,128)(2,1)S(1)} %finish.1.refs_0_), channel_id=1, source_target_pairs={{0,16},{4,20},{8,24},{12,28},{16,0},{20,4},{24,8},{28,12},{1,17},{... | collective-permute-start | bytes 196616 | tf_op jit(solution)/shard_map/ppermute | solution.py:460
  36.2 0.5 %collective-permute-start.14 = (bf16[64,512]{1,0:T(8,128)(2,1)S(1)}, bf16[64,512]{1,0:T(8,128)(2,1)S(1)}, u32[]{:S(2)}, u32[]{:S(2)}) collective-permute-start(bf16[64,512]{1,0:T(8,128)(2,1)S(1)} %finish.1.refs_0_), channel_id=1, source_target_pairs={{0,8},{4,12},{8,0},{12,4},{16,24},{20,28},{24,16},{28,20},{1,9},{5... | collective-permute-start | bytes 196616 | tf_op jit(solution)/shard_map/ppermute | solution.py:460
  36.7 0.9 %project.3.refs_2_ = bf16[64,256]{1,0:T(8,128)(2,1)S(1)} custom-call(bf16[32,3072]{1,0:T(8,128)(2,1)S(1)} %collective-permute-done.2.refs_0_, bf16[32,3072]{1,0:T(8,128)(2,1)S(1)} %collective-permute-done.3.refs_1_.whole, bf16[32,3072]{1,0:T(8,128)(2,1)S(1)} %collective-permute-done.4.refs_2_, bf16[32,3072]{1,0:T(8,128)(2,1)S(1)} %collective-permute-done.12.piece.refs_3_, ...), custom_call_target="tpu_custom_call" | custom-call | tf_op jit(solution)/shard_map/project/pallas_call | solution.py:207
  37.6 0.5 %attend_early.1 = (bf16[128,256]{1,0:T(8,128)(2,1)S(1)}, f32[128,256]{1,0:T(8,128)S(1)}, f32[128,256]{1,0:T(8,128)S(1)}, f32[128,256]{1,0:T(8,128)S(1)}, f32[128,512]{1,0:T(8,128)S(1)}) custom-call(s32[1]{0:T(128)} %bitcast.1.mine, s32[128,1]{1,0:T(8,128)S(1)} %get-tuple-element.55.seg_col, s32[1,128]{1,0:T(1,128)S(1)} %get-tuple-element.56.seg_row, ...), custom_call_target="tpu_custom_call" | custom-call | tf_op jit(solution)/shard_map/attend_early/pallas_call | solution.py:377
  38.1 0.7 %collective-permute-done.18.refs_6_ = bf16[64,512]{1,0:T(8,128)(2,1)S(1)} collective-permute-done((bf16[64,512]{1,0:T(8,128)(2,1)S(1)}, bf16[64,512]{1,0:T(8,128)(2,1)S(1)}, u32[]{:S(2)}, u32[]{:S(2)}) %collective-permute-start.18) | collective-permute-done | bytes 65568 | tf_op jit(solution)/shard_map/ppermute | solution.py:460
  38.8 0.0 collective-permute-start.19
  38.9 1.1 %collective-permute-done.16.refs_4_ = bf16[64,512]{1,0:T(8,128)(2,1)S(1)} collective-permute-done((bf16[64,512]{1,0:T(8,128)(2,1)S(1)}, bf16[64,512]{1,0:T(8,128)(2,1)S(1)}, u32[]{:S(2)}, u32[]{:S(2)}) %collective-permute-start.16) | collective-permute-done | bytes 65568 | tf_op jit(solution)/shard_map/ppermute | solution.py:460
  39.9 0.5 %collective-permute-done.14.refs_2_ = bf16[64,512]{1,0:T(8,128)(2,1)S(1)} collective-permute-done((bf16[64,512]{1,0:T(8,128)(2,1)S(1)}, bf16[64,512]{1,0:T(8,128)(2,1)S(1)}, u32[]{:S(2)}, u32[]{:S(2)}) %collective-permute-start.14) | collective-permute-done | bytes 65568 | tf_op jit(solution)/shard_map/ppermute | solution.py:460
  40.4 0.0 collective-permute-start.15
  40.4 0.7 %collective-permute-done.17.refs_5_ = bf16[64,512]{1,0:T(8,128)(2,1)S(1)} collective-permute-done((bf16[64,512]{1,0:T(8,128)(2,1)S(1)}, bf16[64,512]{1,0:T(8,128)(2,1)S(1)}, u32[]{:S(2)}, u32[]{:S(2)}) %collective-permute-start.17) | collective-permute-done | bytes 65568 | tf_op jit(solution)/shard_map/ppermute | solution.py:467
  41.2 0.5 %collective-permute-done.15.refs_3_ = bf16[64,512]{1,0:T(8,128)(2,1)S(1)} collective-permute-done((bf16[64,512]{1,0:T(8,128)(2,1)S(1)}, bf16[64,512]{1,0:T(8,128)(2,1)S(1)}, u32[]{:S(2)}, u32[]{:S(2)}) %collective-permute-start.15) | collective-permute-done | bytes 65568 | tf_op jit(solution)/shard_map/ppermute | solution.py:467
  41.7 0.7 %attend.1 = (bf16[32,256]{1,0:T(8,128)(2,1)S(1)}, bf16[32,256]{1,0:T(8,128)(2,1)S(1)}, bf16[32,256]{1,0:T(8,128)(2,1)S(1)}, bf16[32,256]{1,0:T(8,128)(2,1)S(1)}) custom-call(s32[1]{0:T(128)} %bitcast.place, bf16[128,256]{1,0:T(8,128)(2,1)S(1)} %get-tuple-element.82.q_all, f32[128,256]{1,0:T(8,128)S(1)} %get-tuple-element.83.sums, ...), custom_call_target="tpu_custom_call" | custom-call | tf_op jit(solution)/shard_map/attend/pallas_call | solution.py:422
  42.3 0.6 %collective-permute-start.20 = (bf16[32,256]{1,0:T(8,128)(2,1)S(1)}, bf16[32,256]{1,0:T(8,128)(2,1)S(1)}, u32[]{:S(2)}, u32[]{:S(2)}) collective-permute-start(bf16[32,256]{1,0:T(8,128)(2,1)S(1)} %get-tuple-element.92), channel_id=1, source_target_pairs={{0,2},{1,3},{2,0},{3,1},{4,6},{5,7},{6,4},{7,5},{8,10},{9,11},{10,... | collective-permute-start | bytes 49160 | tf_op jit(solution)/shard_map/ppermute | solution.py:514
  42.9 1.8 %collective-permute-start.21 = (bf16[32,256]{1,0:T(8,128)(2,1)S(1)}, bf16[32,256]{1,0:T(8,128)(2,1)S(1)}, u32[]{:S(2)}, u32[]{:S(2)}) collective-permute-start(bf16[32,256]{1,0:T(8,128)(2,1)S(1)} %get-tuple-element.93), channel_id=1, source_target_pairs={{0,3},{1,2},{2,1},{3,0},{4,7},{5,6},{6,5},{7,4},{8,11},{9,10},{10,... | collective-permute-start | bytes 49160 | tf_op jit(solution)/shard_map/ppermute | solution.py:514
  44.7 1.2 %collective-permute-start.22 = (bf16[32,256]{1,0:T(8,128)(2,1)S(1)}, bf16[32,256]{1,0:T(8,128)(2,1)S(1)}, u32[]{:S(2)}, u32[]{:S(2)}) collective-permute-start(bf16[32,256]{1,0:T(8,128)(2,1)S(1)} %get-tuple-element.94), channel_id=1, source_target_pairs={{0,1},{1,0},{2,3},{3,2},{4,5},{5,4},{6,7},{7,6},{8,9},{9,8},{10,11... | collective-permute-start | bytes 49160 | tf_op jit(solution)/shard_map/ppermute | solution.py:514
  45.9 1.3 %collective-permute-done.20.refs_1_ = bf16[32,256]{1,0:T(8,128)(2,1)S(1)} collective-permute-done((bf16[32,256]{1,0:T(8,128)(2,1)S(1)}, bf16[32,256]{1,0:T(8,128)(2,1)S(1)}, u32[]{:S(2)}, u32[]{:S(2)}) %collective-permute-start.20) | collective-permute-done | bytes 16416 | tf_op jit(solution)/shard_map/ppermute | solution.py:514
  47.2 1.4 %collective-permute-done.21.refs_2_ = bf16[32,256]{1,0:T(8,128)(2,1)S(1)} collective-permute-done((bf16[32,256]{1,0:T(8,128)(2,1)S(1)}, bf16[32,256]{1,0:T(8,128)(2,1)S(1)}, u32[]{:S(2)}, u32[]{:S(2)}) %collective-permute-start.21) | collective-permute-done | bytes 16416 | tf_op jit(solution)/shard_map/ppermute | solution.py:514
  48.6 0.0 collective-permute-done.22.refs_3_
  48.6 0.6 %place.1 = bf16[1,32,1024]{2,1,0:T(8,128)(2,1)} custom-call(s32[1]{0:T(128)} %bitcast.place, bf16[32,256]{1,0:T(8,128)(2,1)S(1)} %get-tuple-element.91.refs_0_, bf16[32,256]{1,0:T(8,128)(2,1)S(1)} %collective-permute-done.20.refs_1_, bf16[32,256]{1,0:T(8,128)(2,1)S(1)} %collective-permute-done.21.refs_2_, bf16[32,256]{1,0:T(8,128)(2,1)S(1)} %collective-permute-done.22.refs_3_), custom_call_target="tpu_custom_call" | custom-call | tf_op jit(solution)/shard_map/place/pallas_call | solution.py:448
  (7 shorter events, 0.0 us)
Async XLA Ops:
  1.0 10.8 %collective-permute-start = (bf16[32,3072]{1,0:T(8,128)(2,1)S(1)}, bf16[32,3072]{1,0:T(8,128)(2,1)S(1)}, u32[]{:S(2)}, u32[]{:S(2)}) collective-permute-start(bf16[32,3072]{1,0:T(8,128)(2,1)S(1)} %get-tuple-element.53.refs_3_), channel_id=1, source_target_pairs={{0,1},{1,2},{2,3},{3,0},{4,5},{5,6},{6,7},{7,4},{8,9},{9,10},{10,1... | collective-permute-start | bytes 589832 | tf_op jit(solution)/shard_map/ppermute | solution.py:485
  4.1 11.1 %collective-permute-start.1 = (bf16[32,3072]{1,0:T(8,128)(2,1)S(1)}, bf16[32,3072]{1,0:T(8,128)(2,1)S(1)}, u32[]{:S(2)}, u32[]{:S(2)}) collective-permute-start(bf16[32,3072]{1,0:T(8,128)(2,1)S(1)} %get-tuple-element.54.refs_4_), channel_id=1, source_target_pairs={{0,1},{1,2},{2,3},{3,0},{4,5},{5,6},{6,7},{7,4},{8,9},{9,10},{10,1... | collective-permute-start | bytes 589832 | tf_op jit(solution)/shard_map/ppermute | solution.py:485
  11.9 8.8 %collective-permute-start.2 = (bf16[32,3072]{1,0:T(8,128)(2,1)S(1)}, bf16[32,3072]{1,0:T(8,128)(2,1)S(1)}, u32[]{:S(2)}, u32[]{:S(2)}) collective-permute-start(bf16[32,3072]{1,0:T(8,128)(2,1)S(1)} %collective-permute-done.refs_0_), channel_id=1, source_target_pairs={{0,1},{1,2},{2,3},{3,0},{4,5},{5,6},{6,7},{7,4},{8,9},{9,10},{10,1... | collective-permute-start | bytes 589832 | tf_op jit(solution)/shard_map/ppermute | solution.py:490
  15.3 9.0 %collective-permute-start.3 = (bf16[32,3072]{1,0:T(8,128)(2,1)S(1)}, bf16[32,3072]{1,0:T(8,128)(2,1)S(1)}, u32[]{:S(2)}, u32[]{:S(2)}) collective-permute-start(bf16[32,3072]{1,0:T(8,128)(2,1)S(1)} %collective-permute-done.1.refs_1_), channel_id=1, source_target_pairs={{0,1},{1,2},{2,3},{3,0},{4,5},{5,6},{6,7},{7,4},{8,9},{9,10},{10,1... | collective-permute-start | bytes 589832 | tf_op jit(solution)/shard_map/ppermute | solution.py:490
  17.1 7.8 %collective-permute-start.7 = (bf16[64,512]{1,0:T(8,128)(2,1)S(1)}, bf16[64,512]{1,0:T(8,128)(2,1)S(1)}, u32[]{:S(2)}, u32[]{:S(2)}) collective-permute-start(bf16[64,512]{1,0:T(8,128)(2,1)S(1)} %get-tuple-element.74.refs_3_), channel_id=1, source_target_pairs={{0,24},{4,28},{8,16},{12,20},{16,8},{20,12},{24,0},{28,4},{1,25},{... | collective-permute-start | bytes 196616 | tf_op jit(solution)/shard_map/ppermute | solution.py:460
  19.6 5.4 %collective-permute-start.6 = (bf16[64,512]{1,0:T(8,128)(2,1)S(1)}, bf16[64,512]{1,0:T(8,128)(2,1)S(1)}, u32[]{:S(2)}, u32[]{:S(2)}) collective-permute-start(bf16[64,512]{1,0:T(8,128)(2,1)S(1)} %get-tuple-element.74.refs_3_), channel_id=1, source_target_pairs={{0,16},{4,20},{8,24},{12,28},{16,0},{20,4},{24,8},{28,12},{1,17},{... | collective-permute-start | bytes 196616 | tf_op jit(solution)/shard_map/ppermute | solution.py:460
  20.1 4.8 %collective-permute-start.5 = (bf16[64,512]{1,0:T(8,128)(2,1)S(1)}, bf16[64,512]{1,0:T(8,128)(2,1)S(1)}, u32[]{:S(2)}, u32[]{:S(2)}) collective-permute-start(bf16[64,512]{1,0:T(8,128)(2,1)S(1)} %get-tuple-element.74.refs_3_), channel_id=1, source_target_pairs={{0,8},{4,12},{8,0},{12,4},{16,24},{20,28},{24,16},{28,20},{1,9},{5... | collective-permute-start | bytes 196616 | tf_op jit(solution)/shard_map/ppermute | solution.py:460
  20.6 8.1 %collective-permute-start.4 = (bf16[32,3072]{1,0:T(8,128)(2,1)S(1)}, bf16[32,3072]{1,0:T(8,128)(2,1)S(1)}, u32[]{:S(2)}, u32[]{:S(2)}) collective-permute-start(bf16[32,3072]{1,0:T(8,128)(2,1)S(1)} %collective-permute-done.2.refs_0_), channel_id=1, source_target_pairs={{0,1},{1,2},{2,3},{3,0},{4,5},{5,6},{6,7},{7,4},{8,9},{9,10},{10,1... | collective-permute-start | bytes 589832 | tf_op jit(solution)/shard_map/ppermute | solution.py:497
  24.3 8.1 %collective-permute-start.12 = (bf16[32,3072]{1,0:T(8,128)(2,1)S(1)}, bf16[32,3072]{1,0:T(8,128)(2,1)S(1)}, u32[]{:S(2)}, u32[]{:S(2)}) collective-permute-start(bf16[32,3072]{1,0:T(8,128)(2,1)S(1)} %collective-permute-done.3.refs_1_.whole), channel_id=1, source_target_pairs={{0,1},{1,2},{2,3},{3,0},{4,5},{5,6},{6,7},{7,4},{8,9},{9,10},{10,1... | collective-permute-start | bytes 589832 | tf_op jit(solution)/shard_map/ppermute | solution.py:497
  24.9 1.3 %collective-permute-start.8 = (bf16[64,512]{1,0:T(8,128)(2,1)S(1)}, bf16[64,512]{1,0:T(8,128)(2,1)S(1)}, u32[]{:S(2)}, u32[]{:S(2)}) collective-permute-start(bf16[64,512]{1,0:T(8,128)(2,1)S(1)} %get-tuple-element.74.refs_3_), channel_id=1, source_target_pairs={{0,4},{4,0},{8,12},{12,8},{16,20},{20,16},{24,28},{28,24},{1,5},{5... | collective-permute-start | bytes 196616 | tf_op jit(solution)/shard_map/ppermute | solution.py:467
  25.0 1.4 %collective-permute-start.9 = (bf16[64,512]{1,0:T(8,128)(2,1)S(1)}, bf16[64,512]{1,0:T(8,128)(2,1)S(1)}, u32[]{:S(2)}, u32[]{:S(2)}) collective-permute-start(bf16[64,512]{1,0:T(8,128)(2,1)S(1)} %collective-permute-done.5.refs_5_), channel_id=1, source_target_pairs={{0,4},{4,0},{8,12},{12,8},{16,20},{20,16},{24,28},{28,24},{1,5},{5... | collective-permute-start | bytes 196616 | tf_op jit(solution)/shard_map/ppermute | solution.py:467
  25.5 1.3 %collective-permute-start.10 = (bf16[64,512]{1,0:T(8,128)(2,1)S(1)}, bf16[64,512]{1,0:T(8,128)(2,1)S(1)}, u32[]{:S(2)}, u32[]{:S(2)}) collective-permute-start(bf16[64,512]{1,0:T(8,128)(2,1)S(1)} %collective-permute-done.6.refs_7_), channel_id=1, source_target_pairs={{0,4},{4,0},{8,12},{12,8},{16,20},{20,16},{24,28},{28,24},{1,5},{5... | collective-permute-start | bytes 196616 | tf_op jit(solution)/shard_map/ppermute | solution.py:467
  26.3 1.3 %collective-permute-start.11 = (bf16[64,512]{1,0:T(8,128)(2,1)S(1)}, bf16[64,512]{1,0:T(8,128)(2,1)S(1)}, u32[]{:S(2)}, u32[]{:S(2)}) collective-permute-start(bf16[64,512]{1,0:T(8,128)(2,1)S(1)} %collective-permute-done.7.refs_9_), channel_id=1, source_target_pairs={{0,4},{4,0},{8,12},{12,8},{16,20},{20,16},{24,28},{28,24},{1,5},{5... | collective-permute-start | bytes 196616 | tf_op jit(solution)/shard_map/ppermute | solution.py:467
  33.1 5.7 %collective-permute-start.18 = (bf16[64,512]{1,0:T(8,128)(2,1)S(1)}, bf16[64,512]{1,0:T(8,128)(2,1)S(1)}, u32[]{:S(2)}, u32[]{:S(2)}) collective-permute-start(bf16[64,512]{1,0:T(8,128)(2,1)S(1)} %finish.1.refs_0_), channel_id=1, source_target_pairs={{0,24},{4,28},{8,16},{12,20},{16,8},{20,12},{24,0},{28,4},{1,25},{... | collective-permute-start | bytes 196616 | tf_op jit(solution)/shard_map/ppermute | solution.py:460
  35.7 4.3 %collective-permute-start.16 = (bf16[64,512]{1,0:T(8,128)(2,1)S(1)}, bf16[64,512]{1,0:T(8,128)(2,1)S(1)}, u32[]{:S(2)}, u32[]{:S(2)}) collective-permute-start(bf16[64,512]{1,0:T(8,128)(2,1)S(1)} %finish.1.refs_0_), channel_id=1, source_target_pairs={{0,16},{4,20},{8,24},{12,28},{16,0},{20,4},{24,8},{28,12},{1,17},{... | collective-permute-start | bytes 196616 | tf_op jit(solution)/shard_map/ppermute | solution.py:460
  36.2 4.3 %collective-permute-start.14 = (bf16[64,512]{1,0:T(8,128)(2,1)S(1)}, bf16[64,512]{1,0:T(8,128)(2,1)S(1)}, u32[]{:S(2)}, u32[]{:S(2)}) collective-permute-start(bf16[64,512]{1,0:T(8,128)(2,1)S(1)} %finish.1.refs_0_), channel_id=1, source_target_pairs={{0,8},{4,12},{8,0},{12,4},{16,24},{20,28},{24,16},{28,20},{1,9},{5... | collective-permute-start | bytes 196616 | tf_op jit(solution)/shard_map/ppermute | solution.py:460
  36.7 3.7 %collective-permute-start.13 = (bf16[64,512]{1,0:T(8,128)(2,1)S(1)}, bf16[64,512]{1,0:T(8,128)(2,1)S(1)}, u32[]{:S(2)}, u32[]{:S(2)}) collective-permute-start(bf16[64,512]{1,0:T(8,128)(2,1)S(1)} %finish.1.refs_0_), channel_id=1, source_target_pairs={{0,4},{4,0},{8,12},{12,8},{16,20},{20,16},{24,28},{28,24},{1,5},{5... | collective-permute-start | bytes 196616 | tf_op jit(solution)/shard_map/ppermute | solution.py:467
  38.8 1.6 %collective-permute-start.19 = (bf16[64,512]{1,0:T(8,128)(2,1)S(1)}, bf16[64,512]{1,0:T(8,128)(2,1)S(1)}, u32[]{:S(2)}, u32[]{:S(2)}) collective-permute-start(bf16[64,512]{1,0:T(8,128)(2,1)S(1)} %collective-permute-done.18.refs_6_), channel_id=1, source_target_pairs={{0,4},{4,0},{8,12},{12,8},{16,20},{20,16},{24,28},{28,24},{1,5},{5... | collective-permute-start | bytes 196616 | tf_op jit(solution)/shard_map/ppermute | solution.py:467
  39.9 1.3 %collective-permute-start.17 = (bf16[64,512]{1,0:T(8,128)(2,1)S(1)}, bf16[64,512]{1,0:T(8,128)(2,1)S(1)}, u32[]{:S(2)}, u32[]{:S(2)}) collective-permute-start(bf16[64,512]{1,0:T(8,128)(2,1)S(1)} %collective-permute-done.16.refs_4_), channel_id=1, source_target_pairs={{0,4},{4,0},{8,12},{12,8},{16,20},{20,16},{24,28},{28,24},{1,5},{5... | collective-permute-start | bytes 196616 | tf_op jit(solution)/shard_map/ppermute | solution.py:467
  40.4 1.3 %collective-permute-start.15 = (bf16[64,512]{1,0:T(8,128)(2,1)S(1)}, bf16[64,512]{1,0:T(8,128)(2,1)S(1)}, u32[]{:S(2)}, u32[]{:S(2)}) collective-permute-start(bf16[64,512]{1,0:T(8,128)(2,1)S(1)} %collective-permute-done.14.refs_2_), channel_id=1, source_target_pairs={{0,4},{4,0},{8,12},{12,8},{16,20},{20,16},{24,28},{28,24},{1,5},{5... | collective-permute-start | bytes 196616 | tf_op jit(solution)/shard_map/ppermute | solution.py:467
  42.3 4.8 %collective-permute-start.20 = (bf16[32,256]{1,0:T(8,128)(2,1)S(1)}, bf16[32,256]{1,0:T(8,128)(2,1)S(1)}, u32[]{:S(2)}, u32[]{:S(2)}) collective-permute-start(bf16[32,256]{1,0:T(8,128)(2,1)S(1)} %get-tuple-element.92), channel_id=1, source_target_pairs={{0,2},{1,3},{2,0},{3,1},{4,6},{5,7},{6,4},{7,5},{8,10},{9,11},{10,... | collective-permute-start | bytes 49160 | tf_op jit(solution)/shard_map/ppermute | solution.py:514
  42.9 5.6 %collective-permute-start.21 = (bf16[32,256]{1,0:T(8,128)(2,1)S(1)}, bf16[32,256]{1,0:T(8,128)(2,1)S(1)}, u32[]{:S(2)}, u32[]{:S(2)}) collective-permute-start(bf16[32,256]{1,0:T(8,128)(2,1)S(1)} %get-tuple-element.93), channel_id=1, source_target_pairs={{0,3},{1,2},{2,1},{3,0},{4,7},{5,6},{6,5},{7,4},{8,11},{9,10},{10,... | collective-permute-start | bytes 49160 | tf_op jit(solution)/shard_map/ppermute | solution.py:514
  44.7 3.9 %collective-permute-start.22 = (bf16[32,256]{1,0:T(8,128)(2,1)S(1)}, bf16[32,256]{1,0:T(8,128)(2,1)S(1)}, u32[]{:S(2)}, u32[]{:S(2)}) collective-permute-start(bf16[32,256]{1,0:T(8,128)(2,1)S(1)} %get-tuple-element.94), channel_id=1, source_target_pairs={{0,1},{1,0},{2,3},{3,2},{4,5},{5,4},{6,7},{7,6},{8,9},{9,8},{10,11... | collective-permute-start | bytes 49160 | tf_op jit(solution)/shard_map/ppermute | solution.py:514

commit v11 on v10

--- a/solution.py
+++ b/solution.py
@@ -343,14 +343,20 @@
     return [ref[span, start + h * HD : start + (h + 1) * HD] for h in range(count)]
 
 
-def attend_early_kernel(parts, sources, mine, seg_col, seg_row, *refs):
+def attend_early_kernel(shards, parts, sources, mine, place, seg_in, seg_row, *refs):
     queries, refs = refs[:parts], refs[parts:]
     early, refs = refs[:sources], refs[sources:]
-    q_all, sums, bests, totals, barred_late, kv_all = refs
+    q_all, sums, bests, totals, barred_late, kv_all, q_in, seg_col = refs
     filled = 0
     for query in queries:
-        q_all[filled : filled + query.shape[0], :] = query[...]
+        q_in[filled : filled + query.shape[0], :] = query[...]
         filled += query.shape[0]
+    rows = filled // shards
+    for m in range(shards):
+        spot = lax.rem(place[0] - (place[0] ^ m) + shards, shards) * rows
+        taken = pl.ds(pl.multiple_of(spot, rows), rows)
+        q_all[m * rows : (m + 1) * rows, :] = q_in[taken, :]
+        seg_col[m * rows : (m + 1) * rows, :] = seg_in[taken, :]
     stack(early, kv_all)
     many = early[0].shape[0]
     heads = q_all.shape[1] // HD
@@ -371,24 +377,28 @@
         barred_late[span, :] = barred_of(sources, mine, seg_col[span, :], seg_row[:, many:])
 
 
-def attend_early(mine, seg_col, seg_row, queries, early):
+def attend_early(shards, mine, place, seg_col, seg_row, queries, early):
     sources, many = len(early), early[0].shape[0]
     tokc, width = seg_col.shape[0], queries[0].shape[1]
     return pl.pallas_call(
-        functools.partial(attend_early_kernel, len(queries), sources),
-        in_specs=[IN_SMEM] + [IN_VMEM] * (2 + len(queries) + sources),
+        functools.partial(attend_early_kernel, shards, len(queries), sources),
+        in_specs=[IN_SMEM] * 2 + [IN_VMEM] * (2 + len(queries) + sources),
         out_specs=[IN_VMEM] * 5,
         out_shape=[VMEM((tokc, width), jnp.bfloat16)]
         + [VMEM((tokc, width), jnp.float32)] * 3
         + [VMEM((tokc, sources * (tokc - many)), jnp.float32)],
-        scratch_shapes=[pltpu.VMEM((sources * many, 2 * width), jnp.bfloat16)],
+        scratch_shapes=[
+            pltpu.VMEM((sources * many, 2 * width), jnp.bfloat16),
+            pltpu.VMEM((tokc, width), jnp.bfloat16),
+            pltpu.VMEM((tokc, 1), jnp.int32),
+        ],
         compiler_params=params(3 * (sources * tokc // 1024)),
         name="attend_early",
-    )(mine, *near(seg_col, seg_row, *queries, *early))
-
-
-def attend_kernel(shards, sources, place, q_all, sums, bests, totals, barred, *refs):
-    late, outs, kv_all, held = refs[:sources], refs[sources:-2], refs[-2], refs[-1]
+    )(mine, place, *near(seg_col, seg_row, *queries, *early))
+
+
+def attend_kernel(shards, sources, q_all, sums, bests, totals, barred, *refs):
+    late, outs, kv_all = refs[:sources], refs[sources:-1], refs[-1]
     tokc, width = q_all.shape
     rows = tokc // shards
     heads = width // HD
@@ -409,28 +419,27 @@
             fade = jnp.exp(floor - best)
             scale = 1.0 / (total + old_total[:, 0:1] * fade)
             result = ((summed + old_sum * fade) * scale).astype(jnp.bfloat16)
-            held[span, h * HD : (h + 1) * HD] = result
-    for m, out in enumerate(outs):
-        spot = lax.rem(place[0] - (place[0] ^ m) + shards, shards) * rows
-        out[...] = held[pl.ds(pl.multiple_of(spot, rows), rows), :]
-
-
-def attend(shards, place, state, late):
+            for m in range(span.start // rows, span.stop // rows):
+                outs[m][:, h * HD : (h + 1) * HD] = result[
+                    m * rows - span.start : (m + 1) * rows - span.start
+                ]
+
+
+def attend(shards, state, late):
     sources, many = len(late), late[0].shape[0]
     tokc, width = state[0].shape
     rows = tokc // shards
     return pl.pallas_call(
         functools.partial(attend_kernel, shards, sources),
-        in_specs=[IN_SMEM] + [IN_VMEM] * (len(state) + sources),
+        in_specs=[IN_VMEM] * (len(state) + sources),
         out_specs=[IN_VMEM] * shards,
         out_shape=[VMEM((rows, width), jnp.bfloat16)] * shards,
         scratch_shapes=[
             pltpu.VMEM((sources * many, 2 * width), jnp.bfloat16),
-            pltpu.VMEM((tokc, width), jnp.bfloat16),
         ],
         compiler_params=params(3 * (sources * tokc // 1024)),
         name="attend",
-    )(place, *near(*state, *late))
+    )(*near(*state, *late))
 
 
 def place_kernel(order, place, *refs):
@@ -503,11 +512,11 @@
     late = across_chips(keyval, groups)
     query = project(both, gain, weights, (0,))[0]
     queries.append(query)
-    state = attend_early(mine, seg_col, seg_row, queries, early)
+    state = attend_early(shards, mine, place, seg_col, seg_row, queries, early)
     tail = [lax.optimization_barrier((block, state[0]))[0] for block in late[:0:-1]]
     late[1:] = tail[::-1]
     late = across_cores(late, groups)
-    results = attend(shards, place, state, late)
+    results = attend(shards, state, late)
     landed = [results[0]]
     for s in range(1, shards):
         landed.append(

time: 49.4 us -> 49.4 us (level)
  no operation moved by 1% of the time
where the time goes in v11:
time: 49.4 us; the launch traced here: 49.2 us
  starting transfers between devices  20.4 us (41%)
  waiting for transfers between devices  15.5 us (31%)
  Pallas kernels  12.6 us (26%)
  between operations  0.72 us (1%)
    ppermute x6, starting transfers between devices, across_chips(): lax.ppermute(block, 'group', [(i, i ^ m) for i in range(groups)])  7.06 us
    ppermute x4, starting transfers between devices, per_device(): pieces = [lax.ppermute(piece, 'dp', ring) for piece in pieces]  6.16 us
    pallas_call x1, Pallas kernels, begin(): pl.pallas_call(functools.partial(begin_kernel, shards), in_specs=[IN_SMEM...  5.38 us
    ppermute x2, waiting for transfers between devices, per_device(): moved = [lax.ppermute(piece, 'dp', ring) for piece in pieces]  4 us
    ppermute x3, starting transfers between devices, per_device(): lax.ppermute(results[s], 'dp', [(i, i ^ s) for i in range(shards)])  3.55 us
    ppermute x4, waiting for transfers between devices, per_device(): pieces = [lax.ppermute(piece, 'dp', ring) for piece in pieces]  3.47 us
    ppermute x8, waiting for transfers between devices, across_cores(): lax.ppermute(block, 'group', swap)  3.01 us
    ppermute x2, starting transfers between devices, per_device(): moved = [lax.ppermute(piece, 'dp', ring) for piece in pieces]  2.84 us
  transfers between devices with their start and end apart: 23, of which 15 were waited for; matrix products, arithmetic and copies ran while one was open for 0% of the time, Pallas kernels for 19%

profile of v11, /device:TPU:0, one launch (start us, length us, event | category | flops | bytes accessed | tf_op | source)
XLA Modules:
  0.0 49.2 jit_solution(14339916698491485051)
XLA Ops:
  0.0 1.0 %split.1 = (bf16[32,3072]{1,0:T(8,128)(2,1)S(1)}, bf16[32,3072]{1,0:T(8,128)(2,1)S(1)}) custom-call(bf16[1,32,6144]{2,1,0:T(8,128)(2,1)} %x_hbm), custom_call_target="tpu_custom_call" | custom-call | tf_op jit(solution)/shard_map/split/pallas_call | solution.py:58
  1.0 3.1 %collective-permute-start = (bf16[32,3072]{1,0:T(8,128)(2,1)S(1)}, bf16[32,3072]{1,0:T(8,128)(2,1)S(1)}, u32[]{:S(2)}, u32[]{:S(2)}) collective-permute-start(bf16[32,3072]{1,0:T(8,128)(2,1)S(1)} %get-tuple-element.53.refs_3_), channel_id=1, source_target_pairs={{0,1},{1,2},{2,3},{3,0},{4,5},{5,6},{6,7},{7,4},{8,9},{9,10},{10,1... | collective-permute-start | bytes 589832 | tf_op jit(solution)/shard_map/ppermute | solution.py:494
  4.1 1.6 %collective-permute-start.1 = (bf16[32,3072]{1,0:T(8,128)(2,1)S(1)}, bf16[32,3072]{1,0:T(8,128)(2,1)S(1)}, u32[]{:S(2)}, u32[]{:S(2)}) collective-permute-start(bf16[32,3072]{1,0:T(8,128)(2,1)S(1)} %get-tuple-element.54.refs_4_), channel_id=1, source_target_pairs={{0,1},{1,2},{2,3},{3,0},{4,5},{5,6},{6,7},{7,4},{8,9},{9,10},{10,1... | collective-permute-start | bytes 589832 | tf_op jit(solution)/shard_map/ppermute | solution.py:494
  6.3 5.4 %begin.1 = (bf16[32,256]{1,0:T(8,128)(2,1)S(1)}, bf16[32,512]{1,0:T(8,128)(2,1)S(1)}, bf16[6144,256]{1,0:T(8,128)(2,1)S(1)}, bf16[6144,256]{1,0:T(8,128)(2,1)S(1...) custom-call(s32[1]{0:T(128)} %bitcast.place, ...), custom_call_target="tpu_custom_call" | custom-call | tf_op jit(solution)/shard_map/begin/pallas_call | solution.py:150
  11.7 0.1 collective-permute-done.refs_0_
  11.9 1.5 %collective-permute-start.2 = (bf16[32,3072]{1,0:T(8,128)(2,1)S(1)}, bf16[32,3072]{1,0:T(8,128)(2,1)S(1)}, u32[]{:S(2)}, u32[]{:S(2)}) collective-permute-start(bf16[32,3072]{1,0:T(8,128)(2,1)S(1)} %collective-permute-done.refs_0_), channel_id=1, source_target_pairs={{0,1},{1,2},{2,3},{3,0},{4,5},{5,6},{6,7},{7,4},{8,9},{9,10},{10,1... | collective-permute-start | bytes 589832 | tf_op jit(solution)/shard_map/ppermute | solution.py:499
  13.4 1.9 %collective-permute-done.1.refs_1_ = bf16[32,3072]{1,0:T(8,128)(2,1)S(1)} collective-permute-done((bf16[32,3072]{1,0:T(8,128)(2,1)S(1)}, bf16[32,3072]{1,0:T(8,128)(2,1)S(1)}, u32[]{:S(2)}, u32[]{:S(2)}) %collective-permute-start.1) | collective-permute-done | bytes 196640 | tf_op jit(solution)/shard_map/ppermute | solution.py:494
  15.3 1.9 %project.2 = (bf16[32,256]{1,0:T(8,128)(2,1)S(1)}, bf16[64,512]{1,0:T(8,128)(2,1)S(1)}) custom-call(bf16[32,3072]{1,0:T(8,128)(2,1)S(1)} %collective-permute-done.refs_0_, bf16[32,3072]{1,0:T(8,128)(2,1)S(1)} %collective-permute-done.1.refs_1_, f32[2,6144]{1,0:T(2,128)S(1)} %get-tuple-element.73.refs_2_.refs_3_.gain.refs_4_, ...), custom_call_target="tpu_custom_call" | custom-call | tf_op jit(solution)/shard_map/project/pallas_call | solution.py:207
  17.1 2.5 %collective-permute-start.7 = (bf16[64,512]{1,0:T(8,128)(2,1)S(1)}, bf16[64,512]{1,0:T(8,128)(2,1)S(1)}, u32[]{:S(2)}, u32[]{:S(2)}) collective-permute-start(bf16[64,512]{1,0:T(8,128)(2,1)S(1)} %get-tuple-element.74.refs_3_), channel_id=1, source_target_pairs={{0,24},{4,28},{8,16},{12,20},{16,8},{20,12},{24,0},{28,4},{1,25},{... | collective-permute-start | bytes 196616 | tf_op jit(solution)/shard_map/ppermute | solution.py:469
  19.6 0.5 %collective-permute-start.6 = (bf16[64,512]{1,0:T(8,128)(2,1)S(1)}, bf16[64,512]{1,0:T(8,128)(2,1)S(1)}, u32[]{:S(2)}, u32[]{:S(2)}) collective-permute-start(bf16[64,512]{1,0:T(8,128)(2,1)S(1)} %get-tuple-element.74.refs_3_), channel_id=1, source_target_pairs={{0,16},{4,20},{8,24},{12,28},{16,0},{20,4},{24,8},{28,12},{1,17},{... | collective-permute-start | bytes 196616 | tf_op jit(solution)/shard_map/ppermute | solution.py:469
  20.1 0.5 %collective-permute-start.5 = (bf16[64,512]{1,0:T(8,128)(2,1)S(1)}, bf16[64,512]{1,0:T(8,128)(2,1)S(1)}, u32[]{:S(2)}, u32[]{:S(2)}) collective-permute-start(bf16[64,512]{1,0:T(8,128)(2,1)S(1)} %get-tuple-element.74.refs_3_), channel_id=1, source_target_pairs={{0,8},{4,12},{8,0},{12,4},{16,24},{20,28},{24,16},{28,20},{1,9},{5... | collective-permute-start | bytes 196616 | tf_op jit(solution)/shard_map/ppermute | solution.py:469
  20.6 2.2 %collective-permute-start.4 = (bf16[32,3072]{1,0:T(8,128)(2,1)S(1)}, bf16[32,3072]{1,0:T(8,128)(2,1)S(1)}, u32[]{:S(2)}, u32[]{:S(2)}) collective-permute-start(bf16[32,3072]{1,0:T(8,128)(2,1)S(1)} %collective-permute-done.2.refs_0_), channel_id=1, source_target_pairs={{0,1},{1,2},{2,3},{3,0},{4,5},{5,6},{6,7},{7,4},{8,9},{9,10},{10,1... | collective-permute-start | bytes 589832 | tf_op jit(solution)/shard_map/ppermute | solution.py:506
  22.8 1.5 %collective-permute-done.3.refs_1_.whole = bf16[32,3072]{1,0:T(8,128)(2,1)S(1)} collective-permute-done((bf16[32,3072]{1,0:T(8,128)(2,1)S(1)}, bf16[32,3072]{1,0:T(8,128)(2,1)S(1)}, u32[]{:S(2)}, u32[]{:S(2)}) %collective-permute-start.3) | collective-permute-done | bytes 196640 | tf_op jit(solution)/shard_map/ppermute | solution.py:499
  24.3 0.7 %collective-permute-start.12 = (bf16[32,3072]{1,0:T(8,128)(2,1)S(1)}, bf16[32,3072]{1,0:T(8,128)(2,1)S(1)}, u32[]{:S(2)}, u32[]{:S(2)}) collective-permute-start(bf16[32,3072]{1,0:T(8,128)(2,1)S(1)} %collective-permute-done.3.refs_1_.whole), channel_id=1, source_target_pairs={{0,1},{1,2},{2,3},{3,0},{4,5},{5,6},{6,7},{7,4},{8,9},{9,10},{10,1... | collective-permute-start | bytes 589832 | tf_op jit(solution)/shard_map/ppermute | solution.py:506
  24.9 0.0 collective-permute-done.7.refs_9_
  24.9 0.0 collective-permute-done.6.refs_7_
  24.9 0.0 collective-permute-done.5.refs_5_
  24.9 0.1 collective-permute-start.8
  25.0 0.5 %collective-permute-start.9 = (bf16[64,512]{1,0:T(8,128)(2,1)S(1)}, bf16[64,512]{1,0:T(8,128)(2,1)S(1)}, u32[]{:S(2)}, u32[]{:S(2)}) collective-permute-start(bf16[64,512]{1,0:T(8,128)(2,1)S(1)} %collective-permute-done.5.refs_5_), channel_id=1, source_target_pairs={{0,4},{4,0},{8,12},{12,8},{16,20},{20,16},{24,28},{28,24},{1,5},{5... | collective-permute-start | bytes 196616 | tf_op jit(solution)/shard_map/ppermute | solution.py:476
  25.5 0.1 collective-permute-start.10
  25.6 0.7 %collective-permute-done.8.refs_4_ = bf16[64,512]{1,0:T(8,128)(2,1)S(1)} collective-permute-done((bf16[64,512]{1,0:T(8,128)(2,1)S(1)}, bf16[64,512]{1,0:T(8,128)(2,1)S(1)}, u32[]{:S(2)}, u32[]{:S(2)}) %collective-permute-start.8) | collective-permute-done | bytes 65568 | tf_op jit(solution)/shard_map/ppermute | solution.py:476
  26.3 0.2 collective-permute-start.11
  26.4 0.3 collective-permute-done.10.refs_8_
  26.8 0.7 %collective-permute-done.11.refs_10_ = bf16[64,512]{1,0:T(8,128)(2,1)S(1)} collective-permute-done((bf16[64,512]{1,0:T(8,128)(2,1)S(1)}, bf16[64,512]{1,0:T(8,128)(2,1)S(1)}, u32[]{:S(2)}, u32[]{:S(2)}) %collective-permute-start.11) | collective-permute-done | bytes 65568 | tf_op jit(solution)/shard_map/ppermute | solution.py:476
  27.5 1.3 %collective-permute-done.4.refs_2_ = bf16[32,3072]{1,0:T(8,128)(2,1)S(1)} collective-permute-done((bf16[32,3072]{1,0:T(8,128)(2,1)S(1)}, bf16[32,3072]{1,0:T(8,128)(2,1)S(1)}, u32[]{:S(2)}, u32[]{:S(2)}) %collective-permute-start.4) | collective-permute-done | bytes 196640 | tf_op jit(solution)/shard_map/ppermute | solution.py:506
  28.8 0.8 %lead.1.refs_2_ = f32[80,640]{1,0:T(8,128)S(1)} custom-call(bf16[32,3072]{1,0:T(8,128)(2,1)S(1)} %collective-permute-done.2.refs_0_, bf16[32,3072]{1,0:T(8,128)(2,1)S(1)} %collective-permute-done.3.refs_1_.whole, bf16[32,3072]{1,0:T(8,128)(2,1)S(1)} %collective-permute-done.4.refs_2_, f32[2,6144]{1,0:T(2,128)S(1)} %get-tuple-element.73.refs_2_.refs_3_.gain.refs_4_, ...), custom_call_target="tpu_custom_call" | custom-call | tf_op jit(solution)/shard_map/lead/pallas_call | solution.py:257
  29.6 2.7 %collective-permute-done.12.piece.refs_3_ = bf16[32,3072]{1,0:T(8,128)(2,1)S(1)} collective-permute-done((bf16[32,3072]{1,0:T(8,128)(2,1)S(1)}, bf16[32,3072]{1,0:T(8,128)(2,1)S(1)}, u32[]{:S(2)}, u32[]{:S(2)}) %collective-permute-start.12) | collective-permute-done | bytes 196640 | tf_op jit(solution)/shard_map/ppermute | solution.py:506
  32.3 0.8 %finish.1.refs_0_ = bf16[64,512]{1,0:T(8,128)(2,1)S(1)} custom-call(bf16[32,3072]{1,0:T(8,128)(2,1)S(1)} %collective-permute-done.3.refs_1_.whole, bf16[32,3072]{1,0:T(8,128)(2,1)S(1)} %collective-permute-done.12.piece.refs_3_, f32[2,6144]{1,0:T(2,128)S(1)} %get-tuple-element.73.refs_2_.refs_3_.gain.refs_4_, ...), custom_call_target="tpu_custom_call" | custom-call | tf_op jit(solution)/shard_map/finish/pallas_call | solution.py:294
  33.1 2.5 %collective-permute-start.18 = (bf16[64,512]{1,0:T(8,128)(2,1)S(1)}, bf16[64,512]{1,0:T(8,128)(2,1)S(1)}, u32[]{:S(2)}, u32[]{:S(2)}) collective-permute-start(bf16[64,512]{1,0:T(8,128)(2,1)S(1)} %finish.1.refs_0_), channel_id=1, source_target_pairs={{0,24},{4,28},{8,16},{12,20},{16,8},{20,12},{24,0},{28,4},{1,25},{... | collective-permute-start | bytes 196616 | tf_op jit(solution)/shard_map/ppermute | solution.py:469
  35.7 0.5 %collective-permute-start.16 = (bf16[64,512]{1,0:T(8,128)(2,1)S(1)}, bf16[64,512]{1,0:T(8,128)(2,1)S(1)}, u32[]{:S(2)}, u32[]{:S(2)}) collective-permute-start(bf16[64,512]{1,0:T(8,128)(2,1)S(1)} %finish.1.refs_0_), channel_id=1, source_target_pairs={{0,16},{4,20},{8,24},{12,28},{16,0},{20,4},{24,8},{28,12},{1,17},{... | collective-permute-start | bytes 196616 | tf_op jit(solution)/shard_map/ppermute | solution.py:469
  36.2 0.5 %collective-permute-start.14 = (bf16[64,512]{1,0:T(8,128)(2,1)S(1)}, bf16[64,512]{1,0:T(8,128)(2,1)S(1)}, u32[]{:S(2)}, u32[]{:S(2)}) collective-permute-start(bf16[64,512]{1,0:T(8,128)(2,1)S(1)} %finish.1.refs_0_), channel_id=1, source_target_pairs={{0,8},{4,12},{8,0},{12,4},{16,24},{20,28},{24,16},{28,20},{1,9},{5... | collective-permute-start | bytes 196616 | tf_op jit(solution)/shard_map/ppermute | solution.py:469
  36.7 0.9 %project.3.refs_2_ = bf16[64,256]{1,0:T(8,128)(2,1)S(1)} custom-call(bf16[32,3072]{1,0:T(8,128)(2,1)S(1)} %collective-permute-done.2.refs_0_, bf16[32,3072]{1,0:T(8,128)(2,1)S(1)} %collective-permute-done.3.refs_1_.whole, bf16[32,3072]{1,0:T(8,128)(2,1)S(1)} %collective-permute-done.4.refs_2_, bf16[32,3072]{1,0:T(8,128)(2,1)S(1)} %collective-permute-done.12.piece.refs_3_, ...), custom_call_target="tpu_custom_call" | custom-call | tf_op jit(solution)/shard_map/project/pallas_call | solution.py:207
  37.6 0.5 %attend_early.1 = (bf16[128,256]{1,0:T(8,128)(2,1)S(1)}, f32[128,256]{1,0:T(8,128)S(1)}, f32[128,256]{1,0:T(8,128)S(1)}, f32[128,256]{1,0:T(8,128)S(1)}, f32[128,512]{1,0:T(8,128)S(1)}) custom-call(s32[1]{0:T(128)} %bitcast.1.mine, s32[1]{0:T(128)} %bitcast.place, s32[128,1]{1,0:T(8,128)S(1)} %get-tuple-element.55.seg_in, ...), custom_call_target="tpu_custom_call" | custom-call | tf_op jit(solution)/shard_map/attend_early/pallas_call | solution.py:383
  38.1 0.7 %collective-permute-done.18.refs_6_ = bf16[64,512]{1,0:T(8,128)(2,1)S(1)} collective-permute-done((bf16[64,512]{1,0:T(8,128)(2,1)S(1)}, bf16[64,512]{1,0:T(8,128)(2,1)S(1)}, u32[]{:S(2)}, u32[]{:S(2)}) %collective-permute-start.18) | collective-permute-done | bytes 65568 | tf_op jit(solution)/shard_map/ppermute | solution.py:469
  38.8 0.0 collective-permute-start.19
  38.9 1.1 %collective-permute-done.16.refs_4_ = bf16[64,512]{1,0:T(8,128)(2,1)S(1)} collective-permute-done((bf16[64,512]{1,0:T(8,128)(2,1)S(1)}, bf16[64,512]{1,0:T(8,128)(2,1)S(1)}, u32[]{:S(2)}, u32[]{:S(2)}) %collective-permute-start.16) | collective-permute-done | bytes 65568 | tf_op jit(solution)/shard_map/ppermute | solution.py:469
  39.9 0.5 %collective-permute-done.14.refs_2_ = bf16[64,512]{1,0:T(8,128)(2,1)S(1)} collective-permute-done((bf16[64,512]{1,0:T(8,128)(2,1)S(1)}, bf16[64,512]{1,0:T(8,128)(2,1)S(1)}, u32[]{:S(2)}, u32[]{:S(2)}) %collective-permute-start.14) | collective-permute-done | bytes 65568 | tf_op jit(solution)/shard_map/ppermute | solution.py:469
  40.4 0.0 collective-permute-start.15
  40.4 0.7 %collective-permute-done.17.refs_5_ = bf16[64,512]{1,0:T(8,128)(2,1)S(1)} collective-permute-done((bf16[64,512]{1,0:T(8,128)(2,1)S(1)}, bf16[64,512]{1,0:T(8,128)(2,1)S(1)}, u32[]{:S(2)}, u32[]{:S(2)}) %collective-permute-start.17) | collective-permute-done | bytes 65568 | tf_op jit(solution)/shard_map/ppermute | solution.py:476
  41.2 0.5 %collective-permute-done.15.refs_3_ = bf16[64,512]{1,0:T(8,128)(2,1)S(1)} collective-permute-done((bf16[64,512]{1,0:T(8,128)(2,1)S(1)}, bf16[64,512]{1,0:T(8,128)(2,1)S(1)}, u32[]{:S(2)}, u32[]{:S(2)}) %collective-permute-start.15) | collective-permute-done | bytes 65568 | tf_op jit(solution)/shard_map/ppermute | solution.py:476
  41.7 0.7 %attend.1 = (bf16[32,256]{1,0:T(8,128)(2,1)S(1)}, bf16[32,256]{1,0:T(8,128)(2,1)S(1)}, bf16[32,256]{1,0:T(8,128)(2,1)S(1)}, bf16[32,256]{1,0:T(8,128)(2,1)S(1)}) custom-call(bf16[128,256]{1,0:T(8,128)(2,1)S(1)} %get-tuple-element.82.q_all, f32[128,256]{1,0:T(8,128)S(1)} %get-tuple-element.83.sums, f32[128,256]{1,0:T(8,128)S(1)} %get-tuple-element.84.bests, ...), custom_call_target="tpu_custom_call" | custom-call | tf_op jit(solution)/shard_map/attend/pallas_call | solution.py:432
  42.3 0.6 %collective-permute-start.20 = (bf16[32,256]{1,0:T(8,128)(2,1)S(1)}, bf16[32,256]{1,0:T(8,128)(2,1)S(1)}, u32[]{:S(2)}, u32[]{:S(2)}) collective-permute-start(bf16[32,256]{1,0:T(8,128)(2,1)S(1)} %get-tuple-element.92), channel_id=1, source_target_pairs={{0,2},{1,3},{2,0},{3,1},{4,6},{5,7},{6,4},{7,5},{8,10},{9,11},{10,... | collective-permute-start | bytes 49160 | tf_op jit(solution)/shard_map/ppermute | solution.py:523
  42.9 1.8 %collective-permute-start.21 = (bf16[32,256]{1,0:T(8,128)(2,1)S(1)}, bf16[32,256]{1,0:T(8,128)(2,1)S(1)}, u32[]{:S(2)}, u32[]{:S(2)}) collective-permute-start(bf16[32,256]{1,0:T(8,128)(2,1)S(1)} %get-tuple-element.93), channel_id=1, source_target_pairs={{0,3},{1,2},{2,1},{3,0},{4,7},{5,6},{6,5},{7,4},{8,11},{9,10},{10,... | collective-permute-start | bytes 49160 | tf_op jit(solution)/shard_map/ppermute | solution.py:523
  44.7 1.2 %collective-permute-start.22 = (bf16[32,256]{1,0:T(8,128)(2,1)S(1)}, bf16[32,256]{1,0:T(8,128)(2,1)S(1)}, u32[]{:S(2)}, u32[]{:S(2)}) collective-permute-start(bf16[32,256]{1,0:T(8,128)(2,1)S(1)} %get-tuple-element.94), channel_id=1, source_target_pairs={{0,1},{1,0},{2,3},{3,2},{4,5},{5,4},{6,7},{7,6},{8,9},{9,8},{10,11... | collective-permute-start | bytes 49160 | tf_op jit(solution)/shard_map/ppermute | solution.py:523
  45.9 1.3 %collective-permute-done.20.refs_1_ = bf16[32,256]{1,0:T(8,128)(2,1)S(1)} collective-permute-done((bf16[32,256]{1,0:T(8,128)(2,1)S(1)}, bf16[32,256]{1,0:T(8,128)(2,1)S(1)}, u32[]{:S(2)}, u32[]{:S(2)}) %collective-permute-start.20) | collective-permute-done | bytes 16416 | tf_op jit(solution)/shard_map/ppermute | solution.py:523
  47.2 1.4 %collective-permute-done.21.refs_2_ = bf16[32,256]{1,0:T(8,128)(2,1)S(1)} collective-permute-done((bf16[32,256]{1,0:T(8,128)(2,1)S(1)}, bf16[32,256]{1,0:T(8,128)(2,1)S(1)}, u32[]{:S(2)}, u32[]{:S(2)}) %collective-permute-start.21) | collective-permute-done | bytes 16416 | tf_op jit(solution)/shard_map/ppermute | solution.py:523
  48.6 0.0 collective-permute-done.22.refs_3_
  48.6 0.6 %place.1 = bf16[1,32,1024]{2,1,0:T(8,128)(2,1)} custom-call(s32[1]{0:T(128)} %bitcast.place, bf16[32,256]{1,0:T(8,128)(2,1)S(1)} %get-tuple-element.91.refs_0_, bf16[32,256]{1,0:T(8,128)(2,1)S(1)} %collective-permute-done.20.refs_1_, bf16[32,256]{1,0:T(8,128)(2,1)S(1)} %collective-permute-done.21.refs_2_, bf16[32,256]{1,0:T(8,128)(2,1)S(1)} %collective-permute-done.22.refs_3_), custom_call_target="tpu_custom_call" | custom-call | tf_op jit(solution)/shard_map/place/pallas_call | solution.py:457
  (7 shorter events, 0.0 us)
Async XLA Ops:
  1.0 10.8 %collective-permute-start = (bf16[32,3072]{1,0:T(8,128)(2,1)S(1)}, bf16[32,3072]{1,0:T(8,128)(2,1)S(1)}, u32[]{:S(2)}, u32[]{:S(2)}) collective-permute-start(bf16[32,3072]{1,0:T(8,128)(2,1)S(1)} %get-tuple-element.53.refs_3_), channel_id=1, source_target_pairs={{0,1},{1,2},{2,3},{3,0},{4,5},{5,6},{6,7},{7,4},{8,9},{9,10},{10,1... | collective-permute-start | bytes 589832 | tf_op jit(solution)/shard_map/ppermute | solution.py:494
  4.1 11.1 %collective-permute-start.1 = (bf16[32,3072]{1,0:T(8,128)(2,1)S(1)}, bf16[32,3072]{1,0:T(8,128)(2,1)S(1)}, u32[]{:S(2)}, u32[]{:S(2)}) collective-permute-start(bf16[32,3072]{1,0:T(8,128)(2,1)S(1)} %get-tuple-element.54.refs_4_), channel_id=1, source_target_pairs={{0,1},{1,2},{2,3},{3,0},{4,5},{5,6},{6,7},{7,4},{8,9},{9,10},{10,1... | collective-permute-start | bytes 589832 | tf_op jit(solution)/shard_map/ppermute | solution.py:494
  11.9 8.8 %collective-permute-start.2 = (bf16[32,3072]{1,0:T(8,128)(2,1)S(1)}, bf16[32,3072]{1,0:T(8,128)(2,1)S(1)}, u32[]{:S(2)}, u32[]{:S(2)}) collective-permute-start(bf16[32,3072]{1,0:T(8,128)(2,1)S(1)} %collective-permute-done.refs_0_), channel_id=1, source_target_pairs={{0,1},{1,2},{2,3},{3,0},{4,5},{5,6},{6,7},{7,4},{8,9},{9,10},{10,1... | collective-permute-start | bytes 589832 | tf_op jit(solution)/shard_map/ppermute | solution.py:499
  15.3 9.0 %collective-permute-start.3 = (bf16[32,3072]{1,0:T(8,128)(2,1)S(1)}, bf16[32,3072]{1,0:T(8,128)(2,1)S(1)}, u32[]{:S(2)}, u32[]{:S(2)}) collective-permute-start(bf16[32,3072]{1,0:T(8,128)(2,1)S(1)} %collective-permute-done.1.refs_1_), channel_id=1, source_target_pairs={{0,1},{1,2},{2,3},{3,0},{4,5},{5,6},{6,7},{7,4},{8,9},{9,10},{10,1... | collective-permute-start | bytes 589832 | tf_op jit(solution)/shard_map/ppermute | solution.py:499
  17.1 7.8 %collective-permute-start.7 = (bf16[64,512]{1,0:T(8,128)(2,1)S(1)}, bf16[64,512]{1,0:T(8,128)(2,1)S(1)}, u32[]{:S(2)}, u32[]{:S(2)}) collective-permute-start(bf16[64,512]{1,0:T(8,128)(2,1)S(1)} %get-tuple-element.74.refs_3_), channel_id=1, source_target_pairs={{0,24},{4,28},{8,16},{12,20},{16,8},{20,12},{24,0},{28,4},{1,25},{... | collective-permute-start | bytes 196616 | tf_op jit(solution)/shard_map/ppermute | solution.py:469
  19.6 5.4 %collective-permute-start.6 = (bf16[64,512]{1,0:T(8,128)(2,1)S(1)}, bf16[64,512]{1,0:T(8,128)(2,1)S(1)}, u32[]{:S(2)}, u32[]{:S(2)}) collective-permute-start(bf16[64,512]{1,0:T(8,128)(2,1)S(1)} %get-tuple-element.74.refs_3_), channel_id=1, source_target_pairs={{0,16},{4,20},{8,24},{12,28},{16,0},{20,4},{24,8},{28,12},{1,17},{... | collective-permute-start | bytes 196616 | tf_op jit(solution)/shard_map/ppermute | solution.py:469
  20.1 4.8 %collective-permute-start.5 = (bf16[64,512]{1,0:T(8,128)(2,1)S(1)}, bf16[64,512]{1,0:T(8,128)(2,1)S(1)}, u32[]{:S(2)}, u32[]{:S(2)}) collective-permute-start(bf16[64,512]{1,0:T(8,128)(2,1)S(1)} %get-tuple-element.74.refs_3_), channel_id=1, source_target_pairs={{0,8},{4,12},{8,0},{12,4},{16,24},{20,28},{24,16},{28,20},{1,9},{5... | collective-permute-start | bytes 196616 | tf_op jit(solution)/shard_map/ppermute | solution.py:469
  20.6 8.1 %collective-permute-start.4 = (bf16[32,3072]{1,0:T(8,128)(2,1)S(1)}, bf16[32,3072]{1,0:T(8,128)(2,1)S(1)}, u32[]{:S(2)}, u32[]{:S(2)}) collective-permute-start(bf16[32,3072]{1,0:T(8,128)(2,1)S(1)} %collective-permute-done.2.refs_0_), channel_id=1, source_target_pairs={{0,1},{1,2},{2,3},{3,0},{4,5},{5,6},{6,7},{7,4},{8,9},{9,10},{10,1... | collective-permute-start | bytes 589832 | tf_op jit(solution)/shard_map/ppermute | solution.py:506
  24.3 8.1 %collective-permute-start.12 = (bf16[32,3072]{1,0:T(8,128)(2,1)S(1)}, bf16[32,3072]{1,0:T(8,128)(2,1)S(1)}, u32[]{:S(2)}, u32[]{:S(2)}) collective-permute-start(bf16[32,3072]{1,0:T(8,128)(2,1)S(1)} %collective-permute-done.3.refs_1_.whole), channel_id=1, source_target_pairs={{0,1},{1,2},{2,3},{3,0},{4,5},{5,6},{6,7},{7,4},{8,9},{9,10},{10,1... | collective-permute-start | bytes 589832 | tf_op jit(solution)/shard_map/ppermute | solution.py:506
  24.9 1.3 %collective-permute-start.8 = (bf16[64,512]{1,0:T(8,128)(2,1)S(1)}, bf16[64,512]{1,0:T(8,128)(2,1)S(1)}, u32[]{:S(2)}, u32[]{:S(2)}) collective-permute-start(bf16[64,512]{1,0:T(8,128)(2,1)S(1)} %get-tuple-element.74.refs_3_), channel_id=1, source_target_pairs={{0,4},{4,0},{8,12},{12,8},{16,20},{20,16},{24,28},{28,24},{1,5},{5... | collective-permute-start | bytes 196616 | tf_op jit(solution)/shard_map/ppermute | solution.py:476
  25.0 1.4 %collective-permute-start.9 = (bf16[64,512]{1,0:T(8,128)(2,1)S(1)}, bf16[64,512]{1,0:T(8,128)(2,1)S(1)}, u32[]{:S(2)}, u32[]{:S(2)}) collective-permute-start(bf16[64,512]{1,0:T(8,128)(2,1)S(1)} %collective-permute-done.5.refs_5_), channel_id=1, source_target_pairs={{0,4},{4,0},{8,12},{12,8},{16,20},{20,16},{24,28},{28,24},{1,5},{5... | collective-permute-start | bytes 196616 | tf_op jit(solution)/shard_map/ppermute | solution.py:476
  25.5 1.3 %collective-permute-start.10 = (bf16[64,512]{1,0:T(8,128)(2,1)S(1)}, bf16[64,512]{1,0:T(8,128)(2,1)S(1)}, u32[]{:S(2)}, u32[]{:S(2)}) collective-permute-start(bf16[64,512]{1,0:T(8,128)(2,1)S(1)} %collective-permute-done.6.refs_7_), channel_id=1, source_target_pairs={{0,4},{4,0},{8,12},{12,8},{16,20},{20,16},{24,28},{28,24},{1,5},{5... | collective-permute-start | bytes 196616 | tf_op jit(solution)/shard_map/ppermute | solution.py:476
  26.3 1.3 %collective-permute-start.11 = (bf16[64,512]{1,0:T(8,128)(2,1)S(1)}, bf16[64,512]{1,0:T(8,128)(2,1)S(1)}, u32[]{:S(2)}, u32[]{:S(2)}) collective-permute-start(bf16[64,512]{1,0:T(8,128)(2,1)S(1)} %collective-permute-done.7.refs_9_), channel_id=1, source_target_pairs={{0,4},{4,0},{8,12},{12,8},{16,20},{20,16},{24,28},{28,24},{1,5},{5... | collective-permute-start | bytes 196616 | tf_op jit(solution)/shard_map/ppermute | solution.py:476
  33.1 5.7 %collective-permute-start.18 = (bf16[64,512]{1,0:T(8,128)(2,1)S(1)}, bf16[64,512]{1,0:T(8,128)(2,1)S(1)}, u32[]{:S(2)}, u32[]{:S(2)}) collective-permute-start(bf16[64,512]{1,0:T(8,128)(2,1)S(1)} %finish.1.refs_0_), channel_id=1, source_target_pairs={{0,24},{4,28},{8,16},{12,20},{16,8},{20,12},{24,0},{28,4},{1,25},{... | collective-permute-start | bytes 196616 | tf_op jit(solution)/shard_map/ppermute | solution.py:469
  35.7 4.3 %collective-permute-start.16 = (bf16[64,512]{1,0:T(8,128)(2,1)S(1)}, bf16[64,512]{1,0:T(8,128)(2,1)S(1)}, u32[]{:S(2)}, u32[]{:S(2)}) collective-permute-start(bf16[64,512]{1,0:T(8,128)(2,1)S(1)} %finish.1.refs_0_), channel_id=1, source_target_pairs={{0,16},{4,20},{8,24},{12,28},{16,0},{20,4},{24,8},{28,12},{1,17},{... | collective-permute-start | bytes 196616 | tf_op jit(solution)/shard_map/ppermute | solution.py:469
  36.2 4.3 %collective-permute-start.14 = (bf16[64,512]{1,0:T(8,128)(2,1)S(1)}, bf16[64,512]{1,0:T(8,128)(2,1)S(1)}, u32[]{:S(2)}, u32[]{:S(2)}) collective-permute-start(bf16[64,512]{1,0:T(8,128)(2,1)S(1)} %finish.1.refs_0_), channel_id=1, source_target_pairs={{0,8},{4,12},{8,0},{12,4},{16,24},{20,28},{24,16},{28,20},{1,9},{5... | collective-permute-start | bytes 196616 | tf_op jit(solution)/shard_map/ppermute | solution.py:469
  36.7 3.7 %collective-permute-start.13 = (bf16[64,512]{1,0:T(8,128)(2,1)S(1)}, bf16[64,512]{1,0:T(8,128)(2,1)S(1)}, u32[]{:S(2)}, u32[]{:S(2)}) collective-permute-start(bf16[64,512]{1,0:T(8,128)(2,1)S(1)} %finish.1.refs_0_), channel_id=1, source_target_pairs={{0,4},{4,0},{8,12},{12,8},{16,20},{20,16},{24,28},{28,24},{1,5},{5... | collective-permute-start | bytes 196616 | tf_op jit(solution)/shard_map/ppermute | solution.py:476
  38.8 1.6 %collective-permute-start.19 = (bf16[64,512]{1,0:T(8,128)(2,1)S(1)}, bf16[64,512]{1,0:T(8,128)(2,1)S(1)}, u32[]{:S(2)}, u32[]{:S(2)}) collective-permute-start(bf16[64,512]{1,0:T(8,128)(2,1)S(1)} %collective-permute-done.18.refs_6_), channel_id=1, source_target_pairs={{0,4},{4,0},{8,12},{12,8},{16,20},{20,16},{24,28},{28,24},{1,5},{5... | collective-permute-start | bytes 196616 | tf_op jit(solution)/shard_map/ppermute | solution.py:476
  39.9 1.3 %collective-permute-start.17 = (bf16[64,512]{1,0:T(8,128)(2,1)S(1)}, bf16[64,512]{1,0:T(8,128)(2,1)S(1)}, u32[]{:S(2)}, u32[]{:S(2)}) collective-permute-start(bf16[64,512]{1,0:T(8,128)(2,1)S(1)} %collective-permute-done.16.refs_4_), channel_id=1, source_target_pairs={{0,4},{4,0},{8,12},{12,8},{16,20},{20,16},{24,28},{28,24},{1,5},{5... | collective-permute-start | bytes 196616 | tf_op jit(solution)/shard_map/ppermute | solution.py:476
  40.4 1.3 %collective-permute-start.15 = (bf16[64,512]{1,0:T(8,128)(2,1)S(1)}, bf16[64,512]{1,0:T(8,128)(2,1)S(1)}, u32[]{:S(2)}, u32[]{:S(2)}) collective-permute-start(bf16[64,512]{1,0:T(8,128)(2,1)S(1)} %collective-permute-done.14.refs_2_), channel_id=1, source_target_pairs={{0,4},{4,0},{8,12},{12,8},{16,20},{20,16},{24,28},{28,24},{1,5},{5... | collective-permute-start | bytes 196616 | tf_op jit(solution)/shard_map/ppermute | solution.py:476
  42.3 4.8 %collective-permute-start.20 = (bf16[32,256]{1,0:T(8,128)(2,1)S(1)}, bf16[32,256]{1,0:T(8,128)(2,1)S(1)}, u32[]{:S(2)}, u32[]{:S(2)}) collective-permute-start(bf16[32,256]{1,0:T(8,128)(2,1)S(1)} %get-tuple-element.92), channel_id=1, source_target_pairs={{0,2},{1,3},{2,0},{3,1},{4,6},{5,7},{6,4},{7,5},{8,10},{9,11},{10,... | collective-permute-start | bytes 49160 | tf_op jit(solution)/shard_map/ppermute | solution.py:523
  42.9 5.6 %collective-permute-start.21 = (bf16[32,256]{1,0:T(8,128)(2,1)S(1)}, bf16[32,256]{1,0:T(8,128)(2,1)S(1)}, u32[]{:S(2)}, u32[]{:S(2)}) collective-permute-start(bf16[32,256]{1,0:T(8,128)(2,1)S(1)} %get-tuple-element.93), channel_id=1, source_target_pairs={{0,3},{1,2},{2,1},{3,0},{4,7},{5,6},{6,5},{7,4},{8,11},{9,10},{10,... | collective-permute-start | bytes 49160 | tf_op jit(solution)/shard_map/ppermute | solution.py:523
  44.7 3.9 %collective-permute-start.22 = (bf16[32,256]{1,0:T(8,128)(2,1)S(1)}, bf16[32,256]{1,0:T(8,128)(2,1)S(1)}, u32[]{:S(2)}, u32[]{:S(2)}) collective-permute-start(bf16[32,256]{1,0:T(8,128)(2,1)S(1)} %get-tuple-element.94), channel_id=1, source_target_pairs={{0,1},{1,0},{2,3},{3,2},{4,5},{5,4},{6,7},{7,6},{8,9},{9,8},{10,11... | collective-permute-start | bytes 49160 | tf_op jit(solution)/shard_map/ppermute | solution.py:523
